TPU v7x, 32 devices: a whole 2x2x4 slice. The times are simulated.
32 devices in a mesh: replica: 8 (over z, core), fsdp: 4 (over y, x).
Axes of the slice: x: 2, y: 2, z: 4, core: 2. Of those that a mesh axis runs over, the one named last changes fastest.
Arguments:
- hidden_in: bfloat16 [8192, 1152], P(('replica', 'fsdp')), may hold values from -6 to 6
- out_grad: bfloat16 [8192, 1152], P(('replica', 'fsdp')), may hold values from -6 to 6
- segments: int32 [8192], P('replica'), may hold values from 0 to 3, as said below
- positions: int32 [8192], P(('replica', 'fsdp')), may hold values from 0 to 8191, as said below
- norm_in: bfloat16 [1152], P('fsdp'), may hold values from 0.25 to 1.75
- query_weight: bfloat16 [1152, 1024], P('fsdp'), may hold values from -0.1875 to 0.1875
- key_weight: bfloat16 [1152, 256], P('fsdp'), may hold values from -0.1875 to 0.1875
- value_weight: bfloat16 [1152, 256], P('fsdp'), may hold values from -0.1875 to 0.1875
- out_weight: bfloat16 [1152, 1024], P('fsdp'), may hold values from -0.1875 to 0.1875
- norm_attn: bfloat16 [1152], P('fsdp'), may hold values from 0.25 to 1.75
- norm_ffn: bfloat16 [1152], P('fsdp'), may hold values from 0.25 to 1.75
- gate_weight: bfloat16 [6912, 1152], P('fsdp'), may hold values from -0.1875 to 0.1875
- up_weight: bfloat16 [6912, 1152], P('fsdp'), may hold values from -0.1875 to 0.1875
- down_weight: bfloat16 [6912, 1152], P('fsdp'), may hold values from -0.078125 to 0.078125
- norm_out: bfloat16 [1152], P('fsdp'), may hold values from 0.25 to 1.75
- query_gain: bfloat16 [256], P('fsdp'), may hold values from 0.25 to 1.75
- key_gain: bfloat16 [256], P('fsdp'), may hold values from 0.25 to 1.75
Outputs:
- hidden_out: bfloat16 [8192, 1152], P(('replica', 'fsdp'))
- grad_in: float32 [8192, 1152], P(('replica', 'fsdp'))
- grad_norm_in: float32 [1152], P('fsdp')
- grad_query_weight: float32 [1152, 1024], P('fsdp')
- grad_key_weight: float32 [1152, 256], P('fsdp')
- grad_value_weight: float32 [1152, 256], P('fsdp')
- grad_out_weight: float32 [1152, 1024], P('fsdp')
- grad_norm_attn: float32 [1152], P('fsdp')
- grad_norm_ffn: float32 [1152], P('fsdp')
- grad_gate_weight: float32 [6912, 1152], P('fsdp')
- grad_up_weight: float32 [6912, 1152], P('fsdp')
- grad_down_weight: float32 [6912, 1152], P('fsdp')
- grad_norm_out: float32 [1152], P('fsdp')
- grad_query_gain: float32 [256], P('fsdp')
- grad_key_gain: float32 [256], P('fsdp')
Inputs may be any that keep to these rules, and one draw needn't show every extreme that they name: `segments`: within each sequence of 1024 tokens the numbers never fall; every sequence begins in document 0 and ends in document 3. `positions`: within a document the position rises by one from token to token; document 0 of every sequence starts at 0 and the last document of every sequence ends at 8191.
All inputs are finite; a program needn't handle non-finite values.
Results may differ from a plain program's by a relative error of at most 0.025.
Values may be sent and summed in bfloat16 or wider, within the bound.
No kernel may reach another device: no remote copies, remote signals or barrier semaphores. Data moves between devices by JAX's collectives and lax.ppermute only.
A program may use at most 192 MiB of HBM per device.

v0:
```python
import jax
import jax.numpy as jnp
from jax import lax
from jax.sharding import PartitionSpec as P

WINDOW = 512


EPS = 1e-06
NEG = -1e30


def passed_along(block, axis, distance):
    devices = range(lax.axis_size(axis))
    route = [(i - distance, i) for i in devices if i - distance in devices]
    return lax.ppermute(block, axis, route)


def contract(left, right, left_dim, right_dim):
    return lax.dot_general(
        left, right, (((left_dim,), (right_dim,)), ((), ())), preferred_element_type=jnp.float32
    )


def normed(value, gain):
    return value * lax.rsqrt(jnp.mean(value * value, axis=-1, keepdims=True) + EPS) * gain


def norm_back(value, gain, grad):
    _, pull = jax.vjp(normed, value, gain)
    return pull(grad)


def tables(places, half):
    freq = 10000.0 ** (-(2.0 * jnp.arange(half, dtype=jnp.float32)) / (2 * half))
    angle = places.astype(jnp.float32)[:, None] * freq[None, :]
    return (jnp.cos(angle), jnp.sin(angle))


def rotate(value, cosine, sine):
    half = value.shape[-1] // 2
    first = value[..., :half]
    second = value[..., half:]
    return jnp.concatenate(
        [first * cosine - second * sine, second * cosine + first * sine], axis=-1
    )


def head_post(raw, gain, cosine, sine):
    return rotate(normed(raw, gain), cosine, sine)


def gated(gate, upper):
    return jax.nn.gelu(gate, approximate=True) * upper


def gated_back(gate, upper, grad):
    _, pull = jax.vjp(gated, gate, upper)
    grad_gate, grad_upper = pull(grad)
    return (grad_gate.astype(jnp.bfloat16), grad_upper.astype(jnp.bfloat16))


def per_device(
    hidden_in,
    out_grad,
    segments,
    positions,
    norm_in,
    query_weight,
    key_weight,
    value_weight,
    out_weight,
    norm_attn,
    norm_ffn,
    gate_weight,
    up_weight,
    down_weight,
    norm_out,
    query_gain,
    key_gain,
):
    rows = hidden_in.shape[0]
    rank = lax.axis_index("fsdp")
    head_size = key_weight.shape[1]
    heads = query_weight.shape[1] // head_size
    hops = (WINDOW - 1) // rows + 1
    scale = head_size ** (-0.5)
    gain_in, w_query, w_key, w_value, w_out, gain_attn, gain_ffn, gain_out, gain_query, gain_key = (
        lax.all_gather(norm_in, "fsdp", axis=0, tiled=True),
        lax.all_gather(query_weight, "fsdp", axis=0, tiled=True),
        lax.all_gather(key_weight, "fsdp", axis=0, tiled=True),
        lax.all_gather(value_weight, "fsdp", axis=0, tiled=True),
        lax.all_gather(out_weight, "fsdp", axis=0, tiled=True),
        lax.all_gather(norm_attn, "fsdp", axis=0, tiled=True),
        lax.all_gather(norm_ffn, "fsdp", axis=0, tiled=True),
        lax.all_gather(norm_out, "fsdp", axis=0, tiled=True),
        lax.all_gather(query_gain, "fsdp", axis=0, tiled=True),
        lax.all_gather(key_gain, "fsdp", axis=0, tiled=True),
    )
    residual_in = hidden_in.astype(jnp.float32)
    normed_in = normed(residual_in, gain_in).astype(jnp.bfloat16)
    query_raw = jnp.dot(normed_in, w_query, preferred_element_type=jnp.float32).reshape(
        rows, heads, head_size
    )
    key_raw = jnp.dot(normed_in, w_key, preferred_element_type=jnp.float32)
    value_new = jnp.dot(normed_in, w_value, preferred_element_type=jnp.float32).astype(jnp.bfloat16)
    cosine, sine = tables(positions, head_size // 2)
    cosine_heads = cosine[:, None, :]
    sine_heads = sine[:, None, :]
    query_new = head_post(query_raw, gain_query, cosine_heads, sine_heads).astype(jnp.bfloat16)
    key_new = head_post(key_raw, gain_key, cosine, sine).astype(jnp.bfloat16)
    key_parts = [key_new]
    value_parts = [value_new]
    for step in range(1, hops + 1):
        key_far, value_far = passed_along((key_new, value_new), "fsdp", step)
        key_parts.insert(0, key_far)
        value_parts.insert(0, value_far)
    keys = jnp.concatenate(key_parts, axis=0)
    values = jnp.concatenate(value_parts, axis=0)
    width = keys.shape[0]
    seg_padded = jnp.concatenate([jnp.full((hops * rows,), -1, jnp.int32), segments], axis=0)
    key_segs = lax.dynamic_slice_in_dim(seg_padded, rank * rows, width, 0)
    query_segs = lax.dynamic_slice_in_dim(segments, rank * rows, rows, 0)
    gap = hops * rows + jnp.arange(rows)[:, None] - jnp.arange(width)[None, :]
    allowed = (gap >= 0) & (gap < WINDOW) & (query_segs[:, None] == key_segs[None, :])
    query_rows = query_new.reshape(rows * heads, head_size)

    def scores_of():
        raw_scores = (contract(query_rows, keys, 1, 1) * scale).reshape(rows, heads, width)
        return jnp.where(allowed[:, None, :], raw_scores, NEG)

    scores = scores_of()
    highest = jnp.max(scores, axis=-1, keepdims=True)
    expo = jnp.exp(scores - highest)
    weight_sum = jnp.sum(expo, axis=-1, keepdims=True)
    probs = expo / weight_sum
    log_total = highest + jnp.log(weight_sum)
    probs_low = probs.astype(jnp.bfloat16).reshape(rows * heads, width)
    mixed = (
        jnp.dot(probs_low, values, preferred_element_type=jnp.float32)
        .reshape(rows, heads * head_size)
        .astype(jnp.bfloat16)
    )
    attended = contract(mixed, w_out, 1, 1)
    resid = residual_in + normed(attended, gain_attn)
    ffn_in = normed(resid, gain_ffn).astype(jnp.bfloat16)
    ffn_rows = lax.all_gather(ffn_in, "fsdp", axis=0, tiled=True)
    gate = contract(ffn_rows, gate_weight, 1, 1)
    upper = contract(ffn_rows, up_weight, 1, 1)
    hidden = gated(gate, upper).astype(jnp.bfloat16)
    branch = lax.psum_scatter(
        jnp.dot(hidden, down_weight, preferred_element_type=jnp.float32).astype(jnp.bfloat16),
        "fsdp",
        scatter_dimension=0,
        tiled=True,
    ).astype(jnp.float32)
    result = resid + normed(branch, gain_out)
    hidden_out = result.astype(jnp.bfloat16)
    grad_result = out_grad.astype(jnp.float32)
    grad_branch, grad_gain_out = norm_back(branch, gain_out, grad_result)
    grad_branch_low = grad_branch.astype(jnp.bfloat16)
    piece = lax.all_gather(grad_branch_low, "fsdp", axis=0, tiled=True)
    down_sum = contract(hidden, piece, 0, 0)
    grad_hidden = contract(piece, down_weight, 1, 1)
    grad_down, grad_hidden = (down_sum, grad_hidden)
    grad_gate, grad_upper = gated_back(gate, upper, grad_hidden)
    grad_gate_w = contract(grad_gate, ffn_rows, 0, 0)
    grad_up_w = contract(grad_upper, ffn_rows, 0, 0)
    grad_ffn_in = lax.psum_scatter(
        (
            jnp.dot(grad_gate, gate_weight, preferred_element_type=jnp.float32)
            + jnp.dot(grad_upper, up_weight, preferred_element_type=jnp.float32)
        ).astype(jnp.bfloat16),
        "fsdp",
        scatter_dimension=0,
        tiled=True,
    ).astype(jnp.float32)
    grad_resid_part, grad_gain_ffn = norm_back(resid, gain_ffn, grad_ffn_in)
    grad_resid = grad_result + grad_resid_part
    grad_attended, grad_gain_attn = norm_back(attended, gain_attn, grad_resid)
    grad_attended_low = grad_attended.astype(jnp.bfloat16)
    grad_wout = contract(grad_attended_low, mixed, 0, 0)
    grad_mixed = jnp.dot(grad_attended_low, w_out, preferred_element_type=jnp.float32).astype(
        jnp.bfloat16
    )
    grad_mixed_rows = grad_mixed.reshape(rows * heads, head_size)
    scores = scores_of()
    probs = jnp.exp(scores - log_total)
    probs_low = probs.astype(jnp.bfloat16).reshape(rows * heads, width)
    grad_probs = contract(grad_mixed_rows, values, 1, 1).reshape(rows, heads, width)
    delta = jnp.sum(grad_probs * probs, axis=-1, keepdims=True)
    grad_scores = (probs * (grad_probs - delta)).astype(jnp.bfloat16).reshape(rows * heads, width)
    grad_query = (jnp.dot(grad_scores, keys, preferred_element_type=jnp.float32) * scale).reshape(
        rows, heads, head_size
    )
    grad_keys = contract(grad_scores, query_rows, 0, 0) * scale
    grad_values = contract(probs_low, grad_mixed_rows, 0, 0)
    grad_key = grad_keys[hops * rows :]
    grad_value = grad_values[hops * rows :]
    for step in range(1, hops + 1):
        lower = (hops - step) * rows
        back_key, back_value = (
            passed_along(
                grad_keys[lower : lower + rows].astype(jnp.bfloat16), "fsdp", -step
            ).astype(jnp.float32),
            passed_along(
                grad_values[lower : lower + rows].astype(jnp.bfloat16), "fsdp", -step
            ).astype(jnp.float32),
        )
        grad_key = grad_key + back_key
        grad_value = grad_value + back_value
    _, pull_query = jax.vjp(
        lambda raw, gain: head_post(raw, gain, cosine_heads, sine_heads), query_raw, gain_query
    )
    grad_query_raw, grad_gain_query = pull_query(grad_query)
    _, pull_key = jax.vjp(lambda raw, gain: head_post(raw, gain, cosine, sine), key_raw, gain_key)
    grad_key_raw, grad_gain_key = pull_key(grad_key)
    grad_query_low = grad_query_raw.reshape(rows, heads * head_size).astype(jnp.bfloat16)
    grad_key_low = grad_key_raw.astype(jnp.bfloat16)
    grad_value_low = grad_value.astype(jnp.bfloat16)
    grad_wquery = contract(normed_in, grad_query_low, 0, 0)
    grad_wkey = contract(normed_in, grad_key_low, 0, 0)
    grad_wvalue = contract(normed_in, grad_value_low, 0, 0)
    grad_normed_in = (
        contract(grad_query_low, w_query, 1, 1)
        + contract(grad_key_low, w_key, 1, 1)
        + contract(grad_value_low, w_value, 1, 1)
    )
    grad_input_part, grad_gain_in = norm_back(residual_in, gain_in, grad_normed_in)
    grad_in = grad_resid + grad_input_part
    (
        owned_gain_in,
        owned_query,
        owned_key,
        owned_value,
        owned_out,
        owned_gain_attn,
        owned_gain_ffn,
        owned_gain_out,
        owned_gain_query,
        owned_gain_key,
    ) = (
        lax.psum_scatter(grad_gain_in, "fsdp", scatter_dimension=0, tiled=True).astype(jnp.float32),
        lax.psum_scatter(
            grad_wquery.astype(jnp.bfloat16), "fsdp", scatter_dimension=0, tiled=True
        ).astype(jnp.float32),
        lax.psum_scatter(
            grad_wkey.astype(jnp.bfloat16), "fsdp", scatter_dimension=0, tiled=True
        ).astype(jnp.float32),
        lax.psum_scatter(
            grad_wvalue.astype(jnp.bfloat16), "fsdp", scatter_dimension=0, tiled=True
        ).astype(jnp.float32),
        lax.psum_scatter(
            grad_wout.astype(jnp.bfloat16), "fsdp", scatter_dimension=0, tiled=True
        ).astype(jnp.float32),
        lax.psum_scatter(grad_gain_attn, "fsdp", scatter_dimension=0, tiled=True).astype(
            jnp.float32
        ),
        lax.psum_scatter(grad_gain_ffn, "fsdp", scatter_dimension=0, tiled=True).astype(
            jnp.float32
        ),
        lax.psum_scatter(grad_gain_out, "fsdp", scatter_dimension=0, tiled=True).astype(
            jnp.float32
        ),
        lax.psum_scatter(grad_gain_query, "fsdp", scatter_dimension=0, tiled=True).astype(
            jnp.float32
        ),
        lax.psum_scatter(grad_gain_key, "fsdp", scatter_dimension=0, tiled=True).astype(
            jnp.float32
        ),
    )
    (
        owned_gain_in,
        owned_query,
        owned_key,
        owned_value,
        owned_out,
        owned_gain_attn,
        owned_gain_ffn,
        owned_gain_out,
        owned_gain_query,
        owned_gain_key,
        grad_gate_w,
        grad_up_w,
        grad_down,
    ) = (
        lax.psum(owned_gain_in.astype(jnp.bfloat16), "replica").astype(jnp.float32),
        lax.psum(owned_query.astype(jnp.bfloat16), "replica").astype(jnp.float32),
        lax.psum(owned_key.astype(jnp.bfloat16), "replica").astype(jnp.float32),
        lax.psum(owned_value.astype(jnp.bfloat16), "replica").astype(jnp.float32),
        lax.psum(owned_out.astype(jnp.bfloat16), "replica").astype(jnp.float32),
        lax.psum(owned_gain_attn.astype(jnp.bfloat16), "replica").astype(jnp.float32),
        lax.psum(owned_gain_ffn.astype(jnp.bfloat16), "replica").astype(jnp.float32),
        lax.psum(owned_gain_out.astype(jnp.bfloat16), "replica").astype(jnp.float32),
        lax.psum(owned_gain_query.astype(jnp.bfloat16), "replica").astype(jnp.float32),
        lax.psum(owned_gain_key.astype(jnp.bfloat16), "replica").astype(jnp.float32),
        lax.psum(grad_gate_w.astype(jnp.bfloat16), "replica").astype(jnp.float32),
        lax.psum(grad_up_w.astype(jnp.bfloat16), "replica").astype(jnp.float32),
        lax.psum(grad_down.astype(jnp.bfloat16), "replica").astype(jnp.float32),
    )
    return (
        hidden_out,
        grad_in,
        owned_gain_in,
        owned_query,
        owned_key,
        owned_value,
        owned_out,
        owned_gain_attn,
        owned_gain_ffn,
        grad_gate_w,
        grad_up_w,
        grad_down,
        owned_gain_out,
        owned_gain_query,
        owned_gain_key,
    )


def solution(mesh):
    return jax.shard_map(
        per_device,
        mesh=mesh,
        in_specs=(
            P(("replica", "fsdp"), None),
            P(("replica", "fsdp"), None),
            P("replica"),
            P(("replica", "fsdp")),
            P("fsdp"),
            P("fsdp", None),
            P("fsdp", None),
            P("fsdp", None),
            P("fsdp", None),
            P("fsdp"),
            P("fsdp"),
            P("fsdp", None),
            P("fsdp", None),
            P("fsdp", None),
            P("fsdp"),
            P("fsdp"),
            P("fsdp"),
        ),
        out_specs=(
            P(("replica", "fsdp"), None),
            P(("replica", "fsdp"), None),
            P("fsdp"),
            P("fsdp", None),
            P("fsdp", None),
            P("fsdp", None),
            P("fsdp", None),
            P("fsdp"),
            P("fsdp"),
            P("fsdp", None),
            P("fsdp", None),
            P("fsdp", None),
            P("fsdp"),
            P("fsdp"),
            P("fsdp"),
        ),
        check_vma=False,
    )
```

profile of v0, /device:TPU:0, one launch (start us, length us, event | category | flops | bytes accessed | tf_op | source)
XLA Modules:
  0.0 792.4 jit_solution(15216172391201405100)
XLA Ops:
  16.6 18.8 %all-reduce.20 = (bf16[1152]{0:T(1024)(128)(2,1)S(1)}, bf16[256]{0:T(256)(128)(2,1)S(1)}, bf16[256]{0:T(256)(128)(2,1)S(1)}, bf16[1152]{0:T(1024)(128)(2,1)S(1)}...) all-reduce(bf16[1152]{0:T(1024)(128)(2,1)S(1)} %dynamic-update-slic, ...), channel_id=1, replica_groups=mesh['replica'=8,'fsdp'=4] {'fsdp'}, use_global_device_ids=true, to_apply=%add.5 | all-reduce | flops 5120 | bytes 20480
  36.7 15.1 %all_gather.39 = bf16[1152,256]{1,0:T(8,128)(2,1)S(1)} all-gather(bf16[288,256]{1,0:T(8,128)(2,1)} %param.23), channel_id=1, replica_groups=mesh['replica'=8,'fsdp'=4] {'fsdp'}, dimensions={0}, use_global_device_ids=true | all-gather | bytes 737280 | tf_op jit(solution)/shard_map/all_gather | solution.py:91
  54.5 3.7 collective-permute-start
  58.2 3.4 collective-permute-start.1
  61.7 13.0 %all_gather.41 = bf16[1152,256]{1,0:T(8,128)(2,1)S(1)} all-gather(bf16[288,256]{1,0:T(8,128)(2,1)S(1)} %copy-done.42), channel_id=1, replica_groups=mesh['replica'=8,'fsdp'=4] {'fsdp'}, dimensions={0}, use_global_device_ids=true | all-gather | bytes 737280 | tf_op jit(solution)/shard_map/all_gather | solution.py:92
  75.7 5.3 collective-permute-start.2
  106.6 37.6 %all-gather.9.cloned.1.call-done = bf16[1024,1152]{1,0:T(8,128)(2,1)} async-done(((bf16[256,1152]{1,0:T(8,128)(2,1)}), bf16[1024,1152]{1,0:T(8,128)(2,1)}) %all-gather.9.cloned.1.call-update) | async-done | bytes 2359312 | tf_op jit(solution)/shard_map/all_gather | solution.py:147
  144.2 7.4 fusion.98
  151.6 7.8 multiply_convert_fusion.1
  161.2 6.3 convolution_convert_fusion.5
  168.9 36.2 %reduce-scatter.7.cloned.1.call-done = bf16[256,1152]{1,0:T(8,128)(2,1)} async-done(((bf16[1024,1152]{1,0:T(8,128)(2,1)}), bf16[256,1152]{1,0:T(8,128)(2,1)}) %reduce-scatter.7.cloned.1.call-update) | async-done | bytes 589840 | tf_op jit(solution)/shard_map/reduce_scatter | solution.py:151
  211.6 37.2 %all-gather.11.cloned.1.call-done = bf16[1024,1152]{1,0:T(8,128)(2,1)} async-done(((bf16[256,1152]{1,0:T(8,128)(2,1)}), bf16[1024,1152]{1,0:T(8,128)(2,1)}) %all-gather.11.cloned.1.call-update) | async-done | bytes 2359312 | tf_op jit(solution)/shard_map/all_gather | solution.py:162
  248.8 14.8 %multiply_convert_fusion = (bf16[1024,1728]{0,1:T(8,128)(2,1)S(1)}, bf16[1024,1728]{0,1:T(8,128)(2,1)S(1)}) fusion(f32[1024,1728]{0,1:T(8,128)} %copy-done.86, f32[1024,1728]{0,1:T(8,128)} %get-tuple-element.83, bf16[1024,1152]{1,0:T(8,128)(2,1)} %all-gather.11.cloned.1.call-done, bf16[1728,1152]{1,0:T(8,128)(2,1)} %param.30), kind=kOutput, calls=%fused_computation.12 | convolution fusion | flops 4119330816 | bytes 27574272 | tf_op jit(solution)/shard_map/dot_general | solution.py:20
  263.7 5.2 fusion.99
  268.9 6.5 add_convert_fusion
  275.6 4.8 reshape.317
  284.7 28.2 %reduce-scatter.9.cloned.1.call-done = bf16[256,1152]{1,0:T(8,128)(2,1)} async-done(((bf16[1024,1152]{1,0:T(8,128)(2,1)}), bf16[256,1152]{1,0:T(8,128)(2,1)}) %reduce-scatter.9.cloned.1.call-update) | async-done | bytes 589840 | tf_op jit(solution)/shard_map/reduce_scatter | solution.py:169
  315.6 3.8 multiply_reduce_fusion.1
  323.5 3.9 multiply_reduce_fusion
  342.0 3.0 convolution_multiply_fusion.1
  364.8 9.7 %convolution_convert_fusion = bf16[1728,1152]{1,0:T(8,128)(2,1)} fusion(bf16[1024,1728]{0,1:T(8,128)(2,1)} %copy-done.85, bf16[1024,1152]{1,0:T(8,128)(2,1)} %all-gather.11.cloned.1.call-done), kind=kOutput, calls=%fused_computation.2 | convolution fusion | flops 4078854144 | bytes 9879552 | tf_op jit(solution)/shard_map/dot_general | solution.py:20
  374.4 6.2 convolution_convert_fusion.1
  380.7 6.2 convolution_convert_fusion.2
  386.9 23.5 %reduce-scatter.13.cloned.1.call-done = bf16[288,256]{1,0:T(8,128)(2,1)} async-done(((bf16[1152,256]{1,0:T(8,128)(2,1)}), bf16[288,256]{1,0:T(8,128)(2,1)}) %reduce-scatter.13.cloned.1.call-update) | async-done | bytes 147472 | tf_op jit(solution)/shard_map/reduce_scatter | solution.py:247
  410.4 40.5 %reduce-scatter.11.cloned.1.call-done = bf16[288,1024]{1,0:T(8,128)(2,1)} async-done(((bf16[1152,1024]{1,0:T(8,128)(2,1)}), bf16[288,1024]{1,0:T(8,128)(2,1)}) %reduce-scatter.11.cloned.1.call-update) | async-done | bytes 589840 | tf_op jit(solution)/shard_map/reduce_scatter | solution.py:244
  450.8 40.3 %reduce-scatter.17.cloned.1.call-done = bf16[288,1024]{1,0:T(8,128)(2,1)} async-done(((bf16[1152,1024]{1,0:T(8,128)(2,1)}), bf16[288,1024]{1,0:T(8,128)(2,1)}) %reduce-scatter.17.cloned.1.call-update) | async-done | bytes 589840 | tf_op jit(solution)/shard_map/reduce_scatter | solution.py:253
  497.8 15.2 %all-reduce.19 = (bf16[1152]{0:T(1024)(128)(2,1)S(1)}, bf16[1152]{0:T(1024)(128)(2,1)S(1)}, bf16[1152]{0:T(1024)(128)(2,1)S(1)}, bf16[1152]{0:T(1024)(128)(2,1)S...) all-reduce(bf16[1152]{0:T(1024)(128)(2,1)S(1)} %get-tuple-element.2, ...), channel_id=4, replica_groups=mesh['replica'=8,'fsdp'=4] {'fsdp'}, use_global_device_ids=true, to_apply=%region_18.19.clone | all-reduce | flops 5120 | bytes 20480
  513.5 14.9 %all-reduce.17 = (bf16[288]{0:T(512)(128)(2,1)S(1)}, bf16[288]{0:T(512)(128)(2,1)S(1)}, bf16[288]{0:T(512)(128)(2,1)S(1)}, bf16[288]{0:T(512)(128)(2,1)S(1)}, bf...) all-reduce(bf16[288]{0:T(512)(128)(2,1)S(1)} %dynamic-slice.7, ...), channel_id=1, replica_groups=mesh['replica'=8,'fsdp'=4] {'replica'}, use_global_device_ids=true, to_apply=%region_19.20 | all-reduce | flops 1280 | bytes 5120 | tf_op jit(solution)/shard_map/psum | solution.py:287
  534.5 233.6 %all-reduce.23.cloned.1.call-done = (bf16[288,1024]{1,0:T(8,128)(2,1)}, bf16[288,256]{1,0:T(8,128)(2,1)}, bf16[288,256]{1,0:T(8,128)(2,1)}, bf16[288,1024]{1,0:T...) async-done(((bf16[288,1024]{1,0:T(8,128)(2,1)}, bf16[288,256]{1,0:T(8,128)(2,1)}, bf16[288,256]{1,0:T(8,128)(2,1)}, ...) | async-done | bytes 13418512 | tf_op jit(solution)/shard_map/psum | solution.py:288
  768.1 6.0 convert_element_type.272
  774.1 4.0 convert_element_type.274
  778.1 3.8 convert_element_type.276
  (330 shorter events, 108.3 us)
Async XLA Ops:
  7.2 44.7 %copy-start = (bf16[256,1152]{1,0:T(8,128)(2,1)S(1)}, bf16[256,1152]{1,0:T(8,128)(2,1)}, u32[]{:S(2)}) copy-start(bf16[256,1152]{1,0:T(8,128)(2,1)} %param.17) | copy-start | bytes 1769476
  7.2 46.0 %copy-start.76 = (s32[256]{0:T(256)S(1)}, s32[256]{0:T(256)}, u32[]{:S(2)}) copy-start(s32[256]{0:T(256)} %param.20) | copy-start | bytes 3076
  7.2 79.4 %all-gather.5.cloned.1.call-start = ((), (), s32[]{:S(2)}) async-start(), calls=%async_computation.6 | async-start | bytes 2949120 | tf_op jit(solution)/shard_map/all_gather | solution.py:90
  7.9 91.0 %all-gather.7.cloned.1.call-start = ((), (), s32[]{:S(2)}) async-start(), calls=%async_computation.7 | async-start | bytes 2949120 | tf_op jit(solution)/shard_map/all_gather | solution.py:93
  8.7 53.0 %copy-start.42 = (bf16[288,256]{1,0:T(8,128)(2,1)S(1)}, bf16[288,256]{1,0:T(8,128)(2,1)}, u32[]{:S(2)}) copy-start(bf16[288,256]{1,0:T(8,128)(2,1)} %param.24) | copy-start | bytes 442372
  8.7 135.5 %all-gather.9.cloned.1.call-start = ((), (), s32[]{:S(2)}) async-start(), calls=%async_computation.8 | async-start | bytes 2949120 | tf_op jit(solution)/shard_map/all_gather | solution.py:147
  36.7 49.9 %copy-start.59 = (f32[256]{0:T(256)}, f32[256]{0:T(256)S(1)}, u32[]{:S(2)}) copy-start(f32[256]{0:T(256)S(1)} %fusion.72) | copy-start | bytes 3076
  52.4 31.5 %copy-start.73 = (f32[256]{0:T(256)}, f32[256]{0:T(256)S(1)}, u32[]{:S(2)}) copy-start(f32[256]{0:T(256)S(1)} %get-tuple-element.76) | copy-start | bytes 3076
  52.4 31.5 %copy-start.72 = (s32[1024]{0:T(1024)S(1)}, s32[1024]{0:T(1024)}, u32[]{:S(2)}) copy-start(s32[1024]{0:T(1024)} %param.19) | copy-start | bytes 12292
  52.4 31.6 %copy-start.50 = (f32[256]{0:T(256)}, f32[256]{0:T(256)S(1)}, u32[]{:S(2)}) copy-start(f32[256]{0:T(256)S(1)} %fusion.73) | copy-start | bytes 3076
  52.4 31.6 %copy-start.64 = (f32[256]{0:T(256)}, f32[256]{0:T(256)S(1)}, u32[]{:S(2)}) copy-start(f32[256]{0:T(256)S(1)} %convert_element_type.226) | copy-start | bytes 3076
  53.2 32.0 %copy-start.75 = (f32[128]{0:T(128)}, f32[128]{0:T(128)S(1)}, u32[]{:S(2)}) copy-start(f32[128]{0:T(128)S(1)} %multiply_power_fusion) | copy-start | bytes 1540
  53.8 37.7 %copy-start.36 = (bf16[256,128]{0,1:T(8,128)(2,1)}, bf16[256,128]{0,1:T(8,128)(2,1)S(1)}, u32[]{:S(2)}) copy-start(bf16[256,128]{0,1:T(8,128)(2,1)S(1)} %get-tuple-element.70) | copy-start | bytes 196612
  53.8 37.7 %copy-start.38 = (bf16[256,128]{0,1:T(8,128)(2,1)}, bf16[256,128]{0,1:T(8,128)(2,1)S(1)}, u32[]{:S(2)}) copy-start(bf16[256,128]{0,1:T(8,128)(2,1)S(1)} %get-tuple-element.71) | copy-start | bytes 196612
  54.5 37.0 %collective-permute-start = (bf16[256,256]{0,1:T(8,128)(2,1)}, bf16[256,256]{0,1:T(8,128)(2,1)}, u32[]{:S(2)}, u32[]{:S(2)}) collective-permute-start(bf16[256,256]{0,1:T(8,128)(2,1)} %pad_maximum_fusion.3), channel_id=1, source_target_pairs={{0,2},{1,3},{4,6},{5,7},{8,10},{9,11},{12,14},{13,15},{16,18},{17,... | collective-permute-start | bytes 393224 | tf_op jit(solution)/shard_map/ppermute | solution.py:16
  58.2 33.3 %collective-permute-start.1 = (bf16[256,256]{0,1:T(8,128)(2,1)}, bf16[256,256]{0,1:T(8,128)(2,1)}, u32[]{:S(2)}, u32[]{:S(2)}) collective-permute-start(bf16[256,256]{0,1:T(8,128)(2,1)} %pad_maximum_fusion.3), channel_id=1, source_target_pairs={{0,1},{1,2},{2,3},{4,5},{5,6},{6,7},{8,9},{9,10},{10,11},{12,13},{... | collective-permute-start | bytes 393224 | tf_op jit(solution)/shard_map/ppermute | solution.py:16
  75.7 18.7 %collective-permute-start.2 = (bf16[256,256]{1,0:T(8,128)(2,1)}, bf16[256,256]{1,0:T(8,128)(2,1)}, u32[]{:S(2)}, u32[]{:S(2)}) collective-permute-start(bf16[256,256]{1,0:T(8,128)(2,1)} %convolution_convert_fusion.9), channel_id=1, source_target_pairs={{0,2},{1,3},{4,6},{5,7},{8,10},{9,11},{12,14},{13,15},{16,18},{17,... | collective-permute-start | bytes 393224 | tf_op jit(solution)/shard_map/ppermute | solution.py:16
  81.0 13.4 %collective-permute-start.3 = (bf16[256,256]{1,0:T(8,128)(2,1)}, bf16[256,256]{1,0:T(8,128)(2,1)}, u32[]{:S(2)}, u32[]{:S(2)}) collective-permute-start(bf16[256,256]{1,0:T(8,128)(2,1)} %convolution_convert_fusion.9), channel_id=1, source_target_pairs={{0,1},{1,2},{2,3},{4,5},{5,6},{6,7},{8,9},{9,10},{10,11},{12,13},{... | collective-permute-start | bytes 393224 | tf_op jit(solution)/shard_map/ppermute | solution.py:16
  106.3 98.8 %reduce-scatter.7.cloned.1.call-start = ((), (), s32[]{:S(2)}) async-start(), calls=%async_computation.9 | async-start | bytes 2949120 | tf_op jit(solution)/shard_map/reduce_scatter | solution.py:151
  167.5 81.2 %all-gather.11.cloned.1.call-start = ((), (), s32[]{:S(2)}) async-start(), calls=%async_computation.10 | async-start | bytes 2949120 | tf_op jit(solution)/shard_map/all_gather | solution.py:162
  211.1 101.7 %reduce-scatter.9.cloned.1.call-start = ((), (), s32[]{:S(2)}) async-start(), calls=%async_computation.11 | async-start | bytes 2949120 | tf_op jit(solution)/shard_map/reduce_scatter | solution.py:169
  275.3 111.5 %reduce-scatter.15.cloned.1.call-start = ((), (), s32[]{:S(2)}) async-start(), calls=%async_computation.14 | async-start | bytes 737280 | tf_op jit(solution)/shard_map/reduce_scatter | solution.py:250
  334.8 13.0 %collective-permute-start.6 = (bf16[256,256]{1,0:T(8,128)(2,1)}, bf16[256,256]{1,0:T(8,128)(2,1)}, u32[]{:S(2)}, u32[]{:S(2)}) collective-permute-start(bf16[256,256]{1,0:T(8,128)(2,1)} %get-tuple-element.64), channel_id=1, source_target_pairs={{1,0},{2,1},{3,2},{5,4},{6,5},{7,6},{9,8},{10,9},{11,10},{13,12},{... | collective-permute-start | bytes 393224 | tf_op jit(solution)/shard_map/ppermute | solution.py:16
  336.1 11.7 %collective-permute-start.7 = (bf16[256,256]{1,0:T(8,128)(2,1)}, bf16[256,256]{1,0:T(8,128)(2,1)}, u32[]{:S(2)}, u32[]{:S(2)}) collective-permute-start(bf16[256,256]{1,0:T(8,128)(2,1)} %get-tuple-element.65), channel_id=1, source_target_pairs={{2,0},{3,1},{6,4},{7,5},{10,8},{11,9},{14,12},{15,13},{18,16},{19,... | collective-permute-start | bytes 393224 | tf_op jit(solution)/shard_map/ppermute | solution.py:16
  338.1 12.5 %collective-permute-start.4 = (bf16[256,256]{0,1:T(8,128)(2,1)}, bf16[256,256]{0,1:T(8,128)(2,1)}, u32[]{:S(2)}, u32[]{:S(2)}) collective-permute-start(bf16[256,256]{0,1:T(8,128)(2,1)} %get-tuple-element.66), channel_id=1, source_target_pairs={{1,0},{2,1},{3,2},{5,4},{6,5},{7,6},{9,8},{10,9},{11,10},{13,12},{... | collective-permute-start | bytes 393224 | tf_op jit(solution)/shard_map/ppermute | solution.py:16
  339.4 11.2 %collective-permute-start.5 = (bf16[256,256]{0,1:T(8,128)(2,1)}, bf16[256,256]{0,1:T(8,128)(2,1)}, u32[]{:S(2)}, u32[]{:S(2)}) collective-permute-start(bf16[256,256]{0,1:T(8,128)(2,1)} %get-tuple-element.67), channel_id=1, source_target_pairs={{2,0},{3,1},{6,4},{7,5},{10,8},{11,9},{14,12},{15,13},{18,16},{19,... | collective-permute-start | bytes 393224 | tf_op jit(solution)/shard_map/ppermute | solution.py:16
  350.3 60.0 %reduce-scatter.13.cloned.1.call-start = ((), (), s32[]{:S(2)}) async-start(), calls=%async_computation.13 | async-start | bytes 737280 | tf_op jit(solution)/shard_map/reduce_scatter | solution.py:247
  357.7 93.1 %reduce-scatter.11.cloned.1.call-start = ((), (), s32[]{:S(2)}) async-start(), calls=%async_computation.12 | async-start | bytes 2949120 | tf_op jit(solution)/shard_map/reduce_scatter | solution.py:244
  362.4 128.7 %reduce-scatter.17.cloned.1.call-start = ((), (), s32[]{:S(2)}) async-start(), calls=%async_computation.15 | async-start | bytes 2949120 | tf_op jit(solution)/shard_map/reduce_scatter | solution.py:253
  364.7 403.4 %all-reduce.23.cloned.1.call-start = ((), (), s32[]{:S(2)}) async-start(), calls=%async_computation.16 | async-start | bytes 26836992 | tf_op jit(solution)/shard_map/psum | solution.py:288
  496.3 35.6 %copy-start.69 = (f32[256]{0:T(256)S(1)}, f32[256]{0:T(256)}, u32[]{:S(2)}) copy-start(f32[256]{0:T(256)} %copy-done.68) | copy-start | bytes 3076
  496.3 35.6 %copy-start.6 = (f32[256,1152]{1,0:T(8,128)S(1)}, f32[256,1152]{1,0:T(8,128)}, u32[]{:S(2)}) copy-start(f32[256,1152]{1,0:T(8,128)} %copy-done.5) | copy-start | bytes 3538948
  (76 other events, 349.3 us)
Sparse Core Ops, SparseCore 0:
  9.9 44.5 all-gather.4
  56.3 42.5 all-gather.6
  106.5 37.6 all-gather.8
  167.7 37.3 reduce-scatter.6
  211.3 37.4 all-gather.10
  275.5 37.3 reduce-scatter.8
  350.4 31.0 reduce-scatter.14
  385.3 25.0 reduce-scatter.12
  413.4 37.3 reduce-scatter.10
  453.7 37.3 reduce-scatter.16
  494.7 273.3 all-reduce.22
where the time goes:
time: 797 us; the launch traced here: 792 us
  waiting for transfers between devices  480 us (60%)
  matrix products  104 us (13%)
  blocking collectives  77.1 us (10%)
  other arithmetic  56 us (7%)
  local copies, waits for them, and re-layouts  35.9 us (5%)
  starting transfers between devices  21.6 us (3%)
  between operations  18.1 us (2%)
    psum x1, waiting for transfers between devices, per_device(): lax.psum(owned_query.astype(jnp.bfloat16), 'replica').astype(jnp.float32)  234 us
    dot_general x18, matrix products, contract(): lax.dot_general(left, right, (((left_dim,), (right_dim,)), ((), ())), pre...  75.8 us
    reduce_scatter x1, waiting for transfers between devices, per_device(): lax.psum_scatter(grad_wquery.astype(jnp.bfloat16), 'fsdp', scatter_dimens...  40.5 us
    reduce_scatter x1, waiting for transfers between devices, per_device(): lax.psum_scatter(grad_wout.astype(jnp.bfloat16), 'fsdp', scatter_dimensio...  40.3 us
    all_gather x1, waiting for transfers between devices, per_device(): ffn_rows = lax.all_gather(ffn_in, 'fsdp', axis=0, tiled=True)  37.6 us
    all_gather x1, waiting for transfers between devices, per_device(): piece = lax.all_gather(grad_branch_low, 'fsdp', axis=0, tiled=True)  37.2 us
    reduce_scatter x1, waiting for transfers between devices, per_device(): lax.psum_scatter(jnp.dot(hidden, down_weight, preferred_element_type=jnp....  36.2 us
    unnamed x2, blocking collectives  34 us
  transfers between devices with their start and end apart: 19, of which 9 were waited for; matrix products, arithmetic and copies ran while one was open for 11% of the time, Pallas kernels for 0%

commit v1 on v0

v1 whole, which is shorter than its diff:
```python
import jax
import jax.numpy as jnp
from jax import lax
from jax.sharding import PartitionSpec as P

WINDOW = 512


EPS = 1e-06
NEG = -1e30


def swapped(block, axis, mask):
    route = [(i, i ^ mask) for i in range(lax.axis_size(axis))]
    return lax.ppermute(block, axis, route)


def added(left, right):
    total = left.astype(jnp.float32) + right.astype(jnp.float32)
    return lax.optimization_barrier(total.astype(jnp.bfloat16))


def along_line(block, pairs):
    route = [(2 * a + core, 2 * b + core) for a, b in pairs for core in range(2)]
    return lax.ppermute(block, "replica", route)


def line_sum(block):
    places = lax.axis_size("replica") // 2
    place = lax.axis_index("replica") // 2
    middle = places // 2
    for hop in range(middle - 1):
        block = added(block, along_line(block, [(hop, hop + 1), (places - 1 - hop, places - 2 - hop)]))
    block = added(block, along_line(block, [(middle - 1, middle), (middle, middle - 1)]))
    for hop in reversed(range(middle - 1)):
        far = along_line(block, [(hop + 1, hop), (places - 2 - hop, places - 1 - hop)])
        block = jnp.where((place == hop) | (place == places - 1 - hop), far, block)
    return block


def halves(block, axis):
    core = lax.axis_index("replica") % 2
    half = block.shape[axis] // 2
    mine = lax.dynamic_slice_in_dim(block, core * half, half, axis)
    other = lax.dynamic_slice_in_dim(block, (1 - core) * half, half, axis)
    return mine, other


def joined(mine, other, axis):
    core = lax.axis_index("replica") % 2
    return jnp.where(
        core == 0,
        jnp.concatenate([mine, other], axis=axis),
        jnp.concatenate([other, mine], axis=axis),
    )


def core_sum(block, axis):
    mine, other = halves(block, axis)
    return added(mine, swapped(other, "replica", 1))


def core_join(block, axis):
    return joined(block, swapped(block, "replica", 1), axis)


def replica_sum(block):
    return core_join(line_sum(core_sum(block, 0)), 0).astype(jnp.float32)


def owner_sum(blocks):
    rank = lax.axis_index("fsdp")
    part = core_sum(blocks, 1)
    total = lax.dynamic_index_in_dim(part, rank, 0, keepdims=False).astype(jnp.float32)
    for mask in range(1, blocks.shape[0]):
        far = swapped(lax.dynamic_index_in_dim(part, rank ^ mask, 0, keepdims=False), "fsdp", mask)
        total = total + far.astype(jnp.float32)
    total = lax.optimization_barrier(total.astype(jnp.bfloat16))
    return core_join(line_sum(total), 0).astype(jnp.float32)


def in_order(blocks):
    rank = lax.axis_index("fsdp")
    stack = jnp.stack(blocks)
    return [lax.dynamic_index_in_dim(stack, rank ^ i, 0, keepdims=False) for i in range(len(blocks))]


def gathered_rows(own, extra=None):
    group = lax.axis_size("fsdp")
    half = own.shape[0] // 2
    block = halves(own, 0)[0]
    if extra is not None:
        block = jnp.concatenate([block, extra], axis=0)
    got = [swapped(block, "fsdp", mask) for mask in range(1, group)]
    mine = jnp.stack([part[:half] for part in got])
    whole = core_join(mine, 1)
    rows = jnp.concatenate(in_order([own] + list(whole)), axis=0)
    if extra is None:
        return rows
    return rows, in_order([extra] + [part[half:] for part in got])


def passed_along(block, axis, distance):
    devices = range(lax.axis_size(axis))
    route = [(i - distance, i) for i in devices if i - distance in devices]
    return lax.ppermute(block, axis, route)


def contract(left, right, left_dim, right_dim):
    return lax.dot_general(
        left, right, (((left_dim,), (right_dim,)), ((), ())), preferred_element_type=jnp.float32
    )


def normed(value, gain):
    return value * lax.rsqrt(jnp.mean(value * value, axis=-1, keepdims=True) + EPS) * gain


def norm_back(value, gain, grad):
    _, pull = jax.vjp(normed, value, gain)
    return pull(grad)


def tables(places, half):
    freq = 10000.0 ** (-(2.0 * jnp.arange(half, dtype=jnp.float32)) / (2 * half))
    angle = places.astype(jnp.float32)[:, None] * freq[None, :]
    return (jnp.cos(angle), jnp.sin(angle))


def rotate(value, cosine, sine):
    half = value.shape[-1] // 2
    first = value[..., :half]
    second = value[..., half:]
    return jnp.concatenate(
        [first * cosine - second * sine, second * cosine + first * sine], axis=-1
    )


def head_post(raw, gain, cosine, sine):
    return rotate(normed(raw, gain), cosine, sine)


def gated(gate, upper):
    return jax.nn.gelu(gate, approximate=True) * upper


def gated_back(gate, upper, grad):
    _, pull = jax.vjp(gated, gate, upper)
    grad_gate, grad_upper = pull(grad)
    return (grad_gate.astype(jnp.bfloat16), grad_upper.astype(jnp.bfloat16))


def per_device(
    hidden_in,
    out_grad,
    segments,
    positions,
    norm_in,
    query_weight,
    key_weight,
    value_weight,
    out_weight,
    norm_attn,
    norm_ffn,
    gate_weight,
    up_weight,
    down_weight,
    norm_out,
    query_gain,
    key_gain,
):
    rows = hidden_in.shape[0]
    rank = lax.axis_index("fsdp")
    group = lax.axis_size("fsdp")
    masks = range(1, group)
    head_size = key_weight.shape[1]
    heads = query_weight.shape[1] // head_size
    model = hidden_in.shape[1]
    own_model = norm_in.shape[0]
    own_head = query_gain.shape[0]
    hops = (WINDOW - 1) // rows + 1
    scale = head_size ** (-0.5)
    w_own = jnp.concatenate([query_weight, key_weight, value_weight], axis=1)
    wide = w_own.shape[1]
    sizes = [own_model] * 4 + [own_head] * 2
    gains = jnp.concatenate([norm_in, norm_attn, norm_ffn, norm_out, query_gain, key_gain])
    gains = jnp.pad(gains[None, :], ((0, 15), (0, wide - sum(sizes))))
    w_qkv, gain_rows = gathered_rows(w_own, gains)
    w_out = gathered_rows(out_weight)
    spots = [sum(sizes[:i]) for i in range(7)]
    gain_in, gain_attn, gain_ffn, gain_out, gain_query, gain_key = (
        jnp.concatenate([row[0, spots[i] : spots[i + 1]] for row in gain_rows]) for i in range(6)
    )
    residual_in = hidden_in.astype(jnp.float32)
    normed_in = normed(residual_in, gain_in).astype(jnp.bfloat16)
    qkv = jnp.dot(normed_in, w_qkv, preferred_element_type=jnp.float32)
    query_raw = qkv[:, : heads * head_size].reshape(rows, heads, head_size)
    key_raw = qkv[:, heads * head_size : (heads + 1) * head_size]
    value_new = qkv[:, (heads + 1) * head_size :].astype(jnp.bfloat16)
    cosine, sine = tables(positions, head_size // 2)
    cosine_heads = cosine[:, None, :]
    sine_heads = sine[:, None, :]
    query_new = head_post(query_raw, gain_query, cosine_heads, sine_heads).astype(jnp.bfloat16)
    key_new = head_post(key_raw, gain_key, cosine, sine).astype(jnp.bfloat16)
    pair_new = jnp.concatenate([key_new, value_new], axis=1)
    parts = [pair_new]
    for step in range(1, hops + 1):
        parts.insert(0, passed_along(pair_new, "fsdp", step))
    pairs = jnp.concatenate(parts, axis=0)
    keys = pairs[:, :head_size]
    values = pairs[:, head_size:]
    width = keys.shape[0]
    seg_padded = jnp.concatenate([jnp.full((hops * rows,), -1, jnp.int32), segments], axis=0)
    key_segs = lax.dynamic_slice_in_dim(seg_padded, rank * rows, width, 0)
    query_segs = lax.dynamic_slice_in_dim(segments, rank * rows, rows, 0)
    gap = hops * rows + jnp.arange(rows)[:, None] - jnp.arange(width)[None, :]
    allowed = (gap >= 0) & (gap < WINDOW) & (query_segs[:, None] == key_segs[None, :])
    query_rows = query_new.reshape(rows * heads, head_size)

    def scores_of():
        raw_scores = (contract(query_rows, keys, 1, 1) * scale).reshape(rows, heads, width)
        return jnp.where(allowed[:, None, :], raw_scores, NEG)

    scores = scores_of()
    highest = jnp.max(scores, axis=-1, keepdims=True)
    expo = jnp.exp(scores - highest)
    weight_sum = jnp.sum(expo, axis=-1, keepdims=True)
    probs = expo / weight_sum
    log_total = highest + jnp.log(weight_sum)
    probs_low = probs.astype(jnp.bfloat16).reshape(rows * heads, width)
    mixed = (
        jnp.dot(probs_low, values, preferred_element_type=jnp.float32)
        .reshape(rows, heads * head_size)
        .astype(jnp.bfloat16)
    )
    attended = contract(mixed, w_out, 1, 1)
    resid = residual_in + normed(attended, gain_attn)
    ffn_in = normed(resid, gain_ffn).astype(jnp.bfloat16)
    ffn_blocks = [ffn_in] + [swapped(ffn_in, "fsdp", mask) for mask in masks]
    gates, uppers, hiddens = [], [], []
    branch = None
    for mask in range(group):
        gate = contract(ffn_blocks[mask], gate_weight, 1, 1)
        upper = contract(ffn_blocks[mask], up_weight, 1, 1)
        hidden = gated(gate, upper).astype(jnp.bfloat16)
        part = jnp.dot(hidden, down_weight, preferred_element_type=jnp.float32).astype(jnp.bfloat16)
        part = swapped(part, "fsdp", mask) if mask else part
        branch = part.astype(jnp.float32) if mask == 0 else branch + part.astype(jnp.float32)
        gates.append(gate)
        uppers.append(upper)
        hiddens.append(hidden)
    result = resid + normed(branch, gain_out)
    hidden_out = result.astype(jnp.bfloat16)
    grad_result = out_grad.astype(jnp.float32)
    grad_branch, grad_gain_out = norm_back(branch, gain_out, grad_result)
    grad_branch_low = grad_branch.astype(jnp.bfloat16)
    pieces = [grad_branch_low] + [swapped(grad_branch_low, "fsdp", mask) for mask in masks]
    ffn_rows = jnp.concatenate(ffn_blocks, axis=0)
    grad_down = contract(jnp.concatenate(hiddens, axis=0), jnp.concatenate(pieces, axis=0), 0, 0)
    cut = grad_down.shape[0] // 2

    def cut_sum(grad):
        grad = grad.astype(jnp.bfloat16)
        return jnp.concatenate([replica_sum(grad[:cut]), replica_sum(grad[cut:])], axis=0)

    grad_down = cut_sum(grad_down)
    grad_gates, grad_uppers = [], []
    grad_ffn_in = None
    for mask in range(group):
        grad_hidden = contract(pieces[mask], down_weight, 1, 1)
        grad_gate, grad_upper = gated_back(gates[mask], uppers[mask], grad_hidden)
        part = (
            jnp.dot(grad_gate, gate_weight, preferred_element_type=jnp.float32)
            + jnp.dot(grad_upper, up_weight, preferred_element_type=jnp.float32)
        ).astype(jnp.bfloat16)
        part = swapped(part, "fsdp", mask) if mask else part
        grad_ffn_in = part.astype(jnp.float32) if mask == 0 else grad_ffn_in + part.astype(jnp.float32)
        grad_gates.append(grad_gate)
        grad_uppers.append(grad_upper)
    grad_gate_w = cut_sum(contract(jnp.concatenate(grad_gates, axis=0), ffn_rows, 0, 0))
    grad_up_w = cut_sum(contract(jnp.concatenate(grad_uppers, axis=0), ffn_rows, 0, 0))
    grad_resid_part, grad_gain_ffn = norm_back(resid, gain_ffn, grad_ffn_in)
    grad_resid = grad_result + grad_resid_part
    grad_attended, grad_gain_attn = norm_back(attended, gain_attn, grad_resid)
    grad_attended_low = grad_attended.astype(jnp.bfloat16)
    grad_wout = contract(grad_attended_low, mixed, 0, 0).astype(jnp.bfloat16)
    owned_out = owner_sum(grad_wout.reshape(group, own_model, -1))
    grad_mixed = jnp.dot(grad_attended_low, w_out, preferred_element_type=jnp.float32).astype(
        jnp.bfloat16
    )
    grad_mixed_rows = grad_mixed.reshape(rows * heads, head_size)
    scores = scores_of()
    probs = jnp.exp(scores - log_total)
    probs_low = probs.astype(jnp.bfloat16).reshape(rows * heads, width)
    grad_probs = contract(grad_mixed_rows, values, 1, 1).reshape(rows, heads, width)
    delta = jnp.sum(grad_probs * probs, axis=-1, keepdims=True)
    grad_scores = (probs * (grad_probs - delta)).astype(jnp.bfloat16).reshape(rows * heads, width)
    grad_query = (jnp.dot(grad_scores, keys, preferred_element_type=jnp.float32) * scale).reshape(
        rows, heads, head_size
    )
    grad_keys = contract(grad_scores, query_rows, 0, 0) * scale
    grad_values = contract(probs_low, grad_mixed_rows, 0, 0)
    grad_pairs = jnp.concatenate([grad_keys, grad_values], axis=1)
    grad_pair = grad_pairs[hops * rows :]
    for step in range(1, hops + 1):
        lower = (hops - step) * rows
        back = passed_along(grad_pairs[lower : lower + rows].astype(jnp.bfloat16), "fsdp", -step)
        grad_pair = grad_pair + back.astype(jnp.float32)
    grad_key = grad_pair[:, :head_size]
    grad_value = grad_pair[:, head_size:]
    _, pull_query = jax.vjp(
        lambda raw, gain: head_post(raw, gain, cosine_heads, sine_heads), query_raw, gain_query
    )
    grad_query_raw, grad_gain_query = pull_query(grad_query)
    _, pull_key = jax.vjp(lambda raw, gain: head_post(raw, gain, cosine, sine), key_raw, gain_key)
    grad_key_raw, grad_gain_key = pull_key(grad_key)
    grad_query_low = grad_query_raw.reshape(rows, heads * head_size).astype(jnp.bfloat16)
    grad_key_low = grad_key_raw.astype(jnp.bfloat16)
    grad_value_low = grad_value.astype(jnp.bfloat16)
    grad_qkv = jnp.concatenate([grad_query_low, grad_key_low, grad_value_low], axis=1)
    grad_wqkv = contract(normed_in, grad_qkv, 0, 0).astype(jnp.bfloat16)
    grad_normed_in = contract(grad_qkv, w_qkv, 1, 1)
    grad_input_part, grad_gain_in = norm_back(residual_in, gain_in, grad_normed_in)
    grad_in = grad_resid + grad_input_part
    gain_grads = jnp.concatenate(
        [
            grad.astype(jnp.bfloat16).reshape(group, -1)
            for grad in (
                grad_gain_in,
                grad_gain_attn,
                grad_gain_ffn,
                grad_gain_out,
                grad_gain_query,
                grad_gain_key,
            )
        ],
        axis=1,
    )
    gain_grads = jnp.pad(gain_grads[:, None, :], ((0, 0), (0, 31), (0, wide - sum(sizes))))
    owned = owner_sum(
        jnp.concatenate([grad_wqkv.reshape(group, own_model, wide), gain_grads], axis=1)
    )
    owned_query = owned[:own_model, : heads * head_size]
    owned_key = owned[:own_model, heads * head_size : (heads + 1) * head_size]
    owned_value = owned[:own_model, (heads + 1) * head_size :]
    owned_gain_in, owned_gain_attn, owned_gain_ffn, owned_gain_out, owned_gain_query, owned_gain_key = (
        owned[own_model, spots[i] : spots[i + 1]] for i in range(6)
    )
    return (
        hidden_out,
        grad_in,
        owned_gain_in,
        owned_query,
        owned_key,
        owned_value,
        owned_out,
        owned_gain_attn,
        owned_gain_ffn,
        grad_gate_w,
        grad_up_w,
        grad_down,
        owned_gain_out,
        owned_gain_query,
        owned_gain_key,
    )


def solution(mesh):
    return jax.shard_map(
        per_device,
        mesh=mesh,
        in_specs=(
            P(("replica", "fsdp"), None),
            P(("replica", "fsdp"), None),
            P("replica"),
            P(("replica", "fsdp")),
            P("fsdp"),
            P("fsdp", None),
            P("fsdp", None),
            P("fsdp", None),
            P("fsdp", None),
            P("fsdp"),
            P("fsdp"),
            P("fsdp", None),
            P("fsdp", None),
            P("fsdp", None),
            P("fsdp"),
            P("fsdp"),
            P("fsdp"),
        ),
        out_specs=(
            P(("replica", "fsdp"), None),
            P(("replica", "fsdp"), None),
            P("fsdp"),
            P("fsdp", None),
            P("fsdp", None),
            P("fsdp", None),
            P("fsdp", None),
            P("fsdp"),
            P("fsdp"),
            P("fsdp", None),
            P("fsdp", None),
            P("fsdp", None),
            P("fsdp"),
            P("fsdp"),
            P("fsdp"),
        ),
        check_vma=False,
    )
```

time: 797 us -> 715 us (0.90)
  waiting for transfers between devices: 480 us -> 337 us
  starting transfers between devices: 21.6 us -> 116 us
  blocking collectives: 77.1 us -> 0 us
  local copies, waits for them, and re-layouts: 35.9 us -> 70.3 us
  between operations: 18.1 us -> 3.32 us
  other arithmetic: 56 us -> 67.3 us
    ppermute x0 -> x66, waiting for transfers between devices: none -> 324 us  [the longest x24 253 us: along_line(): return lax.ppermute(block, 'replica', route)]
    psum x1 -> x0, waiting for transfers between devices: 234 us -> none  [per_device(): lax.psum(owned_query.astype(jnp.bfloat16), 'replica').astype(jnp.float32)]
    reduce_scatter x6 -> x0, waiting for transfers between devices: 169 us -> none  [the longest x1 40.5 us: per_device(): lax.psum_scatter(grad_wquery.astype(jnp.bfloat16), 'fsdp', scatter_dimens...]
    ppermute x0 -> x66, starting transfers between devices: none -> 106 us  [the longest x24 65.2 us: along_line(): return lax.ppermute(block, 'replica', route)]
    all_gather x4 -> x0, waiting for transfers between devices: 76.1 us -> none  [the longest x1 37.6 us: per_device(): ffn_rows = lax.all_gather(ffn_in, 'fsdp', axis=0, tiled=True)]
    unnamed x2 -> x0, blocking collectives: 34 us -> none
    all_gather x2 -> x0, blocking collectives: 28.1 us -> none  [the longest x1 15.1 us: per_device(): lax.all_gather(key_weight, 'fsdp', axis=0, tiled=True)]
    psum x1 -> x0, blocking collectives: 14.9 us -> none  [per_device(): lax.psum(owned_gain_in.astype(jnp.bfloat16), 'replica').astype(jnp.float32)]
  transfers between devices with their start and end apart: 19 -> 70, of which waited for: 9 -> 32; matrix products, arithmetic and copies ran while one was open for 11% -> 29% of each run, Pallas kernels for 0% -> 0%
where the time goes in v1:
time: 715 us; the launch traced here: 703 us
  waiting for transfers between devices  337 us (47%)
  starting transfers between devices  116 us (16%)
  matrix products  110 us (15%)
  local copies, waits for them, and re-layouts  70.3 us (10%)
  other arithmetic  67.3 us (9%)
    ppermute x24, waiting for transfers between devices, along_line(): return lax.ppermute(block, 'replica', route)  253 us
    dot_general x23, matrix products, contract(): lax.dot_general(left, right, (((left_dim,), (right_dim,)), ((), ())), pre...  78.1 us
    ppermute x42, waiting for transfers between devices, swapped(): return lax.ppermute(block, axis, route)  71.1 us
    ppermute x24, starting transfers between devices, along_line(): return lax.ppermute(block, 'replica', route)  65.2 us
    ppermute x42, starting transfers between devices, swapped(): return lax.ppermute(block, axis, route)  41.2 us
  transfers between devices with their start and end apart: 70, of which 32 were waited for; matrix products, arithmetic and copies ran while one was open for 29% of the time, Pallas kernels for 0%

profile of v1, /device:TPU:0, one launch (start us, length us, event | category | flops | bytes accessed | tf_op | source)
XLA Modules:
  0.0 703.3 jit_solution(16778666812343325717)
XLA Ops:
  22.5 8.9 %collective-permute-done.2 = bf16[160,1536]{1,0:T(8,128)(2,1)} collective-permute-done((bf16[160,1536]{1,0:T(8,128)(2,1)}, bf16[160,1536]{1,0:T(8,128)(2,1)}, u32[]{:S(2)}, u32[]{:S(2)}) %collective-permute-start.2) | collective-permute-done | bytes 491552 | tf_op jit(solution)/shard_map/ppermute | solution.py:15
  32.5 8.6 %collective-permute-done.1 = bf16[160,1536]{1,0:T(8,128)(2,1)} collective-permute-done((bf16[160,1536]{1,0:T(8,128)(2,1)}, bf16[160,1536]{1,0:T(8,128)(2,1)}, u32[]{:S(2)}, u32[]{:S(2)}) %collective-permute-start.1) | collective-permute-done | bytes 491552 | tf_op jit(solution)/shard_map/ppermute | solution.py:15
  79.9 4.9 collective-permute-done.4
  98.4 5.0 fusion.177
  103.4 8.2 %collective-permute-done.14 = bf16[256,1152]{1,0:T(8,128)(2,1)S(1)} collective-permute-done((bf16[256,1152]{1,0:T(8,128)(2,1)}, bf16[256,1152]{1,0:T(8,128)(2,1)S(1)}, u32[]{:S(2)}, u32[]{:S(2)}) %collective-permute-start.14) | collective-permute-done | bytes 589856 | tf_op jit(solution)/shard_map/ppermute | solution.py:15
  118.5 5.7 collective-permute-done.12
  138.6 5.0 reshape.517
  175.9 9.8 %collective-permute-done.18 = bf16[256,1152]{1,0:T(8,128)(2,1)} collective-permute-done((bf16[256,1152]{1,0:T(8,128)(2,1)}, bf16[256,1152]{1,0:T(8,128)(2,1)}, u32[]{:S(2)}, u32[]{:S(2)}) %collective-permute-start.18) | collective-permute-done | bytes 589856 | tf_op jit(solution)/shard_map/ppermute | solution.py:15
  186.6 6.5 convolution_convert_fusion
  224.9 5.9 convolution_convert_fusion.2
  232.0 7.5 %convolution_convert_fusion.1 = bf16[1728,1152]{1,0:T(8,128)(2,1)S(1)} fusion(bf16[256,1728]{0,1:T(8,128)(2,1)} %copy-done.111, bf16[256,1728]{0,1:T(8,128)(2,1)} %copy-done.110, bf16[256,1728]{0,1:T(8,128)(2,1)} %copy-done.109, bf16[256,1728]{0,1:T(8,128)(2,1)S(1)} %copy-done.42, bf16[256,1152]{1,0:T(8,128)(2,1)S(1)} %copy-done.104, ...), kind=kOutput, calls=%fused_computation.3 | convolution fusion | flops 4102447104 | bytes 9879552 | tf_op jit(solution)/shard_map/dot_general | solution.py:110
  281.3 5.8 collective-permute-done.22
  293.6 5.4 fusion.79
  326.9 14.3 %collective-permute-done.66 = bf16[432,1152]{1,0:T(8,128)(2,1)S(1)} collective-permute-done((bf16[432,1152]{1,0:T(8,128)(2,1)S(1)}, bf16[432,1152]{1,0:T(8,128)(2,1)S(1)}, u32[]{:S(2)}, u32[]{:S(2)}) %collective-permute-start.66) | collective-permute-done | bytes 995360 | tf_op jit(solution)/shard_map/ppermute | solution.py:25
  345.9 16.6 %collective-permute-done.61 = bf16[432,1152]{1,0:T(8,128)(2,1)S(1)} collective-permute-done((bf16[432,1152]{1,0:T(8,128)(2,1)S(1)}, bf16[432,1152]{1,0:T(8,128)(2,1)S(1)}, u32[]{:S(2)}, u32[]{:S(2)}) %collective-permute-start.61) | collective-permute-done | bytes 995360 | tf_op jit(solution)/shard_map/ppermute | solution.py:25
  362.5 5.8 collective-permute-start.33
  368.6 15.3 %collective-permute-done.46 = bf16[432,1152]{1,0:T(8,128)(2,1)S(1)} collective-permute-done((bf16[432,1152]{1,0:T(8,128)(2,1)S(1)}, bf16[432,1152]{1,0:T(8,128)(2,1)S(1)}, u32[]{:S(2)}, u32[]{:S(2)}) %collective-permute-start.46) | collective-permute-done | bytes 995360 | tf_op jit(solution)/shard_map/ppermute | solution.py:25
  388.9 16.3 %collective-permute-done.41 = bf16[432,1152]{1,0:T(8,128)(2,1)S(1)} collective-permute-done((bf16[432,1152]{1,0:T(8,128)(2,1)S(1)}, bf16[432,1152]{1,0:T(8,128)(2,1)S(1)}, u32[]{:S(2)}, u32[]{:S(2)}) %collective-permute-start.41) | collective-permute-done | bytes 995360 | tf_op jit(solution)/shard_map/ppermute | solution.py:25
  414.2 12.3 %collective-permute-done.56 = bf16[432,1152]{1,0:T(8,128)(2,1)S(1)} collective-permute-done((bf16[432,1152]{1,0:T(8,128)(2,1)S(1)}, bf16[432,1152]{1,0:T(8,128)(2,1)S(1)}, u32[]{:S(2)}, u32[]{:S(2)}) %collective-permute-start.56) | collective-permute-done | bytes 995360 | tf_op jit(solution)/shard_map/ppermute | solution.py:25
  431.2 22.5 %collective-permute-done.36 = bf16[144,1024]{1,0:T(8,128)(2,1)S(1)} collective-permute-done((bf16[144,1024]{1,0:T(8,128)(2,1)S(1)}, bf16[144,1024]{1,0:T(8,128)(2,1)S(1)}, u32[]{:S(2)}, u32[]{:S(2)}) %collective-permute-start.36) | collective-permute-done | bytes 294944 | tf_op jit(solution)/shard_map/ppermute | solution.py:25
  458.3 40.1 %collective-permute-done.38 = bf16[144,1024]{1,0:T(8,128)(2,1)S(1)} collective-permute-done((bf16[144,1024]{1,0:T(8,128)(2,1)S(1)}, bf16[144,1024]{1,0:T(8,128)(2,1)S(1)}, u32[]{:S(2)}, u32[]{:S(2)}) %collective-permute-start.38) | collective-permute-done | bytes 294944 | tf_op jit(solution)/shard_map/ppermute | solution.py:25
  500.2 5.8 collective-permute-start.25
  508.7 9.5 %collective-permute-done.25 = bf16[160,1536]{1,0:T(8,128)(2,1)S(1)} collective-permute-done((bf16[160,1536]{1,0:T(8,128)(2,1)S(1)}, bf16[160,1536]{1,0:T(8,128)(2,1)S(1)}, u32[]{:S(2)}, u32[]{:S(2)}) %collective-permute-start.25) | collective-permute-done | bytes 491552 | tf_op jit(solution)/shard_map/ppermute | solution.py:15
  519.5 5.6 collective-permute-done.27
  529.5 27.6 %collective-permute-start.28 = (bf16[160,1536]{1,0:T(8,128)(2,1)S(1)}, bf16[160,1536]{1,0:T(8,128)(2,1)S(1)}, u32[]{:S(2)}, u32[]{:S(2)}) collective-permute-start(bf16[160,1536]{1,0:T(8,128)(2,1)S(1)} %fusion.91), channel_id=1, source_target_pairs={{0,8},{4,12},{24,16},{28,20},{1,9},{5,13},{25,17},{29,21},{2,10},{... | collective-permute-start | bytes 1474568 | tf_op jit(solution)/shard_map/ppermute | solution.py:25
  559.8 5.7 collective-permute-done.28
  568.4 13.5 %collective-permute-done.63 = bf16[432,1152]{1,0:T(8,128)(2,1)S(1)} collective-permute-done((bf16[432,1152]{1,0:T(8,128)(2,1)S(1)}, bf16[432,1152]{1,0:T(8,128)(2,1)S(1)}, u32[]{:S(2)}, u32[]{:S(2)}) %collective-permute-start.63) | collective-permute-done | bytes 995360 | tf_op jit(solution)/shard_map/ppermute | solution.py:25
  582.6 20.5 %collective-permute-done.48 = bf16[432,1152]{1,0:T(8,128)(2,1)S(1)} collective-permute-done((bf16[432,1152]{1,0:T(8,128)(2,1)S(1)}, bf16[432,1152]{1,0:T(8,128)(2,1)S(1)}, u32[]{:S(2)}, u32[]{:S(2)}) %collective-permute-start.48) | collective-permute-done | bytes 995360 | tf_op jit(solution)/shard_map/ppermute | solution.py:25
  603.3 21.2 %collective-permute-done.43 = bf16[432,1152]{1,0:T(8,128)(2,1)S(1)} collective-permute-done((bf16[432,1152]{1,0:T(8,128)(2,1)S(1)}, bf16[432,1152]{1,0:T(8,128)(2,1)S(1)}, u32[]{:S(2)}, u32[]{:S(2)}) %collective-permute-start.43) | collective-permute-done | bytes 995360 | tf_op jit(solution)/shard_map/ppermute | solution.py:25
  624.6 21.2 %collective-permute-done.58 = bf16[432,1152]{1,0:T(8,128)(2,1)S(1)} collective-permute-done((bf16[432,1152]{1,0:T(8,128)(2,1)S(1)}, bf16[432,1152]{1,0:T(8,128)(2,1)S(1)}, u32[]{:S(2)}, u32[]{:S(2)}) %collective-permute-start.58) | collective-permute-done | bytes 995360 | tf_op jit(solution)/shard_map/ppermute | solution.py:25
  646.7 20.3 %collective-permute-done.53 = bf16[432,1152]{1,0:T(8,128)(2,1)S(1)} collective-permute-done((bf16[432,1152]{1,0:T(8,128)(2,1)S(1)}, bf16[432,1152]{1,0:T(8,128)(2,1)S(1)}, u32[]{:S(2)}, u32[]{:S(2)}) %collective-permute-start.53) | collective-permute-done | bytes 995360 | tf_op jit(solution)/shard_map/ppermute | solution.py:25
  668.6 13.3 %collective-permute-done.30 = bf16[160,1536]{1,0:T(8,128)(2,1)S(1)} collective-permute-done((bf16[160,1536]{1,0:T(8,128)(2,1)S(1)}, bf16[160,1536]{1,0:T(8,128)(2,1)S(1)}, u32[]{:S(2)}, u32[]{:S(2)}) %collective-permute-start.30) | collective-permute-done | bytes 491552 | tf_op jit(solution)/shard_map/ppermute | solution.py:25
  (584 shorter events, 305.4 us)
Async XLA Ops:
  22.5 34.5 %collective-permute-start.9 = (bf16[3,144,1024]{2,1,0:T(8,128)(2,1)}, bf16[3,144,1024]{2,1,0:T(8,128)(2,1)}, u32[]{:S(2)}, u32[]{:S(2)}) collective-permute-start(bf16[3,144,1024]{2,1,0:T(8,128)(2,1)} %pad_maximum_fusion.5), channel_id=1, source_target_pairs={{0,4},{4,0},{8,12},{12,8},{16,20},{20,16},{24,28},{28,24},{1,5},{5... | collective-permute-start | bytes 2654216 | tf_op jit(solution)/shard_map/ppermute | solution.py:15
  96.9 35.3 %collective-permute-start.10 = (bf16[256,1152]{1,0:T(8,128)(2,1)}, bf16[256,1152]{1,0:T(8,128)(2,1)S(1)}, u32[]{:S(2)}, u32[]{:S(2)}) collective-permute-start(bf16[256,1152]{1,0:T(8,128)(2,1)} %multiply_convert_fusion.9), channel_id=1, source_target_pairs={{0,1},{1,0},{2,3},{3,2},{4,5},{5,4},{6,7},{7,6},{8,9},{9,8},{10,11... | collective-permute-start | bytes 1769480 | tf_op jit(solution)/shard_map/ppermute | solution.py:15
  196.4 112.2 %collective-permute-start.65 = (bf16[432,1152]{1,0:T(8,128)(2,1)}, bf16[432,1152]{1,0:T(8,128)(2,1)}, u32[]{:S(2)}, u32[]{:S(2)}) collective-permute-start(bf16[432,1152]{1,0:T(8,128)(2,1)} %constant_dynamic-slice_fusion), channel_id=1, source_target_pairs={{0,4},{4,0},{8,12},{12,8},{16,20},{20,16},{24,28},{28,24},{1,5},{5... | collective-permute-start | bytes 2985992 | tf_op jit(solution)/shard_map/ppermute | solution.py:15
  196.4 115.1 %collective-permute-start.60 = (bf16[432,1152]{1,0:T(8,128)(2,1)}, bf16[432,1152]{1,0:T(8,128)(2,1)}, u32[]{:S(2)}, u32[]{:S(2)}) collective-permute-start(bf16[432,1152]{1,0:T(8,128)(2,1)} %constant_dynamic-slice_fusion.1), channel_id=1, source_target_pairs={{0,4},{4,0},{8,12},{12,8},{16,20},{20,16},{24,28},{28,24},{1,5},{5... | collective-permute-start | bytes 2985992 | tf_op jit(solution)/shard_map/ppermute | solution.py:15
  206.7 37.9 %collective-permute-start.17 = (bf16[256,1152]{1,0:T(8,128)(2,1)}, bf16[256,1152]{1,0:T(8,128)(2,1)S(1)}, u32[]{:S(2)}, u32[]{:S(2)}) collective-permute-start(bf16[256,1152]{1,0:T(8,128)(2,1)} %fusion.29), channel_id=1, source_target_pairs={{0,1},{1,0},{2,3},{3,2},{4,5},{5,4},{6,7},{7,6},{8,9},{9,8},{10,11... | collective-permute-start | bytes 1769480 | tf_op jit(solution)/shard_map/ppermute | solution.py:15
  244.6 69.0 %collective-permute-start.45 = (bf16[432,1152]{1,0:T(8,128)(2,1)}, bf16[432,1152]{1,0:T(8,128)(2,1)}, u32[]{:S(2)}, u32[]{:S(2)}) collective-permute-start(bf16[432,1152]{1,0:T(8,128)(2,1)} %constant_dynamic-slice_fusion.4), channel_id=1, source_target_pairs={{0,4},{4,0},{8,12},{12,8},{16,20},{20,16},{24,28},{28,24},{1,5},{5... | collective-permute-start | bytes 2985992 | tf_op jit(solution)/shard_map/ppermute | solution.py:15
  288.6 31.8 %collective-permute-start.55 = (bf16[432,1152]{1,0:T(8,128)(2,1)}, bf16[432,1152]{1,0:T(8,128)(2,1)}, u32[]{:S(2)}, u32[]{:S(2)}) collective-permute-start(bf16[432,1152]{1,0:T(8,128)(2,1)} %constant_dynamic-slice_fusion.2), channel_id=1, source_target_pairs={{0,4},{4,0},{8,12},{12,8},{16,20},{20,16},{24,28},{28,24},{1,5},{5... | collective-permute-start | bytes 2985992 | tf_op jit(solution)/shard_map/ppermute | solution.py:15
  313.6 142.8 %collective-permute-start.24 = (bf16[4,160,1536]{2,1,0:T(8,128)(2,1)S(1)}, bf16[4,160,1536]{2,1,0:T(8,128)(2,1)S(1)}, u32[]{:S(2)}, u32[]{:S(2)}) collective-permute-start(bf16[4,160,1536]{2,1,0:T(8,128)(2,1)S(1)} %constant_dynamic-slice_fusion.7), channel_id=1, source_target_pairs={{0,4},{4,0},{8,12},{12,8},{16,20},{20,16},{24,28},{28,24},{1,5},{5... | collective-permute-start | bytes 5898248 | tf_op jit(solution)/shard_map/ppermute | solution.py:15
  320.5 42.1 %collective-permute-start.61 = (bf16[432,1152]{1,0:T(8,128)(2,1)S(1)}, bf16[432,1152]{1,0:T(8,128)(2,1)S(1)}, u32[]{:S(2)}, u32[]{:S(2)}) collective-permute-start(bf16[432,1152]{1,0:T(8,128)(2,1)S(1)} %add_convert_fusion.7), channel_id=1, source_target_pairs={{0,8},{4,12},{24,16},{28,20},{1,9},{5,13},{25,17},{29,21},{2,10},{... | collective-permute-start | bytes 2985992 | tf_op jit(solution)/shard_map/ppermute | solution.py:25
  323.4 60.4 %collective-permute-start.46 = (bf16[432,1152]{1,0:T(8,128)(2,1)S(1)}, bf16[432,1152]{1,0:T(8,128)(2,1)S(1)}, u32[]{:S(2)}, u32[]{:S(2)}) collective-permute-start(bf16[432,1152]{1,0:T(8,128)(2,1)S(1)} %add_convert_fusion.16), channel_id=1, source_target_pairs={{0,8},{4,12},{24,16},{28,20},{1,9},{5,13},{25,17},{29,21},{2,10},{... | collective-permute-start | bytes 2985992 | tf_op jit(solution)/shard_map/ppermute | solution.py:25
  325.0 80.2 %collective-permute-start.41 = (bf16[432,1152]{1,0:T(8,128)(2,1)S(1)}, bf16[432,1152]{1,0:T(8,128)(2,1)S(1)}, u32[]{:S(2)}, u32[]{:S(2)}) collective-permute-start(bf16[432,1152]{1,0:T(8,128)(2,1)S(1)} %add_convert_fusion.19), channel_id=1, source_target_pairs={{0,8},{4,12},{24,16},{28,20},{1,9},{5,13},{25,17},{29,21},{2,10},{... | collective-permute-start | bytes 2985992 | tf_op jit(solution)/shard_map/ppermute | solution.py:25
  341.2 85.3 %collective-permute-start.56 = (bf16[432,1152]{1,0:T(8,128)(2,1)S(1)}, bf16[432,1152]{1,0:T(8,128)(2,1)S(1)}, u32[]{:S(2)}, u32[]{:S(2)}) collective-permute-start(bf16[432,1152]{1,0:T(8,128)(2,1)S(1)} %add_convert_fusion.10), channel_id=1, source_target_pairs={{0,8},{4,12},{24,16},{28,20},{1,9},{5,13},{25,17},{29,21},{2,10},{... | collective-permute-start | bytes 2985992 | tf_op jit(solution)/shard_map/ppermute | solution.py:25
  362.5 42.9 %collective-permute-start.33 = (bf16[144,1024]{1,0:T(8,128)(2,1)S(1)}, bf16[144,1024]{1,0:T(8,128)(2,1)S(1)}, u32[]{:S(2)}, u32[]{:S(2)}) collective-permute-start(bf16[144,1024]{1,0:T(8,128)(2,1)S(1)} %get-tuple-element.88), channel_id=1, source_target_pairs={{0,1},{1,0},{2,3},{3,2},{4,5},{5,4},{6,7},{7,6},{8,9},{9,8},{10,11... | collective-permute-start | bytes 884744 | tf_op jit(solution)/shard_map/ppermute | solution.py:15
  405.4 49.1 %collective-permute-start.51 = (bf16[432,1152]{1,0:T(8,128)(2,1)S(1)}, bf16[432,1152]{1,0:T(8,128)(2,1)S(1)}, u32[]{:S(2)}, u32[]{:S(2)}) collective-permute-start(bf16[432,1152]{1,0:T(8,128)(2,1)S(1)} %add_convert_fusion.13), channel_id=1, source_target_pairs={{0,8},{4,12},{24,16},{28,20},{1,9},{5,13},{25,17},{29,21},{2,10},{... | collective-permute-start | bytes 2985992 | tf_op jit(solution)/shard_map/ppermute | solution.py:25
  410.3 88.9 %collective-permute-start.67 = (bf16[432,1152]{1,0:T(8,128)(2,1)S(1)}, bf16[432,1152]{1,0:T(8,128)(2,1)S(1)}, u32[]{:S(2)}, u32[]{:S(2)}) collective-permute-start(bf16[432,1152]{1,0:T(8,128)(2,1)S(1)} %add_convert_fusion.3), channel_id=1, source_target_pairs={{8,16},{12,20},{16,8},{20,12},{9,17},{13,21},{17,9},{21,13},{10,18... | collective-permute-start | bytes 2985992 | tf_op jit(solution)/shard_map/ppermute | solution.py:25
  413.3 86.9 %collective-permute-start.62 = (bf16[432,1152]{1,0:T(8,128)(2,1)S(1)}, bf16[432,1152]{1,0:T(8,128)(2,1)S(1)}, u32[]{:S(2)}, u32[]{:S(2)}) collective-permute-start(bf16[432,1152]{1,0:T(8,128)(2,1)S(1)} %add_convert_fusion.6), channel_id=1, source_target_pairs={{8,16},{12,20},{16,8},{20,12},{9,17},{13,21},{17,9},{21,13},{10,18... | collective-permute-start | bytes 2985992 | tf_op jit(solution)/shard_map/ppermute | solution.py:25
  453.7 52.6 %collective-permute-start.47 = (bf16[432,1152]{1,0:T(8,128)(2,1)S(1)}, bf16[432,1152]{1,0:T(8,128)(2,1)S(1)}, u32[]{:S(2)}, u32[]{:S(2)}) collective-permute-start(bf16[432,1152]{1,0:T(8,128)(2,1)S(1)} %add_convert_fusion.15), channel_id=1, source_target_pairs={{8,16},{12,20},{16,8},{20,12},{9,17},{13,21},{17,9},{21,13},{10,18... | collective-permute-start | bytes 2985992 | tf_op jit(solution)/shard_map/ppermute | solution.py:25
  455.5 51.1 %collective-permute-start.42 = (bf16[432,1152]{1,0:T(8,128)(2,1)S(1)}, bf16[432,1152]{1,0:T(8,128)(2,1)S(1)}, u32[]{:S(2)}, u32[]{:S(2)}) collective-permute-start(bf16[432,1152]{1,0:T(8,128)(2,1)S(1)} %add_convert_fusion.18), channel_id=1, source_target_pairs={{8,16},{12,20},{16,8},{20,12},{9,17},{13,21},{17,9},{21,13},{10,18... | collective-permute-start | bytes 2985992 | tf_op jit(solution)/shard_map/ppermute | solution.py:25
  456.3 42.1 %collective-permute-start.38 = (bf16[144,1024]{1,0:T(8,128)(2,1)S(1)}, bf16[144,1024]{1,0:T(8,128)(2,1)S(1)}, u32[]{:S(2)}, u32[]{:S(2)}) collective-permute-start(bf16[144,1024]{1,0:T(8,128)(2,1)S(1)} %add_convert_fusion.23), channel_id=1, source_target_pairs={{8,0},{12,4},{16,24},{20,28},{9,1},{13,5},{17,25},{21,29},{10,2},{... | collective-permute-start | bytes 884744 | tf_op jit(solution)/shard_map/ppermute | solution.py:25
  508.4 48.9 %collective-permute-start.39 = (bf16[144,1024]{1,0:T(8,128)(2,1)S(1)}, bf16[144,1024]{1,0:T(8,128)(2,1)S(1)}, u32[]{:S(2)}, u32[]{:S(2)}) collective-permute-start(bf16[144,1024]{1,0:T(8,128)(2,1)S(1)} %broadcast_select_fusion.10), channel_id=1, source_target_pairs={{0,4},{4,0},{8,12},{12,8},{16,20},{20,16},{24,28},{28,24},{1,5},{5... | collective-permute-start | bytes 884744 | tf_op jit(solution)/shard_map/ppermute | solution.py:15
  518.2 48.7 %collective-permute-start.68 = (bf16[432,1152]{1,0:T(8,128)(2,1)S(1)}, bf16[432,1152]{1,0:T(8,128)(2,1)S(1)}, u32[]{:S(2)}, u32[]{:S(2)}) collective-permute-start(bf16[432,1152]{1,0:T(8,128)(2,1)S(1)} %add_convert_fusion.2), channel_id=1, source_target_pairs={{8,0},{12,4},{16,24},{20,28},{9,1},{13,5},{17,25},{21,29},{10,2},{... | collective-permute-start | bytes 2985992 | tf_op jit(solution)/shard_map/ppermute | solution.py:25
  525.1 56.7 %collective-permute-start.63 = (bf16[432,1152]{1,0:T(8,128)(2,1)S(1)}, bf16[432,1152]{1,0:T(8,128)(2,1)S(1)}, u32[]{:S(2)}, u32[]{:S(2)}) collective-permute-start(bf16[432,1152]{1,0:T(8,128)(2,1)S(1)} %add_convert_fusion.5), channel_id=1, source_target_pairs={{8,0},{12,4},{16,24},{20,28},{9,1},{13,5},{17,25},{21,29},{10,2},{... | collective-permute-start | bytes 2985992 | tf_op jit(solution)/shard_map/ppermute | solution.py:25
  527.9 75.3 %collective-permute-start.48 = (bf16[432,1152]{1,0:T(8,128)(2,1)S(1)}, bf16[432,1152]{1,0:T(8,128)(2,1)S(1)}, u32[]{:S(2)}, u32[]{:S(2)}) collective-permute-start(bf16[432,1152]{1,0:T(8,128)(2,1)S(1)} %add_convert_fusion.14), channel_id=1, source_target_pairs={{8,0},{12,4},{16,24},{20,28},{9,1},{13,5},{17,25},{21,29},{10,2},{... | collective-permute-start | bytes 2985992 | tf_op jit(solution)/shard_map/ppermute | solution.py:25
  529.5 36.0 %collective-permute-start.28 = (bf16[160,1536]{1,0:T(8,128)(2,1)S(1)}, bf16[160,1536]{1,0:T(8,128)(2,1)S(1)}, u32[]{:S(2)}, u32[]{:S(2)}) collective-permute-start(bf16[160,1536]{1,0:T(8,128)(2,1)S(1)} %fusion.91), channel_id=1, source_target_pairs={{0,8},{4,12},{24,16},{28,20},{1,9},{5,13},{25,17},{29,21},{2,10},{... | collective-permute-start | bytes 1474568 | tf_op jit(solution)/shard_map/ppermute | solution.py:25
  557.3 67.2 %collective-permute-start.43 = (bf16[432,1152]{1,0:T(8,128)(2,1)S(1)}, bf16[432,1152]{1,0:T(8,128)(2,1)S(1)}, u32[]{:S(2)}, u32[]{:S(2)}) collective-permute-start(bf16[432,1152]{1,0:T(8,128)(2,1)S(1)} %add_convert_fusion.17), channel_id=1, source_target_pairs={{8,0},{12,4},{16,24},{20,28},{9,1},{13,5},{17,25},{21,29},{10,2},{... | collective-permute-start | bytes 2985992 | tf_op jit(solution)/shard_map/ppermute | solution.py:25
  565.5 80.3 %collective-permute-start.58 = (bf16[432,1152]{1,0:T(8,128)(2,1)S(1)}, bf16[432,1152]{1,0:T(8,128)(2,1)S(1)}, u32[]{:S(2)}, u32[]{:S(2)}) collective-permute-start(bf16[432,1152]{1,0:T(8,128)(2,1)S(1)} %add_convert_fusion.8), channel_id=1, source_target_pairs={{8,0},{12,4},{16,24},{20,28},{9,1},{13,5},{17,25},{21,29},{10,2},{... | collective-permute-start | bytes 2985992 | tf_op jit(solution)/shard_map/ppermute | solution.py:25
  566.9 100.0 %collective-permute-start.53 = (bf16[432,1152]{1,0:T(8,128)(2,1)S(1)}, bf16[432,1152]{1,0:T(8,128)(2,1)S(1)}, u32[]{:S(2)}, u32[]{:S(2)}) collective-permute-start(bf16[432,1152]{1,0:T(8,128)(2,1)S(1)} %add_convert_fusion.11), channel_id=1, source_target_pairs={{8,0},{12,4},{16,24},{20,28},{9,1},{13,5},{17,25},{21,29},{10,2},{... | collective-permute-start | bytes 2985992 | tf_op jit(solution)/shard_map/ppermute | solution.py:25
  581.8 64.1 %collective-permute-start.29 = (bf16[160,1536]{1,0:T(8,128)(2,1)S(1)}, bf16[160,1536]{1,0:T(8,128)(2,1)S(1)}, u32[]{:S(2)}, u32[]{:S(2)}) collective-permute-start(bf16[160,1536]{1,0:T(8,128)(2,1)S(1)} %add_convert_fusion.22), channel_id=1, source_target_pairs={{8,16},{12,20},{16,8},{20,12},{9,17},{13,21},{17,9},{21,13},{10,18... | collective-permute-start | bytes 1474568 | tf_op jit(solution)/shard_map/ppermute | solution.py:25
  603.2 78.8 %collective-permute-start.69 = (bf16[432,1152]{1,0:T(8,128)(2,1)S(1)}, bf16[432,1152]{1,0:T(8,128)(2,1)S(1)}, u32[]{:S(2)}, u32[]{:S(2)}) collective-permute-start(bf16[432,1152]{1,0:T(8,128)(2,1)S(1)} %broadcast_select_fusion.3), channel_id=1, source_target_pairs={{0,4},{4,0},{8,12},{12,8},{16,20},{20,16},{24,28},{28,24},{1,5},{5... | collective-permute-start | bytes 2985992 | tf_op jit(solution)/shard_map/ppermute | solution.py:15
  624.5 70.6 %collective-permute-start.64 = (bf16[432,1152]{1,0:T(8,128)(2,1)S(1)}, bf16[432,1152]{1,0:T(8,128)(2,1)S(1)}, u32[]{:S(2)}, u32[]{:S(2)}) collective-permute-start(bf16[432,1152]{1,0:T(8,128)(2,1)S(1)} %broadcast_select_fusion.4), channel_id=1, source_target_pairs={{0,4},{4,0},{8,12},{12,8},{16,20},{20,16},{24,28},{28,24},{1,5},{5... | collective-permute-start | bytes 2985992 | tf_op jit(solution)/shard_map/ppermute | solution.py:15
  645.8 37.5 %collective-permute-start.49 = (bf16[432,1152]{1,0:T(8,128)(2,1)S(1)}, bf16[432,1152]{1,0:T(8,128)(2,1)S(1)}, u32[]{:S(2)}, u32[]{:S(2)}) collective-permute-start(bf16[432,1152]{1,0:T(8,128)(2,1)S(1)} %broadcast_select_fusion.7), channel_id=1, source_target_pairs={{0,4},{4,0},{8,12},{12,8},{16,20},{20,16},{24,28},{28,24},{1,5},{5... | collective-permute-start | bytes 2985992 | tf_op jit(solution)/shard_map/ppermute | solution.py:15
  646.0 44.5 %collective-permute-start.44 = (bf16[432,1152]{1,0:T(8,128)(2,1)S(1)}, bf16[432,1152]{1,0:T(8,128)(2,1)S(1)}, u32[]{:S(2)}, u32[]{:S(2)}) collective-permute-start(bf16[432,1152]{1,0:T(8,128)(2,1)S(1)} %broadcast_select_fusion.8), channel_id=1, source_target_pairs={{0,4},{4,0},{8,12},{12,8},{16,20},{20,16},{24,28},{28,24},{1,5},{5... | collective-permute-start | bytes 2985992 | tf_op jit(solution)/shard_map/ppermute | solution.py:15
  (167 other events, 1356.6 us)

commit v2 on v1

--- a/solution.py
+++ b/solution.py
@@ -1,6 +1,7 @@
 import jax
 import jax.numpy as jnp
 from jax import lax
+from jax.experimental import pallas as pl
 from jax.sharding import PartitionSpec as P
 
 WINDOW = 512
@@ -25,17 +26,68 @@
     return lax.ppermute(block, "replica", route)
 
 
-def line_sum(block):
+def tied(arrays):
+    place = pl.BlockSpec(memory_space=pl.ANY)
+    return pl.pallas_call(
+        lambda *refs: None,
+        out_shape=[jax.ShapeDtypeStruct(array.shape, array.dtype) for array in arrays],
+        in_specs=[place] * len(arrays),
+        out_specs=[place] * len(arrays),
+        input_output_aliases={i: i for i in range(len(arrays))},
+        name="tie",
+    )(*arrays)
+
+
+def line_steps():
     places = lax.axis_size("replica") // 2
+    middle = places // 2
+    inward = [("add", [(hop, hop + 1), (places - 1 - hop, places - 2 - hop)]) for hop in range(middle - 1)]
+    across = [("add", [(middle - 1, middle), (middle, middle - 1)])]
+    outward = [
+        ("take", [(hop + 1, hop), (places - 2 - hop, places - 1 - hop)])
+        for hop in reversed(range(middle - 1))
+    ]
+    return inward + across + outward
+
+
+def line_combine(step, block, far):
+    kind, pairs = step
+    if kind == "add":
+        return added(block, far)
     place = lax.axis_index("replica") // 2
-    middle = places // 2
-    for hop in range(middle - 1):
-        block = added(block, along_line(block, [(hop, hop + 1), (places - 1 - hop, places - 2 - hop)]))
-    block = added(block, along_line(block, [(middle - 1, middle), (middle, middle - 1)]))
-    for hop in reversed(range(middle - 1)):
-        far = along_line(block, [(hop + 1, hop), (places - 2 - hop, places - 1 - hop)])
-        block = jnp.where((place == hop) | (place == places - 1 - hop), far, block)
-    return block
+    ends = [b for _, b in pairs]
+    return jnp.where((place == ends[0]) | (place == ends[1]), far, block)
+
+
+class Line:
+    def __init__(self):
+        self.steps = line_steps()
+        self.moving = []
+        self.done = {}
+
+    def advance(self, fresh, gate=None):
+        arrays, state = [], []
+        for name, block, far, step in self.moving:
+            arrays.append(line_combine(self.steps[step], block, far))
+            state.append((name, step + 1))
+        for name, block in fresh:
+            arrays.append(block)
+            state.append((name, 0))
+        if gate is not None:
+            arrays.append(gate)
+        arrays = tied(arrays)
+        self.moving = []
+        for (name, step), block in zip(state, arrays):
+            if step == len(self.steps):
+                self.done[name] = block
+            else:
+                self.moving.append((name, block, along_line(block, self.steps[step][1]), step))
+        return arrays[-1]
+
+    def finished(self, name):
+        while name not in self.done:
+            self.advance([])
+        return self.done[name]
 
 
 def halves(block, axis):
@@ -64,19 +116,27 @@
     return joined(block, swapped(block, "replica", 1), axis)
 
 
-def replica_sum(block):
-    return core_join(line_sum(core_sum(block, 0)), 0).astype(jnp.float32)
-
-
-def owner_sum(blocks):
+def cut_sums(grad):
+    grad = grad.reshape(2, grad.shape[0] // 2, grad.shape[1])
+    mine, other = halves(grad, 1)
+    far = swapped(other, "replica", 1)
+    return added(mine[0], far[0]), added(mine[1], far[1])
+
+
+def cut_join(first, second):
+    mine = jnp.stack([first, second])
+    whole = core_join(mine, 1).astype(jnp.float32)
+    return whole.reshape(-1, whole.shape[2])
+
+
+def owner_part(blocks):
     rank = lax.axis_index("fsdp")
     part = core_sum(blocks, 1)
     total = lax.dynamic_index_in_dim(part, rank, 0, keepdims=False).astype(jnp.float32)
     for mask in range(1, blocks.shape[0]):
         far = swapped(lax.dynamic_index_in_dim(part, rank ^ mask, 0, keepdims=False), "fsdp", mask)
         total = total + far.astype(jnp.float32)
-    total = lax.optimization_barrier(total.astype(jnp.bfloat16))
-    return core_join(line_sum(total), 0).astype(jnp.float32)
+    return lax.optimization_barrier(total.astype(jnp.bfloat16))
 
 
 def in_order(blocks):
@@ -257,34 +317,37 @@
     pieces = [grad_branch_low] + [swapped(grad_branch_low, "fsdp", mask) for mask in masks]
     ffn_rows = jnp.concatenate(ffn_blocks, axis=0)
     grad_down = contract(jnp.concatenate(hiddens, axis=0), jnp.concatenate(pieces, axis=0), 0, 0)
-    cut = grad_down.shape[0] // 2
-
-    def cut_sum(grad):
-        grad = grad.astype(jnp.bfloat16)
-        return jnp.concatenate([replica_sum(grad[:cut]), replica_sum(grad[cut:])], axis=0)
-
-    grad_down = cut_sum(grad_down)
-    grad_gates, grad_uppers = [], []
-    grad_ffn_in = None
-    for mask in range(group):
+    grad_down = grad_down.astype(jnp.bfloat16)
+    line = Line()
+    down_first, down_second = cut_sums(grad_down)
+    grad_gates, grad_uppers = {}, {}
+    order = list(masks) + [0]
+    returned = []
+    for mask in order:
         grad_hidden = contract(pieces[mask], down_weight, 1, 1)
         grad_gate, grad_upper = gated_back(gates[mask], uppers[mask], grad_hidden)
         part = (
             jnp.dot(grad_gate, gate_weight, preferred_element_type=jnp.float32)
             + jnp.dot(grad_upper, up_weight, preferred_element_type=jnp.float32)
         ).astype(jnp.bfloat16)
-        part = swapped(part, "fsdp", mask) if mask else part
-        grad_ffn_in = part.astype(jnp.float32) if mask == 0 else grad_ffn_in + part.astype(jnp.float32)
-        grad_gates.append(grad_gate)
-        grad_uppers.append(grad_upper)
-    grad_gate_w = cut_sum(contract(jnp.concatenate(grad_gates, axis=0), ffn_rows, 0, 0))
-    grad_up_w = cut_sum(contract(jnp.concatenate(grad_uppers, axis=0), ffn_rows, 0, 0))
+        returned.append(swapped(part, "fsdp", mask) if mask else part)
+        grad_gates[mask] = grad_gate
+        grad_uppers[mask] = grad_upper
+        if mask == order[0]:
+            pieces[order[1]] = line.advance([("down_first", down_first)], pieces[order[1]])
+    grad_gates[0] = line.advance([("down_second", down_second)], grad_gates[0])
+    grad_gate_w = contract(jnp.concatenate([grad_gates[i] for i in range(group)], axis=0), ffn_rows, 0, 0)
+    grad_up_w = contract(jnp.concatenate([grad_uppers[i] for i in range(group)], axis=0), ffn_rows, 0, 0)
+    gate_first, gate_second = cut_sums(grad_gate_w.astype(jnp.bfloat16))
+    up_first, up_second = cut_sums(grad_up_w.astype(jnp.bfloat16))
+    grad_ffn_in = sum(part.astype(jnp.float32) for part in returned)
     grad_resid_part, grad_gain_ffn = norm_back(resid, gain_ffn, grad_ffn_in)
     grad_resid = grad_result + grad_resid_part
     grad_attended, grad_gain_attn = norm_back(attended, gain_attn, grad_resid)
     grad_attended_low = grad_attended.astype(jnp.bfloat16)
+    grad_attended_low = line.advance([("gate_first", gate_first)], grad_attended_low)
     grad_wout = contract(grad_attended_low, mixed, 0, 0).astype(jnp.bfloat16)
-    owned_out = owner_sum(grad_wout.reshape(group, own_model, -1))
+    out_part = owner_part(grad_wout.reshape(group, own_model, -1))
     grad_mixed = jnp.dot(grad_attended_low, w_out, preferred_element_type=jnp.float32).astype(
         jnp.bfloat16
     )
@@ -295,6 +358,7 @@
     grad_probs = contract(grad_mixed_rows, values, 1, 1).reshape(rows, heads, width)
     delta = jnp.sum(grad_probs * probs, axis=-1, keepdims=True)
     grad_scores = (probs * (grad_probs - delta)).astype(jnp.bfloat16).reshape(rows * heads, width)
+    grad_scores = line.advance([("gate_second", gate_second)], grad_scores)
     grad_query = (jnp.dot(grad_scores, keys, preferred_element_type=jnp.float32) * scale).reshape(
         rows, heads, head_size
     )
@@ -306,6 +370,7 @@
         lower = (hops - step) * rows
         back = passed_along(grad_pairs[lower : lower + rows].astype(jnp.bfloat16), "fsdp", -step)
         grad_pair = grad_pair + back.astype(jnp.float32)
+    grad_pair = line.advance([("up_first", up_first)], grad_pair)
     grad_key = grad_pair[:, :head_size]
     grad_value = grad_pair[:, head_size:]
     _, pull_query = jax.vjp(
@@ -337,9 +402,16 @@
         axis=1,
     )
     gain_grads = jnp.pad(gain_grads[:, None, :], ((0, 0), (0, 31), (0, wide - sum(sizes))))
-    owned = owner_sum(
+    qkv_part = owner_part(
         jnp.concatenate([grad_wqkv.reshape(group, own_model, wide), gain_grads], axis=1)
     )
+    line.advance([("up_second", up_second), ("out", out_part)])
+    grad_down = cut_join(line.finished("down_first"), line.finished("down_second"))
+    line.advance([("qkv", qkv_part)])
+    grad_gate_w = cut_join(line.finished("gate_first"), line.finished("gate_second"))
+    grad_up_w = cut_join(line.finished("up_first"), line.finished("up_second"))
+    owned_out = core_join(line.finished("out"), 0).astype(jnp.float32)
+    owned = core_join(line.finished("qkv"), 0).astype(jnp.float32)
     owned_query = owned[:own_model, : heads * head_size]
     owned_key = owned[:own_model, heads * head_size : (heads + 1) * head_size]
     owned_value = owned[:own_model, (heads + 1) * head_size :]

time: 715 us -> 649 us (0.908)
  waiting for transfers between devices: 337 us -> 180 us
  other arithmetic: 67.3 us -> 135 us
  local copies, waits for them, and re-layouts: 70.3 us -> 89.8 us
  matrix products: 110 us -> 128 us
  starting transfers between devices: 116 us -> 103 us
    ppermute x24, waiting for transfers between devices: 253 us -> 118 us  [along_line(): return lax.ppermute(block, 'replica', route)]
    convert_element_type x24 -> x21, other arithmetic: 11.9 us -> 38.8 us  [added(): return lax.optimization_barrier(total.astype(jnp.bfloat16))]
    convert_element_type x5 -> x7, other arithmetic: 2.9 us -> 20.4 us  [the longest x3 15.9 us: cut_join(): whole = core_join(mine, 1).astype(jnp.float32)]
    dot_general x23, matrix products: 78.1 us -> 92.3 us  [contract(): lax.dot_general(left, right, (((left_dim,), (right_dim,)), ((), ())), pre...]
    ppermute x42 -> x36, waiting for transfers between devices: 71.1 us -> 57 us  [swapped(): return lax.ppermute(block, axis, route)]
    dot_general x0 -> x4, local copies, waits for them, and re-layouts: none -> 11.7 us  [contract(): lax.dot_general(left, right, (((left_dim,), (right_dim,)), ((), ())), pre...]
    concatenate x3 -> x0, other arithmetic: 11.3 us -> none  [cut_sum(): jnp.concatenate([replica_sum(grad[:cut]), replica_sum(grad[cut:])], axis=0)]
    integer_pow x0 -> x4, local copies, waits for them, and re-layouts: none -> 9.43 us  [gated(): return jax.nn.gelu(gate, approximate=True) * upper]
  transfers between devices with their start and end apart: 70 -> 64, of which waited for: 32 -> 23; matrix products, arithmetic and copies ran while one was open for 29% -> 44% of each run, Pallas kernels for 0% -> 0%
where the time goes in v2:
time: 649 us; the launch traced here: 639 us
  waiting for transfers between devices  180 us (28%)
  other arithmetic  135 us (21%)
  matrix products  128 us (20%)
  starting transfers between devices  103 us (16%)
  local copies, waits for them, and re-layouts  89.8 us (14%)
    ppermute x24, waiting for transfers between devices, along_line(): return lax.ppermute(block, 'replica', route)  118 us
    dot_general x23, matrix products, contract(): lax.dot_general(left, right, (((left_dim,), (right_dim,)), ((), ())), pre...  92.3 us
    ppermute x36, waiting for transfers between devices, swapped(): return lax.ppermute(block, axis, route)  57 us
    ppermute x24, starting transfers between devices, along_line(): return lax.ppermute(block, 'replica', route)  56.1 us
    convert_element_type x21, other arithmetic, added(): return lax.optimization_barrier(total.astype(jnp.bfloat16))  38.8 us
    ppermute x36, starting transfers between devices, swapped(): return lax.ppermute(block, axis, route)  36.4 us
    select_n x5, other arithmetic, joined(): jnp.where(core == 0, jnp.concatenate([mine, other], axis=axis), jnp.conca...  18.3 us
    unnamed x337, local copies, waits for them, and re-layouts  16 us
  transfers between devices with their start and end apart: 64, of which 23 were waited for; matrix products, arithmetic and copies ran while one was open for 44% of the time, Pallas kernels for 0%

profile of v2, /device:TPU:0, one launch (start us, length us, event | category | flops | bytes accessed | tf_op | source)
XLA Modules:
  0.0 638.9 jit_solution(11178551220552036206)
XLA Ops:
  22.1 9.8 %collective-permute-done.6 = bf16[144,1024]{1,0:T(8,128)(2,1)S(1)} collective-permute-done((bf16[144,1024]{1,0:T(8,128)(2,1)}, bf16[144,1024]{1,0:T(8,128)(2,1)S(1)}, u32[]{:S(2)}, u32[]{:S(2)}) %collective-permute-start.6) | collective-permute-done | bytes 294944 | tf_op jit(solution)/shard_map/ppermute | solution.py:16
  33.4 14.0 %collective-permute-done.7 = bf16[144,1024]{1,0:T(8,128)(2,1)S(1)} collective-permute-done((bf16[144,1024]{1,0:T(8,128)(2,1)}, bf16[144,1024]{1,0:T(8,128)(2,1)S(1)}, u32[]{:S(2)}, u32[]{:S(2)}) %collective-permute-start.7) | collective-permute-done | bytes 294944 | tf_op jit(solution)/shard_map/ppermute | solution.py:16
  86.8 5.7 collective-permute-done.4
  106.7 5.4 fusion.167
  112.1 6.8 %collective-permute-done.10 = bf16[256,1152]{1,0:T(8,128)(2,1)S(1)} collective-permute-done((bf16[256,1152]{1,0:T(8,128)(2,1)}, bf16[256,1152]{1,0:T(8,128)(2,1)S(1)}, u32[]{:S(2)}, u32[]{:S(2)}) %collective-permute-start.10) | collective-permute-done | bytes 589856 | tf_op jit(solution)/shard_map/ppermute | solution.py:16
  127.8 5.7 multiply_convert_fusion.7
  144.9 5.7 multiply_convert_fusion.6
  165.0 6.2 multiply_convert_fusion.5
  185.6 5.0 multiply_convert_fusion.8
  220.8 6.8 %convolution_convert_fusion.2 = bf16[1728,1152]{1,0:T(8,128)(2,1)S(1)} fusion(bf16[256,1728]{1,0:T(8,128)(2,1)S(1)} %copy-done.93, bf16[256,1728]{1,0:T(8,128)(2,1)S(1)} %copy-done.91, bf16[256,1728]{1,0:T(8,128)(2,1)S(1)} %copy-done.89, bf16[256,1728]{1,0:T(8,128)(2,1)S(1)} %copy-done.95, bf16[256,1152]{1,0:T(8,128)(2,1)} %collective-permute-done.19, ...), kind=kOutput, calls=%fused_computation.5 | convolution fusion | flops 4102447104 | bytes 9879552 | tf_op jit(solution)/shard_map/dot_general | solution.py:170
  243.5 5.7 multiply_convert_fusion.3
  258.1 6.3 convolution_convert_fusion
  278.4 5.6 collective-permute-start.25
  284.1 7.1 %convolution_convert_fusion.1 = bf16[1728,1152]{1,0:T(8,128)(2,1)S(1)} fusion(bf16[256,1728]{1,0:T(8,128)(2,1)} %copy-done.165, bf16[256,1728]{1,0:T(8,128)(2,1)} %copy-done.166, bf16[256,1728]{1,0:T(8,128)(2,1)S(1)} %copy-done.164, bf16[256,1728]{1,0:T(8,128)(2,1)} %get-tuple-element.55, bf16[256,1152]{1,0:T(8,128)(2,1)} %collective-permute-done.14, ...), kind=kOutput, calls=%fused_computation.4 | convolution fusion | flops 4102447104 | bytes 9879552 | tf_op jit(solution)/shard_map/dot_general | solution.py:170
  297.0 5.3 collective-permute-done.25
  318.3 16.9 %collective-permute-start.29 = (bf16[432,1152]{1,0:T(8,128)(2,1)}, bf16[432,1152]{1,0:T(8,128)(2,1)}, u32[]{:S(2)}, u32[]{:S(2)}) collective-permute-start(bf16[432,1152]{1,0:T(8,128)(2,1)} %get-tuple-element.58), channel_id=1, source_target_pairs={{0,8},{4,12},{24,16},{28,20},{1,9},{5,13},{25,17},{29,21},{2,10},{... | collective-permute-start | bytes 2985992 | tf_op jit(solution)/shard_map/ppermute | solution.py:26
  335.3 6.6 %multiply_convert_fusion = bf16[256,4,768]{2,0,1:T(8,128)(2,1)} fusion(f32[256,4,768]{2,0,1:T(8,128)S(1)} %fusion.118, f32[256,4,768]{2,1,0:T(4,128)S(1)} %copy-done.63, f32[256,4]{0,1:T(4,128)S(1)} %copy.257, pred[256,768]{1,0:T(8,128)(4,1)S(1)} %copy-done.105), kind=kOutput, calls=%fused_computation.54 | output fusion | flops 6293247 | bytes 8065024 | tf_op jit(solution)/shard_map/sub | solution.py:360
  363.4 13.1 %collective-permute-done.27 = bf16[432,1152]{1,0:T(8,128)(2,1)S(1)} collective-permute-done((bf16[432,1152]{1,0:T(8,128)(2,1)S(1)}, bf16[432,1152]{1,0:T(8,128)(2,1)S(1)}, u32[]{:S(2)}, u32[]{:S(2)}) %collective-permute-start.27) | collective-permute-done | bytes 995360 | tf_op jit(solution)/shard_map/ppermute | solution.py:26
  409.7 5.1 collective-permute-done.41
  420.9 10.4 %collective-permute-done.30 = bf16[432,1152]{1,0:T(8,128)(2,1)S(1)} collective-permute-done((bf16[432,1152]{1,0:T(8,128)(2,1)S(1)}, bf16[432,1152]{1,0:T(8,128)(2,1)S(1)}, u32[]{:S(2)}, u32[]{:S(2)}) %collective-permute-start.30) | collective-permute-done | bytes 995360 | tf_op jit(solution)/shard_map/ppermute | solution.py:26
  454.0 8.6 %collective-permute-done.38 = bf16[432,1152]{1,0:T(8,128)(2,1)} collective-permute-done((bf16[432,1152]{1,0:T(8,128)(2,1)}, bf16[432,1152]{1,0:T(8,128)(2,1)}, u32[]{:S(2)}, u32[]{:S(2)}) %collective-permute-start.38) | collective-permute-done | bytes 995360 | tf_op jit(solution)/shard_map/ppermute | solution.py:26
  466.6 12.4 %collective-permute-done.36 = bf16[432,1152]{1,0:T(8,128)(2,1)S(1)} collective-permute-done((bf16[432,1152]{1,0:T(8,128)(2,1)S(1)}, bf16[432,1152]{1,0:T(8,128)(2,1)S(1)}, u32[]{:S(2)}, u32[]{:S(2)}) %collective-permute-start.36) | collective-permute-done | bytes 995360 | tf_op jit(solution)/shard_map/ppermute | solution.py:26
  496.1 13.4 %collective-permute-done.45 = bf16[432,1152]{1,0:T(8,128)(2,1)S(1)} collective-permute-done((bf16[432,1152]{1,0:T(8,128)(2,1)}, bf16[432,1152]{1,0:T(8,128)(2,1)S(1)}, u32[]{:S(2)}, u32[]{:S(2)}) %collective-permute-start.45) | collective-permute-done | bytes 995360 | tf_op jit(solution)/shard_map/ppermute | solution.py:26
  515.9 5.4 maximum_select_fusion.2
  521.3 10.8 %collective-permute-done.49 = bf16[160,1536]{1,0:T(8,128)(2,1)S(1)} collective-permute-done((bf16[160,1536]{1,0:T(8,128)(2,1)S(1)}, bf16[160,1536]{1,0:T(8,128)(2,1)S(1)}, u32[]{:S(2)}, u32[]{:S(2)}) %collective-permute-start.49) | collective-permute-done | bytes 491552 | tf_op jit(solution)/shard_map/ppermute | solution.py:16
  548.7 15.2 %collective-permute-done.51 = bf16[432,1152]{1,0:T(8,128)(2,1)S(1)} collective-permute-done((bf16[432,1152]{1,0:T(8,128)(2,1)}, bf16[432,1152]{1,0:T(8,128)(2,1)S(1)}, u32[]{:S(2)}, u32[]{:S(2)}) %collective-permute-start.51) | collective-permute-done | bytes 995360 | tf_op jit(solution)/shard_map/ppermute | solution.py:26
  568.4 5.9 bitcast_convert_fusion
  574.3 8.2 %collective-permute-done.56 = bf16[144,1024]{1,0:T(8,128)(2,1)S(1)} collective-permute-done((bf16[144,1024]{1,0:T(8,128)(2,1)}, bf16[144,1024]{1,0:T(8,128)(2,1)S(1)}, u32[]{:S(2)}, u32[]{:S(2)}) %collective-permute-start.56) | collective-permute-done | bytes 294944 | tf_op jit(solution)/shard_map/ppermute | solution.py:26
  584.2 15.8 %collective-permute-done.55 = bf16[432,1152]{1,0:T(8,128)(2,1)S(1)} collective-permute-done((bf16[432,1152]{1,0:T(8,128)(2,1)}, bf16[432,1152]{1,0:T(8,128)(2,1)S(1)}, u32[]{:S(2)}, u32[]{:S(2)}) %collective-permute-start.55) | collective-permute-done | bytes 995360 | tf_op jit(solution)/shard_map/ppermute | solution.py:26
  605.9 5.4 maximum_select_fusion
  611.3 8.3 %collective-permute-done.58 = bf16[160,1536]{1,0:T(8,128)(2,1)S(1)} collective-permute-done((bf16[160,1536]{1,0:T(8,128)(2,1)S(1)}, bf16[160,1536]{1,0:T(8,128)(2,1)S(1)}, u32[]{:S(2)}, u32[]{:S(2)}) %collective-permute-start.58) | collective-permute-done | bytes 491552 | tf_op jit(solution)/shard_map/ppermute | solution.py:26
  620.4 5.9 bitcast_convert_fusion.2
  (651 shorter events, 367.0 us)
Async XLA Ops:
  8.9 39.6 %collective-permute-start.2 = (bf16[160,1536]{1,0:T(8,128)(2,1)}, bf16[160,1536]{1,0:T(8,128)(2,1)}, u32[]{:S(2)}, u32[]{:S(2)}) collective-permute-start(bf16[160,1536]{1,0:T(8,128)(2,1)} %pad_maximum_fusion.13), channel_id=1, source_target_pairs={{0,3},{1,2},{2,1},{3,0},{4,7},{5,6},{6,5},{7,4},{8,11},{9,10},{10,... | collective-permute-start | bytes 1474568 | tf_op jit(solution)/shard_map/ppermute | solution.py:16
  12.7 36.7 %collective-permute-start.1 = (bf16[160,1536]{1,0:T(8,128)(2,1)}, bf16[160,1536]{1,0:T(8,128)(2,1)}, u32[]{:S(2)}, u32[]{:S(2)}) collective-permute-start(bf16[160,1536]{1,0:T(8,128)(2,1)} %pad_maximum_fusion.13), channel_id=1, source_target_pairs={{0,2},{1,3},{2,0},{3,1},{4,6},{5,7},{6,4},{7,5},{8,10},{9,11},{10,... | collective-permute-start | bytes 1474568 | tf_op jit(solution)/shard_map/ppermute | solution.py:16
  14.1 33.3 %collective-permute-start.7 = (bf16[144,1024]{1,0:T(8,128)(2,1)}, bf16[144,1024]{1,0:T(8,128)(2,1)S(1)}, u32[]{:S(2)}, u32[]{:S(2)}) collective-permute-start(bf16[144,1024]{1,0:T(8,128)(2,1)} %constant_dynamic-slice_fusion.5), channel_id=1, source_target_pairs={{0,2},{1,3},{2,0},{3,1},{4,6},{5,7},{6,4},{7,5},{8,10},{9,11},{10,... | collective-permute-start | bytes 884744 | tf_op jit(solution)/shard_map/ppermute | solution.py:16
  16.0 31.3 %collective-permute-start.8 = (bf16[144,1024]{1,0:T(8,128)(2,1)}, bf16[144,1024]{1,0:T(8,128)(2,1)S(1)}, u32[]{:S(2)}, u32[]{:S(2)}) collective-permute-start(bf16[144,1024]{1,0:T(8,128)(2,1)} %constant_dynamic-slice_fusion.5), channel_id=1, source_target_pairs={{0,3},{1,2},{2,1},{3,0},{4,7},{5,6},{6,5},{7,4},{8,11},{9,10},{10,... | collective-permute-start | bytes 884744 | tf_op jit(solution)/shard_map/ppermute | solution.py:16
  102.6 33.0 %collective-permute-start.12 = (bf16[256,1152]{1,0:T(8,128)(2,1)}, bf16[256,1152]{1,0:T(8,128)(2,1)}, u32[]{:S(2)}, u32[]{:S(2)}) collective-permute-start(bf16[256,1152]{1,0:T(8,128)(2,1)} %multiply_convert_fusion.9), channel_id=1, source_target_pairs={{0,2},{1,3},{2,0},{3,1},{4,6},{5,7},{6,4},{7,5},{8,10},{9,11},{10,... | collective-permute-start | bytes 1769480 | tf_op jit(solution)/shard_map/ppermute | solution.py:16
  105.2 50.1 %collective-permute-start.14 = (bf16[256,1152]{1,0:T(8,128)(2,1)}, bf16[256,1152]{1,0:T(8,128)(2,1)}, u32[]{:S(2)}, u32[]{:S(2)}) collective-permute-start(bf16[256,1152]{1,0:T(8,128)(2,1)} %multiply_convert_fusion.9), channel_id=1, source_target_pairs={{0,3},{1,2},{2,1},{3,0},{4,7},{5,6},{6,5},{7,4},{8,11},{9,10},{10,... | collective-permute-start | bytes 1769480 | tf_op jit(solution)/shard_map/ppermute | solution.py:16
  135.6 55.0 %collective-permute-start.11 = (bf16[256,1152]{1,0:T(8,128)(2,1)}, bf16[256,1152]{1,0:T(8,128)(2,1)}, u32[]{:S(2)}, u32[]{:S(2)}) collective-permute-start(bf16[256,1152]{1,0:T(8,128)(2,1)} %convolution_convert_fusion.7), channel_id=1, source_target_pairs={{0,1},{1,0},{2,3},{3,2},{4,5},{5,4},{6,7},{7,6},{8,9},{9,8},{10,11... | collective-permute-start | bytes 1769480 | tf_op jit(solution)/shard_map/ppermute | solution.py:16
  152.8 37.8 %collective-permute-start.13 = (bf16[256,1152]{1,0:T(8,128)(2,1)}, bf16[256,1152]{1,0:T(8,128)(2,1)}, u32[]{:S(2)}, u32[]{:S(2)}) collective-permute-start(bf16[256,1152]{1,0:T(8,128)(2,1)} %convolution_convert_fusion.6), channel_id=1, source_target_pairs={{0,2},{1,3},{2,0},{3,1},{4,6},{5,7},{6,4},{7,5},{8,10},{9,11},{10,... | collective-permute-start | bytes 1769480 | tf_op jit(solution)/shard_map/ppermute | solution.py:16
  197.9 22.8 %collective-permute-start.19 = (bf16[256,1152]{1,0:T(8,128)(2,1)}, bf16[256,1152]{1,0:T(8,128)(2,1)}, u32[]{:S(2)}, u32[]{:S(2)}) collective-permute-start(bf16[256,1152]{1,0:T(8,128)(2,1)} %get-tuple-element.158), channel_id=1, source_target_pairs={{0,3},{1,2},{2,1},{3,0},{4,7},{5,6},{6,5},{7,4},{8,11},{9,10},{10,... | collective-permute-start | bytes 1769480 | tf_op jit(solution)/shard_map/ppermute | solution.py:16
  232.0 35.0 %collective-permute-start.17 = (bf16[256,1152]{1,0:T(8,128)(2,1)}, bf16[256,1152]{1,0:T(8,128)(2,1)}, u32[]{:S(2)}, u32[]{:S(2)}) collective-permute-start(bf16[256,1152]{1,0:T(8,128)(2,1)} %fusion.29), channel_id=1, source_target_pairs={{0,1},{1,0},{2,3},{3,2},{4,5},{5,4},{6,7},{7,6},{8,9},{9,8},{10,11... | collective-permute-start | bytes 1769480 | tf_op jit(solution)/shard_map/ppermute | solution.py:16
  240.2 26.9 %collective-permute-start.22 = (bf16[256,1152]{1,0:T(8,128)(2,1)}, bf16[256,1152]{1,0:T(8,128)(2,1)}, u32[]{:S(2)}, u32[]{:S(2)}) collective-permute-start(bf16[256,1152]{1,0:T(8,128)(2,1)} %fusion.31), channel_id=1, source_target_pairs={{0,3},{1,2},{2,1},{3,0},{4,7},{5,6},{6,5},{7,4},{8,11},{9,10},{10,... | collective-permute-start | bytes 1769480 | tf_op jit(solution)/shard_map/ppermute | solution.py:16
  254.6 22.7 %collective-permute-start.23 = (bf16[432,1152]{1,0:T(8,128)(2,1)S(1)}, bf16[432,1152]{1,0:T(8,128)(2,1)S(1)}, u32[]{:S(2)}, u32[]{:S(2)}) collective-permute-start(bf16[432,1152]{1,0:T(8,128)(2,1)S(1)} %copy-done.34), channel_id=1, source_target_pairs={{0,8},{4,12},{24,16},{28,20},{1,9},{5,13},{25,17},{29,21},{2,10},{... | collective-permute-start | bytes 2985992 | tf_op jit(solution)/shard_map/ppermute | solution.py:26
  267.0 40.2 %collective-permute-start.33 = (bf16[2,432,1152]{2,1,0:T(8,128)(2,1)}, bf16[2,432,1152]{2,1,0:T(8,128)(2,1)}, u32[]{:S(2)}, u32[]{:S(2)}) collective-permute-start(bf16[2,432,1152]{2,1,0:T(8,128)(2,1)} %constant_dynamic-slice_fusion.2), channel_id=1, source_target_pairs={{0,4},{4,0},{8,12},{12,8},{16,20},{20,16},{24,28},{28,24},{1,5},{5... | collective-permute-start | bytes 5971976 | tf_op jit(solution)/shard_map/ppermute | solution.py:16
  278.4 23.9 %collective-permute-start.25 = (bf16[432,1152]{1,0:T(8,128)(2,1)}, bf16[432,1152]{1,0:T(8,128)(2,1)}, u32[]{:S(2)}, u32[]{:S(2)}) collective-permute-start(bf16[432,1152]{1,0:T(8,128)(2,1)} %get-tuple-element.54), channel_id=1, source_target_pairs={{0,8},{4,12},{24,16},{28,20},{1,9},{5,13},{25,17},{29,21},{2,10},{... | collective-permute-start | bytes 2985992 | tf_op jit(solution)/shard_map/ppermute | solution.py:26
  318.3 41.1 %collective-permute-start.29 = (bf16[432,1152]{1,0:T(8,128)(2,1)}, bf16[432,1152]{1,0:T(8,128)(2,1)}, u32[]{:S(2)}, u32[]{:S(2)}) collective-permute-start(bf16[432,1152]{1,0:T(8,128)(2,1)} %get-tuple-element.58), channel_id=1, source_target_pairs={{0,8},{4,12},{24,16},{28,20},{1,9},{5,13},{25,17},{29,21},{2,10},{... | collective-permute-start | bytes 2985992 | tf_op jit(solution)/shard_map/ppermute | solution.py:26
  351.4 25.1 %collective-permute-start.27 = (bf16[432,1152]{1,0:T(8,128)(2,1)S(1)}, bf16[432,1152]{1,0:T(8,128)(2,1)S(1)}, u32[]{:S(2)}, u32[]{:S(2)}) collective-permute-start(bf16[432,1152]{1,0:T(8,128)(2,1)S(1)} %copy-done.37), channel_id=1, source_target_pairs={{8,0},{12,4},{16,24},{20,28},{9,1},{13,5},{17,25},{21,29},{10,2},{... | collective-permute-start | bytes 2985992 | tf_op jit(solution)/shard_map/ppermute | solution.py:26
  356.2 38.3 %collective-permute-start.39 = (bf16[4,144,1024]{2,1,0:T(8,128)(2,1)}, bf16[4,144,1024]{2,1,0:T(8,128)(2,1)}, u32[]{:S(2)}, u32[]{:S(2)}) collective-permute-start(bf16[4,144,1024]{2,1,0:T(8,128)(2,1)} %constant_dynamic-slice_fusion.1), channel_id=1, source_target_pairs={{0,4},{4,0},{8,12},{12,8},{16,20},{20,16},{24,28},{28,24},{1,5},{5... | collective-permute-start | bytes 3538952 | tf_op jit(solution)/shard_map/ppermute | solution.py:16
  383.1 22.4 %collective-permute-start.35 = (bf16[256,512]{1,0:T(8,128)(2,1)}, bf16[256,512]{1,0:T(8,128)(2,1)}, u32[]{:S(2)}, u32[]{:S(2)}) collective-permute-start(bf16[256,512]{1,0:T(8,128)(2,1)} %get-tuple-element.164), channel_id=1, source_target_pairs={{2,0},{3,1},{6,4},{7,5},{10,8},{11,9},{14,12},{15,13},{18,16},{19,... | collective-permute-start | bytes 786440 | tf_op jit(solution)/shard_map/ppermute | solution.py:166
  384.4 32.6 %collective-permute-start.32 = (bf16[432,1152]{1,0:T(8,128)(2,1)}, bf16[432,1152]{1,0:T(8,128)(2,1)}, u32[]{:S(2)}, u32[]{:S(2)}) collective-permute-start(bf16[432,1152]{1,0:T(8,128)(2,1)} %get-tuple-element.63), channel_id=1, source_target_pairs={{0,8},{4,12},{24,16},{28,20},{1,9},{5,13},{25,17},{29,21},{2,10},{... | collective-permute-start | bytes 2985992 | tf_op jit(solution)/shard_map/ppermute | solution.py:26
  408.3 22.9 %collective-permute-start.30 = (bf16[432,1152]{1,0:T(8,128)(2,1)S(1)}, bf16[432,1152]{1,0:T(8,128)(2,1)S(1)}, u32[]{:S(2)}, u32[]{:S(2)}) collective-permute-start(bf16[432,1152]{1,0:T(8,128)(2,1)S(1)} %copy-done.31), channel_id=1, source_target_pairs={{8,0},{12,4},{16,24},{20,28},{9,1},{13,5},{17,25},{21,29},{10,2},{... | collective-permute-start | bytes 2985992 | tf_op jit(solution)/shard_map/ppermute | solution.py:26
  447.4 68.4 %collective-permute-start.63 = (bf16[2,432,1152]{2,1,0:T(8,128)(2,1)}, bf16[2,432,1152]{2,1,0:T(8,128)(2,1)}, u32[]{:S(2)}, u32[]{:S(2)}) collective-permute-start(bf16[2,432,1152]{2,1,0:T(8,128)(2,1)} %pad_maximum_fusion.5), channel_id=1, source_target_pairs={{0,4},{4,0},{8,12},{12,8},{16,20},{20,16},{24,28},{28,24},{1,5},{5... | collective-permute-start | bytes 5971976 | tf_op jit(solution)/shard_map/ppermute | solution.py:16
  452.1 40.2 %collective-permute-start.47 = (bf16[4,160,1536]{2,1,0:T(8,128)(2,1)}, bf16[4,160,1536]{2,1,0:T(8,128)(2,1)}, u32[]{:S(2)}, u32[]{:S(2)}) collective-permute-start(bf16[4,160,1536]{2,1,0:T(8,128)(2,1)} %constant_dynamic-slice_fusion), channel_id=1, source_target_pairs={{0,4},{4,0},{8,12},{12,8},{16,20},{20,16},{24,28},{28,24},{1,5},{5... | collective-permute-start | bytes 5898248 | tf_op jit(solution)/shard_map/ppermute | solution.py:16
  452.6 26.4 %collective-permute-start.36 = (bf16[432,1152]{1,0:T(8,128)(2,1)S(1)}, bf16[432,1152]{1,0:T(8,128)(2,1)S(1)}, u32[]{:S(2)}, u32[]{:S(2)}) collective-permute-start(bf16[432,1152]{1,0:T(8,128)(2,1)S(1)} %copy-done.32), channel_id=1, source_target_pairs={{8,0},{12,4},{16,24},{20,28},{9,1},{13,5},{17,25},{21,29},{10,2},{... | collective-permute-start | bytes 2985992 | tf_op jit(solution)/shard_map/ppermute | solution.py:26
  484.5 24.9 %collective-permute-start.45 = (bf16[432,1152]{1,0:T(8,128)(2,1)}, bf16[432,1152]{1,0:T(8,128)(2,1)S(1)}, u32[]{:S(2)}, u32[]{:S(2)}) collective-permute-start(bf16[432,1152]{1,0:T(8,128)(2,1)} %get-tuple-element.70), channel_id=1, source_target_pairs={{0,8},{4,12},{24,16},{28,20},{1,9},{5,13},{25,17},{29,21},{2,10},{... | collective-permute-start | bytes 2985992 | tf_op jit(solution)/shard_map/ppermute | solution.py:26
  485.9 26.3 %collective-permute-start.44 = (bf16[432,1152]{1,0:T(8,128)(2,1)}, bf16[432,1152]{1,0:T(8,128)(2,1)S(1)}, u32[]{:S(2)}, u32[]{:S(2)}) collective-permute-start(bf16[432,1152]{1,0:T(8,128)(2,1)} %get-tuple-element.69), channel_id=1, source_target_pairs={{8,16},{12,20},{16,8},{20,12},{9,17},{13,21},{17,9},{21,13},{10,18... | collective-permute-start | bytes 2985992 | tf_op jit(solution)/shard_map/ppermute | solution.py:26
  489.3 25.5 %collective-permute-start.43 = (bf16[432,1152]{1,0:T(8,128)(2,1)}, bf16[432,1152]{1,0:T(8,128)(2,1)S(1)}, u32[]{:S(2)}, u32[]{:S(2)}) collective-permute-start(bf16[432,1152]{1,0:T(8,128)(2,1)} %get-tuple-element.68), channel_id=1, source_target_pairs={{8,0},{12,4},{16,24},{20,28},{9,1},{13,5},{17,25},{21,29},{10,2},{... | collective-permute-start | bytes 2985992 | tf_op jit(solution)/shard_map/ppermute | solution.py:26
  494.5 26.7 %collective-permute-start.48 = (bf16[160,1536]{1,0:T(8,128)(2,1)S(1)}, bf16[160,1536]{1,0:T(8,128)(2,1)S(1)}, u32[]{:S(2)}, u32[]{:S(2)}) collective-permute-start(bf16[160,1536]{1,0:T(8,128)(2,1)S(1)} %get-tuple-element.151), channel_id=1, source_target_pairs={{0,1},{1,0},{2,3},{3,2},{4,5},{5,4},{6,7},{7,6},{8,9},{9,8},{10,11... | collective-permute-start | bytes 1474568 | tf_op jit(solution)/shard_map/ppermute | solution.py:16
  509.5 22.6 %collective-permute-start.49 = (bf16[160,1536]{1,0:T(8,128)(2,1)S(1)}, bf16[160,1536]{1,0:T(8,128)(2,1)S(1)}, u32[]{:S(2)}, u32[]{:S(2)}) collective-permute-start(bf16[160,1536]{1,0:T(8,128)(2,1)S(1)} %get-tuple-element.153), channel_id=1, source_target_pairs={{0,2},{1,3},{2,0},{3,1},{4,6},{5,7},{6,4},{7,5},{8,10},{9,11},{10,... | collective-permute-start | bytes 1474568 | tf_op jit(solution)/shard_map/ppermute | solution.py:16
  539.0 25.0 %collective-permute-start.51 = (bf16[432,1152]{1,0:T(8,128)(2,1)}, bf16[432,1152]{1,0:T(8,128)(2,1)S(1)}, u32[]{:S(2)}, u32[]{:S(2)}) collective-permute-start(bf16[432,1152]{1,0:T(8,128)(2,1)} %get-tuple-element.72), channel_id=1, source_target_pairs={{8,0},{12,4},{16,24},{20,28},{9,1},{13,5},{17,25},{21,29},{10,2},{... | collective-permute-start | bytes 2985992 | tf_op jit(solution)/shard_map/ppermute | solution.py:26
  543.1 62.8 %collective-permute-start.61 = (bf16[2,432,1152]{2,1,0:T(8,128)(2,1)}, bf16[2,432,1152]{2,1,0:T(8,128)(2,1)}, u32[]{:S(2)}, u32[]{:S(2)}) collective-permute-start(bf16[2,432,1152]{2,1,0:T(8,128)(2,1)} %pad_maximum_fusion.3), channel_id=1, source_target_pairs={{0,4},{4,0},{8,12},{12,8},{16,20},{20,16},{24,28},{28,24},{1,5},{5... | collective-permute-start | bytes 5971976 | tf_op jit(solution)/shard_map/ppermute | solution.py:16
  567.0 32.9 %collective-permute-start.55 = (bf16[432,1152]{1,0:T(8,128)(2,1)}, bf16[432,1152]{1,0:T(8,128)(2,1)S(1)}, u32[]{:S(2)}, u32[]{:S(2)}) collective-permute-start(bf16[432,1152]{1,0:T(8,128)(2,1)} %get-tuple-element.76), channel_id=1, source_target_pairs={{8,0},{12,4},{16,24},{20,28},{9,1},{13,5},{17,25},{21,29},{10,2},{... | collective-permute-start | bytes 2985992 | tf_op jit(solution)/shard_map/ppermute | solution.py:26
  604.0 26.9 %collective-permute-start.62 = (bf16[2,432,1152]{2,1,0:T(8,128)(2,1)}, bf16[2,432,1152]{2,1,0:T(8,128)(2,1)}, u32[]{:S(2)}, u32[]{:S(2)}) collective-permute-start(bf16[2,432,1152]{2,1,0:T(8,128)(2,1)} %pad_maximum_fusion.4), channel_id=1, source_target_pairs={{0,4},{4,0},{8,12},{12,8},{16,20},{20,16},{24,28},{28,24},{1,5},{5... | collective-permute-start | bytes 5971976 | tf_op jit(solution)/shard_map/ppermute | solution.py:16
  (199 other events, 1448.1 us)

commit v3 on v1

--- a/solution.py
+++ b/solution.py
@@ -1,6 +1,8 @@
 import jax
 import jax.numpy as jnp
 from jax import lax
+from jax.experimental import pallas as pl
+from jax.experimental.pallas import tpu as pltpu
 from jax.sharding import PartitionSpec as P
 
 WINDOW = 512
@@ -20,22 +22,337 @@
     return lax.optimization_barrier(total.astype(jnp.bfloat16))
 
 
-def along_line(block, pairs):
+VMEM_LIMIT = 56 * 1024 * 1024
+
+
+def params(*semantics):
+    return pltpu.CompilerParams(vmem_limit_bytes=VMEM_LIMIT)
+
+
+def dot(left, right, left_dim, right_dim):
+    return lax.dot_general(
+        left, right, (((left_dim,), (right_dim,)), ((), ())), preferred_element_type=jnp.float32
+    )
+
+
+def tile_of(size, most):
+    return max(tile for tile in range(16, most + 1, 16) if size % tile == 0)
+
+
+GELU_A = (2.0 / 3.141592653589793) ** 0.5
+GELU_B = 0.044715
+
+
+def ffn_forward_kernel(x_ref, gate_ref, up_ref, down_ref, hidden_ref, slope_ref, act_ref, out_ref, acc):
+    step = pl.program_id(0)
+    x = x_ref[...]
+    gate = dot(gate_ref[...], x, 1, 1)
+    upper = dot(up_ref[...], x, 1, 1)
+    square = gate * gate
+    bend = jnp.tanh(GELU_A * gate * (1.0 + GELU_B * square))
+    half = 0.5 + 0.5 * bend
+    act = gate * half
+    slope = half + 0.5 * gate * (1.0 - bend * bend) * (GELU_A * (1.0 + 3.0 * GELU_B * square))
+    hidden = (act * upper).astype(jnp.bfloat16)
+    hidden_ref[...] = hidden
+    slope_ref[...] = (slope * upper).astype(jnp.bfloat16)
+    act_ref[...] = act.astype(jnp.bfloat16)
+    part = dot(hidden, down_ref[...], 0, 0)
+
+    @pl.when(step == 0)
+    def _():
+        acc[...] = part
+
+    @pl.when(step > 0)
+    def _():
+        acc[...] += part
+
+    @pl.when(step == pl.num_programs(0) - 1)
+    def _():
+        out_ref[...] = acc[...].astype(jnp.bfloat16)
+
+
+def ffn_forward(x, gate_weight, up_weight, down_weight):
+    rows, model = x.shape
+    units = gate_weight.shape[0]
+    tile = tile_of(units, 432)
+    weight = pl.BlockSpec((tile, model), lambda i: (i, 0))
+    flat = pl.BlockSpec((tile, rows), lambda i: (i, 0))
+    whole = pl.BlockSpec((rows, model), lambda i: (0, 0))
+    kept = jax.ShapeDtypeStruct((units, rows), jnp.bfloat16)
+    return pl.pallas_call(
+        ffn_forward_kernel,
+        grid=(units // tile,),
+        out_shape=[kept, kept, kept, jax.ShapeDtypeStruct((rows, model), jnp.bfloat16)],
+        in_specs=[whole, weight, weight, weight],
+        out_specs=[flat, flat, flat, whole],
+        scratch_shapes=[pltpu.VMEM((rows, model), jnp.float32)],
+        compiler_params=params(),
+        name="ffn_forward",
+    )(x, gate_weight, up_weight, down_weight)
+
+
+def ffn_backward_kernel(
+    grad_ref, gate_ref, up_ref, down_ref, slope_ref, act_ref, gate_grad_ref, up_grad_ref, out_ref, acc
+):
+    step = pl.program_id(0)
+    grad_hidden = dot(down_ref[...], grad_ref[...], 1, 1)
+    grad_gate = (grad_hidden * slope_ref[...].astype(jnp.float32)).astype(jnp.bfloat16)
+    grad_upper = (grad_hidden * act_ref[...].astype(jnp.float32)).astype(jnp.bfloat16)
+    gate_grad_ref[...] = grad_gate
+    up_grad_ref[...] = grad_upper
+    part = dot(grad_gate, gate_ref[...], 0, 0) + dot(grad_upper, up_ref[...], 0, 0)
+
+    @pl.when(step == 0)
+    def _():
+        acc[...] = part
+
+    @pl.when(step > 0)
+    def _():
+        acc[...] += part
+
+    @pl.when(step == pl.num_programs(0) - 1)
+    def _():
+        out_ref[...] = acc[...].astype(jnp.bfloat16)
+
+
+def ffn_backward(grad, gate_weight, up_weight, down_weight, slope, act):
+    rows, model = grad.shape
+    units = gate_weight.shape[0]
+    tile = tile_of(units, 432)
+    weight = pl.BlockSpec((tile, model), lambda i: (i, 0))
+    flat = pl.BlockSpec((tile, rows), lambda i: (i, 0))
+    whole = pl.BlockSpec((rows, model), lambda i: (0, 0))
+    kept = jax.ShapeDtypeStruct((units, rows), jnp.bfloat16)
+    return pl.pallas_call(
+        ffn_backward_kernel,
+        grid=(units // tile,),
+        out_shape=[kept, kept, jax.ShapeDtypeStruct((rows, model), jnp.bfloat16)],
+        in_specs=[whole, weight, weight, weight, flat, flat],
+        out_specs=[flat, flat, whole],
+        scratch_shapes=[pltpu.VMEM((rows, model), jnp.float32)],
+        compiler_params=params(),
+        name="ffn_backward",
+    )(grad, gate_weight, up_weight, down_weight, slope, act)
+
+
+def chunks_of(units):
+    return 2 if units % 64 == 0 else 1
+
+
+def weight_grad(lefts, rights):
+    group = len(lefts)
+    units, rows = lefts[0].shape
+    model = rights[0].shape[1]
+    chunks = chunks_of(units)
+    tile = units // (2 * chunks)
+    core = (lax.axis_index("replica") % 2).astype(jnp.int32).reshape(1)
+
+    def kernel(core_ref, *refs):
+        left = jnp.concatenate([ref[...] for ref in refs[:group]], axis=1)
+        right = jnp.concatenate([ref[...] for ref in refs[group : 2 * group]], axis=0)
+        value = dot(left, right, 1, 0).astype(jnp.bfloat16)
+        other_ref, mine_ref = refs[2 * group :]
+
+        @pl.when(pl.program_id(0) == 0)
+        def _():
+            other_ref[0] = value
+
+        @pl.when(pl.program_id(0) == 1)
+        def _():
+            mine_ref[0] = value
+
+    def left_map(side, chunk, core_ref):
+        return (2 * chunk + jnp.where(side == 0, 1 - core_ref[0], core_ref[0]), 0)
+
+    shape = jax.ShapeDtypeStruct((chunks, tile, model), jnp.bfloat16)
+    return pl.pallas_call(
+        kernel,
+        grid_spec=pltpu.PrefetchScalarGridSpec(
+            num_scalar_prefetch=1,
+            grid=(2, chunks),
+            in_specs=[pl.BlockSpec((tile, rows), left_map)] * group
+            + [pl.BlockSpec((rows, model), lambda side, chunk, core_ref: (0, 0))] * group,
+            out_specs=[
+                pl.BlockSpec(
+                    (1, tile, model),
+                    lambda side, chunk, core_ref: (jnp.where(side == 0, chunk, chunks - 1), 0, 0),
+                ),
+                pl.BlockSpec(
+                    (1, tile, model),
+                    lambda side, chunk, core_ref: (jnp.where(side == 0, 0, chunk), 0, 0),
+                ),
+            ],
+        ),
+        out_shape=[shape, shape],
+        compiler_params=params(),
+        name="weight_grad",
+    )(core, *lefts, *rights)
+
+
+def line_edges():
+    places = lax.axis_size("replica") // 2
+    outer = places // 2 - 1
+    return places, outer
+
+
+def exchanged(block, pairs):
     route = [(2 * a + core, 2 * b + core) for a, b in pairs for core in range(2)]
     return lax.ppermute(block, "replica", route)
 
 
-def line_sum(block):
-    places = lax.axis_size("replica") // 2
-    place = lax.axis_index("replica") // 2
-    middle = places // 2
-    for hop in range(middle - 1):
-        block = added(block, along_line(block, [(hop, hop + 1), (places - 1 - hop, places - 2 - hop)]))
-    block = added(block, along_line(block, [(middle - 1, middle), (middle, middle - 1)]))
-    for hop in reversed(range(middle - 1)):
-        far = along_line(block, [(hop + 1, hop), (places - 2 - hop, places - 1 - hop)])
-        block = jnp.where((place == hop) | (place == places - 1 - hop), far, block)
-    return block
+class Line:
+    def __init__(self):
+        self.places, self.outer = line_edges()
+        self.steps = 2 * self.outer + 1
+        self.moving = []
+        self.done = {}
+
+    def advance(self, fresh, gate=None):
+        places, outer, steps = self.places, self.outer, self.steps
+        place = (lax.axis_index("replica") // 2).astype(jnp.int32).reshape(1)
+        operands, plan = [], []
+
+        def operand(entry):
+            array, index = entry if isinstance(entry, tuple) else (entry, None)
+            for spot, (known, known_index) in enumerate(operands):
+                if known is array and known_index == index:
+                    return spot
+            operands.append((array, index))
+            return len(operands) - 1
+
+        for name, block, step, far in self.moving:
+            plan.append((name, step + 1, [operand(block), operand(far)], step))
+        for name, terms in fresh:
+            plan.append((name, 0, [operand(term) for term in terms], None))
+        sizes = [operands[spots[0]][0].shape[-2:] for _, _, spots, _ in plan]
+        by_step = {step: index for index, (_, step, _, _) in enumerate(plan)}
+        pairs = []
+        for edge in range(outer):
+            inward, outward = by_step.get(edge), by_step.get(2 * outer - edge)
+            if inward is not None and outward is not None and sizes[inward] == sizes[outward]:
+                pairs.append((edge, inward, outward))
+        cuts = 3 if all(size[0] % 48 == 0 for size in sizes) else 1
+
+        def kernel(place_ref, *refs):
+            here = place_ref[0]
+            inputs = refs[: len(operands)]
+            if gate is not None:
+                refs = refs[: len(operands)] + refs[len(operands) + 1 :]
+            outputs = refs[len(operands) :]
+            states = []
+            for spot, (_, _, terms, last) in enumerate(plan):
+                value = inputs[terms[0]][...]
+                if len(terms) == 2:
+                    far = inputs[terms[1]][...]
+                    total = (value.astype(jnp.float32) + far.astype(jnp.float32)).astype(jnp.bfloat16)
+                    if last is None:
+                        value = total
+                    elif last <= outer:
+                        edge = last
+                        value = jnp.where((here == edge + 1) | (here == places - 2 - edge), total, value)
+                    else:
+                        edge = 2 * outer - last
+                        value = jnp.where((here == edge) | (here == places - 1 - edge), far, value)
+                states.append(value)
+                outputs[spot][...] = value
+            for spot, (edge, inward, outward) in enumerate(pairs):
+                outputs[len(plan) + spot][...] = jnp.where(
+                    (here == edge) | (here == places - 1 - edge), states[inward], states[outward]
+                )
+
+        def spec(size, index):
+            if index is None:
+                return pl.BlockSpec((size[0] // cuts, size[1]), lambda i, place_ref: (i, 0))
+            return pl.BlockSpec((None, size[0] // cuts, size[1]), lambda i, place_ref: (index, i, 0))
+
+        in_specs = [spec(array.shape[-2:], index) for array, index in operands]
+        arrays = [array for array, _ in operands]
+        out_sizes = sizes + [sizes[inward] for _, inward, _ in pairs]
+        out_specs = [spec(size, None) for size in out_sizes]
+        out_shape = [jax.ShapeDtypeStruct(size, jnp.bfloat16) for size in out_sizes]
+        aliases = {}
+        if gate is not None:
+            aliases = {1 + len(arrays): len(out_shape)}
+            in_specs.append(pl.BlockSpec(memory_space=pl.ANY))
+            out_specs.append(pl.BlockSpec(memory_space=pl.ANY))
+            out_shape.append(jax.ShapeDtypeStruct(gate.shape, gate.dtype))
+            arrays.append(gate)
+        outs = pl.pallas_call(
+            kernel,
+            grid_spec=pltpu.PrefetchScalarGridSpec(
+                num_scalar_prefetch=1, grid=(cuts,), in_specs=in_specs, out_specs=out_specs
+            ),
+            out_shape=out_shape,
+            input_output_aliases=aliases,
+            compiler_params=params(),
+            name="line_step",
+        )(place, *arrays)
+        received = {}
+        for spot, (edge, inward, outward) in enumerate(pairs):
+            ends = [(edge, edge + 1), (places - 1 - edge, places - 2 - edge)]
+            far = exchanged(outs[len(plan) + spot], ends + [(b, a) for a, b in ends])
+            received[inward] = received[outward] = far
+        self.moving = []
+        for index, (name, step, _, _) in enumerate(plan):
+            block = outs[index]
+            if step == steps:
+                self.done[name] = block
+                continue
+            if index not in received:
+                edge = step if step <= outer else 2 * outer - step
+                route = [(edge, edge + 1), (places - 1 - edge, places - 2 - edge)]
+                if step > outer:
+                    route = [(b, a) for a, b in route]
+                received[index] = exchanged(block, route)
+            self.moving.append((name, block, step, received[index]))
+        return outs[-1]
+
+    def finished(self, name):
+        while name not in self.done:
+            self.advance([])
+        return self.done[name]
+
+
+def line_names(name, units):
+    return [(name, chunk) for chunk in range(chunks_of(units))]
+
+
+def whole_grad(line, name, units, dtype=jnp.float32):
+    names = line_names(name, units)
+    mines = [line.finished(chunk) for chunk in names]
+    others = [swapped(mine, "replica", 1) for mine in mines]
+    chunks = len(mines)
+    tile, model = mines[0].shape
+    core = (lax.axis_index("replica") % 2).astype(jnp.int32).reshape(1)
+
+    def kernel(core_ref, *refs):
+        out_ref = refs[-1]
+        for chunk in range(chunks):
+            for side in range(2):
+
+                @pl.when((pl.program_id(0) == chunk) & (pl.program_id(1) == side))
+                def _():
+                    @pl.when(core_ref[0] == side)
+                    def _():
+                        out_ref[...] = refs[chunk][...].astype(dtype)
+
+                    @pl.when(core_ref[0] != side)
+                    def _():
+                        out_ref[...] = refs[chunks + chunk][...].astype(dtype)
+
+    return pl.pallas_call(
+        kernel,
+        grid_spec=pltpu.PrefetchScalarGridSpec(
+            num_scalar_prefetch=1,
+            grid=(chunks, 2),
+            in_specs=[pl.BlockSpec((tile, model), lambda chunk, side, core_ref: (0, 0))] * (2 * chunks),
+            out_specs=pl.BlockSpec((tile, model), lambda chunk, side, core_ref: (2 * chunk + side, 0)),
+        ),
+        out_shape=jax.ShapeDtypeStruct((units, model), dtype),
+        compiler_params=params(),
+        name="whole_grad",
+    )(core, *mines, *others)
 
 
 def halves(block, axis):
@@ -64,19 +381,14 @@
     return joined(block, swapped(block, "replica", 1), axis)
 
 
-def replica_sum(block):
-    return core_join(line_sum(core_sum(block, 0)), 0).astype(jnp.float32)
-
-
-def owner_sum(blocks):
+def owner_part(blocks):
     rank = lax.axis_index("fsdp")
     part = core_sum(blocks, 1)
     total = lax.dynamic_index_in_dim(part, rank, 0, keepdims=False).astype(jnp.float32)
     for mask in range(1, blocks.shape[0]):
         far = swapped(lax.dynamic_index_in_dim(part, rank ^ mask, 0, keepdims=False), "fsdp", mask)
         total = total + far.astype(jnp.float32)
-    total = lax.optimization_barrier(total.astype(jnp.bfloat16))
-    return core_join(line_sum(total), 0).astype(jnp.float32)
+    return lax.optimization_barrier(total.astype(jnp.bfloat16))
 
 
 def in_order(blocks):
@@ -138,16 +450,6 @@
 
 def head_post(raw, gain, cosine, sine):
     return rotate(normed(raw, gain), cosine, sine)
-
-
-def gated(gate, upper):
-    return jax.nn.gelu(gate, approximate=True) * upper
-
-
-def gated_back(gate, upper, grad):
-    _, pull = jax.vjp(gated, gate, upper)
-    grad_gate, grad_upper = pull(grad)
-    return (grad_gate.astype(jnp.bfloat16), grad_upper.astype(jnp.bfloat16))
 
 
 def per_device(
@@ -237,54 +539,49 @@
     resid = residual_in + normed(attended, gain_attn)
     ffn_in = normed(resid, gain_ffn).astype(jnp.bfloat16)
     ffn_blocks = [ffn_in] + [swapped(ffn_in, "fsdp", mask) for mask in masks]
-    gates, uppers, hiddens = [], [], []
-    branch = None
+    hiddens, slopes, acts, parts = [], [], [], []
     for mask in range(group):
-        gate = contract(ffn_blocks[mask], gate_weight, 1, 1)
-        upper = contract(ffn_blocks[mask], up_weight, 1, 1)
-        hidden = gated(gate, upper).astype(jnp.bfloat16)
-        part = jnp.dot(hidden, down_weight, preferred_element_type=jnp.float32).astype(jnp.bfloat16)
-        part = swapped(part, "fsdp", mask) if mask else part
-        branch = part.astype(jnp.float32) if mask == 0 else branch + part.astype(jnp.float32)
-        gates.append(gate)
-        uppers.append(upper)
+        hidden, slope, act, part = ffn_forward(ffn_blocks[mask], gate_weight, up_weight, down_weight)
+        parts.append(swapped(part, "fsdp", mask) if mask else part)
         hiddens.append(hidden)
+        slopes.append(slope)
+        acts.append(act)
+    branch = sum(part.astype(jnp.float32) for part in parts)
     result = resid + normed(branch, gain_out)
     hidden_out = result.astype(jnp.bfloat16)
     grad_result = out_grad.astype(jnp.float32)
     grad_branch, grad_gain_out = norm_back(branch, gain_out, grad_result)
     grad_branch_low = grad_branch.astype(jnp.bfloat16)
     pieces = [grad_branch_low] + [swapped(grad_branch_low, "fsdp", mask) for mask in masks]
-    ffn_rows = jnp.concatenate(ffn_blocks, axis=0)
-    grad_down = contract(jnp.concatenate(hiddens, axis=0), jnp.concatenate(pieces, axis=0), 0, 0)
-    cut = grad_down.shape[0] // 2
-
-    def cut_sum(grad):
-        grad = grad.astype(jnp.bfloat16)
-        return jnp.concatenate([replica_sum(grad[:cut]), replica_sum(grad[cut:])], axis=0)
-
-    grad_down = cut_sum(grad_down)
-    grad_gates, grad_uppers = [], []
-    grad_ffn_in = None
-    for mask in range(group):
-        grad_hidden = contract(pieces[mask], down_weight, 1, 1)
-        grad_gate, grad_upper = gated_back(gates[mask], uppers[mask], grad_hidden)
-        part = (
-            jnp.dot(grad_gate, gate_weight, preferred_element_type=jnp.float32)
-            + jnp.dot(grad_upper, up_weight, preferred_element_type=jnp.float32)
-        ).astype(jnp.bfloat16)
-        part = swapped(part, "fsdp", mask) if mask else part
-        grad_ffn_in = part.astype(jnp.float32) if mask == 0 else grad_ffn_in + part.astype(jnp.float32)
-        grad_gates.append(grad_gate)
-        grad_uppers.append(grad_upper)
-    grad_gate_w = cut_sum(contract(jnp.concatenate(grad_gates, axis=0), ffn_rows, 0, 0))
-    grad_up_w = cut_sum(contract(jnp.concatenate(grad_uppers, axis=0), ffn_rows, 0, 0))
+    units = gate_weight.shape[0]
+    line = Line()
+
+    def fresh(name, other, mine):
+        far = swapped(other, "replica", 1)
+        return [(key, [(mine, key[1]), (far, key[1])]) for key in line_names(name, units)]
+
+    waiting = fresh("down", *weight_grad(hiddens, pieces))
+    grad_gates, grad_uppers = {}, {}
+    order = list(masks) + [0]
+    returned = {}
+    for mask in order:
+        grad_gates[mask], grad_uppers[mask], part = ffn_backward(
+            pieces[mask], gate_weight, up_weight, down_weight, slopes[mask], acts[mask]
+        )
+        returned[mask] = swapped(part, "fsdp", mask) if mask else part
+        if mask == order[0]:
+            pieces[order[1]] = line.advance([waiting.pop(0)], pieces[order[1]])
+    waiting += fresh("gate", *weight_grad([grad_gates[i] for i in range(group)], ffn_blocks))
+    waiting += fresh("up", *weight_grad([grad_uppers[i] for i in range(group)], ffn_blocks))
+    returned[0] = line.advance([waiting.pop(0)], returned[0])
+    grad_ffn_in = sum(returned[i].astype(jnp.float32) for i in range(group))
     grad_resid_part, grad_gain_ffn = norm_back(resid, gain_ffn, grad_ffn_in)
     grad_resid = grad_result + grad_resid_part
     grad_attended, grad_gain_attn = norm_back(attended, gain_attn, grad_resid)
     grad_attended_low = grad_attended.astype(jnp.bfloat16)
+    grad_attended_low = line.advance([waiting.pop(0)] if waiting else [], grad_attended_low)
     grad_wout = contract(grad_attended_low, mixed, 0, 0).astype(jnp.bfloat16)
-    owned_out = owner_sum(grad_wout.reshape(group, own_model, -1))
+    out_part = owner_part(grad_wout.reshape(group, own_model, -1))
     grad_mixed = jnp.dot(grad_attended_low, w_out, preferred_element_type=jnp.float32).astype(
         jnp.bfloat16
     )
@@ -295,6 +592,7 @@
     grad_probs = contract(grad_mixed_rows, values, 1, 1).reshape(rows, heads, width)
     delta = jnp.sum(grad_probs * probs, axis=-1, keepdims=True)
     grad_scores = (probs * (grad_probs - delta)).astype(jnp.bfloat16).reshape(rows * heads, width)
+    grad_scores = line.advance([waiting.pop(0)] if waiting else [], grad_scores)
     grad_query = (jnp.dot(grad_scores, keys, preferred_element_type=jnp.float32) * scale).reshape(
         rows, heads, head_size
     )
@@ -306,6 +604,7 @@
         lower = (hops - step) * rows
         back = passed_along(grad_pairs[lower : lower + rows].astype(jnp.bfloat16), "fsdp", -step)
         grad_pair = grad_pair + back.astype(jnp.float32)
+    grad_pair = line.advance([waiting.pop(0)] if waiting else [], grad_pair)
     grad_key = grad_pair[:, :head_size]
     grad_value = grad_pair[:, head_size:]
     _, pull_query = jax.vjp(
@@ -337,9 +636,17 @@
         axis=1,
     )
     gain_grads = jnp.pad(gain_grads[:, None, :], ((0, 0), (0, 31), (0, wide - sum(sizes))))
-    owned = owner_sum(
+    qkv_part = owner_part(
         jnp.concatenate([grad_wqkv.reshape(group, own_model, wide), gain_grads], axis=1)
     )
+    while waiting:
+        line.advance([waiting.pop(0)])
+    grad_down = whole_grad(line, "down", units)
+    line.advance([("out", [out_part]), ("qkv", [qkv_part])])
+    grad_gate_w = whole_grad(line, "gate", units)
+    grad_up_w = whole_grad(line, "up", units)
+    owned = core_join(line.finished("qkv"), 0).astype(jnp.float32)
+    owned_out = core_join(line.finished("out"), 0).astype(jnp.float32)
     owned_query = owned[:own_model, : heads * head_size]
     owned_key = owned[:own_model, heads * head_size : (heads + 1) * head_size]
     owned_value = owned[:own_model, (heads + 1) * head_size :]

time: 715 us -> 611 us (0.85)
  Pallas kernels: 0 us -> 181 us
  waiting for transfers between devices: 337 us -> 160 us
  matrix products: 110 us -> 21.6 us
  starting transfers between devices: 116 us -> 87.8 us
    pallas_call x0 -> x24, Pallas kernels: none -> 181 us  [the longest x4 47.5 us: ffn_backward(): pl.pallas_call(ffn_backward_kernel, grid=(units // tile,), out_shape=[kep...]
    ppermute x24 -> x20, waiting for transfers between devices: 253 us -> 77.9 us  [exchanged(): return lax.ppermute(block, 'replica', route)]
    dot_general x23 -> x8, matrix products: 78.1 us -> 15.9 us  [contract(): lax.dot_general(left, right, (((left_dim,), (right_dim,)), ((), ())), pre...]
    dot_general x12 -> x0, matrix products: 27 us -> none  [the longest x4 9.74 us: per_device(): jnp.dot(hidden, down_weight, preferred_element_type=jnp.float32)]
    ppermute x24 -> x20, starting transfers between devices: 65.2 us -> 43.5 us  [exchanged(): return lax.ppermute(block, 'replica', route)]
    concatenate x3 -> x0, other arithmetic: 11.3 us -> none  [cut_sum(): jnp.concatenate([replica_sum(grad[:cut]), replica_sum(grad[cut:])], axis=0)]
    sub x0 -> x1, other arithmetic: none -> 10.8 us  [per_device(): grad_probs - delta]
    convert_element_type x24 -> x2, other arithmetic: 11.9 us -> 4.16 us  [added(): return lax.optimization_barrier(total.astype(jnp.bfloat16))]
  transfers between devices with their start and end apart: 70 -> 63, of which waited for: 32 -> 21; matrix products, arithmetic and copies ran while one was open for 29% -> 19% of each run, Pallas kernels for 0% -> 24%
where the time goes in v3:
time: 611 us; the launch traced here: 601 us
  Pallas kernels  181 us (30%)
  waiting for transfers between devices  160 us (26%)
  starting transfers between devices  87.8 us (14%)
  local copies, waits for them, and re-layouts  77.4 us (13%)
  other arithmetic  70.3 us (12%)
  matrix products  21.6 us (4%)
    ppermute x20, waiting for transfers between devices, exchanged(): return lax.ppermute(block, 'replica', route)  77.9 us
    ppermute x39, waiting for transfers between devices, swapped(): return lax.ppermute(block, axis, route)  74.1 us
    pallas_call x4, Pallas kernels, ffn_backward(): pl.pallas_call(ffn_backward_kernel, grid=(units // tile,), out_shape=[kep...  47.5 us
    pallas_call x10, Pallas kernels, advance(): pl.pallas_call(kernel, grid_spec=pltpu.PrefetchScalarGridSpec(num_scalar_...  47 us
    ppermute x20, starting transfers between devices, exchanged(): return lax.ppermute(block, 'replica', route)  43.5 us
    pallas_call x4, Pallas kernels, ffn_forward(): pl.pallas_call(ffn_forward_kernel, grid=(units // tile,), out_shape=[kept...  41.4 us
    ppermute x39, starting transfers between devices, swapped(): return lax.ppermute(block, axis, route)  34.3 us
    pallas_call x3, Pallas kernels, weight_grad(): pl.pallas_call(kernel, grid_spec=pltpu.PrefetchScalarGridSpec(num_scalar_...  28.1 us
  transfers between devices with their start and end apart: 63, of which 21 were waited for; matrix products, arithmetic and copies ran while one was open for 19% of the time, Pallas kernels for 24%

profile of v3, /device:TPU:0, one launch (start us, length us, event | category | flops | bytes accessed | tf_op | source)
XLA Modules:
  0.0 601.5 jit_solution(4287926702570209656)
XLA Ops:
  21.6 9.8 %collective-permute-done.8 = bf16[144,1024]{1,0:T(8,128)(2,1)S(1)} collective-permute-done((bf16[144,1024]{1,0:T(8,128)(2,1)}, bf16[144,1024]{1,0:T(8,128)(2,1)S(1)}, u32[]{:S(2)}, u32[]{:S(2)}) %collective-permute-start.8) | collective-permute-done | bytes 294944 | tf_op jit(solution)/shard_map/ppermute | solution.py:17
  33.4 14.1 %collective-permute-done.7 = bf16[144,1024]{1,0:T(8,128)(2,1)} collective-permute-done((bf16[144,1024]{1,0:T(8,128)(2,1)}, bf16[144,1024]{1,0:T(8,128)(2,1)}, u32[]{:S(2)}, u32[]{:S(2)}) %collective-permute-start.7) | collective-permute-done | bytes 294944 | tf_op jit(solution)/shard_map/ppermute | solution.py:17
  88.2 6.6 %collective-permute-done.4 = bf16[256,512]{1,0:T(8,128)(2,1)} collective-permute-done((bf16[256,512]{1,0:T(8,128)(2,1)}, bf16[256,512]{1,0:T(8,128)(2,1)}, u32[]{:S(2)}, u32[]{:S(2)}) %collective-permute-start.4) | collective-permute-done | bytes 262176 | tf_op jit(solution)/shard_map/ppermute | solution.py:418
  109.9 13.2 %collective-permute-done.14.x_ref.refs_7_ = bf16[256,1152]{1,0:T(8,128)(2,1)S(1)} collective-permute-done((bf16[256,1152]{1,0:T(8,128)(2,1)S(1)}, bf16[256,1152]{1,0:T(8,128)(2,1)S(1)}, u32[]{:S(2)}, u32[]{:S(2)}) %collective-permute-start.14) | collective-permute-done | bytes 589856 | tf_op jit(solution)/shard_map/ppermute | solution.py:17
  123.9 10.5 %ffn_forward.7 = (bf16[1728,256]{1,0:T(8,128)(2,1)}, bf16[1728,256]{1,0:T(8,128)(2,1)}, bf16[1728,256]{1,0:T(8,128)(2,1)}, bf16[256,1152]{1,0:T(8,128)(2,1)}) custom-call(bf16[256,1152]{1,0:T(8,128)(2,1)} %copy-done.8, bf16[1728,1152]{1,0:T(8,128)(2,1)} %gate_ref.15, bf16[1728,1152]{1,0:T(8,128)(2,1)} %up_ref.15, bf16[1728,1152]{1,0:T(8,128)(2,1)} %down_ref.15), custom_call_target="tpu_custom_call" | custom-call | tf_op jit(solution)/shard_map/ffn_forward/pallas_call | solution.py:83
  135.5 10.3 %ffn_forward.6 = (bf16[1728,256]{1,0:T(8,128)(2,1)}, bf16[1728,256]{1,0:T(8,128)(2,1)}, bf16[1728,256]{1,0:T(8,128)(2,1)}, bf16[256,1152]{1,0:T(8,128)(2,1)}) custom-call(bf16[256,1152]{1,0:T(8,128)(2,1)} %copy-done.9, bf16[1728,1152]{1,0:T(8,128)(2,1)} %gate_ref.15, bf16[1728,1152]{1,0:T(8,128)(2,1)} %up_ref.15, bf16[1728,1152]{1,0:T(8,128)(2,1)} %down_ref.15), custom_call_target="tpu_custom_call" | custom-call | tf_op jit(solution)/shard_map/ffn_forward/pallas_call | solution.py:83
  149.0 10.3 %ffn_forward.5 = (bf16[1728,256]{1,0:T(8,128)(2,1)}, bf16[1728,256]{1,0:T(8,128)(2,1)}, bf16[1728,256]{1,0:T(8,128)(2,1)}, bf16[256,1152]{1,0:T(8,128)(2,1)}) custom-call(bf16[256,1152]{1,0:T(8,128)(2,1)} %copy-done.10, bf16[1728,1152]{1,0:T(8,128)(2,1)} %gate_ref.15, bf16[1728,1152]{1,0:T(8,128)(2,1)} %up_ref.15, bf16[1728,1152]{1,0:T(8,128)(2,1)} %down_ref.15), custom_call_target="tpu_custom_call" | custom-call | tf_op jit(solution)/shard_map/ffn_forward/pallas_call | solution.py:83
  165.0 10.3 %ffn_forward.4 = (bf16[1728,256]{1,0:T(8,128)(2,1)}, bf16[1728,256]{1,0:T(8,128)(2,1)}, bf16[1728,256]{1,0:T(8,128)(2,1)}, bf16[256,1152]{1,0:T(8,128)(2,1)}) custom-call(bf16[256,1152]{1,0:T(8,128)(2,1)} %copy-done.6, bf16[1728,1152]{1,0:T(8,128)(2,1)} %gate_ref.15, bf16[1728,1152]{1,0:T(8,128)(2,1)} %up_ref.15, bf16[1728,1152]{1,0:T(8,128)(2,1)} %down_ref.15), custom_call_target="tpu_custom_call" | custom-call | tf_op jit(solution)/shard_map/ffn_forward/pallas_call | solution.py:83
  184.7 13.7 %collective-permute-done.18.refs_7_.grad_ref = bf16[256,1152]{1,0:T(8,128)(2,1)S(1)} collective-permute-done((bf16[256,1152]{1,0:T(8,128)(2,1)S(1)}, bf16[256,1152]{1,0:T(8,128)(2,1)S(1)}, u32[]{:S(2)}, u32[]{:S(2)}) %collective-permute-start.18) | collective-permute-done | bytes 589856 | tf_op jit(solution)/shard_map/ppermute | solution.py:17
  198.4 9.5 %collective-permute-done.16.refs_5_.grad_ref = bf16[256,1152]{1,0:T(8,128)(2,1)S(1)} collective-permute-done((bf16[256,1152]{1,0:T(8,128)(2,1)S(1)}, bf16[256,1152]{1,0:T(8,128)(2,1)S(1)}, u32[]{:S(2)}, u32[]{:S(2)}) %collective-permute-start.16) | collective-permute-done | bytes 589856 | tf_op jit(solution)/shard_map/ppermute | solution.py:17
  209.0 9.3 %weight_grad.3 = (bf16[2,432,1152]{2,1,0:T(8,128)(2,1)}, bf16[2,432,1152]{2,1,0:T(8,128)(2,1)}) custom-call(s32[1]{0:T(128)} %bitcast.35.core_ref, bf16[1728,256]{1,0:T(8,128)(2,1)} %get-tuple-element.94.refs_0_, bf16[1728,256]{1,0:T(8,128)(2,1)} %get-tuple-element.95.refs_1_, bf16[1728,256]{1,0:T(8,128)(2,1)} %get-tuple-element.96.refs_2_, ...), custom_call_target="tpu_custom_call" | custom-call | tf_op jit(solution)/shard_map/weight_grad/pallas_call | solution.py:169
  230.4 12.2 %ffn_backward.7 = (bf16[1728,256]{1,0:T(8,128)(2,1)}, bf16[1728,256]{1,0:T(8,128)(2,1)}, bf16[256,1152]{1,0:T(8,128)(2,1)}) custom-call(bf16[256,1152]{1,0:T(8,128)(2,1)} %copy-done.28, bf16[1728,1152]{1,0:T(8,128)(2,1)} %gate_ref.15, bf16[1728,1152]{1,0:T(8,128)(2,1)} %up_ref.15, bf16[1728,1152]{1,0:T(8,128)(2,1)} %down_ref.15, ...), custom_call_target="tpu_custom_call" | custom-call | tf_op jit(solution)/shard_map/ffn_backward/pallas_call | solution.py:127
  243.7 11.7 %ffn_backward.5 = (bf16[1728,256]{1,0:T(8,128)(2,1)}, bf16[1728,256]{1,0:T(8,128)(2,1)}, bf16[256,1152]{1,0:T(8,128)(2,1)}) custom-call(bf16[256,1152]{1,0:T(8,128)(2,1)} %copy-done.27, bf16[1728,1152]{1,0:T(8,128)(2,1)} %gate_ref.15, bf16[1728,1152]{1,0:T(8,128)(2,1)} %up_ref.15, bf16[1728,1152]{1,0:T(8,128)(2,1)} %down_ref.15, ...), custom_call_target="tpu_custom_call" | custom-call | tf_op jit(solution)/shard_map/ffn_backward/pallas_call | solution.py:127
  257.2 11.8 %ffn_backward.6 = (bf16[1728,256]{1,0:T(8,128)(2,1)}, bf16[1728,256]{1,0:T(8,128)(2,1)}, bf16[256,1152]{1,0:T(8,128)(2,1)}) custom-call(bf16[256,1152]{1,0:T(8,128)(2,1)} %get-tuple-element.108.grad_ref, bf16[1728,1152]{1,0:T(8,128)(2,1)} %gate_ref.15, bf16[1728,1152]{1,0:T(8,128)(2,1)} %up_ref.15, bf16[1728,1152]{1,0:T(8,128)(2,1)} %down_ref.15, ...), custom_call_target="tpu_custom_call" | custom-call | tf_op jit(solution)/shard_map/ffn_backward/pallas_call | solution.py:127
  269.9 11.7 %ffn_backward.4 = (bf16[1728,256]{1,0:T(8,128)(2,1)}, bf16[1728,256]{1,0:T(8,128)(2,1)}, bf16[256,1152]{1,0:T(8,128)(2,1)}) custom-call(bf16[256,1152]{1,0:T(8,128)(2,1)} %copy-done.11, bf16[1728,1152]{1,0:T(8,128)(2,1)} %gate_ref.15, bf16[1728,1152]{1,0:T(8,128)(2,1)} %up_ref.15, bf16[1728,1152]{1,0:T(8,128)(2,1)} %down_ref.15, ...), custom_call_target="tpu_custom_call" | custom-call | tf_op jit(solution)/shard_map/ffn_backward/pallas_call | solution.py:127
  281.6 9.4 %weight_grad.4 = (bf16[2,432,1152]{2,1,0:T(8,128)(2,1)}, bf16[2,432,1152]{2,1,0:T(8,128)(2,1)}) custom-call(s32[1]{0:T(128)} %bitcast.35.core_ref, bf16[1728,256]{1,0:T(8,128)(2,1)} %get-tuple-element.117.refs_0_, bf16[1728,256]{1,0:T(8,128)(2,1)} %get-tuple-element.118.refs_1_, bf16[1728,256]{1,0:T(8,128)(2,1)} %get-tuple-element.119.refs_2_, ...), custom_call_target="tpu_custom_call" | custom-call | tf_op jit(solution)/shard_map/weight_grad/pallas_call | solution.py:169
  301.6 9.4 %weight_grad.5 = (bf16[2,432,1152]{2,1,0:T(8,128)(2,1)}, bf16[2,432,1152]{2,1,0:T(8,128)(2,1)}) custom-call(s32[1]{0:T(128)} %bitcast.35.core_ref, bf16[1728,256]{1,0:T(8,128)(2,1)} %get-tuple-element.133.refs_0_, bf16[1728,256]{1,0:T(8,128)(2,1)} %get-tuple-element.134.refs_1_, bf16[1728,256]{1,0:T(8,128)(2,1)} %get-tuple-element.135.refs_2_, ...), custom_call_target="tpu_custom_call" | custom-call | tf_op jit(solution)/shard_map/weight_grad/pallas_call | solution.py:169
  332.2 9.2 %collective-permute-done.25.refs_3_ = bf16[432,1152]{1,0:T(8,128)(2,1)} collective-permute-done((bf16[432,1152]{1,0:T(8,128)(2,1)}, bf16[432,1152]{1,0:T(8,128)(2,1)}, u32[]{:S(2)}, u32[]{:S(2)}) %collective-permute-start.25) | collective-permute-done | bytes 995360 | tf_op jit(solution)/shard_map/ppermute | solution.py:201
  341.4 5.7 line_step.12
  356.6 10.8 %multiply_convert_fusion = bf16[256,4,768]{2,0,1:T(8,128)(2,1)S(1)} fusion(f32[256,4,768]{2,0,1:T(8,128)} %fusion.66, f32[256,4,768]{2,1,0:T(4,128)} %reshape.539, f32[256,4]{0,1:T(4,128)S(1)} %copy-done.116, pred[256,768]{1,0:T(8,128)(4,1)S(1)} %copy-done.59), kind=kOutput, calls=%fused_computation.24 | output fusion | flops 6293247 | bytes 8065024 | tf_op jit(solution)/shard_map/sub | solution.py:594
  376.7 6.4 %line_step.13 = (bf16[432,1152]{1,0:T(8,128)(2,1)}, bf16[432,1152]{1,0:T(8,128)(2,1)}, bf16[432,1152]{1,0:T(8,128)(2,1)}, bf16[432,1152]{1,0:T(8,128)(2,1)}, bf1...) custom-call(s32[1]{0:T(128)} %bitcast.34.place_ref, ...), custom_call_target="tpu_custom_call", output_to_operand_aliasing={{5}: (8, {})} | custom-call | tf_op jit(solution)/shard_map/line_step/pallas_call | solution.py:281
  406.2 6.6 %line_step.14 = (bf16[432,1152]{1,0:T(8,128)(2,1)}, bf16[432,1152]{1,0:T(8,128)(2,1)}, bf16[432,1152]{1,0:T(8,128)(2,1)}, bf16[432,1152]{1,0:T(8,128)(2,1)}, bf1...) custom-call(s32[1]{0:T(128)} %bitcast.34.place_ref, ...), custom_call_target="tpu_custom_call", output_to_operand_aliasing={{5}: (8, {})} | custom-call | tf_op jit(solution)/shard_map/line_step/pallas_call | solution.py:281
  451.3 5.9 collective-permute-done.34.refs_1_
  458.7 6.0 %line_step.15 = (bf16[432,1152]{1,0:T(8,128)(2,1)}, bf16[432,1152]{1,0:T(8,128)(2,1)}, bf16[432,1152]{1,0:T(8,128)(2,1)}, bf16[432,1152]{1,0:T(8,128)(2,1)}, bf16[432,1152]{1,0:T(8,128)(2,1)}) custom-call(s32[1]{0:T(128)} %bitcast.34.place_ref, bf16[432,1152]{1,0:T(8,128)(2,1)} %get-tuple-element.140.refs_0_, bf16[432,1152]{1,0:T(8,128)(2,1)} %copy-done.38, ...), custom_call_target="tpu_custom_call" | custom-call | tf_op jit(solution)/shard_map/line_step/pallas_call | solution.py:281
  478.9 10.1 %collective-permute-done.36.refs_1_ = bf16[432,1152]{1,0:T(8,128)(2,1)S(1)} collective-permute-done((bf16[432,1152]{1,0:T(8,128)(2,1)}, bf16[432,1152]{1,0:T(8,128)(2,1)S(1)}, u32[]{:S(2)}, u32[]{:S(2)}) %collective-permute-start.36) | collective-permute-done | bytes 995360 | tf_op jit(solution)/shard_map/ppermute | solution.py:201
  496.8 7.4 %collective-permute-start.49 = (bf16[160,1536]{1,0:T(8,128)(2,1)}, bf16[160,1536]{1,0:T(8,128)(2,1)S(1)}, u32[]{:S(2)}, u32[]{:S(2)}) collective-permute-start(bf16[160,1536]{1,0:T(8,128)(2,1)} %get-tuple-element.151.refs_6_), channel_id=1, source_target_pairs={{0,8},{4,12},{24,16},{28,20},{1,9},{5,13},{25,17},{29,21},{2,10},{... | collective-permute-start | bytes 1474568 | tf_op jit(solution)/shard_map/ppermute | solution.py:201
  505.9 13.2 %collective-permute-done.48.refs_5_ = bf16[144,1024]{1,0:T(8,128)(2,1)S(1)} collective-permute-done((bf16[144,1024]{1,0:T(8,128)(2,1)}, bf16[144,1024]{1,0:T(8,128)(2,1)S(1)}, u32[]{:S(2)}, u32[]{:S(2)}) %collective-permute-start.48) | collective-permute-done | bytes 294944 | tf_op jit(solution)/shard_map/ppermute | solution.py:201
  528.8 20.6 %collective-permute-done.50.refs_1_ = bf16[432,1152]{1,0:T(8,128)(2,1)} collective-permute-done((bf16[432,1152]{1,0:T(8,128)(2,1)}, bf16[432,1152]{1,0:T(8,128)(2,1)}, u32[]{:S(2)}, u32[]{:S(2)}) %collective-permute-start.50) | collective-permute-done | bytes 995360 | tf_op jit(solution)/shard_map/ppermute | solution.py:201
  555.9 8.9 %collective-permute-done.53.refs_1_ = bf16[144,1024]{1,0:T(8,128)(2,1)S(1)} collective-permute-done((bf16[144,1024]{1,0:T(8,128)(2,1)}, bf16[144,1024]{1,0:T(8,128)(2,1)S(1)}, u32[]{:S(2)}, u32[]{:S(2)}) %collective-permute-start.53) | collective-permute-done | bytes 294944 | tf_op jit(solution)/shard_map/ppermute | solution.py:201
  564.8 5.9 collective-permute-done.54.refs_3_
  575.7 5.7 whole_grad.5
  581.5 5.7 whole_grad.3
  (501 shorter events, 286.8 us)
Async XLA Ops:
  8.9 40.7 %collective-permute-start.2 = (bf16[160,1536]{1,0:T(8,128)(2,1)}, bf16[160,1536]{1,0:T(8,128)(2,1)}, u32[]{:S(2)}, u32[]{:S(2)}) collective-permute-start(bf16[160,1536]{1,0:T(8,128)(2,1)} %pad_maximum_fusion.9), channel_id=1, source_target_pairs={{0,3},{1,2},{2,1},{3,0},{4,7},{5,6},{6,5},{7,4},{8,11},{9,10},{10,... | collective-permute-start | bytes 1474568 | tf_op jit(solution)/shard_map/ppermute | solution.py:17
  12.8 37.9 %collective-permute-start.1 = (bf16[160,1536]{1,0:T(8,128)(2,1)}, bf16[160,1536]{1,0:T(8,128)(2,1)}, u32[]{:S(2)}, u32[]{:S(2)}) collective-permute-start(bf16[160,1536]{1,0:T(8,128)(2,1)} %pad_maximum_fusion.9), channel_id=1, source_target_pairs={{0,2},{1,3},{2,0},{3,1},{4,6},{5,7},{6,4},{7,5},{8,10},{9,11},{10,... | collective-permute-start | bytes 1474568 | tf_op jit(solution)/shard_map/ppermute | solution.py:17
  15.5 32.0 %collective-permute-start.7 = (bf16[144,1024]{1,0:T(8,128)(2,1)}, bf16[144,1024]{1,0:T(8,128)(2,1)}, u32[]{:S(2)}, u32[]{:S(2)}) collective-permute-start(bf16[144,1024]{1,0:T(8,128)(2,1)} %constant_dynamic-slice_fusion.2), channel_id=1, source_target_pairs={{0,2},{1,3},{2,0},{3,1},{4,6},{5,7},{6,4},{7,5},{8,10},{9,11},{10,... | collective-permute-start | bytes 884744 | tf_op jit(solution)/shard_map/ppermute | solution.py:17
  15.5 31.9 %collective-permute-start.6 = (bf16[144,1024]{1,0:T(8,128)(2,1)}, bf16[144,1024]{1,0:T(8,128)(2,1)}, u32[]{:S(2)}, u32[]{:S(2)}) collective-permute-start(bf16[144,1024]{1,0:T(8,128)(2,1)} %constant_dynamic-slice_fusion.2), channel_id=1, source_target_pairs={{0,1},{1,0},{2,3},{3,2},{4,5},{5,4},{6,7},{7,6},{8,9},{9,8},{10,11... | collective-permute-start | bytes 884744 | tf_op jit(solution)/shard_map/ppermute | solution.py:17
  106.0 28.7 %collective-permute-start.12 = (bf16[256,1152]{1,0:T(8,128)(2,1)S(1)}, bf16[256,1152]{1,0:T(8,128)(2,1)S(1)}, u32[]{:S(2)}, u32[]{:S(2)}) collective-permute-start(bf16[256,1152]{1,0:T(8,128)(2,1)S(1)} %multiply_convert_fusion.1.x_ref.refs_4_), channel_id=1, source_target_pairs={{0,2},{1,3},{2,0},{3,1},{4,6},{5,7},{6,4},{7,5},{8,10},{9,11},{10,... | collective-permute-start | bytes 1769480 | tf_op jit(solution)/shard_map/ppermute | solution.py:17
  108.5 39.6 %collective-permute-start.10 = (bf16[256,1152]{1,0:T(8,128)(2,1)S(1)}, bf16[256,1152]{1,0:T(8,128)(2,1)S(1)}, u32[]{:S(2)}, u32[]{:S(2)}) collective-permute-start(bf16[256,1152]{1,0:T(8,128)(2,1)S(1)} %multiply_convert_fusion.1.x_ref.refs_4_), channel_id=1, source_target_pairs={{0,1},{1,0},{2,3},{3,2},{4,5},{5,4},{6,7},{7,6},{8,9},{9,8},{10,11... | collective-permute-start | bytes 1769480 | tf_op jit(solution)/shard_map/ppermute | solution.py:17
  134.5 40.8 %collective-permute-start.15 = (bf16[256,1152]{1,0:T(8,128)(2,1)}, bf16[256,1152]{1,0:T(8,128)(2,1)S(1)}, u32[]{:S(2)}, u32[]{:S(2)}) collective-permute-start(bf16[256,1152]{1,0:T(8,128)(2,1)} %get-tuple-element.93), channel_id=1, source_target_pairs={{0,3},{1,2},{2,1},{3,0},{4,7},{5,6},{6,5},{7,4},{8,11},{9,10},{10,... | collective-permute-start | bytes 1769480 | tf_op jit(solution)/shard_map/ppermute | solution.py:17
  145.8 29.5 %collective-permute-start.13 = (bf16[256,1152]{1,0:T(8,128)(2,1)}, bf16[256,1152]{1,0:T(8,128)(2,1)}, u32[]{:S(2)}, u32[]{:S(2)}) collective-permute-start(bf16[256,1152]{1,0:T(8,128)(2,1)} %get-tuple-element.92), channel_id=1, source_target_pairs={{0,2},{1,3},{2,0},{3,1},{4,6},{5,7},{6,4},{7,5},{8,10},{9,11},{10,... | collective-permute-start | bytes 1769480 | tf_op jit(solution)/shard_map/ppermute | solution.py:17
  182.7 25.3 %collective-permute-start.16 = (bf16[256,1152]{1,0:T(8,128)(2,1)S(1)}, bf16[256,1152]{1,0:T(8,128)(2,1)S(1)}, u32[]{:S(2)}, u32[]{:S(2)}) collective-permute-start(bf16[256,1152]{1,0:T(8,128)(2,1)S(1)} %get-tuple-element.221.refs_4_.grad_ref), channel_id=1, source_target_pairs={{0,1},{1,0},{2,3},{3,2},{4,5},{5,4},{6,7},{7,6},{8,9},{9,8},{10,11... | collective-permute-start | bytes 1769480 | tf_op jit(solution)/shard_map/ppermute | solution.py:17
  184.7 23.3 %collective-permute-start.17 = (bf16[256,1152]{1,0:T(8,128)(2,1)S(1)}, bf16[256,1152]{1,0:T(8,128)(2,1)S(1)}, u32[]{:S(2)}, u32[]{:S(2)}) collective-permute-start(bf16[256,1152]{1,0:T(8,128)(2,1)S(1)} %get-tuple-element.221.refs_4_.grad_ref), channel_id=1, source_target_pairs={{0,2},{1,3},{2,0},{3,1},{4,6},{5,7},{6,4},{7,5},{8,10},{9,11},{10,... | collective-permute-start | bytes 1769480 | tf_op jit(solution)/shard_map/ppermute | solution.py:17
  226.0 85.0 %collective-permute-start.20 = (bf16[432,1152]{1,0:T(8,128)(2,1)}, bf16[432,1152]{1,0:T(8,128)(2,1)}, u32[]{:S(2)}, u32[]{:S(2)}) collective-permute-start(bf16[432,1152]{1,0:T(8,128)(2,1)} %get-tuple-element.100.refs_0_), channel_id=1, source_target_pairs={{0,8},{4,12},{24,16},{28,20},{1,9},{5,13},{25,17},{29,21},{2,10},{... | collective-permute-start | bytes 2985992 | tf_op jit(solution)/shard_map/ppermute | solution.py:201
  242.7 73.0 %collective-permute-start.23 = (bf16[256,1152]{1,0:T(8,128)(2,1)}, bf16[256,1152]{1,0:T(8,128)(2,1)S(1)}, u32[]{:S(2)}, u32[]{:S(2)}) collective-permute-start(bf16[256,1152]{1,0:T(8,128)(2,1)} %get-tuple-element.114), channel_id=1, source_target_pairs={{0,3},{1,2},{2,1},{3,0},{4,7},{5,6},{6,5},{7,4},{8,11},{9,10},{10,... | collective-permute-start | bytes 1769480 | tf_op jit(solution)/shard_map/ppermute | solution.py:17
  255.4 62.1 %collective-permute-start.21 = (bf16[256,1152]{1,0:T(8,128)(2,1)}, bf16[256,1152]{1,0:T(8,128)(2,1)S(1)}, u32[]{:S(2)}, u32[]{:S(2)}) collective-permute-start(bf16[256,1152]{1,0:T(8,128)(2,1)} %get-tuple-element.107), channel_id=1, source_target_pairs={{0,1},{1,0},{2,3},{3,2},{4,5},{5,4},{6,7},{7,6},{8,9},{9,8},{10,11... | collective-permute-start | bytes 1769480 | tf_op jit(solution)/shard_map/ppermute | solution.py:17
  269.0 52.0 %collective-permute-start.22 = (bf16[256,1152]{1,0:T(8,128)(2,1)}, bf16[256,1152]{1,0:T(8,128)(2,1)}, u32[]{:S(2)}, u32[]{:S(2)}) collective-permute-start(bf16[256,1152]{1,0:T(8,128)(2,1)} %get-tuple-element.111), channel_id=1, source_target_pairs={{0,2},{1,3},{2,0},{3,1},{4,6},{5,7},{6,4},{7,5},{8,10},{9,11},{10,... | collective-permute-start | bytes 1769480 | tf_op jit(solution)/shard_map/ppermute | solution.py:17
  291.0 50.3 %collective-permute-start.26 = (bf16[2,432,1152]{2,1,0:T(8,128)(2,1)}, bf16[2,432,1152]{2,1,0:T(8,128)(2,1)}, u32[]{:S(2)}, u32[]{:S(2)}) collective-permute-start(bf16[2,432,1152]{2,1,0:T(8,128)(2,1)} %get-tuple-element.122), channel_id=1, source_target_pairs={{0,4},{4,0},{8,12},{12,8},{16,20},{20,16},{24,28},{28,24},{1,5},{5... | collective-permute-start | bytes 5971976 | tf_op jit(solution)/shard_map/ppermute | solution.py:17
  311.0 91.1 %collective-permute-start.31 = (bf16[2,432,1152]{2,1,0:T(8,128)(2,1)}, bf16[2,432,1152]{2,1,0:T(8,128)(2,1)}, u32[]{:S(2)}, u32[]{:S(2)}) collective-permute-start(bf16[2,432,1152]{2,1,0:T(8,128)(2,1)} %get-tuple-element.138), channel_id=1, source_target_pairs={{0,4},{4,0},{8,12},{12,8},{16,20},{20,16},{24,28},{28,24},{1,5},{5... | collective-permute-start | bytes 5971976 | tf_op jit(solution)/shard_map/ppermute | solution.py:17
  317.5 23.9 %collective-permute-start.25 = (bf16[432,1152]{1,0:T(8,128)(2,1)}, bf16[432,1152]{1,0:T(8,128)(2,1)}, u32[]{:S(2)}, u32[]{:S(2)}) collective-permute-start(bf16[432,1152]{1,0:T(8,128)(2,1)} %get-tuple-element.116.refs_2_), channel_id=1, source_target_pairs={{0,8},{4,12},{24,16},{28,20},{1,9},{5,13},{25,17},{29,21},{2,10},{... | collective-permute-start | bytes 2985992 | tf_op jit(solution)/shard_map/ppermute | solution.py:201
  347.1 29.6 %collective-permute-start.27 = (bf16[432,1152]{1,0:T(8,128)(2,1)}, bf16[432,1152]{1,0:T(8,128)(2,1)}, u32[]{:S(2)}, u32[]{:S(2)}) collective-permute-start(bf16[432,1152]{1,0:T(8,128)(2,1)} %get-tuple-element.124), channel_id=1, source_target_pairs={{0,8},{4,12},{24,16},{28,20},{8,0},{12,4},{16,24},{20,28},{1,9},{5... | collective-permute-start | bytes 2985992 | tf_op jit(solution)/shard_map/ppermute | solution.py:201
  349.5 27.2 %collective-permute-start.28 = (bf16[432,1152]{1,0:T(8,128)(2,1)}, bf16[432,1152]{1,0:T(8,128)(2,1)}, u32[]{:S(2)}, u32[]{:S(2)}) collective-permute-start(bf16[432,1152]{1,0:T(8,128)(2,1)} %get-tuple-element.125.refs_2_), channel_id=1, source_target_pairs={{8,16},{12,20},{16,8},{20,12},{9,17},{13,21},{17,9},{21,13},{10,18... | collective-permute-start | bytes 2985992 | tf_op jit(solution)/shard_map/ppermute | solution.py:201
  383.1 23.1 %collective-permute-start.29 = (bf16[432,1152]{1,0:T(8,128)(2,1)}, bf16[432,1152]{1,0:T(8,128)(2,1)}, u32[]{:S(2)}, u32[]{:S(2)}) collective-permute-start(bf16[432,1152]{1,0:T(8,128)(2,1)} %get-tuple-element.130), channel_id=1, source_target_pairs={{0,8},{4,12},{24,16},{28,20},{8,0},{12,4},{16,24},{20,28},{1,9},{5... | collective-permute-start | bytes 2985992 | tf_op jit(solution)/shard_map/ppermute | solution.py:201
  384.4 21.7 %collective-permute-start.30 = (bf16[432,1152]{1,0:T(8,128)(2,1)}, bf16[432,1152]{1,0:T(8,128)(2,1)}, u32[]{:S(2)}, u32[]{:S(2)}) collective-permute-start(bf16[432,1152]{1,0:T(8,128)(2,1)} %get-tuple-element.131.refs_2_), channel_id=1, source_target_pairs={{8,16},{12,20},{16,8},{20,12},{9,17},{13,21},{17,9},{21,13},{10,18... | collective-permute-start | bytes 2985992 | tf_op jit(solution)/shard_map/ppermute | solution.py:201
  431.1 26.0 %collective-permute-start.34 = (bf16[432,1152]{1,0:T(8,128)(2,1)}, bf16[432,1152]{1,0:T(8,128)(2,1)S(1)}, u32[]{:S(2)}, u32[]{:S(2)}) collective-permute-start(bf16[432,1152]{1,0:T(8,128)(2,1)} %get-tuple-element.141), channel_id=1, source_target_pairs={{0,8},{4,12},{24,16},{28,20},{8,0},{12,4},{16,24},{20,28},{1,9},{5... | collective-permute-start | bytes 2985992 | tf_op jit(solution)/shard_map/ppermute | solution.py:201
  434.8 23.6 %collective-permute-start.35 = (bf16[432,1152]{1,0:T(8,128)(2,1)}, bf16[432,1152]{1,0:T(8,128)(2,1)}, u32[]{:S(2)}, u32[]{:S(2)}) collective-permute-start(bf16[432,1152]{1,0:T(8,128)(2,1)} %get-tuple-element.142.refs_2_), channel_id=1, source_target_pairs={{8,16},{12,20},{16,8},{20,12},{9,17},{13,21},{17,9},{21,13},{10,18... | collective-permute-start | bytes 2985992 | tf_op jit(solution)/shard_map/ppermute | solution.py:201
  440.4 24.3 %collective-permute-start.40 = (bf16[144,1024]{1,0:T(8,128)(2,1)}, bf16[144,1024]{1,0:T(8,128)(2,1)}, u32[]{:S(2)}, u32[]{:S(2)}) collective-permute-start(bf16[144,1024]{1,0:T(8,128)(2,1)} %get-tuple-element.225), channel_id=1, source_target_pairs={{0,2},{1,3},{2,0},{3,1},{4,6},{5,7},{6,4},{7,5},{8,10},{9,11},{10,... | collective-permute-start | bytes 884744 | tf_op jit(solution)/shard_map/ppermute | solution.py:17
  441.4 26.3 %collective-permute-start.39 = (bf16[144,1024]{1,0:T(8,128)(2,1)S(1)}, bf16[144,1024]{1,0:T(8,128)(2,1)}, u32[]{:S(2)}, u32[]{:S(2)}) collective-permute-start(bf16[144,1024]{1,0:T(8,128)(2,1)S(1)} %get-tuple-element.223), channel_id=1, source_target_pairs={{0,1},{1,0},{2,3},{3,2},{4,5},{5,4},{6,7},{7,6},{8,9},{9,8},{10,11... | collective-permute-start | bytes 884744 | tf_op jit(solution)/shard_map/ppermute | solution.py:17
  464.7 24.3 %collective-permute-start.36 = (bf16[432,1152]{1,0:T(8,128)(2,1)}, bf16[432,1152]{1,0:T(8,128)(2,1)S(1)}, u32[]{:S(2)}, u32[]{:S(2)}) collective-permute-start(bf16[432,1152]{1,0:T(8,128)(2,1)} %get-tuple-element.145), channel_id=1, source_target_pairs={{0,8},{4,12},{24,16},{28,20},{8,0},{12,4},{16,24},{20,28},{1,9},{5... | collective-permute-start | bytes 2985992 | tf_op jit(solution)/shard_map/ppermute | solution.py:201
  494.8 24.4 %collective-permute-start.46 = (bf16[432,1152]{1,0:T(8,128)(2,1)}, bf16[432,1152]{1,0:T(8,128)(2,1)S(1)}, u32[]{:S(2)}, u32[]{:S(2)}) collective-permute-start(bf16[432,1152]{1,0:T(8,128)(2,1)} %get-tuple-element.148.refs_0_), channel_id=1, source_target_pairs={{8,0},{12,4},{16,24},{20,28},{9,1},{13,5},{17,25},{21,29},{10,2},{... | collective-permute-start | bytes 2985992 | tf_op jit(solution)/shard_map/ppermute | solution.py:201
  496.1 23.2 %collective-permute-start.47 = (bf16[432,1152]{1,0:T(8,128)(2,1)}, bf16[432,1152]{1,0:T(8,128)(2,1)S(1)}, u32[]{:S(2)}, u32[]{:S(2)}) collective-permute-start(bf16[432,1152]{1,0:T(8,128)(2,1)} %get-tuple-element.149.refs_2_), channel_id=1, source_target_pairs={{8,16},{12,20},{16,8},{20,12},{9,17},{13,21},{17,9},{21,13},{10,18... | collective-permute-start | bytes 2985992 | tf_op jit(solution)/shard_map/ppermute | solution.py:201
  496.8 22.3 %collective-permute-start.49 = (bf16[160,1536]{1,0:T(8,128)(2,1)}, bf16[160,1536]{1,0:T(8,128)(2,1)S(1)}, u32[]{:S(2)}, u32[]{:S(2)}) collective-permute-start(bf16[160,1536]{1,0:T(8,128)(2,1)} %get-tuple-element.151.refs_6_), channel_id=1, source_target_pairs={{0,8},{4,12},{24,16},{28,20},{1,9},{5,13},{25,17},{29,21},{2,10},{... | collective-permute-start | bytes 1474568 | tf_op jit(solution)/shard_map/ppermute | solution.py:201
  525.7 23.7 %collective-permute-start.50 = (bf16[432,1152]{1,0:T(8,128)(2,1)}, bf16[432,1152]{1,0:T(8,128)(2,1)}, u32[]{:S(2)}, u32[]{:S(2)}) collective-permute-start(bf16[432,1152]{1,0:T(8,128)(2,1)} %get-tuple-element.152.refs_0_), channel_id=1, source_target_pairs={{8,0},{12,4},{16,24},{20,28},{9,1},{13,5},{17,25},{21,29},{10,2},{... | collective-permute-start | bytes 2985992 | tf_op jit(solution)/shard_map/ppermute | solution.py:201
  528.0 45.8 %collective-permute-start.61 = (bf16[432,1152]{1,0:T(8,128)(2,1)S(1)}, bf16[432,1152]{1,0:T(8,128)(2,1)}, u32[]{:S(2)}, u32[]{:S(2)}) collective-permute-start(bf16[432,1152]{1,0:T(8,128)(2,1)S(1)} %copy-done.39), channel_id=1, source_target_pairs={{0,4},{4,0},{8,12},{12,8},{16,20},{20,16},{24,28},{28,24},{1,5},{5... | collective-permute-start | bytes 2985992 | tf_op jit(solution)/shard_map/ppermute | solution.py:17
  555.4 26.1 %collective-permute-start.57 = (bf16[432,1152]{1,0:T(8,128)(2,1)S(1)}, bf16[432,1152]{1,0:T(8,128)(2,1)}, u32[]{:S(2)}, u32[]{:S(2)}) collective-permute-start(bf16[432,1152]{1,0:T(8,128)(2,1)S(1)} %copy-done.41), channel_id=1, source_target_pairs={{0,4},{4,0},{8,12},{12,8},{16,20},{20,16},{24,28},{28,24},{1,5},{5... | collective-permute-start | bytes 2985992 | tf_op jit(solution)/shard_map/ppermute | solution.py:17
  (153 other events, 1363.0 us)

commit v4 on v3

--- a/solution.py
+++ b/solution.py
@@ -35,105 +35,120 @@
     )
 
 
-def tile_of(size, most):
-    return max(tile for tile in range(16, most + 1, 16) if size % tile == 0)
+def after(array, *others):
+    place = pl.BlockSpec(memory_space=pl.ANY)
+    return pl.pallas_call(
+        lambda *refs: None,
+        out_shape=jax.ShapeDtypeStruct(array.shape, array.dtype),
+        in_specs=[place] * (1 + len(others)),
+        out_specs=place,
+        input_output_aliases={0: 0},
+        name="after",
+    )(array, *others)
+
+
+def scalar(value):
+    return value.astype(jnp.int32).reshape(1)
+
+
+def packed(weights, extra=None):
+    half = weights[0].shape[0] // 2
+    wide = sum(weight.shape[1] for weight in weights)
+    below = 0 if extra is None else extra.shape[0]
+
+    def kernel(core_ref, *refs):
+        out_ref = refs[-1]
+        for side in range(2):
+
+            @pl.when(core_ref[0] == side)
+            def _():
+                at = 0
+                for ref in refs[: len(weights)]:
+                    out_ref[:half, at : at + ref.shape[1]] = ref[side * half : (side + 1) * half, :]
+                    at += ref.shape[1]
+
+        if extra is not None:
+            out_ref[half:, :] = refs[len(weights)][...]
+
+    arrays = list(weights) + ([] if extra is None else [extra])
+    return pl.pallas_call(
+        kernel,
+        grid_spec=pltpu.PrefetchScalarGridSpec(
+            num_scalar_prefetch=1,
+            grid=(1,),
+            in_specs=[pl.BlockSpec(array.shape, lambda i, core_ref: (0, 0)) for array in arrays],
+            out_specs=pl.BlockSpec((half + below, wide), lambda i, core_ref: (0, 0)),
+        ),
+        out_shape=jax.ShapeDtypeStruct((half + below, wide), jnp.bfloat16),
+        compiler_params=params(),
+        name="pack",
+    )(scalar(lax.axis_index("replica") % 2), *arrays)
+
+
+def unpacked(weights, got, peers):
+    rows = weights[0].shape[0]
+    half = rows // 2
+    group = len(got) + 1
+    wide = sum(weight.shape[1] for weight in weights)
+    own = len(weights)
+
+    def kernel(core_ref, rank_ref, *refs):
+        out_ref = refs[-1]
+        mask = rank_ref[0] ^ pl.program_id(0)
+
+        @pl.when(mask == 0)
+        def _():
+            at = 0
+            for ref in refs[:own]:
+                out_ref[:, at : at + ref.shape[1]] = ref[...]
+                at += ref.shape[1]
+
+        for other in range(1, group):
+            for side in range(2):
+
+                @pl.when((mask == other) & (core_ref[0] == side))
+                def _():
+                    out_ref[side * half : (side + 1) * half, :] = refs[own + other - 1][:half, :]
+                    out_ref[(1 - side) * half : (2 - side) * half, :] = refs[own + group - 2 + other][:half, :]
+
+    arrays = list(weights) + list(got) + list(peers)
+    return pl.pallas_call(
+        kernel,
+        grid_spec=pltpu.PrefetchScalarGridSpec(
+            num_scalar_prefetch=2,
+            grid=(group,),
+            in_specs=[pl.BlockSpec(array.shape, lambda i, *refs: (0, 0)) for array in arrays],
+            out_specs=pl.BlockSpec((rows, wide), lambda i, *refs: (i, 0)),
+        ),
+        out_shape=jax.ShapeDtypeStruct((group * rows, wide), jnp.bfloat16),
+        compiler_params=params(),
+        name="unpack",
+    )(scalar(lax.axis_index("replica") % 2), scalar(lax.axis_index("fsdp")), *arrays)
 
 
 GELU_A = (2.0 / 3.141592653589793) ** 0.5
 GELU_B = 0.044715
 
 
-def ffn_forward_kernel(x_ref, gate_ref, up_ref, down_ref, hidden_ref, slope_ref, act_ref, out_ref, acc):
-    step = pl.program_id(0)
-    x = x_ref[...]
-    gate = dot(gate_ref[...], x, 1, 1)
-    upper = dot(up_ref[...], x, 1, 1)
+def ffn_forward(x, gate_weight, up_weight, down_weight):
+    gate = contract(gate_weight, x, 1, 1)
+    upper = contract(up_weight, x, 1, 1)
     square = gate * gate
     bend = jnp.tanh(GELU_A * gate * (1.0 + GELU_B * square))
     half = 0.5 + 0.5 * bend
     act = gate * half
     slope = half + 0.5 * gate * (1.0 - bend * bend) * (GELU_A * (1.0 + 3.0 * GELU_B * square))
     hidden = (act * upper).astype(jnp.bfloat16)
-    hidden_ref[...] = hidden
-    slope_ref[...] = (slope * upper).astype(jnp.bfloat16)
-    act_ref[...] = act.astype(jnp.bfloat16)
-    part = dot(hidden, down_ref[...], 0, 0)
-
-    @pl.when(step == 0)
-    def _():
-        acc[...] = part
-
-    @pl.when(step > 0)
-    def _():
-        acc[...] += part
-
-    @pl.when(step == pl.num_programs(0) - 1)
-    def _():
-        out_ref[...] = acc[...].astype(jnp.bfloat16)
-
-
-def ffn_forward(x, gate_weight, up_weight, down_weight):
-    rows, model = x.shape
-    units = gate_weight.shape[0]
-    tile = tile_of(units, 432)
-    weight = pl.BlockSpec((tile, model), lambda i: (i, 0))
-    flat = pl.BlockSpec((tile, rows), lambda i: (i, 0))
-    whole = pl.BlockSpec((rows, model), lambda i: (0, 0))
-    kept = jax.ShapeDtypeStruct((units, rows), jnp.bfloat16)
-    return pl.pallas_call(
-        ffn_forward_kernel,
-        grid=(units // tile,),
-        out_shape=[kept, kept, kept, jax.ShapeDtypeStruct((rows, model), jnp.bfloat16)],
-        in_specs=[whole, weight, weight, weight],
-        out_specs=[flat, flat, flat, whole],
-        scratch_shapes=[pltpu.VMEM((rows, model), jnp.float32)],
-        compiler_params=params(),
-        name="ffn_forward",
-    )(x, gate_weight, up_weight, down_weight)
-
-
-def ffn_backward_kernel(
-    grad_ref, gate_ref, up_ref, down_ref, slope_ref, act_ref, gate_grad_ref, up_grad_ref, out_ref, acc
-):
-    step = pl.program_id(0)
-    grad_hidden = dot(down_ref[...], grad_ref[...], 1, 1)
-    grad_gate = (grad_hidden * slope_ref[...].astype(jnp.float32)).astype(jnp.bfloat16)
-    grad_upper = (grad_hidden * act_ref[...].astype(jnp.float32)).astype(jnp.bfloat16)
-    gate_grad_ref[...] = grad_gate
-    up_grad_ref[...] = grad_upper
-    part = dot(grad_gate, gate_ref[...], 0, 0) + dot(grad_upper, up_ref[...], 0, 0)
-
-    @pl.when(step == 0)
-    def _():
-        acc[...] = part
-
-    @pl.when(step > 0)
-    def _():
-        acc[...] += part
-
-    @pl.when(step == pl.num_programs(0) - 1)
-    def _():
-        out_ref[...] = acc[...].astype(jnp.bfloat16)
+    part = contract(hidden, down_weight, 0, 0).astype(jnp.bfloat16)
+    return hidden, (slope * upper).astype(jnp.bfloat16), act.astype(jnp.bfloat16), part
 
 
 def ffn_backward(grad, gate_weight, up_weight, down_weight, slope, act):
-    rows, model = grad.shape
-    units = gate_weight.shape[0]
-    tile = tile_of(units, 432)
-    weight = pl.BlockSpec((tile, model), lambda i: (i, 0))
-    flat = pl.BlockSpec((tile, rows), lambda i: (i, 0))
-    whole = pl.BlockSpec((rows, model), lambda i: (0, 0))
-    kept = jax.ShapeDtypeStruct((units, rows), jnp.bfloat16)
-    return pl.pallas_call(
-        ffn_backward_kernel,
-        grid=(units // tile,),
-        out_shape=[kept, kept, jax.ShapeDtypeStruct((rows, model), jnp.bfloat16)],
-        in_specs=[whole, weight, weight, weight, flat, flat],
-        out_specs=[flat, flat, whole],
-        scratch_shapes=[pltpu.VMEM((rows, model), jnp.float32)],
-        compiler_params=params(),
-        name="ffn_backward",
-    )(grad, gate_weight, up_weight, down_weight, slope, act)
+    grad_hidden = contract(down_weight, grad, 1, 1)
+    grad_gate = (grad_hidden * slope.astype(jnp.float32)).astype(jnp.bfloat16)
+    grad_upper = (grad_hidden * act.astype(jnp.float32)).astype(jnp.bfloat16)
+    part = contract(grad_gate, gate_weight, 0, 0) + contract(grad_upper, up_weight, 0, 0)
+    return grad_gate, grad_upper, part.astype(jnp.bfloat16)
 
 
 def chunks_of(units):
@@ -149,10 +164,16 @@
     core = (lax.axis_index("replica") % 2).astype(jnp.int32).reshape(1)
 
     def kernel(core_ref, *refs):
-        left = jnp.concatenate([ref[...] for ref in refs[:group]], axis=1)
-        right = jnp.concatenate([ref[...] for ref in refs[group : 2 * group]], axis=0)
-        value = dot(left, right, 1, 0).astype(jnp.bfloat16)
-        other_ref, mine_ref = refs[2 * group :]
+        other_ref, mine_ref, left_ref, right_ref = refs[2 * group :]
+
+        @pl.when((pl.program_id(0) == 0) & (pl.program_id(1) == 0))
+        def _():
+            for spot in range(group):
+                right_ref[spot * rows : (spot + 1) * rows, :] = refs[group + spot][...]
+
+        for spot in range(group):
+            left_ref[:, spot * rows : (spot + 1) * rows] = refs[spot][...]
+        value = dot(left_ref[...], right_ref[...], 1, 0).astype(jnp.bfloat16)
 
         @pl.when(pl.program_id(0) == 0)
         def _():
@@ -182,6 +203,10 @@
                     (1, tile, model),
                     lambda side, chunk, core_ref: (jnp.where(side == 0, 0, chunk), 0, 0),
                 ),
+            ],
+            scratch_shapes=[
+                pltpu.VMEM((tile, group * rows), jnp.bfloat16),
+                pltpu.VMEM((group * rows, model), jnp.bfloat16),
             ],
         ),
         out_shape=[shape, shape],
@@ -391,25 +416,9 @@
     return lax.optimization_barrier(total.astype(jnp.bfloat16))
 
 
-def in_order(blocks):
-    rank = lax.axis_index("fsdp")
-    stack = jnp.stack(blocks)
-    return [lax.dynamic_index_in_dim(stack, rank ^ i, 0, keepdims=False) for i in range(len(blocks))]
-
-
-def gathered_rows(own, extra=None):
-    group = lax.axis_size("fsdp")
-    half = own.shape[0] // 2
-    block = halves(own, 0)[0]
-    if extra is not None:
-        block = jnp.concatenate([block, extra], axis=0)
-    got = [swapped(block, "fsdp", mask) for mask in range(1, group)]
-    mine = jnp.stack([part[:half] for part in got])
-    whole = core_join(mine, 1)
-    rows = jnp.concatenate(in_order([own] + list(whole)), axis=0)
-    if extra is None:
-        return rows
-    return rows, in_order([extra] + [part[half:] for part in got])
+def fetched(block):
+    got = [swapped(block, "fsdp", mask) for mask in range(1, lax.axis_size("fsdp"))]
+    return got, [swapped(part, "replica", 1) for part in got]
 
 
 def passed_along(block, axis, distance):
@@ -482,16 +491,21 @@
     own_head = query_gain.shape[0]
     hops = (WINDOW - 1) // rows + 1
     scale = head_size ** (-0.5)
-    w_own = jnp.concatenate([query_weight, key_weight, value_weight], axis=1)
-    wide = w_own.shape[1]
+    qkv_weights = (query_weight, key_weight, value_weight)
+    wide = sum(weight.shape[1] for weight in qkv_weights)
     sizes = [own_model] * 4 + [own_head] * 2
     gains = jnp.concatenate([norm_in, norm_attn, norm_ffn, norm_out, query_gain, key_gain])
     gains = jnp.pad(gains[None, :], ((0, 15), (0, wide - sum(sizes))))
-    w_qkv, gain_rows = gathered_rows(w_own, gains)
-    w_out = gathered_rows(out_weight)
+    got, peers = fetched(packed(qkv_weights, gains))
+    w_qkv = unpacked(qkv_weights, got, peers)
+    gain_stack = jnp.stack([gains[0]] + [part[-16] for part in got])
+    gain_rows = [
+        lax.dynamic_index_in_dim(gain_stack, rank ^ i, 0, keepdims=False) for i in range(group)
+    ]
+    got, peers = fetched(after(packed([out_weight]), w_qkv))
     spots = [sum(sizes[:i]) for i in range(7)]
     gain_in, gain_attn, gain_ffn, gain_out, gain_query, gain_key = (
-        jnp.concatenate([row[0, spots[i] : spots[i + 1]] for row in gain_rows]) for i in range(6)
+        jnp.concatenate([row[spots[i] : spots[i + 1]] for row in gain_rows]) for i in range(6)
     )
     residual_in = hidden_in.astype(jnp.float32)
     normed_in = normed(residual_in, gain_in).astype(jnp.bfloat16)
@@ -535,6 +549,7 @@
         .reshape(rows, heads * head_size)
         .astype(jnp.bfloat16)
     )
+    w_out = unpacked([out_weight], got, peers)
     attended = contract(mixed, w_out, 1, 1)
     resid = residual_in + normed(attended, gain_attn)
     ffn_in = normed(resid, gain_ffn).astype(jnp.bfloat16)
@@ -542,10 +557,11 @@
     hiddens, slopes, acts, parts = [], [], [], []
     for mask in range(group):
         hidden, slope, act, part = ffn_forward(ffn_blocks[mask], gate_weight, up_weight, down_weight)
-        parts.append(swapped(part, "fsdp", mask) if mask else part)
+        parts.append(part)
         hiddens.append(hidden)
         slopes.append(slope)
         acts.append(act)
+    parts = parts[:1] + [swapped(parts[mask], "fsdp", mask) for mask in masks]
     branch = sum(part.astype(jnp.float32) for part in parts)
     result = resid + normed(branch, gain_out)
     hidden_out = result.astype(jnp.bfloat16)
@@ -560,17 +576,18 @@
         far = swapped(other, "replica", 1)
         return [(key, [(mine, key[1]), (far, key[1])]) for key in line_names(name, units)]
 
-    waiting = fresh("down", *weight_grad(hiddens, pieces))
-    grad_gates, grad_uppers = {}, {}
-    order = list(masks) + [0]
-    returned = {}
-    for mask in order:
+    grad_gates, grad_uppers, returned = {}, {}, {}
+    last = group - 1
+    for mask in range(group):
+        if mask == last:
+            waiting = fresh("down", *weight_grad(hiddens, pieces))
+            pieces[mask] = line.advance([waiting.pop(0)], pieces[mask])
         grad_gates[mask], grad_uppers[mask], part = ffn_backward(
             pieces[mask], gate_weight, up_weight, down_weight, slopes[mask], acts[mask]
         )
+        if mask < last:
+            pieces[mask + 1] = after(pieces[mask + 1], part)
         returned[mask] = swapped(part, "fsdp", mask) if mask else part
-        if mask == order[0]:
-            pieces[order[1]] = line.advance([waiting.pop(0)], pieces[order[1]])
     waiting += fresh("gate", *weight_grad([grad_gates[i] for i in range(group)], ffn_blocks))
     waiting += fresh("up", *weight_grad([grad_uppers[i] for i in range(group)], ffn_blocks))
     returned[0] = line.advance([waiting.pop(0)], returned[0])
@@ -642,8 +659,9 @@
     while waiting:
         line.advance([waiting.pop(0)])
     grad_down = whole_grad(line, "down", units)
-    line.advance([("out", [out_part]), ("qkv", [qkv_part])])
+    grad_down = line.advance([("out", [out_part]), ("qkv", [qkv_part])], grad_down)
     grad_gate_w = whole_grad(line, "gate", units)
+    grad_gate_w = line.advance([], grad_gate_w)
     grad_up_w = whole_grad(line, "up", units)
     owned = core_join(line.finished("qkv"), 0).astype(jnp.float32)
     owned_out = core_join(line.finished("out"), 0).astype(jnp.float32)

time: 611 us -> 565 us (0.925)
  Pallas kernels: 181 us -> 105 us
  matrix products: 21.6 us -> 83.2 us
  other arithmetic: 70.3 us -> 55 us
  local copies, waits for them, and re-layouts: 77.4 us -> 67 us
  waiting for transfers between devices: 160 us -> 152 us
    pallas_call x8, Pallas kernels: 88.9 us -> 12.2 us  [the longest x2 8.43 us: unpacked(): pl.pallas_call(kernel, grid_spec=pltpu.PrefetchScalarGridSpec(num_scalar_...]
    dot_general x8 -> x32, matrix products: 15.9 us -> 76.3 us  [contract(): lax.dot_general(left, right, (((left_dim,), (right_dim,)), ((), ())), pre...]
    ppermute x39 -> x43, waiting for transfers between devices: 74.1 us -> 64.4 us  [swapped(): return lax.ppermute(block, axis, route)]
    concatenate x7 -> x5, local copies, waits for them, and re-layouts: 12.4 us -> 3.79 us  [per_device(): jnp.concatenate([row[spots[i]:spots[i + 1]] for row in gain_rows])]
    unnamed x247 -> x273, local copies, waits for them, and re-layouts: 19.7 us -> 23.2 us
    ppermute x39 -> x43, starting transfers between devices: 34.3 us -> 35.1 us  [swapped(): return lax.ppermute(block, axis, route)]
  transfers between devices with their start and end apart: 63 -> 67, of which waited for: 21 -> 22; matrix products, arithmetic and copies ran while one was open for 19% -> 30% of each run, Pallas kernels for 24% -> 12%
where the time goes in v4:
time: 565 us; the launch traced here: 555 us
  waiting for transfers between devices  152 us (27%)
  Pallas kernels  105 us (19%)
  starting transfers between devices  90 us (16%)
  matrix products  83.2 us (15%)
  local copies, waits for them, and re-layouts  67 us (12%)
  other arithmetic  55 us (10%)
    ppermute x20, waiting for transfers between devices, exchanged(): return lax.ppermute(block, 'replica', route)  79.3 us
    dot_general x32, matrix products, contract(): lax.dot_general(left, right, (((left_dim,), (right_dim,)), ((), ())), pre...  76.3 us
    ppermute x43, waiting for transfers between devices, swapped(): return lax.ppermute(block, axis, route)  64.4 us
    pallas_call x10, Pallas kernels, advance(): pl.pallas_call(kernel, grid_spec=pltpu.PrefetchScalarGridSpec(num_scalar_...  46.7 us
    ppermute x20, starting transfers between devices, exchanged(): return lax.ppermute(block, 'replica', route)  45 us
    ppermute x43, starting transfers between devices, swapped(): return lax.ppermute(block, axis, route)  35.1 us
    pallas_call x3, Pallas kernels, weight_grad(): pl.pallas_call(kernel, grid_spec=pltpu.PrefetchScalarGridSpec(num_scalar_...  28.7 us
    unnamed x273, local copies, waits for them, and re-layouts  23.2 us
  transfers between devices with their start and end apart: 67, of which 22 were waited for; matrix products, arithmetic and copies ran while one was open for 30% of the time, Pallas kernels for 12%

profile of v4, /device:TPU:0, one launch (start us, length us, event | category | flops | bytes accessed | tf_op | source)
XLA Modules:
  0.0 554.8 jit_solution(14623092665267412132)
XLA Ops:
  22.8 11.1 %collective-permute-done.1.refs_4_ = bf16[160,1536]{1,0:T(8,128)(2,1)S(1)} collective-permute-done((bf16[160,1536]{1,0:T(8,128)(2,1)}, bf16[160,1536]{1,0:T(8,128)(2,1)S(1)}, u32[]{:S(2)}, u32[]{:S(2)}) %collective-permute-start.1) | collective-permute-done | bytes 491552 | tf_op jit(solution)/shard_map/ppermute | solution.py:17
  60.9 8.2 %collective-permute-done.6 = bf16[256,512]{1,0:T(8,128)(2,1)} collective-permute-done((bf16[256,512]{1,0:T(8,128)(2,1)S(1)}, bf16[256,512]{1,0:T(8,128)(2,1)}, u32[]{:S(2)}, u32[]{:S(2)}) %collective-permute-start.6) | collective-permute-done | bytes 262176 | tf_op jit(solution)/shard_map/ppermute | solution.py:427
  92.9 8.3 %collective-permute-done.14.refs_5_ = bf16[256,1152]{1,0:T(8,128)(2,1)} collective-permute-done((bf16[256,1152]{1,0:T(8,128)(2,1)}, bf16[256,1152]{1,0:T(8,128)(2,1)}, u32[]{:S(2)}, u32[]{:S(2)}) %collective-permute-start.14) | collective-permute-done | bytes 589856 | tf_op jit(solution)/shard_map/ppermute | solution.py:17
  110.8 7.3 %collective-permute-done.16.refs_6_ = bf16[256,1152]{1,0:T(8,128)(2,1)S(1)} collective-permute-done((bf16[256,1152]{1,0:T(8,128)(2,1)}, bf16[256,1152]{1,0:T(8,128)(2,1)S(1)}, u32[]{:S(2)}, u32[]{:S(2)}) %collective-permute-start.16) | collective-permute-done | bytes 589856 | tf_op jit(solution)/shard_map/ppermute | solution.py:17
  138.0 13.5 %collective-permute-done.17 = bf16[256,1152]{1,0:T(8,128)(2,1)S(1)} collective-permute-done((bf16[256,1152]{1,0:T(8,128)(2,1)S(1)}, bf16[256,1152]{1,0:T(8,128)(2,1)S(1)}, u32[]{:S(2)}, u32[]{:S(2)}) %collective-permute-start.17) | collective-permute-done | bytes 589856 | tf_op jit(solution)/shard_map/ppermute | solution.py:17
  166.2 6.1 %collective-permute-done.20.refs_0_ = bf16[256,1152]{1,0:T(8,128)(2,1)} collective-permute-done((bf16[256,1152]{1,0:T(8,128)(2,1)}, bf16[256,1152]{1,0:T(8,128)(2,1)}, u32[]{:S(2)}, u32[]{:S(2)}) %collective-permute-start.20) | collective-permute-done | bytes 589856 | tf_op jit(solution)/shard_map/ppermute | solution.py:17
  172.3 5.7 %multiply_convert_fusion.7 = (bf16[1728,256]{1,0:T(8,128)(2,1)S(1)}, bf16[1728,256]{1,0:T(8,128)(2,1)S(1)}) fusion(f32[1728,256]{1,0:T(8,128)} %copy-done.135, f32[1728,256]{1,0:T(8,128)} %get-tuple-element.203, bf16[256,1152]{1,0:T(8,128)(2,1)} %after.5.refs_5_, bf16[1728,1152]{1,0:T(8,128)(2,1)} %param.30), kind=kOutput, calls=%fused_computation.58 | convolution fusion | flops 1030717440 | bytes 9879552 | tf_op jit(solution)/shard_map/dot_general | solution.py:431
  183.6 5.7 %multiply_convert_fusion.4 = (bf16[1728,256]{1,0:T(8,128)(2,1)S(1)}, bf16[1728,256]{1,0:T(8,128)(2,1)S(1)}) fusion(f32[1728,256]{1,0:T(8,128)} %copy-done.134, f32[1728,256]{1,0:T(8,128)} %get-tuple-element.199, bf16[256,1152]{1,0:T(8,128)(2,1)} %after.6.refs_6_, bf16[1728,1152]{1,0:T(8,128)(2,1)} %param.30), kind=kOutput, calls=%fused_computation.55 | convolution fusion | flops 1030717440 | bytes 9879552 | tf_op jit(solution)/shard_map/dot_general | solution.py:431
  194.4 9.5 %weight_grad.3 = (bf16[2,432,1152]{2,1,0:T(8,128)(2,1)}, bf16[2,432,1152]{2,1,0:T(8,128)(2,1)}) custom-call(s32[1]{0:T(128)} %bitcast.core_ref, bf16[1728,256]{1,0:T(8,128)(2,1)} %copy-done.11, bf16[1728,256]{1,0:T(8,128)(2,1)} %copy-done.54, bf16[1728,256]{1,0:T(8,128)(2,1)} %copy-done.56, bf16[1728,256]{1,0:T(8,128)(2,1)} %copy-done.57, ...), custom_call_target="tpu_custom_call" | custom-call | tf_op jit(solution)/shard_map/weight_grad/pallas_call | solution.py:190
  212.0 4.8 collective-permute-start.24
  216.8 4.5 multiply_convert_fusion.1
  228.0 9.6 %weight_grad.4 = (bf16[2,432,1152]{2,1,0:T(8,128)(2,1)}, bf16[2,432,1152]{2,1,0:T(8,128)(2,1)}) custom-call(s32[1]{0:T(128)} %bitcast.core_ref, bf16[1728,256]{1,0:T(8,128)(2,1)} %copy-done.55, bf16[1728,256]{1,0:T(8,128)(2,1)} %copy-done.58, bf16[1728,256]{1,0:T(8,128)(2,1)} %copy-done.59, bf16[1728,256]{1,0:T(8,128)(2,1)} %copy-done.61, ...), custom_call_target="tpu_custom_call" | custom-call | tf_op jit(solution)/shard_map/weight_grad/pallas_call | solution.py:190
  237.7 4.8 reshape.572
  248.2 9.5 %weight_grad.5 = (bf16[2,432,1152]{2,1,0:T(8,128)(2,1)}, bf16[2,432,1152]{2,1,0:T(8,128)(2,1)}) custom-call(s32[1]{0:T(128)} %bitcast.core_ref, bf16[1728,256]{1,0:T(8,128)(2,1)} %copy-done.51, bf16[1728,256]{1,0:T(8,128)(2,1)} %copy-done.52, bf16[1728,256]{1,0:T(8,128)(2,1)} %copy-done.53, bf16[1728,256]{1,0:T(8,128)(2,1)} %copy-done.60, ...), custom_call_target="tpu_custom_call" | custom-call | tf_op jit(solution)/shard_map/weight_grad/pallas_call | solution.py:190
  279.9 7.8 %collective-permute-done.29.refs_3_ = bf16[432,1152]{1,0:T(8,128)(2,1)} collective-permute-done((bf16[432,1152]{1,0:T(8,128)(2,1)}, bf16[432,1152]{1,0:T(8,128)(2,1)}, u32[]{:S(2)}, u32[]{:S(2)}) %collective-permute-start.29) | collective-permute-done | bytes 995360 | tf_op jit(solution)/shard_map/ppermute | solution.py:226
  287.8 5.7 %line_step.12 = (bf16[432,1152]{1,0:T(8,128)(2,1)}, bf16[432,1152]{1,0:T(8,128)(2,1)}, bf16[432,1152]{1,0:T(8,128)(2,1)}, bf16[432,1152]{1,0:T(8,128)(2,1)}, bf16[256,1152]{1,0:T(8,128)(2,1)}) custom-call(s32[1]{0:T(128)} %bitcast.20.place_ref, bf16[432,1152]{1,0:T(8,128)(2,1)} %get-tuple-element.69.refs_0_, ...), custom_call_target="tpu_custom_call", output_to_operand_aliasing={{4}: (7, {})} | custom-call | tf_op jit(solution)/shard_map/line_step/pallas_call | solution.py:306
  300.3 6.6 %multiply_convert_fusion = bf16[256,4,768]{2,0,1:T(8,128)(2,1)} fusion(f32[256,4,768]{2,0,1:T(8,128)S(1)} %fusion.57, f32[256,4,768]{2,1,0:T(4,128)S(1)} %copy-done.23, f32[256,4]{0,1:T(4,128)S(1)} %copy-done.120, pred[256,768]{1,0:T(8,128)(4,1)S(1)} %copy-done.63), kind=kOutput, calls=%fused_computation.11 | output fusion | flops 6293247 | bytes 8065024 | tf_op jit(solution)/shard_map/sub | solution.py:611
  320.0 6.2 %line_step.13 = (bf16[432,1152]{1,0:T(8,128)(2,1)}, bf16[432,1152]{1,0:T(8,128)(2,1)}, bf16[432,1152]{1,0:T(8,128)(2,1)}, bf16[432,1152]{1,0:T(8,128)(2,1)}, bf1...) custom-call(s32[1]{0:T(128)} %bitcast.20.place_ref, ...), custom_call_target="tpu_custom_call", output_to_operand_aliasing={{5}: (8, {})} | custom-call | tf_op jit(solution)/shard_map/line_step/pallas_call | solution.py:306
  352.3 4.8 collective-permute-done.33.refs_1_
  357.1 6.1 %line_step.14 = (bf16[432,1152]{1,0:T(8,128)(2,1)}, bf16[432,1152]{1,0:T(8,128)(2,1)}, bf16[432,1152]{1,0:T(8,128)(2,1)}, bf16[432,1152]{1,0:T(8,128)(2,1)}, bf1...) custom-call(s32[1]{0:T(128)} %bitcast.20.place_ref, ...), custom_call_target="tpu_custom_call", output_to_operand_aliasing={{5}: (8, {})} | custom-call | tf_op jit(solution)/shard_map/line_step/pallas_call | solution.py:306
  401.3 4.8 collective-permute-done.45
  406.6 7.3 %collective-permute-done.38.refs_1_ = bf16[432,1152]{1,0:T(8,128)(2,1)S(1)} collective-permute-done((bf16[432,1152]{1,0:T(8,128)(2,1)}, bf16[432,1152]{1,0:T(8,128)(2,1)S(1)}, u32[]{:S(2)}, u32[]{:S(2)}) %collective-permute-start.38) | collective-permute-done | bytes 995360 | tf_op jit(solution)/shard_map/ppermute | solution.py:226
  415.7 6.2 %line_step.15 = (bf16[432,1152]{1,0:T(8,128)(2,1)}, bf16[432,1152]{1,0:T(8,128)(2,1)}, bf16[432,1152]{1,0:T(8,128)(2,1)}, bf16[432,1152]{1,0:T(8,128)(2,1)}, bf16[432,1152]{1,0:T(8,128)(2,1)}) custom-call(s32[1]{0:T(128)} %bitcast.20.place_ref, bf16[432,1152]{1,0:T(8,128)(2,1)} %get-tuple-element.86.refs_0_, bf16[432,1152]{1,0:T(8,128)(2,1)} %copy-done.37, ...), custom_call_target="tpu_custom_call" | custom-call | tf_op jit(solution)/shard_map/line_step/pallas_call | solution.py:306
  427.3 5.7 %whole_grad.3.refs_7_ = f32[1728,1152]{1,0:T(8,128)} custom-call(s32[1]{0:T(128)} %bitcast.core_ref, bf16[432,1152]{1,0:T(8,128)(2,1)} %get-tuple-element.94.refs_0_, bf16[432,1152]{1,0:T(8,128)(2,1)} %get-tuple-element.95.refs_1_, bf16[432,1152]{1,0:T(8,128)(2,1)} %collective-permute-done.50.refs_2_, bf16[432,1152]{1,0:T(8,128)(2,1)} %collective-permute-done.51.refs_3_), custom_call_target="tpu_custom_call" | custom-call | tf_op jit(solution)/shard_map/whole_grad/pallas_call | solution.py:369
  439.6 6.3 %collective-permute-done.40.refs_1_ = bf16[432,1152]{1,0:T(8,128)(2,1)S(1)} collective-permute-done((bf16[432,1152]{1,0:T(8,128)(2,1)}, bf16[432,1152]{1,0:T(8,128)(2,1)S(1)}, u32[]{:S(2)}, u32[]{:S(2)}) %collective-permute-start.40) | collective-permute-done | bytes 995360 | tf_op jit(solution)/shard_map/ppermute | solution.py:226
  447.2 4.8 line_step.16
  454.0 8.2 %collective-permute-start.55 = (bf16[160,1536]{1,0:T(8,128)(2,1)}, bf16[160,1536]{1,0:T(8,128)(2,1)S(1)}, u32[]{:S(2)}, u32[]{:S(2)}) collective-permute-start(bf16[160,1536]{1,0:T(8,128)(2,1)} %get-tuple-element.99.refs_6_), channel_id=1, source_target_pairs={{0,8},{4,12},{24,16},{28,20},{1,9},{5,13},{25,17},{29,21},{2,10},{... | collective-permute-start | bytes 1474568 | tf_op jit(solution)/shard_map/ppermute | solution.py:226
  464.6 5.6 %whole_grad.4.refs_8_ = f32[1728,1152]{1,0:T(8,128)} custom-call(s32[1]{0:T(128)} %bitcast.core_ref, bf16[432,1152]{1,0:T(8,128)(2,1)} %get-tuple-element.100.refs_0_, bf16[432,1152]{1,0:T(8,128)(2,1)} %get-tuple-element.101.refs_1_, bf16[432,1152]{1,0:T(8,128)(2,1)} %copy-done.42, bf16[432,1152]{1,0:T(8,128)(2,1)} %copy-done.49), custom_call_target="tpu_custom_call" | custom-call | tf_op jit(solution)/shard_map/whole_grad/pallas_call | solution.py:369
  470.2 9.5 %collective-permute-done.54.refs_5_ = bf16[144,1024]{1,0:T(8,128)(2,1)S(1)} collective-permute-done((bf16[144,1024]{1,0:T(8,128)(2,1)}, bf16[144,1024]{1,0:T(8,128)(2,1)S(1)}, u32[]{:S(2)}, u32[]{:S(2)}) %collective-permute-start.54) | collective-permute-done | bytes 294944 | tf_op jit(solution)/shard_map/ppermute | solution.py:226
  489.3 22.8 %collective-permute-done.58.refs_1_ = bf16[432,1152]{1,0:T(8,128)(2,1)S(1)} collective-permute-done((bf16[432,1152]{1,0:T(8,128)(2,1)}, bf16[432,1152]{1,0:T(8,128)(2,1)S(1)}, u32[]{:S(2)}, u32[]{:S(2)}) %collective-permute-start.58) | collective-permute-done | bytes 995360 | tf_op jit(solution)/shard_map/ppermute | solution.py:226
  518.9 17.8 %collective-permute-done.61.refs_1_ = bf16[144,1024]{1,0:T(8,128)(2,1)} collective-permute-done((bf16[144,1024]{1,0:T(8,128)(2,1)}, bf16[144,1024]{1,0:T(8,128)(2,1)}, u32[]{:S(2)}, u32[]{:S(2)}) %collective-permute-start.61) | collective-permute-done | bytes 294944 | tf_op jit(solution)/shard_map/ppermute | solution.py:226
  548.8 5.6 %whole_grad.5 = f32[1728,1152]{1,0:T(8,128)} custom-call(s32[1]{0:T(128)} %bitcast.core_ref, bf16[432,1152]{1,0:T(8,128)(2,1)} %get-tuple-element.110.refs_0_, bf16[432,1152]{1,0:T(8,128)(2,1)} %get-tuple-element.111.refs_1_, bf16[432,1152]{1,0:T(8,128)(2,1)} %copy-done.47, bf16[432,1152]{1,0:T(8,128)(2,1)} %copy-done.48), custom_call_target="tpu_custom_call" | custom-call | tf_op jit(solution)/shard_map/whole_grad/pallas_call | solution.py:369
  (543 shorter events, 301.2 us)
Async XLA Ops:
  10.5 23.4 %collective-permute-start.1 = (bf16[160,1536]{1,0:T(8,128)(2,1)}, bf16[160,1536]{1,0:T(8,128)(2,1)S(1)}, u32[]{:S(2)}, u32[]{:S(2)}) collective-permute-start(bf16[160,1536]{1,0:T(8,128)(2,1)} %pack.2), channel_id=1, source_target_pairs={{0,2},{1,3},{2,0},{3,1},{4,6},{5,7},{6,4},{7,5},{8,10},{9,11},{10,... | collective-permute-start | bytes 1474568 | tf_op jit(solution)/shard_map/ppermute | solution.py:17
  43.1 29.0 %collective-permute-start.8 = (bf16[144,1024]{1,0:T(8,128)(2,1)}, bf16[144,1024]{1,0:T(8,128)(2,1)}, u32[]{:S(2)}, u32[]{:S(2)}) collective-permute-start(bf16[144,1024]{1,0:T(8,128)(2,1)} %after.4), channel_id=1, source_target_pairs={{0,1},{1,0},{2,3},{3,2},{4,5},{5,4},{6,7},{7,6},{8,9},{9,8},{10,11... | collective-permute-start | bytes 884744 | tf_op jit(solution)/shard_map/ppermute | solution.py:17
  43.7 28.5 %collective-permute-start.9 = (bf16[144,1024]{1,0:T(8,128)(2,1)}, bf16[144,1024]{1,0:T(8,128)(2,1)}, u32[]{:S(2)}, u32[]{:S(2)}) collective-permute-start(bf16[144,1024]{1,0:T(8,128)(2,1)} %after.4), channel_id=1, source_target_pairs={{0,2},{1,3},{2,0},{3,1},{4,6},{5,7},{6,4},{7,5},{8,10},{9,11},{10,... | collective-permute-start | bytes 884744 | tf_op jit(solution)/shard_map/ppermute | solution.py:17
  45.1 27.6 %collective-permute-start.10 = (bf16[144,1024]{1,0:T(8,128)(2,1)}, bf16[144,1024]{1,0:T(8,128)(2,1)}, u32[]{:S(2)}, u32[]{:S(2)}) collective-permute-start(bf16[144,1024]{1,0:T(8,128)(2,1)} %after.4), channel_id=1, source_target_pairs={{0,3},{1,2},{2,1},{3,0},{4,7},{5,6},{6,5},{7,4},{8,11},{9,10},{10,... | collective-permute-start | bytes 884744 | tf_op jit(solution)/shard_map/ppermute | solution.py:17
  88.9 29.2 %collective-permute-start.16 = (bf16[256,1152]{1,0:T(8,128)(2,1)}, bf16[256,1152]{1,0:T(8,128)(2,1)S(1)}, u32[]{:S(2)}, u32[]{:S(2)}) collective-permute-start(bf16[256,1152]{1,0:T(8,128)(2,1)} %multiply_convert_fusion.17.refs_4_), channel_id=1, source_target_pairs={{0,2},{1,3},{2,0},{3,1},{4,6},{5,7},{6,4},{7,5},{8,10},{9,11},{10,... | collective-permute-start | bytes 1769480 | tf_op jit(solution)/shard_map/ppermute | solution.py:17
  91.5 34.0 %collective-permute-start.18 = (bf16[256,1152]{1,0:T(8,128)(2,1)}, bf16[256,1152]{1,0:T(8,128)(2,1)S(1)}, u32[]{:S(2)}, u32[]{:S(2)}) collective-permute-start(bf16[256,1152]{1,0:T(8,128)(2,1)} %multiply_convert_fusion.17.refs_4_), channel_id=1, source_target_pairs={{0,3},{1,2},{2,1},{3,0},{4,7},{5,6},{6,5},{7,4},{8,11},{9,10},{10,... | collective-permute-start | bytes 1769480 | tf_op jit(solution)/shard_map/ppermute | solution.py:17
  110.8 27.2 %collective-permute-start.15 = (bf16[256,1152]{1,0:T(8,128)(2,1)S(1)}, bf16[256,1152]{1,0:T(8,128)(2,1)S(1)}, u32[]{:S(2)}, u32[]{:S(2)}) collective-permute-start(bf16[256,1152]{1,0:T(8,128)(2,1)S(1)} %convolution_convert_fusion.4), channel_id=1, source_target_pairs={{0,1},{1,0},{2,3},{3,2},{4,5},{5,4},{6,7},{7,6},{8,9},{9,8},{10,11... | collective-permute-start | bytes 1769480 | tf_op jit(solution)/shard_map/ppermute | solution.py:17
  123.7 27.7 %collective-permute-start.17 = (bf16[256,1152]{1,0:T(8,128)(2,1)S(1)}, bf16[256,1152]{1,0:T(8,128)(2,1)S(1)}, u32[]{:S(2)}, u32[]{:S(2)}) collective-permute-start(bf16[256,1152]{1,0:T(8,128)(2,1)S(1)} %convolution_convert_fusion.3), channel_id=1, source_target_pairs={{0,2},{1,3},{2,0},{3,1},{4,6},{5,7},{6,4},{7,5},{8,10},{9,11},{10,... | collective-permute-start | bytes 1769480 | tf_op jit(solution)/shard_map/ppermute | solution.py:17
  157.2 26.5 %collective-permute-start.21 = (bf16[256,1152]{1,0:T(8,128)(2,1)}, bf16[256,1152]{1,0:T(8,128)(2,1)}, u32[]{:S(2)}, u32[]{:S(2)}) collective-permute-start(bf16[256,1152]{1,0:T(8,128)(2,1)} %get-tuple-element.169.refs_4_), channel_id=1, source_target_pairs={{0,2},{1,3},{2,0},{3,1},{4,6},{5,7},{6,4},{7,5},{8,10},{9,11},{10,... | collective-permute-start | bytes 1769480 | tf_op jit(solution)/shard_map/ppermute | solution.py:17
  158.6 35.8 %collective-permute-start.22 = (bf16[256,1152]{1,0:T(8,128)(2,1)}, bf16[256,1152]{1,0:T(8,128)(2,1)}, u32[]{:S(2)}, u32[]{:S(2)}) collective-permute-start(bf16[256,1152]{1,0:T(8,128)(2,1)} %get-tuple-element.169.refs_4_), channel_id=1, source_target_pairs={{0,3},{1,2},{2,1},{3,0},{4,7},{5,6},{6,5},{7,4},{8,11},{9,10},{10,... | collective-permute-start | bytes 1769480 | tf_op jit(solution)/shard_map/ppermute | solution.py:17
  203.9 58.5 %collective-permute-start.26 = (bf16[256,1152]{1,0:T(8,128)(2,1)}, bf16[256,1152]{1,0:T(8,128)(2,1)}, u32[]{:S(2)}, u32[]{:S(2)}) collective-permute-start(bf16[256,1152]{1,0:T(8,128)(2,1)} %fusion.10.refs_1_), channel_id=1, source_target_pairs={{0,2},{1,3},{2,0},{3,1},{4,6},{5,7},{6,4},{7,5},{8,10},{9,11},{10,... | collective-permute-start | bytes 1769480 | tf_op jit(solution)/shard_map/ppermute | solution.py:17
  205.1 59.0 %collective-permute-start.25 = (bf16[256,1152]{1,0:T(8,128)(2,1)}, bf16[256,1152]{1,0:T(8,128)(2,1)}, u32[]{:S(2)}, u32[]{:S(2)}) collective-permute-start(bf16[256,1152]{1,0:T(8,128)(2,1)} %fusion.9.refs_1_), channel_id=1, source_target_pairs={{0,1},{1,0},{2,3},{3,2},{4,5},{5,4},{6,7},{7,6},{8,9},{9,8},{10,11... | collective-permute-start | bytes 1769480 | tf_op jit(solution)/shard_map/ppermute | solution.py:17
  212.0 45.7 %collective-permute-start.24 = (bf16[432,1152]{1,0:T(8,128)(2,1)}, bf16[432,1152]{1,0:T(8,128)(2,1)}, u32[]{:S(2)}, u32[]{:S(2)}) collective-permute-start(bf16[432,1152]{1,0:T(8,128)(2,1)} %get-tuple-element.66.refs_0_), channel_id=1, source_target_pairs={{0,8},{4,12},{24,16},{28,20},{1,9},{5,13},{25,17},{29,21},{2,10},{... | collective-permute-start | bytes 2985992 | tf_op jit(solution)/shard_map/ppermute | solution.py:226
  226.3 41.0 %collective-permute-start.27 = (bf16[256,1152]{1,0:T(8,128)(2,1)}, bf16[256,1152]{1,0:T(8,128)(2,1)}, u32[]{:S(2)}, u32[]{:S(2)}) collective-permute-start(bf16[256,1152]{1,0:T(8,128)(2,1)} %fusion.11), channel_id=1, source_target_pairs={{0,3},{1,2},{2,1},{3,0},{4,7},{5,6},{6,5},{7,4},{8,11},{9,10},{10,... | collective-permute-start | bytes 1769480 | tf_op jit(solution)/shard_map/ppermute | solution.py:17
  237.6 42.3 %collective-permute-start.30 = (bf16[2,432,1152]{2,1,0:T(8,128)(2,1)}, bf16[2,432,1152]{2,1,0:T(8,128)(2,1)}, u32[]{:S(2)}, u32[]{:S(2)}) collective-permute-start(bf16[2,432,1152]{2,1,0:T(8,128)(2,1)} %get-tuple-element.72), channel_id=1, source_target_pairs={{0,4},{4,0},{8,12},{12,8},{16,20},{20,16},{24,28},{28,24},{1,5},{5... | collective-permute-start | bytes 5971976 | tf_op jit(solution)/shard_map/ppermute | solution.py:17
  257.7 94.6 %collective-permute-start.35 = (bf16[2,432,1152]{2,1,0:T(8,128)(2,1)}, bf16[2,432,1152]{2,1,0:T(8,128)(2,1)}, u32[]{:S(2)}, u32[]{:S(2)}) collective-permute-start(bf16[2,432,1152]{2,1,0:T(8,128)(2,1)} %get-tuple-element.84), channel_id=1, source_target_pairs={{0,4},{4,0},{8,12},{12,8},{16,20},{20,16},{24,28},{28,24},{1,5},{5... | collective-permute-start | bytes 5971976 | tf_op jit(solution)/shard_map/ppermute | solution.py:17
  264.0 23.7 %collective-permute-start.29 = (bf16[432,1152]{1,0:T(8,128)(2,1)}, bf16[432,1152]{1,0:T(8,128)(2,1)}, u32[]{:S(2)}, u32[]{:S(2)}) collective-permute-start(bf16[432,1152]{1,0:T(8,128)(2,1)} %get-tuple-element.70.refs_2_), channel_id=1, source_target_pairs={{0,8},{4,12},{24,16},{28,20},{1,9},{5,13},{25,17},{29,21},{2,10},{... | collective-permute-start | bytes 2985992 | tf_op jit(solution)/shard_map/ppermute | solution.py:226
  296.1 23.9 %collective-permute-start.31 = (bf16[432,1152]{1,0:T(8,128)(2,1)}, bf16[432,1152]{1,0:T(8,128)(2,1)}, u32[]{:S(2)}, u32[]{:S(2)}) collective-permute-start(bf16[432,1152]{1,0:T(8,128)(2,1)} %get-tuple-element.74), channel_id=1, source_target_pairs={{0,8},{4,12},{24,16},{28,20},{8,0},{12,4},{16,24},{20,28},{1,9},{5... | collective-permute-start | bytes 2985992 | tf_op jit(solution)/shard_map/ppermute | solution.py:226
  332.6 24.5 %collective-permute-start.33 = (bf16[432,1152]{1,0:T(8,128)(2,1)}, bf16[432,1152]{1,0:T(8,128)(2,1)}, u32[]{:S(2)}, u32[]{:S(2)}) collective-permute-start(bf16[432,1152]{1,0:T(8,128)(2,1)} %get-tuple-element.80), channel_id=1, source_target_pairs={{0,8},{4,12},{24,16},{28,20},{8,0},{12,4},{16,24},{20,28},{1,9},{5... | collective-permute-start | bytes 2985992 | tf_op jit(solution)/shard_map/ppermute | solution.py:226
  350.2 28.3 %collective-permute-start.42 = (bf16[4,144,1024]{2,1,0:T(8,128)(2,1)}, bf16[4,144,1024]{2,1,0:T(8,128)(2,1)}, u32[]{:S(2)}, u32[]{:S(2)}) collective-permute-start(bf16[4,144,1024]{2,1,0:T(8,128)(2,1)} %constant_dynamic-slice_fusion.5), channel_id=1, source_target_pairs={{0,4},{4,0},{8,12},{12,8},{16,20},{20,16},{24,28},{28,24},{1,5},{5... | collective-permute-start | bytes 3538952 | tf_op jit(solution)/shard_map/ppermute | solution.py:17
  387.4 26.5 %collective-permute-start.38 = (bf16[432,1152]{1,0:T(8,128)(2,1)}, bf16[432,1152]{1,0:T(8,128)(2,1)S(1)}, u32[]{:S(2)}, u32[]{:S(2)}) collective-permute-start(bf16[432,1152]{1,0:T(8,128)(2,1)} %get-tuple-element.87), channel_id=1, source_target_pairs={{0,8},{4,12},{24,16},{28,20},{8,0},{12,4},{16,24},{20,28},{1,9},{5... | collective-permute-start | bytes 2985992 | tf_op jit(solution)/shard_map/ppermute | solution.py:226
  392.3 29.5 %collective-permute-start.50 = (bf16[432,1152]{1,0:T(8,128)(2,1)}, bf16[432,1152]{1,0:T(8,128)(2,1)}, u32[]{:S(2)}, u32[]{:S(2)}) collective-permute-start(bf16[432,1152]{1,0:T(8,128)(2,1)} %get-tuple-element.94.refs_0_), channel_id=1, source_target_pairs={{0,4},{4,0},{8,12},{12,8},{16,20},{20,16},{24,28},{28,24},{1,5},{5... | collective-permute-start | bytes 2985992 | tf_op jit(solution)/shard_map/ppermute | solution.py:17
  395.5 28.9 %collective-permute-start.51 = (bf16[432,1152]{1,0:T(8,128)(2,1)}, bf16[432,1152]{1,0:T(8,128)(2,1)}, u32[]{:S(2)}, u32[]{:S(2)}) collective-permute-start(bf16[432,1152]{1,0:T(8,128)(2,1)} %get-tuple-element.95.refs_1_), channel_id=1, source_target_pairs={{0,4},{4,0},{8,12},{12,8},{16,20},{20,16},{24,28},{28,24},{1,5},{5... | collective-permute-start | bytes 2985992 | tf_op jit(solution)/shard_map/ppermute | solution.py:17
  406.1 27.0 %collective-permute-start.47 = (bf16[160,1536]{1,0:T(8,128)(2,1)S(1)}, bf16[160,1536]{1,0:T(8,128)(2,1)S(1)}, u32[]{:S(2)}, u32[]{:S(2)}) collective-permute-start(bf16[160,1536]{1,0:T(8,128)(2,1)S(1)} %get-tuple-element.162), channel_id=1, source_target_pairs={{0,1},{1,0},{2,3},{3,2},{4,5},{5,4},{6,7},{7,6},{8,9},{9,8},{10,11... | collective-permute-start | bytes 1474568 | tf_op jit(solution)/shard_map/ppermute | solution.py:17
  413.9 23.4 %collective-permute-start.48 = (bf16[160,1536]{1,0:T(8,128)(2,1)}, bf16[160,1536]{1,0:T(8,128)(2,1)}, u32[]{:S(2)}, u32[]{:S(2)}) collective-permute-start(bf16[160,1536]{1,0:T(8,128)(2,1)} %get-tuple-element.164), channel_id=1, source_target_pairs={{0,2},{1,3},{2,0},{3,1},{4,6},{5,7},{6,4},{7,5},{8,10},{9,11},{10,... | collective-permute-start | bytes 1474568 | tf_op jit(solution)/shard_map/ppermute | solution.py:17
  414.2 23.1 %collective-permute-start.49 = (bf16[160,1536]{1,0:T(8,128)(2,1)S(1)}, bf16[160,1536]{1,0:T(8,128)(2,1)}, u32[]{:S(2)}, u32[]{:S(2)}) collective-permute-start(bf16[160,1536]{1,0:T(8,128)(2,1)S(1)} %get-tuple-element.163), channel_id=1, source_target_pairs={{0,3},{1,2},{2,1},{3,0},{4,7},{5,6},{6,5},{7,4},{8,11},{9,10},{10,... | collective-permute-start | bytes 1474568 | tf_op jit(solution)/shard_map/ppermute | solution.py:17
  421.8 24.1 %collective-permute-start.40 = (bf16[432,1152]{1,0:T(8,128)(2,1)}, bf16[432,1152]{1,0:T(8,128)(2,1)S(1)}, u32[]{:S(2)}, u32[]{:S(2)}) collective-permute-start(bf16[432,1152]{1,0:T(8,128)(2,1)} %get-tuple-element.91), channel_id=1, source_target_pairs={{0,8},{4,12},{24,16},{28,20},{8,0},{12,4},{16,24},{20,28},{1,9},{5... | collective-permute-start | bytes 2985992 | tf_op jit(solution)/shard_map/ppermute | solution.py:226
  433.8 28.4 %collective-permute-start.56 = (bf16[432,1152]{1,0:T(8,128)(2,1)S(1)}, bf16[432,1152]{1,0:T(8,128)(2,1)S(1)}, u32[]{:S(2)}, u32[]{:S(2)}) collective-permute-start(bf16[432,1152]{1,0:T(8,128)(2,1)S(1)} %copy-done.40), channel_id=1, source_target_pairs={{0,4},{4,0},{8,12},{12,8},{16,20},{20,16},{24,28},{28,24},{1,5},{5... | collective-permute-start | bytes 2985992 | tf_op jit(solution)/shard_map/ppermute | solution.py:17
  452.0 27.7 %collective-permute-start.52 = (bf16[432,1152]{1,0:T(8,128)(2,1)}, bf16[432,1152]{1,0:T(8,128)(2,1)S(1)}, u32[]{:S(2)}, u32[]{:S(2)}) collective-permute-start(bf16[432,1152]{1,0:T(8,128)(2,1)} %get-tuple-element.96.refs_0_), channel_id=1, source_target_pairs={{8,0},{12,4},{16,24},{20,28},{9,1},{13,5},{17,25},{21,29},{10,2},{... | collective-permute-start | bytes 2985992 | tf_op jit(solution)/shard_map/ppermute | solution.py:226
  453.3 26.5 %collective-permute-start.53 = (bf16[432,1152]{1,0:T(8,128)(2,1)}, bf16[432,1152]{1,0:T(8,128)(2,1)S(1)}, u32[]{:S(2)}, u32[]{:S(2)}) collective-permute-start(bf16[432,1152]{1,0:T(8,128)(2,1)} %get-tuple-element.97.refs_2_), channel_id=1, source_target_pairs={{8,16},{12,20},{16,8},{20,12},{9,17},{13,21},{17,9},{21,13},{10,18... | collective-permute-start | bytes 2985992 | tf_op jit(solution)/shard_map/ppermute | solution.py:226
  454.0 25.7 %collective-permute-start.55 = (bf16[160,1536]{1,0:T(8,128)(2,1)}, bf16[160,1536]{1,0:T(8,128)(2,1)S(1)}, u32[]{:S(2)}, u32[]{:S(2)}) collective-permute-start(bf16[160,1536]{1,0:T(8,128)(2,1)} %get-tuple-element.99.refs_6_), channel_id=1, source_target_pairs={{0,8},{4,12},{24,16},{28,20},{1,9},{5,13},{25,17},{29,21},{2,10},{... | collective-permute-start | bytes 1474568 | tf_op jit(solution)/shard_map/ppermute | solution.py:226
  486.4 25.7 %collective-permute-start.58 = (bf16[432,1152]{1,0:T(8,128)(2,1)}, bf16[432,1152]{1,0:T(8,128)(2,1)S(1)}, u32[]{:S(2)}, u32[]{:S(2)}) collective-permute-start(bf16[432,1152]{1,0:T(8,128)(2,1)} %get-tuple-element.102.refs_0_), channel_id=1, source_target_pairs={{8,0},{12,4},{16,24},{20,28},{9,1},{13,5},{17,25},{21,29},{10,2},{... | collective-permute-start | bytes 2985992 | tf_op jit(solution)/shard_map/ppermute | solution.py:226
  (171 other events, 1196.2 us)

commit v5 on v4

--- a/solution.py
+++ b/solution.py
@@ -215,6 +215,140 @@
     )(core, *lefts, *rights)
 
 
+def allowed_mask(query_segs_ref, key_segs_ref, rows, width):
+    gap = (
+        width
+        - rows
+        + lax.broadcasted_iota(jnp.int32, (rows, width), 0)
+        - lax.broadcasted_iota(jnp.int32, (rows, width), 1)
+    )
+    return (gap >= 0) & (gap < WINDOW) & (query_segs_ref[...] == key_segs_ref[...])
+
+
+def head_probs(query, keys, allowed, scale):
+    scores = jnp.where(allowed, dot(query, keys, 1, 1) * scale, NEG)
+    expo = jnp.exp(scores - jnp.max(scores, axis=-1, keepdims=True))
+    return expo / jnp.sum(expo, axis=-1, keepdims=True)
+
+
+def attention_specs(rows, size, width, heads):
+    head = pl.BlockSpec((rows, size), lambda h: (0, h))
+    whole = lambda *shape: pl.BlockSpec(shape, lambda h: (0, 0))
+    common = [
+        head,
+        whole(1, size),
+        whole(rows, size // 2),
+        whole(rows, size // 2),
+        whole(width, 2 * size),
+        whole(rows, 1),
+        whole(1, width),
+    ]
+    return head, whole, common
+
+
+def attention_forward(qkv, gain, cosine, sine, pairs, query_segs, key_segs, heads):
+    rows, width, size = qkv.shape[0], pairs.shape[0], pairs.shape[1] // 2
+    head, _, common = attention_specs(rows, size, width, heads)
+
+    def kernel(raw_ref, gain_ref, cos_ref, sin_ref, pairs_ref, qseg_ref, kseg_ref, query_ref, mixed_ref):
+        query = head_post(raw_ref[...], gain_ref[...], cos_ref[...], sin_ref[...]).astype(jnp.bfloat16)
+        query_ref[...] = query
+        allowed = allowed_mask(qseg_ref, kseg_ref, rows, width)
+        probs = head_probs(query, pairs_ref[:, :size], allowed, size**-0.5).astype(jnp.bfloat16)
+        mixed_ref[...] = dot(probs, pairs_ref[:, size:], 1, 0).astype(jnp.bfloat16)
+
+    shape = jax.ShapeDtypeStruct((rows, heads * size), jnp.bfloat16)
+    return pl.pallas_call(
+        kernel,
+        grid=(heads,),
+        in_specs=common,
+        out_specs=[head, head],
+        out_shape=[shape, shape],
+        compiler_params=params(),
+        name="attention_forward",
+    )(qkv, gain, cosine, sine, pairs, query_segs, key_segs)
+
+
+def attention_backward(qkv, gain, cosine, sine, pairs, query_segs, key_segs, query, grad_mixed, heads):
+    rows, width, size = qkv.shape[0], pairs.shape[0], pairs.shape[1] // 2
+    head, whole, common = attention_specs(rows, size, width, heads)
+    before = width - rows
+
+    def kernel(
+        raw_ref, gain_ref, cos_ref, sin_ref, pairs_ref, qseg_ref, kseg_ref, query_ref, grad_ref,
+        raw_grad_ref, gain_grad_ref, far_ref, own_ref, acc,
+    ):
+        step = pl.program_id(0)
+        query = query_ref[...]
+        grad = grad_ref[...]
+        allowed = allowed_mask(qseg_ref, kseg_ref, rows, width)
+        keys = pairs_ref[:, :size]
+        probs = head_probs(query, keys, allowed, size**-0.5)
+        grad_probs = dot(grad, pairs_ref[:, size:], 1, 1)
+        delta = jnp.sum(grad_probs * probs, axis=-1, keepdims=True)
+        grad_scores = (probs * (grad_probs - delta)).astype(jnp.bfloat16)
+        grad_query = dot(grad_scores, keys, 1, 0) * size**-0.5
+        grad_keys = dot(grad_scores, query, 0, 0) * size**-0.5
+        grad_values = dot(probs.astype(jnp.bfloat16), grad, 0, 0)
+
+        @pl.when(step == 0)
+        def _():
+            acc[:, :size] = grad_keys
+            acc[:, size:] = grad_values
+
+        @pl.when(step > 0)
+        def _():
+            acc[:, :size] += grad_keys
+            acc[:, size:] += grad_values
+
+        first = grad_query[:, : size // 2]
+        second = grad_query[:, size // 2 :]
+        cosine_part, sine_part = cos_ref[...], sin_ref[...]
+        turned = jnp.concatenate(
+            [
+                first * cosine_part + second * sine_part,
+                second * cosine_part - first * sine_part,
+            ],
+            axis=-1,
+        )
+        raw = raw_ref[...]
+        scale = lax.rsqrt(jnp.mean(raw * raw, axis=-1, keepdims=True) + EPS)
+        unit = raw * scale
+        inner = turned * gain_ref[...].astype(jnp.float32)
+        raw_grad = scale * (inner - unit * jnp.mean(inner * unit, axis=-1, keepdims=True))
+        raw_grad_ref[...] = raw_grad.astype(jnp.bfloat16)
+        gain_grad = jnp.sum(turned * unit, axis=0, keepdims=True)
+
+        @pl.when(step == 0)
+        def _():
+            gain_grad_ref[...] = gain_grad
+
+        @pl.when(step > 0)
+        def _():
+            gain_grad_ref[...] += gain_grad
+
+        @pl.when(step == heads - 1)
+        def _():
+            far_ref[...] = acc[:before, :].astype(jnp.bfloat16)
+            own_ref[...] = acc[before:, :]
+
+    return pl.pallas_call(
+        kernel,
+        grid=(heads,),
+        in_specs=common + [head, head],
+        out_specs=[head, whole(1, size), whole(before, 2 * size), whole(rows, 2 * size)],
+        out_shape=[
+            jax.ShapeDtypeStruct((rows, heads * size), jnp.bfloat16),
+            jax.ShapeDtypeStruct((1, size), jnp.float32),
+            jax.ShapeDtypeStruct((before, 2 * size), jnp.bfloat16),
+            jax.ShapeDtypeStruct((rows, 2 * size), jnp.float32),
+        ],
+        scratch_shapes=[pltpu.VMEM((width, 2 * size), jnp.float32)],
+        compiler_params=params(),
+        name="attention_backward",
+    )(qkv, gain, cosine, sine, pairs, query_segs, key_segs, query, grad_mixed)
+
+
 def line_edges():
     places = lax.axis_size("replica") // 2
     outer = places // 2 - 1
@@ -250,6 +384,8 @@
             plan.append((name, step + 1, [operand(block), operand(far)], step))
         for name, terms in fresh:
             plan.append((name, 0, [operand(term) for term in terms], None))
+        if not plan:
+            return gate
         sizes = [operands[spots[0]][0].shape[-2:] for _, _, spots, _ in plan]
         by_step = {step: index for index, (_, step, _, _) in enumerate(plan)}
         pairs = []
@@ -343,9 +479,9 @@
     return [(name, chunk) for chunk in range(chunks_of(units))]
 
 
-def whole_grad(line, name, units, dtype=jnp.float32):
+def whole_grad(lines, name, units, dtype=jnp.float32):
     names = line_names(name, units)
-    mines = [line.finished(chunk) for chunk in names]
+    mines = [lines[chunk[1]].finished(chunk) for chunk in names]
     others = [swapped(mine, "replica", 1) for mine in mines]
     chunks = len(mines)
     tile, model = mines[0].shape
@@ -510,45 +646,29 @@
     residual_in = hidden_in.astype(jnp.float32)
     normed_in = normed(residual_in, gain_in).astype(jnp.bfloat16)
     qkv = jnp.dot(normed_in, w_qkv, preferred_element_type=jnp.float32)
-    query_raw = qkv[:, : heads * head_size].reshape(rows, heads, head_size)
     key_raw = qkv[:, heads * head_size : (heads + 1) * head_size]
     value_new = qkv[:, (heads + 1) * head_size :].astype(jnp.bfloat16)
     cosine, sine = tables(positions, head_size // 2)
-    cosine_heads = cosine[:, None, :]
-    sine_heads = sine[:, None, :]
-    query_new = head_post(query_raw, gain_query, cosine_heads, sine_heads).astype(jnp.bfloat16)
     key_new = head_post(key_raw, gain_key, cosine, sine).astype(jnp.bfloat16)
     pair_new = jnp.concatenate([key_new, value_new], axis=1)
     parts = [pair_new]
     for step in range(1, hops + 1):
         parts.insert(0, passed_along(pair_new, "fsdp", step))
     pairs = jnp.concatenate(parts, axis=0)
-    keys = pairs[:, :head_size]
-    values = pairs[:, head_size:]
-    width = keys.shape[0]
+    width = pairs.shape[0]
     seg_padded = jnp.concatenate([jnp.full((hops * rows,), -1, jnp.int32), segments], axis=0)
     key_segs = lax.dynamic_slice_in_dim(seg_padded, rank * rows, width, 0)
     query_segs = lax.dynamic_slice_in_dim(segments, rank * rows, rows, 0)
-    gap = hops * rows + jnp.arange(rows)[:, None] - jnp.arange(width)[None, :]
-    allowed = (gap >= 0) & (gap < WINDOW) & (query_segs[:, None] == key_segs[None, :])
-    query_rows = query_new.reshape(rows * heads, head_size)
-
-    def scores_of():
-        raw_scores = (contract(query_rows, keys, 1, 1) * scale).reshape(rows, heads, width)
-        return jnp.where(allowed[:, None, :], raw_scores, NEG)
-
-    scores = scores_of()
-    highest = jnp.max(scores, axis=-1, keepdims=True)
-    expo = jnp.exp(scores - highest)
-    weight_sum = jnp.sum(expo, axis=-1, keepdims=True)
-    probs = expo / weight_sum
-    log_total = highest + jnp.log(weight_sum)
-    probs_low = probs.astype(jnp.bfloat16).reshape(rows * heads, width)
-    mixed = (
-        jnp.dot(probs_low, values, preferred_element_type=jnp.float32)
-        .reshape(rows, heads * head_size)
-        .astype(jnp.bfloat16)
-    )
+    attention_args = (
+        qkv,
+        gain_query[None, :],
+        cosine,
+        sine,
+        pairs,
+        query_segs[:, None],
+        key_segs[None, :],
+    )
+    query_new, mixed = attention_forward(*attention_args, heads)
     w_out = unpacked([out_weight], got, peers)
     attended = contract(mixed, w_out, 1, 1)
     resid = residual_in + normed(attended, gain_attn)
@@ -570,69 +690,62 @@
     grad_branch_low = grad_branch.astype(jnp.bfloat16)
     pieces = [grad_branch_low] + [swapped(grad_branch_low, "fsdp", mask) for mask in masks]
     units = gate_weight.shape[0]
-    line = Line()
+    lines = [Line(), Line()]
 
     def fresh(name, other, mine):
         far = swapped(other, "replica", 1)
         return [(key, [(mine, key[1]), (far, key[1])]) for key in line_names(name, units)]
 
     grad_gates, grad_uppers, returned = {}, {}, {}
-    last = group - 1
+    early = group // 2
     for mask in range(group):
-        if mask == last:
+        if mask == early:
+            pieces[mask] = after(pieces[mask], part)
             waiting = fresh("down", *weight_grad(hiddens, pieces))
-            pieces[mask] = line.advance([waiting.pop(0)], pieces[mask])
+            pieces[mask] = lines[0].advance([waiting.pop(0)], pieces[mask])
+        if mask == early + 1 and waiting:
+            pieces[mask] = lines[1].advance([waiting.pop(0)], pieces[mask])
         grad_gates[mask], grad_uppers[mask], part = ffn_backward(
             pieces[mask], gate_weight, up_weight, down_weight, slopes[mask], acts[mask]
         )
-        if mask < last:
+        if mask + 1 < early:
             pieces[mask + 1] = after(pieces[mask + 1], part)
         returned[mask] = swapped(part, "fsdp", mask) if mask else part
+    waiting = []
     waiting += fresh("gate", *weight_grad([grad_gates[i] for i in range(group)], ffn_blocks))
     waiting += fresh("up", *weight_grad([grad_uppers[i] for i in range(group)], ffn_blocks))
-    returned[0] = line.advance([waiting.pop(0)], returned[0])
+
+    def advance(spot, gate=None):
+        ready = [entry for entry in waiting if entry[0][1] == spot][:1]
+        for entry in ready:
+            waiting.remove(entry)
+        return lines[spot].advance(ready, gate)
+
+    returned[0] = advance(0, returned[0])
     grad_ffn_in = sum(returned[i].astype(jnp.float32) for i in range(group))
     grad_resid_part, grad_gain_ffn = norm_back(resid, gain_ffn, grad_ffn_in)
     grad_resid = grad_result + grad_resid_part
     grad_attended, grad_gain_attn = norm_back(attended, gain_attn, grad_resid)
-    grad_attended_low = grad_attended.astype(jnp.bfloat16)
-    grad_attended_low = line.advance([waiting.pop(0)] if waiting else [], grad_attended_low)
+    grad_attended_low = advance(1, grad_attended.astype(jnp.bfloat16))
     grad_wout = contract(grad_attended_low, mixed, 0, 0).astype(jnp.bfloat16)
-    out_part = owner_part(grad_wout.reshape(group, own_model, -1))
     grad_mixed = jnp.dot(grad_attended_low, w_out, preferred_element_type=jnp.float32).astype(
         jnp.bfloat16
     )
-    grad_mixed_rows = grad_mixed.reshape(rows * heads, head_size)
-    scores = scores_of()
-    probs = jnp.exp(scores - log_total)
-    probs_low = probs.astype(jnp.bfloat16).reshape(rows * heads, width)
-    grad_probs = contract(grad_mixed_rows, values, 1, 1).reshape(rows, heads, width)
-    delta = jnp.sum(grad_probs * probs, axis=-1, keepdims=True)
-    grad_scores = (probs * (grad_probs - delta)).astype(jnp.bfloat16).reshape(rows * heads, width)
-    grad_scores = line.advance([waiting.pop(0)] if waiting else [], grad_scores)
-    grad_query = (jnp.dot(grad_scores, keys, preferred_element_type=jnp.float32) * scale).reshape(
-        rows, heads, head_size
-    )
-    grad_keys = contract(grad_scores, query_rows, 0, 0) * scale
-    grad_values = contract(probs_low, grad_mixed_rows, 0, 0)
-    grad_pairs = jnp.concatenate([grad_keys, grad_values], axis=1)
-    grad_pair = grad_pairs[hops * rows :]
+    grad_query_low, grad_gain_query, grad_far, grad_pair = attention_backward(
+        *attention_args, query_new, grad_mixed, heads
+    )
+    grad_gain_query = grad_gain_query[0]
+    grad_far = advance(0, grad_far)
     for step in range(1, hops + 1):
         lower = (hops - step) * rows
-        back = passed_along(grad_pairs[lower : lower + rows].astype(jnp.bfloat16), "fsdp", -step)
+        back = passed_along(grad_far[lower : lower + rows], "fsdp", -step)
         grad_pair = grad_pair + back.astype(jnp.float32)
-    grad_pair = line.advance([waiting.pop(0)] if waiting else [], grad_pair)
+    grad_pair = advance(1, grad_pair)
     grad_key = grad_pair[:, :head_size]
-    grad_value = grad_pair[:, head_size:]
-    _, pull_query = jax.vjp(
-        lambda raw, gain: head_post(raw, gain, cosine_heads, sine_heads), query_raw, gain_query
-    )
-    grad_query_raw, grad_gain_query = pull_query(grad_query)
+    grad_value_low = grad_pair[:, head_size:].astype(jnp.bfloat16)
     _, pull_key = jax.vjp(lambda raw, gain: head_post(raw, gain, cosine, sine), key_raw, gain_key)
     grad_key_raw, grad_gain_key = pull_key(grad_key)
-    grad_query_low = grad_query_raw.reshape(rows, heads * head_size).astype(jnp.bfloat16)
     grad_key_low = grad_key_raw.astype(jnp.bfloat16)
-    grad_value_low = grad_value.astype(jnp.bfloat16)
     grad_qkv = jnp.concatenate([grad_query_low, grad_key_low, grad_value_low], axis=1)
     grad_wqkv = contract(normed_in, grad_qkv, 0, 0).astype(jnp.bfloat16)
     grad_normed_in = contract(grad_qkv, w_qkv, 1, 1)
@@ -653,21 +766,23 @@
         axis=1,
     )
     gain_grads = jnp.pad(gain_grads[:, None, :], ((0, 0), (0, 31), (0, wide - sum(sizes))))
-    qkv_part = owner_part(
-        jnp.concatenate([grad_wqkv.reshape(group, own_model, wide), gain_grads], axis=1)
-    )
-    while waiting:
-        line.advance([waiting.pop(0)])
-    grad_down = whole_grad(line, "down", units)
-    grad_down = line.advance([("out", [out_part]), ("qkv", [qkv_part])], grad_down)
-    grad_gate_w = whole_grad(line, "gate", units)
-    grad_gate_w = line.advance([], grad_gate_w)
-    grad_up_w = whole_grad(line, "up", units)
-    owned = core_join(line.finished("qkv"), 0).astype(jnp.float32)
-    owned_out = core_join(line.finished("out"), 0).astype(jnp.float32)
+    grad_weights = jnp.concatenate([grad_wqkv, grad_wout], axis=1).reshape(group, own_model, -1)
+    gain_grads = jnp.pad(gain_grads, ((0, 0), (0, 0), (0, grad_wout.shape[1])))
+    weights_part = owner_part(jnp.concatenate([grad_weights, gain_grads], axis=1))
+    advance(0)
+    advance(1)
+    lines[0].advance([("weights", [weights_part])])
+    lines[1].advance([])
+    grad_down = whole_grad(lines, "down", units)
+    grad_down = lines[0].advance([], grad_down)
+    grad_gate_w = whole_grad(lines, "gate", units)
+    grad_gate_w = lines[1].advance([], grad_gate_w)
+    grad_up_w = whole_grad(lines, "up", units)
+    owned = core_join(lines[0].finished("weights"), 0).astype(jnp.float32)
+    owned_out = owned[:own_model, wide:]
     owned_query = owned[:own_model, : heads * head_size]
     owned_key = owned[:own_model, heads * head_size : (heads + 1) * head_size]
-    owned_value = owned[:own_model, (heads + 1) * head_size :]
+    owned_value = owned[:own_model, (heads + 1) * head_size : wide]
     owned_gain_in, owned_gain_attn, owned_gain_ffn, owned_gain_out, owned_gain_query, owned_gain_key = (
         owned[own_model, spots[i] : spots[i + 1]] for i in range(6)
     )

time: 565 us -> 550 us (0.973)
  other arithmetic: 55 us -> 30.1 us
  Pallas kernels: 105 us -> 129 us
  local copies, waits for them, and re-layouts: 67 us -> 44 us
  waiting for transfers between devices: 152 us -> 173 us
  matrix products: 83.2 us -> 76.6 us
    ppermute x20 -> x19, waiting for transfers between devices: 79.3 us -> 99.1 us  [exchanged(): return lax.ppermute(block, 'replica', route)]
    pallas_call x0 -> x2, Pallas kernels: none -> 15 us  [the longest x1 9.1 us: attention_backward(): pl.pallas_call(kernel, grid=(heads,), in_specs=common + [head, head], out...]
    reshape x5 -> x0, local copies, waits for them, and re-layouts: 10.3 us -> none  [the longest x1 4.84 us: scores_of(): (contract(query_rows, keys, 1, 1) * scale).reshape(rows, heads, width)]
    pallas_call x10 -> x14, Pallas kernels: 46.7 us -> 56.3 us  [advance(): pl.pallas_call(kernel, grid_spec=pltpu.PrefetchScalarGridSpec(num_scalar_...]
    sub x1 -> x0, other arithmetic: 6.64 us -> none  [per_device(): grad_probs - delta]
    dot_general x32 -> x28, matrix products: 76.3 us -> 70.6 us  [contract(): lax.dot_general(left, right, (((left_dim,), (right_dim,)), ((), ())), pre...]
    unnamed x273 -> x222, local copies, waits for them, and re-layouts: 23.2 us -> 17.6 us
    ppermute x43 -> x38, starting transfers between devices: 35.1 us -> 30.9 us  [swapped(): return lax.ppermute(block, axis, route)]
  transfers between devices with their start and end apart: 67 -> 61, of which waited for: 22 -> 23; matrix products, arithmetic and copies ran while one was open for 30% -> 18% of each run, Pallas kernels for 12% -> 19%
where the time goes in v5:
time: 550 us; the launch traced here: 542 us
  waiting for transfers between devices  173 us (31%)
  Pallas kernels  129 us (23%)
  starting transfers between devices  86.4 us (16%)
  matrix products  76.6 us (14%)
  local copies, waits for them, and re-layouts  44 us (8%)
  other arithmetic  30.1 us (5%)
    ppermute x19, waiting for transfers between devices, exchanged(): return lax.ppermute(block, 'replica', route)  99.1 us
    dot_general x28, matrix products, contract(): lax.dot_general(left, right, (((left_dim,), (right_dim,)), ((), ())), pre...  70.6 us
    ppermute x38, waiting for transfers between devices, swapped(): return lax.ppermute(block, axis, route)  61.8 us
    pallas_call x14, Pallas kernels, advance(): pl.pallas_call(kernel, grid_spec=pltpu.PrefetchScalarGridSpec(num_scalar_...  56.3 us
    ppermute x19, starting transfers between devices, exchanged(): return lax.ppermute(block, 'replica', route)  47 us
    ppermute x38, starting transfers between devices, swapped(): return lax.ppermute(block, axis, route)  30.9 us
    pallas_call x3, Pallas kernels, weight_grad(): pl.pallas_call(kernel, grid_spec=pltpu.PrefetchScalarGridSpec(num_scalar_...  29 us
    unnamed x222, local copies, waits for them, and re-layouts  17.6 us
  transfers between devices with their start and end apart: 61, of which 23 were waited for; matrix products, arithmetic and copies ran while one was open for 18% of the time, Pallas kernels for 19%

profile of v5, /device:TPU:0, one launch (start us, length us, event | category | flops | bytes accessed | tf_op | source)
XLA Modules:
  0.0 542.1 jit_solution(18297088359875064432)
XLA Ops:
  12.2 21.4 %collective-permute-done.refs_3_ = bf16[160,1536]{1,0:T(8,128)(2,1)S(1)} collective-permute-done((bf16[160,1536]{1,0:T(8,128)(2,1)}, bf16[160,1536]{1,0:T(8,128)(2,1)S(1)}, u32[]{:S(2)}, u32[]{:S(2)}) %collective-permute-start) | collective-permute-done | bytes 491552 | tf_op jit(solution)/shard_map/ppermute | solution.py:17
  57.0 6.1 %collective-permute-done.9.refs_2_ = bf16[144,1024]{1,0:T(8,128)(2,1)S(1)} collective-permute-done((bf16[144,1024]{1,0:T(8,128)(2,1)}, bf16[144,1024]{1,0:T(8,128)(2,1)S(1)}, u32[]{:S(2)}, u32[]{:S(2)}) %collective-permute-start.9) | collective-permute-done | bytes 294944 | tf_op jit(solution)/shard_map/ppermute | solution.py:17
  66.6 5.8 %collective-permute-done.6 = bf16[256,512]{1,0:T(8,128)(2,1)S(1)} collective-permute-done((bf16[256,512]{1,0:T(8,128)(2,1)S(1)}, bf16[256,512]{1,0:T(8,128)(2,1)S(1)}, u32[]{:S(2)}, u32[]{:S(2)}) %collective-permute-start.6) | collective-permute-done | bytes 262176 | tf_op jit(solution)/shard_map/ppermute | solution.py:563
  73.3 5.9 %attention_forward.1 = (bf16[256,1024]{1,0:T(8,128)(2,1)}, bf16[256,1024]{1,0:T(8,128)(2,1)}) custom-call(f32[256,1536]{1,0:T(8,128)} %copy-done.4, bf16[1,256]{1,0:T(2,128)(2,1)} %broadcast_in_dim.21.gain_ref, f32[256,128]{1,0:T(8,128)} %get-tuple-element.180.cos_ref, f32[256,128]{1,0:T(8,128)} %get-tuple-element.179.sin_ref, ...), custom_call_target="tpu_custom_call" | custom-call | tf_op jit(solution)/shard_map/attention_forward/pallas_call | solution.py:261
  97.1 9.1 %collective-permute-done.18.refs_7_ = bf16[256,1152]{1,0:T(8,128)(2,1)S(1)} collective-permute-done((bf16[256,1152]{1,0:T(8,128)(2,1)S(1)}, bf16[256,1152]{1,0:T(8,128)(2,1)S(1)}, u32[]{:S(2)}, u32[]{:S(2)}) %collective-permute-start.18) | collective-permute-done | bytes 589856 | tf_op jit(solution)/shard_map/ppermute | solution.py:17
  135.7 7.4 %collective-permute-done.17 = bf16[256,1152]{1,0:T(8,128)(2,1)S(1)} collective-permute-done((bf16[256,1152]{1,0:T(8,128)(2,1)S(1)}, bf16[256,1152]{1,0:T(8,128)(2,1)S(1)}, u32[]{:S(2)}, u32[]{:S(2)}) %collective-permute-start.17) | collective-permute-done | bytes 589856 | tf_op jit(solution)/shard_map/ppermute | solution.py:17
  162.4 6.1 %collective-permute-done.20.refs_0_ = bf16[256,1152]{1,0:T(8,128)(2,1)} collective-permute-done((bf16[256,1152]{1,0:T(8,128)(2,1)}, bf16[256,1152]{1,0:T(8,128)(2,1)}, u32[]{:S(2)}, u32[]{:S(2)}) %collective-permute-start.20) | collective-permute-done | bytes 589856 | tf_op jit(solution)/shard_map/ppermute | solution.py:17
  168.5 5.7 %multiply_convert_fusion.6 = (bf16[1728,256]{1,0:T(8,128)(2,1)S(1)}, bf16[1728,256]{1,0:T(8,128)(2,1)S(1)}) fusion(f32[1728,256]{1,0:T(8,128)} %copy-done.110, f32[1728,256]{1,0:T(8,128)} %get-tuple-element.190, bf16[256,1152]{1,0:T(8,128)(2,1)} %after.4.refs_5_, bf16[1728,1152]{1,0:T(8,128)(2,1)} %param.30), kind=kOutput, calls=%fused_computation.43 | convolution fusion | flops 1030717440 | bytes 9879552 | tf_op jit(solution)/shard_map/dot_general | solution.py:567
  180.8 9.5 %weight_grad.3 = (bf16[2,432,1152]{2,1,0:T(8,128)(2,1)}, bf16[2,432,1152]{2,1,0:T(8,128)(2,1)}) custom-call(s32[1]{0:T(128)} %bitcast.core_ref, bf16[1728,256]{1,0:T(8,128)(2,1)} %copy-done.7, bf16[1728,256]{1,0:T(8,128)(2,1)} %copy-done.50, bf16[1728,256]{1,0:T(8,128)(2,1)} %copy-done.48, bf16[1728,256]{1,0:T(8,128)(2,1)} %copy-done.47, ...), custom_call_target="tpu_custom_call" | custom-call | tf_op jit(solution)/shard_map/weight_grad/pallas_call | solution.py:190
  198.4 5.6 %multiply_convert_fusion = (bf16[1728,256]{1,0:T(8,128)(2,1)}, bf16[1728,256]{1,0:T(8,128)(2,1)}) fusion(f32[1728,256]{1,0:T(8,128)} %copy-done.109, f32[1728,256]{1,0:T(8,128)} %get-tuple-element.184, bf16[256,1152]{1,0:T(8,128)(2,1)} %get-tuple-element.68, bf16[1728,1152]{1,0:T(8,128)(2,1)S(1)} %copy-done.3), kind=kOutput, calls=%fused_computation.37 | convolution fusion | flops 1030717440 | bytes 9879552 | tf_op jit(solution)/shard_map/dot_general | solution.py:567
  207.4 5.6 %multiply_convert_fusion.1 = (bf16[1728,256]{1,0:T(8,128)(2,1)}, bf16[1728,256]{1,0:T(8,128)(2,1)}) fusion(f32[1728,256]{1,0:T(8,128)} %copy-done.108, f32[1728,256]{1,0:T(8,128)} %get-tuple-element.186, bf16[256,1152]{1,0:T(8,128)(2,1)} %get-tuple-element.67, bf16[1728,1152]{1,0:T(8,128)(2,1)S(1)} %copy-done.3), kind=kOutput, calls=%fused_computation.38 | convolution fusion | flops 1030717440 | bytes 9879552 | tf_op jit(solution)/shard_map/dot_general | solution.py:567
  213.0 9.9 %weight_grad.4 = (bf16[2,432,1152]{2,1,0:T(8,128)(2,1)}, bf16[2,432,1152]{2,1,0:T(8,128)(2,1)}) custom-call(s32[1]{0:T(128)} %bitcast.core_ref, bf16[1728,256]{1,0:T(8,128)(2,1)} %copy-done.49, bf16[1728,256]{1,0:T(8,128)(2,1)} %copy-done.51, bf16[1728,256]{1,0:T(8,128)(2,1)} %get-tuple-element.147.refs_2_, bf16[1728,256]{1,0:T(8,128)(2,1)} %get-tuple-element.149.refs_3_, ...), custom_call_target="tpu_custom_call" | custom-call | tf_op jit(solution)/shard_map/weight_grad/pallas_call | solution.py:190
  241.4 9.6 %weight_grad.5 = (bf16[2,432,1152]{2,1,0:T(8,128)(2,1)}, bf16[2,432,1152]{2,1,0:T(8,128)(2,1)}) custom-call(s32[1]{0:T(128)} %bitcast.core_ref, bf16[1728,256]{1,0:T(8,128)(2,1)} %copy-done.45, bf16[1728,256]{1,0:T(8,128)(2,1)} %copy-done.46, bf16[1728,256]{1,0:T(8,128)(2,1)} %get-tuple-element.146.refs_2_, bf16[1728,256]{1,0:T(8,128)(2,1)} %get-tuple-element.148.refs_3_, ...), custom_call_target="tpu_custom_call" | custom-call | tf_op jit(solution)/shard_map/weight_grad/pallas_call | solution.py:190
  251.0 4.9 collective-permute-done.24.refs_1_
  276.9 5.8 %collective-permute-done.29.refs_1_ = bf16[432,1152]{1,0:T(8,128)(2,1)S(1)} collective-permute-done((bf16[432,1152]{1,0:T(8,128)(2,1)S(1)}, bf16[432,1152]{1,0:T(8,128)(2,1)S(1)}, u32[]{:S(2)}, u32[]{:S(2)}) %collective-permute-start.29) | collective-permute-done | bytes 995360 | tf_op jit(solution)/shard_map/ppermute | solution.py:360
  289.5 7.2 %collective-permute-start.31 = (bf16[432,1152]{1,0:T(8,128)(2,1)}, bf16[432,1152]{1,0:T(8,128)(2,1)}, u32[]{:S(2)}, u32[]{:S(2)}) collective-permute-start(bf16[432,1152]{1,0:T(8,128)(2,1)} %get-tuple-element.77.refs_2_), channel_id=1, source_target_pairs={{0,8},{4,12},{24,16},{28,20},{1,9},{5,13},{25,17},{29,21},{2,10},{... | collective-permute-start | bytes 2985992 | tf_op jit(solution)/shard_map/ppermute | solution.py:360
  300.8 9.1 %attention_backward.1 = (bf16[256,1024]{1,0:T(8,128)(2,1)}, f32[1,256]{1,0:T(1,128)}, bf16[512,512]{1,0:T(8,128)(2,1)}, f32[256,512]{1,0:T(8,128)}) custom-call(f32[256,1536]{1,0:T(8,128)} %copy-done.4, bf16[1,256]{1,0:T(2,128)(2,1)} %broadcast_in_dim.21.gain_ref, f32[256,128]{1,0:T(8,128)} %get-tuple-element.180.cos_ref, ...), custom_call_target="tpu_custom_call" | custom-call | tf_op jit(solution)/shard_map/attention_backward/pallas_call | solution.py:335
  311.2 5.6 %line_step.18 = (bf16[432,1152]{1,0:T(8,128)(2,1)}, bf16[432,1152]{1,0:T(8,128)(2,1)}, bf16[432,1152]{1,0:T(8,128)(2,1)}, bf16[432,1152]{1,0:T(8,128)(2,1)}, bf16[512,512]{1,0:T(8,128)(2,1)}) custom-call(s32[1]{0:T(128)} %bitcast.19.place_ref, bf16[432,1152]{1,0:T(8,128)(2,1)} %get-tuple-element.81.refs_0_, ...), custom_call_target="tpu_custom_call", output_to_operand_aliasing={{4}: (7, {})} | custom-call | tf_op jit(solution)/shard_map/line_step/pallas_call | solution.py:442
  321.4 4.8 collective-permute-done.36
  328.5 6.0 %line_step.19 = (bf16[432,1152]{1,0:T(8,128)(2,1)}, bf16[432,1152]{1,0:T(8,128)(2,1)}, bf16[432,1152]{1,0:T(8,128)(2,1)}, bf16[432,1152]{1,0:T(8,128)(2,1)}, f32[256,512]{1,0:T(8,128)}) custom-call(s32[1]{0:T(128)} %bitcast.19.place_ref, bf16[432,1152]{1,0:T(8,128)(2,1)} %get-tuple-element.76.refs_0_, ...), custom_call_target="tpu_custom_call", output_to_operand_aliasing={{4}: (7, {})} | custom-call | tf_op jit(solution)/shard_map/line_step/pallas_call | solution.py:442
  367.9 11.5 %collective-permute-done.37.refs_1_ = bf16[432,1152]{1,0:T(8,128)(2,1)S(1)} collective-permute-done((bf16[432,1152]{1,0:T(8,128)(2,1)}, bf16[432,1152]{1,0:T(8,128)(2,1)S(1)}, u32[]{:S(2)}, u32[]{:S(2)}) %collective-permute-start.37) | collective-permute-done | bytes 995360 | tf_op jit(solution)/shard_map/ppermute | solution.py:360
  389.1 11.2 %collective-permute-done.47.refs_1_ = bf16[432,1152]{1,0:T(8,128)(2,1)S(1)} collective-permute-done((bf16[432,1152]{1,0:T(8,128)(2,1)}, bf16[432,1152]{1,0:T(8,128)(2,1)S(1)}, u32[]{:S(2)}, u32[]{:S(2)}) %collective-permute-start.47) | collective-permute-done | bytes 995360 | tf_op jit(solution)/shard_map/ppermute | solution.py:360
  403.3 4.9 line_step.22
  411.7 14.6 %collective-permute-done.39.refs_1_ = bf16[432,1152]{1,0:T(8,128)(2,1)} collective-permute-done((bf16[432,1152]{1,0:T(8,128)(2,1)}, bf16[432,1152]{1,0:T(8,128)(2,1)}, u32[]{:S(2)}, u32[]{:S(2)}) %collective-permute-start.39) | collective-permute-done | bytes 995360 | tf_op jit(solution)/shard_map/ppermute | solution.py:360
  431.8 7.5 %collective-permute-start.46 = (bf16[160,2560]{1,0:T(8,128)(2,1)}, bf16[160,2560]{1,0:T(8,128)(2,1)}, u32[]{:S(2)}, u32[]{:S(2)}) collective-permute-start(bf16[160,2560]{1,0:T(8,128)(2,1)} %get-tuple-element.94.refs_2_), channel_id=1, source_target_pairs={{0,8},{4,12},{24,16},{28,20},{1,9},{5,13},{25,17},{29,21},{2,10},{... | collective-permute-start | bytes 2457608 | tf_op jit(solution)/shard_map/ppermute | solution.py:360
  442.9 5.6 %whole_grad.3.refs_4_ = f32[1728,1152]{1,0:T(8,128)} custom-call(s32[1]{0:T(128)} %bitcast.core_ref, bf16[432,1152]{1,0:T(8,128)(2,1)} %get-tuple-element.95.refs_0_, bf16[432,1152]{1,0:T(8,128)(2,1)} %get-tuple-element.100.refs_1_, bf16[432,1152]{1,0:T(8,128)(2,1)} %copy-done.33, bf16[432,1152]{1,0:T(8,128)(2,1)} %copy-done.36), custom_call_target="tpu_custom_call" | custom-call | tf_op jit(solution)/shard_map/whole_grad/pallas_call | solution.py:505
  448.5 6.5 %collective-permute-done.46.refs_3_ = bf16[160,2560]{1,0:T(8,128)(2,1)} collective-permute-done((bf16[160,2560]{1,0:T(8,128)(2,1)}, bf16[160,2560]{1,0:T(8,128)(2,1)}, u32[]{:S(2)}, u32[]{:S(2)}) %collective-permute-start.46) | collective-permute-done | bytes 819232 | tf_op jit(solution)/shard_map/ppermute | solution.py:360
  464.7 14.2 %collective-permute-done.54.refs_1_ = bf16[432,1152]{1,0:T(8,128)(2,1)} collective-permute-done((bf16[432,1152]{1,0:T(8,128)(2,1)S(1)}, bf16[432,1152]{1,0:T(8,128)(2,1)}, u32[]{:S(2)}, u32[]{:S(2)}) %collective-permute-start.54) | collective-permute-done | bytes 995360 | tf_op jit(solution)/shard_map/ppermute | solution.py:360
  492.5 5.6 %whole_grad.4.refs_2_ = f32[1728,1152]{1,0:T(8,128)} custom-call(s32[1]{0:T(128)} %bitcast.core_ref, bf16[432,1152]{1,0:T(8,128)(2,1)} %get-tuple-element.105.refs_0_, bf16[432,1152]{1,0:T(8,128)(2,1)} %get-tuple-element.106.refs_1_, bf16[432,1152]{1,0:T(8,128)(2,1)} %copy-done.39, bf16[432,1152]{1,0:T(8,128)(2,1)} %copy-done.37), custom_call_target="tpu_custom_call" | custom-call | tf_op jit(solution)/shard_map/whole_grad/pallas_call | solution.py:505
  498.1 13.2 %collective-permute-done.56.refs_1_ = bf16[432,1152]{1,0:T(8,128)(2,1)S(1)} collective-permute-done((bf16[432,1152]{1,0:T(8,128)(2,1)}, bf16[432,1152]{1,0:T(8,128)(2,1)S(1)}, u32[]{:S(2)}, u32[]{:S(2)}) %collective-permute-start.56) | collective-permute-done | bytes 995360 | tf_op jit(solution)/shard_map/ppermute | solution.py:360
  515.7 12.5 %collective-permute-done.52.refs_1_ = bf16[160,2560]{1,0:T(8,128)(2,1)} collective-permute-done((bf16[160,2560]{1,0:T(8,128)(2,1)}, bf16[160,2560]{1,0:T(8,128)(2,1)}, u32[]{:S(2)}, u32[]{:S(2)}) %collective-permute-start.52) | collective-permute-done | bytes 819232 | tf_op jit(solution)/shard_map/ppermute | solution.py:360
  531.9 5.7 %whole_grad.5 = f32[1728,1152]{1,0:T(8,128)} custom-call(s32[1]{0:T(128)} %bitcast.core_ref, bf16[432,1152]{1,0:T(8,128)(2,1)} %get-tuple-element.108.refs_0_, bf16[432,1152]{1,0:T(8,128)(2,1)} %get-tuple-element.109.refs_1_, bf16[432,1152]{1,0:T(8,128)(2,1)} %collective-permute-done.59.refs_2_, bf16[432,1152]{1,0:T(8,128)(2,1)} %collective-permute-done.60.refs_3_), custom_call_target="tpu_custom_call" | custom-call | tf_op jit(solution)/shard_map/whole_grad/pallas_call | solution.py:505
  (449 shorter events, 275.4 us)
Async XLA Ops:
  7.5 26.7 %collective-permute-start.2 = (bf16[160,1536]{1,0:T(8,128)(2,1)}, bf16[160,1536]{1,0:T(8,128)(2,1)S(1)}, u32[]{:S(2)}, u32[]{:S(2)}) collective-permute-start(bf16[160,1536]{1,0:T(8,128)(2,1)} %pack.2), channel_id=1, source_target_pairs={{0,3},{1,2},{2,1},{3,0},{4,7},{5,6},{6,5},{7,4},{8,11},{9,10},{10,... | collective-permute-start | bytes 1474568 | tf_op jit(solution)/shard_map/ppermute | solution.py:17
  93.2 25.5 %collective-permute-start.16 = (bf16[256,1152]{1,0:T(8,128)(2,1)S(1)}, bf16[256,1152]{1,0:T(8,128)(2,1)S(1)}, u32[]{:S(2)}, u32[]{:S(2)}) collective-permute-start(bf16[256,1152]{1,0:T(8,128)(2,1)S(1)} %multiply_convert_fusion.16.refs_4_), channel_id=1, source_target_pairs={{0,2},{1,3},{2,0},{3,1},{4,6},{5,7},{6,4},{7,5},{8,10},{9,11},{10,... | collective-permute-start | bytes 1769480 | tf_op jit(solution)/shard_map/ppermute | solution.py:17
  95.7 31.2 %collective-permute-start.14 = (bf16[256,1152]{1,0:T(8,128)(2,1)S(1)}, bf16[256,1152]{1,0:T(8,128)(2,1)S(1)}, u32[]{:S(2)}, u32[]{:S(2)}) collective-permute-start(bf16[256,1152]{1,0:T(8,128)(2,1)S(1)} %multiply_convert_fusion.16.refs_4_), channel_id=1, source_target_pairs={{0,1},{1,0},{2,3},{3,2},{4,5},{5,4},{6,7},{7,6},{8,9},{9,8},{10,11... | collective-permute-start | bytes 1769480 | tf_op jit(solution)/shard_map/ppermute | solution.py:17
  152.2 27.0 %collective-permute-start.21 = (bf16[256,1152]{1,0:T(8,128)(2,1)}, bf16[256,1152]{1,0:T(8,128)(2,1)S(1)}, u32[]{:S(2)}, u32[]{:S(2)}) collective-permute-start(bf16[256,1152]{1,0:T(8,128)(2,1)} %get-tuple-element.163.refs_4_), channel_id=1, source_target_pairs={{0,2},{1,3},{2,0},{3,1},{4,6},{5,7},{6,4},{7,5},{8,10},{9,11},{10,... | collective-permute-start | bytes 1769480 | tf_op jit(solution)/shard_map/ppermute | solution.py:17
  152.5 27.5 %collective-permute-start.22 = (bf16[256,1152]{1,0:T(8,128)(2,1)}, bf16[256,1152]{1,0:T(8,128)(2,1)S(1)}, u32[]{:S(2)}, u32[]{:S(2)}) collective-permute-start(bf16[256,1152]{1,0:T(8,128)(2,1)} %get-tuple-element.163.refs_4_), channel_id=1, source_target_pairs={{0,3},{1,2},{2,1},{3,0},{4,7},{5,6},{6,5},{7,4},{8,11},{9,10},{10,... | collective-permute-start | bytes 1769480 | tf_op jit(solution)/shard_map/ppermute | solution.py:17
  190.4 74.2 %collective-permute-start.26 = (bf16[256,1152]{1,0:T(8,128)(2,1)}, bf16[256,1152]{1,0:T(8,128)(2,1)S(1)}, u32[]{:S(2)}, u32[]{:S(2)}) collective-permute-start(bf16[256,1152]{1,0:T(8,128)(2,1)} %fusion.4.refs_1_), channel_id=1, source_target_pairs={{0,1},{1,0},{2,3},{3,2},{4,5},{5,4},{6,7},{7,6},{8,9},{9,8},{10,11... | collective-permute-start | bytes 1769480 | tf_op jit(solution)/shard_map/ppermute | solution.py:17
  222.9 37.5 %collective-permute-start.25 = (bf16[2,432,1152]{2,1,0:T(8,128)(2,1)}, bf16[2,432,1152]{2,1,0:T(8,128)(2,1)}, u32[]{:S(2)}, u32[]{:S(2)}) collective-permute-start(bf16[2,432,1152]{2,1,0:T(8,128)(2,1)} %get-tuple-element.70), channel_id=1, source_target_pairs={{0,4},{4,0},{8,12},{12,8},{16,20},{20,16},{24,28},{28,24},{1,5},{5... | collective-permute-start | bytes 5971976 | tf_op jit(solution)/shard_map/ppermute | solution.py:17
  229.0 37.2 %collective-permute-start.28 = (bf16[256,1152]{1,0:T(8,128)(2,1)}, bf16[256,1152]{1,0:T(8,128)(2,1)S(1)}, u32[]{:S(2)}, u32[]{:S(2)}) collective-permute-start(bf16[256,1152]{1,0:T(8,128)(2,1)} %fusion.6), channel_id=1, source_target_pairs={{0,3},{1,2},{2,1},{3,0},{4,7},{5,6},{6,5},{7,4},{8,11},{9,10},{10,... | collective-permute-start | bytes 1769480 | tf_op jit(solution)/shard_map/ppermute | solution.py:17
  230.4 25.5 %collective-permute-start.24 = (bf16[432,1152]{1,0:T(8,128)(2,1)}, bf16[432,1152]{1,0:T(8,128)(2,1)}, u32[]{:S(2)}, u32[]{:S(2)}) collective-permute-start(bf16[432,1152]{1,0:T(8,128)(2,1)} %get-tuple-element.66.refs_0_), channel_id=1, source_target_pairs={{0,8},{4,12},{24,16},{28,20},{1,9},{5,13},{25,17},{29,21},{2,10},{... | collective-permute-start | bytes 2985992 | tf_op jit(solution)/shard_map/ppermute | solution.py:360
  238.6 31.7 %collective-permute-start.27 = (bf16[256,1152]{1,0:T(8,128)(2,1)}, bf16[256,1152]{1,0:T(8,128)(2,1)}, u32[]{:S(2)}, u32[]{:S(2)}) collective-permute-start(bf16[256,1152]{1,0:T(8,128)(2,1)} %fusion.5), channel_id=1, source_target_pairs={{0,2},{1,3},{2,0},{3,1},{4,6},{5,7},{6,4},{7,5},{8,10},{9,11},{10,... | collective-permute-start | bytes 1769480 | tf_op jit(solution)/shard_map/ppermute | solution.py:17
  255.9 26.8 %collective-permute-start.29 = (bf16[432,1152]{1,0:T(8,128)(2,1)S(1)}, bf16[432,1152]{1,0:T(8,128)(2,1)S(1)}, u32[]{:S(2)}, u32[]{:S(2)}) collective-permute-start(bf16[432,1152]{1,0:T(8,128)(2,1)S(1)} %copy-done.43), channel_id=1, source_target_pairs={{0,8},{4,12},{24,16},{28,20},{1,9},{5,13},{25,17},{29,21},{2,10},{... | collective-permute-start | bytes 2985992 | tf_op jit(solution)/shard_map/ppermute | solution.py:360
  260.3 50.9 %collective-permute-start.32 = (bf16[2,432,1152]{2,1,0:T(8,128)(2,1)}, bf16[2,432,1152]{2,1,0:T(8,128)(2,1)}, u32[]{:S(2)}, u32[]{:S(2)}) collective-permute-start(bf16[2,432,1152]{2,1,0:T(8,128)(2,1)} %get-tuple-element.79), channel_id=1, source_target_pairs={{0,4},{4,0},{8,12},{12,8},{16,20},{20,16},{24,28},{28,24},{1,5},{5... | collective-permute-start | bytes 5971976 | tf_op jit(solution)/shard_map/ppermute | solution.py:17
  264.6 46.6 %collective-permute-start.33 = (bf16[432,1152]{1,0:T(8,128)(2,1)}, bf16[432,1152]{1,0:T(8,128)(2,1)}, u32[]{:S(2)}, u32[]{:S(2)}) collective-permute-start(bf16[432,1152]{1,0:T(8,128)(2,1)} %get-tuple-element.81.refs_0_), channel_id=1, source_target_pairs={{8,16},{12,20},{16,8},{20,12},{9,17},{13,21},{17,9},{21,13},{10,18... | collective-permute-start | bytes 2985992 | tf_op jit(solution)/shard_map/ppermute | solution.py:360
  266.3 44.9 %collective-permute-start.34 = (bf16[432,1152]{1,0:T(8,128)(2,1)}, bf16[432,1152]{1,0:T(8,128)(2,1)}, u32[]{:S(2)}, u32[]{:S(2)}) collective-permute-start(bf16[432,1152]{1,0:T(8,128)(2,1)} %get-tuple-element.82.refs_2_), channel_id=1, source_target_pairs={{0,8},{4,12},{24,16},{28,20},{1,9},{5,13},{25,17},{29,21},{2,10},{... | collective-permute-start | bytes 2985992 | tf_op jit(solution)/shard_map/ppermute | solution.py:360
  287.8 40.7 %collective-permute-start.30 = (bf16[432,1152]{1,0:T(8,128)(2,1)}, bf16[432,1152]{1,0:T(8,128)(2,1)}, u32[]{:S(2)}, u32[]{:S(2)}) collective-permute-start(bf16[432,1152]{1,0:T(8,128)(2,1)} %get-tuple-element.76.refs_0_), channel_id=1, source_target_pairs={{8,16},{12,20},{16,8},{20,12},{9,17},{13,21},{17,9},{21,13},{10,18... | collective-permute-start | bytes 2985992 | tf_op jit(solution)/shard_map/ppermute | solution.py:360
  289.5 39.0 %collective-permute-start.31 = (bf16[432,1152]{1,0:T(8,128)(2,1)}, bf16[432,1152]{1,0:T(8,128)(2,1)}, u32[]{:S(2)}, u32[]{:S(2)}) collective-permute-start(bf16[432,1152]{1,0:T(8,128)(2,1)} %get-tuple-element.77.refs_2_), channel_id=1, source_target_pairs={{0,8},{4,12},{24,16},{28,20},{1,9},{5,13},{25,17},{29,21},{2,10},{... | collective-permute-start | bytes 2985992 | tf_op jit(solution)/shard_map/ppermute | solution.py:360
  354.4 25.0 %collective-permute-start.37 = (bf16[432,1152]{1,0:T(8,128)(2,1)}, bf16[432,1152]{1,0:T(8,128)(2,1)S(1)}, u32[]{:S(2)}, u32[]{:S(2)}) collective-permute-start(bf16[432,1152]{1,0:T(8,128)(2,1)} %get-tuple-element.87), channel_id=1, source_target_pairs={{0,8},{4,12},{24,16},{28,20},{8,0},{12,4},{16,24},{20,28},{1,9},{5... | collective-permute-start | bytes 2985992 | tf_op jit(solution)/shard_map/ppermute | solution.py:360
  354.4 27.7 %collective-permute-start.38 = (bf16[432,1152]{1,0:T(8,128)(2,1)S(1)}, bf16[432,1152]{1,0:T(8,128)(2,1)S(1)}, u32[]{:S(2)}, u32[]{:S(2)}) collective-permute-start(bf16[432,1152]{1,0:T(8,128)(2,1)S(1)} %copy-done.28), channel_id=1, source_target_pairs={{8,16},{12,20},{16,8},{20,12},{9,17},{13,21},{17,9},{21,13},{10,18... | collective-permute-start | bytes 2985992 | tf_op jit(solution)/shard_map/ppermute | solution.py:360
  355.1 45.2 %collective-permute-start.47 = (bf16[432,1152]{1,0:T(8,128)(2,1)}, bf16[432,1152]{1,0:T(8,128)(2,1)S(1)}, u32[]{:S(2)}, u32[]{:S(2)}) collective-permute-start(bf16[432,1152]{1,0:T(8,128)(2,1)} %get-tuple-element.97), channel_id=1, source_target_pairs={{0,8},{4,12},{24,16},{28,20},{8,0},{12,4},{16,24},{20,28},{1,9},{5... | collective-permute-start | bytes 2985992 | tf_op jit(solution)/shard_map/ppermute | solution.py:360
  358.8 42.8 %collective-permute-start.48 = (bf16[432,1152]{1,0:T(8,128)(2,1)S(1)}, bf16[432,1152]{1,0:T(8,128)(2,1)}, u32[]{:S(2)}, u32[]{:S(2)}) collective-permute-start(bf16[432,1152]{1,0:T(8,128)(2,1)S(1)} %copy-done.29), channel_id=1, source_target_pairs={{8,16},{12,20},{16,8},{20,12},{9,17},{13,21},{17,9},{21,13},{10,18... | collective-permute-start | bytes 2985992 | tf_op jit(solution)/shard_map/ppermute | solution.py:360
  365.9 42.3 %collective-permute-start.44 = (bf16[160,2560]{1,0:T(8,128)(2,1)}, bf16[160,2560]{1,0:T(8,128)(2,1)}, u32[]{:S(2)}, u32[]{:S(2)}) collective-permute-start(bf16[160,2560]{1,0:T(8,128)(2,1)} %get-tuple-element.161), channel_id=1, source_target_pairs={{0,3},{1,2},{2,1},{3,0},{4,7},{5,6},{6,5},{7,4},{8,11},{9,10},{10,... | collective-permute-start | bytes 2457608 | tf_op jit(solution)/shard_map/ppermute | solution.py:17
  379.4 28.9 %collective-permute-start.43 = (bf16[160,2560]{1,0:T(8,128)(2,1)}, bf16[160,2560]{1,0:T(8,128)(2,1)}, u32[]{:S(2)}, u32[]{:S(2)}) collective-permute-start(bf16[160,2560]{1,0:T(8,128)(2,1)} %get-tuple-element.162), channel_id=1, source_target_pairs={{0,2},{1,3},{2,0},{3,1},{4,6},{5,7},{6,4},{7,5},{8,10},{9,11},{10,... | collective-permute-start | bytes 2457608 | tf_op jit(solution)/shard_map/ppermute | solution.py:17
  383.0 25.8 %collective-permute-start.42 = (bf16[160,2560]{1,0:T(8,128)(2,1)}, bf16[160,2560]{1,0:T(8,128)(2,1)}, u32[]{:S(2)}, u32[]{:S(2)}) collective-permute-start(bf16[160,2560]{1,0:T(8,128)(2,1)} %get-tuple-element.160), channel_id=1, source_target_pairs={{0,1},{1,0},{2,3},{3,2},{4,5},{5,4},{6,7},{7,6},{8,9},{9,8},{10,11... | collective-permute-start | bytes 2457608 | tf_op jit(solution)/shard_map/ppermute | solution.py:17
  400.4 26.0 %collective-permute-start.39 = (bf16[432,1152]{1,0:T(8,128)(2,1)}, bf16[432,1152]{1,0:T(8,128)(2,1)}, u32[]{:S(2)}, u32[]{:S(2)}) collective-permute-start(bf16[432,1152]{1,0:T(8,128)(2,1)} %get-tuple-element.90.refs_0_), channel_id=1, source_target_pairs={{8,0},{12,4},{16,24},{20,28},{9,1},{13,5},{17,25},{21,29},{10,2},{... | collective-permute-start | bytes 2985992 | tf_op jit(solution)/shard_map/ppermute | solution.py:360
  408.2 32.7 %collective-permute-start.49 = (bf16[432,1152]{1,0:T(8,128)(2,1)S(1)}, bf16[432,1152]{1,0:T(8,128)(2,1)S(1)}, u32[]{:S(2)}, u32[]{:S(2)}) collective-permute-start(bf16[432,1152]{1,0:T(8,128)(2,1)S(1)} %copy-done.31), channel_id=1, source_target_pairs={{0,4},{4,0},{8,12},{12,8},{16,20},{20,16},{24,28},{28,24},{1,5},{5... | collective-permute-start | bytes 2985992 | tf_op jit(solution)/shard_map/ppermute | solution.py:17
  408.3 33.4 %collective-permute-start.50 = (bf16[432,1152]{1,0:T(8,128)(2,1)}, bf16[432,1152]{1,0:T(8,128)(2,1)S(1)}, u32[]{:S(2)}, u32[]{:S(2)}) collective-permute-start(bf16[432,1152]{1,0:T(8,128)(2,1)} %get-tuple-element.100.refs_1_), channel_id=1, source_target_pairs={{0,4},{4,0},{8,12},{12,8},{16,20},{20,16},{24,28},{28,24},{1,5},{5... | collective-permute-start | bytes 2985992 | tf_op jit(solution)/shard_map/ppermute | solution.py:17
  430.6 29.0 %collective-permute-start.45 = (bf16[432,1152]{1,0:T(8,128)(2,1)}, bf16[432,1152]{1,0:T(8,128)(2,1)S(1)}, u32[]{:S(2)}, u32[]{:S(2)}) collective-permute-start(bf16[432,1152]{1,0:T(8,128)(2,1)} %get-tuple-element.93.refs_0_), channel_id=1, source_target_pairs={{8,0},{12,4},{16,24},{20,28},{9,1},{13,5},{17,25},{21,29},{10,2},{... | collective-permute-start | bytes 2985992 | tf_op jit(solution)/shard_map/ppermute | solution.py:360
  439.4 39.5 %collective-permute-start.54 = (bf16[432,1152]{1,0:T(8,128)(2,1)S(1)}, bf16[432,1152]{1,0:T(8,128)(2,1)}, u32[]{:S(2)}, u32[]{:S(2)}) collective-permute-start(bf16[432,1152]{1,0:T(8,128)(2,1)S(1)} %copy-done.40), channel_id=1, source_target_pairs={{8,0},{12,4},{16,24},{20,28},{9,1},{13,5},{17,25},{21,29},{10,2},{... | collective-permute-start | bytes 2985992 | tf_op jit(solution)/shard_map/ppermute | solution.py:360
  440.9 38.0 %collective-permute-start.55 = (bf16[432,1152]{1,0:T(8,128)(2,1)S(1)}, bf16[432,1152]{1,0:T(8,128)(2,1)S(1)}, u32[]{:S(2)}, u32[]{:S(2)}) collective-permute-start(bf16[432,1152]{1,0:T(8,128)(2,1)S(1)} %copy-done.41), channel_id=1, source_target_pairs={{8,16},{12,20},{16,8},{20,12},{9,17},{13,21},{17,9},{21,13},{10,18... | collective-permute-start | bytes 2985992 | tf_op jit(solution)/shard_map/ppermute | solution.py:360
  484.4 27.0 %collective-permute-start.56 = (bf16[432,1152]{1,0:T(8,128)(2,1)}, bf16[432,1152]{1,0:T(8,128)(2,1)S(1)}, u32[]{:S(2)}, u32[]{:S(2)}) collective-permute-start(bf16[432,1152]{1,0:T(8,128)(2,1)} %get-tuple-element.104.refs_0_), channel_id=1, source_target_pairs={{8,0},{12,4},{16,24},{20,28},{9,1},{13,5},{17,25},{21,29},{10,2},{... | collective-permute-start | bytes 2985992 | tf_op jit(solution)/shard_map/ppermute | solution.py:360
  489.2 39.0 %collective-permute-start.52 = (bf16[160,2560]{1,0:T(8,128)(2,1)}, bf16[160,2560]{1,0:T(8,128)(2,1)}, u32[]{:S(2)}, u32[]{:S(2)}) collective-permute-start(bf16[160,2560]{1,0:T(8,128)(2,1)} %line_step.24.refs_0_), channel_id=1, source_target_pairs={{8,0},{12,4},{16,24},{20,28},{9,1},{13,5},{17,25},{21,29},{10,2},{... | collective-permute-start | bytes 2457608 | tf_op jit(solution)/shard_map/ppermute | solution.py:360
  490.4 41.5 %collective-permute-start.59 = (bf16[432,1152]{1,0:T(8,128)(2,1)}, bf16[432,1152]{1,0:T(8,128)(2,1)}, u32[]{:S(2)}, u32[]{:S(2)}) collective-permute-start(bf16[432,1152]{1,0:T(8,128)(2,1)} %get-tuple-element.108.refs_0_), channel_id=1, source_target_pairs={{0,4},{4,0},{8,12},{12,8},{16,20},{20,16},{24,28},{28,24},{1,5},{5... | collective-permute-start | bytes 2985992 | tf_op jit(solution)/shard_map/ppermute | solution.py:17
  (140 other events, 1218.8 us)

commit v6 on v5

--- a/solution.py
+++ b/solution.py
@@ -51,13 +51,18 @@
     return value.astype(jnp.int32).reshape(1)
 
 
-def packed(weights, extra=None):
+def packed(weights, gains=()):
     half = weights[0].shape[0] // 2
     wide = sum(weight.shape[1] for weight in weights)
-    below = 0 if extra is None else extra.shape[0]
+    below = 16 if gains else 0
 
     def kernel(core_ref, *refs):
         out_ref = refs[-1]
+        if gains:
+            out_ref[half:, :] = jnp.zeros((below, wide), jnp.bfloat16)
+        for spot in range(len(gains)):
+            ref = refs[len(weights) + spot]
+            out_ref[half + spot : half + spot + 1, : ref.shape[1]] = ref[...]
         for side in range(2):
 
             @pl.when(core_ref[0] == side)
@@ -67,10 +72,7 @@
                     out_ref[:half, at : at + ref.shape[1]] = ref[side * half : (side + 1) * half, :]
                     at += ref.shape[1]
 
-        if extra is not None:
-            out_ref[half:, :] = refs[len(weights)][...]
-
-    arrays = list(weights) + ([] if extra is None else [extra])
+    arrays = list(weights) + [gain[None, :] for gain in gains]
     return pl.pallas_call(
         kernel,
         grid_spec=pltpu.PrefetchScalarGridSpec(
@@ -151,68 +153,302 @@
     return grad_gate, grad_upper, part.astype(jnp.bfloat16)
 
 
-def chunks_of(units):
-    return 2 if units % 64 == 0 else 1
-
-
-def weight_grad(lefts, rights):
-    group = len(lefts)
-    units, rows = lefts[0].shape
-    model = rights[0].shape[1]
-    chunks = chunks_of(units)
-    tile = units // (2 * chunks)
-    core = (lax.axis_index("replica") % 2).astype(jnp.int32).reshape(1)
+def tile_of(size, most):
+    return max(tile for tile in range(16, most + 1, 16) if size % tile == 0)
+
+
+def ffn_backward_blocks(grads, gate_weight, up_weight, down_weight, slopes, acts):
+    count = len(grads)
+    rows, model = grads[0].shape
+    units = gate_weight.shape[0]
+    tile = tile_of(units, 432)
+    steps = units // tile
+
+    def kernel(*refs):
+        step = pl.program_id(0)
+        grad_refs, refs = refs[:count], refs[count:]
+        (gate_ref, up_ref, down_ref), refs = refs[:3], refs[3:]
+        slope_refs, act_refs, refs = refs[:count], refs[count : 2 * count], refs[2 * count :]
+        gate_outs, up_outs, part_outs, (grad_ref, acc) = (
+            refs[:count],
+            refs[count : 2 * count],
+            refs[2 * count : 3 * count],
+            refs[3 * count :],
+        )
+
+        @pl.when(step == 0)
+        def _():
+            for spot in range(count):
+                grad_ref[spot * rows : (spot + 1) * rows, :] = grad_refs[spot][...]
+            acc[...] = jnp.zeros_like(acc)
+
+        grad_hidden = dot(down_ref[...], grad_ref[...], 1, 1)
+        slope = jnp.concatenate([ref[...] for ref in slope_refs], axis=1).astype(jnp.float32)
+        act = jnp.concatenate([ref[...] for ref in act_refs], axis=1).astype(jnp.float32)
+        grad_gate = (grad_hidden * slope).astype(jnp.bfloat16)
+        grad_upper = (grad_hidden * act).astype(jnp.bfloat16)
+        for spot in range(count):
+            gate_outs[spot][...] = grad_gate[:, spot * rows : (spot + 1) * rows]
+            up_outs[spot][...] = grad_upper[:, spot * rows : (spot + 1) * rows]
+        acc[...] += dot(grad_gate, gate_ref[...], 0, 0) + dot(grad_upper, up_ref[...], 0, 0)
+
+        @pl.when(step == steps - 1)
+        def _():
+            for spot in range(count):
+                part_outs[spot][...] = acc[spot * rows : (spot + 1) * rows, :].astype(jnp.bfloat16)
+
+    weight = pl.BlockSpec((tile, model), lambda i: (i, 0))
+    flat = pl.BlockSpec((tile, rows), lambda i: (i, 0))
+    whole = pl.BlockSpec((rows, model), lambda i: (0, 0))
+    kept = jax.ShapeDtypeStruct((units, rows), jnp.bfloat16)
+    outs = pl.pallas_call(
+        kernel,
+        grid=(steps,),
+        out_shape=[kept] * (2 * count) + [jax.ShapeDtypeStruct((rows, model), jnp.bfloat16)] * count,
+        in_specs=[whole] * count + [weight] * 3 + [flat] * (2 * count),
+        out_specs=[flat] * (2 * count) + [whole] * count,
+        scratch_shapes=[
+            pltpu.VMEM((count * rows, model), jnp.bfloat16),
+            pltpu.VMEM((count * rows, model), jnp.float32),
+        ],
+        compiler_params=params(),
+        name="ffn_backward",
+    )(*grads, gate_weight, up_weight, down_weight, *slopes, *acts)
+    return outs[:count], outs[count : 2 * count], outs[2 * count :]
+
+
+def norm_pull(value, gain, grad):
+    scale = lax.rsqrt(jnp.mean(value * value, axis=-1, keepdims=True) + EPS)
+    unit = value * scale
+    inner = grad * gain
+    return scale * (inner - unit * jnp.mean(inner * unit, axis=-1, keepdims=True)), grad * unit
+
+
+def resid_backward(parts, resid, attended, out_grad, gain_ffn, gain_attn, w_out):
+    count = len(parts)
+    rows, model = resid.shape
+    tile = min(rows, 128)
+
+    def kernel(*refs):
+        part_refs, refs = refs[:count], refs[count:]
+        resid_ref, attended_ref, out_ref, ffn_ref, attn_ref, weight_ref, refs = *refs[:6], refs[6:]
+        grad_resid_ref, grad_attended_ref, grad_mixed_ref, ffn_grad_ref, attn_grad_ref = refs
+        grad = sum(ref[...].astype(jnp.float32) for ref in part_refs)
+        pulled, ffn_rows = norm_pull(resid_ref[...], ffn_ref[...].astype(jnp.float32), grad)
+        grad_resid = out_ref[...].astype(jnp.float32) + pulled
+        grad_resid_ref[...] = grad_resid
+        pulled, attn_rows = norm_pull(attended_ref[...], attn_ref[...].astype(jnp.float32), grad_resid)
+        grad_attended = pulled.astype(jnp.bfloat16)
+        grad_attended_ref[...] = grad_attended
+        grad_mixed_ref[...] = dot(grad_attended, weight_ref[...], 1, 0).astype(jnp.bfloat16)
+        ffn_grad = jnp.sum(ffn_rows, axis=0, keepdims=True)
+        attn_grad = jnp.sum(attn_rows, axis=0, keepdims=True)
+
+        @pl.when(pl.program_id(0) == 0)
+        def _():
+            ffn_grad_ref[...] = ffn_grad
+            attn_grad_ref[...] = attn_grad
+
+        @pl.when(pl.program_id(0) > 0)
+        def _():
+            ffn_grad_ref[...] += ffn_grad
+            attn_grad_ref[...] += attn_grad
+
+    block = pl.BlockSpec((tile, model), lambda i: (i, 0))
+    vector = pl.BlockSpec((1, model), lambda i: (0, 0))
+    inner = w_out.shape[1]
+    return pl.pallas_call(
+        kernel,
+        grid=(rows // tile,),
+        in_specs=[block] * (count + 3) + [vector] * 2 + [pl.BlockSpec(w_out.shape, lambda i: (0, 0))],
+        out_specs=[block, block, pl.BlockSpec((tile, inner), lambda i: (i, 0)), vector, vector],
+        out_shape=[
+            jax.ShapeDtypeStruct((rows, model), jnp.float32),
+            jax.ShapeDtypeStruct((rows, model), jnp.bfloat16),
+            jax.ShapeDtypeStruct((rows, inner), jnp.bfloat16),
+            jax.ShapeDtypeStruct((1, model), jnp.float32),
+            jax.ShapeDtypeStruct((1, model), jnp.float32),
+        ],
+        compiler_params=params(),
+        name="resid_backward",
+    )(*parts, resid, attended, out_grad, gain_ffn[None, :], gain_attn[None, :], w_out)
+
+
+def input_backward(
+    own_pair, backs, qkv, cosine, sine, gain_key, normed_in, grad_query, w_qkv, hidden_in, gain_in, grad_resid,
+    grad_attended, mixed, gain_grads, group,
+):
+    rows, model = hidden_in.shape
+    size = own_pair.shape[1] // 2
+    inner = grad_query.shape[1]
+    own_rows = model // group
+    half = inner + size
+    hops = len(backs)
+    count = len(gain_grads)
 
     def kernel(core_ref, *refs):
-        other_ref, mine_ref, left_ref, right_ref = refs[2 * group :]
-
-        @pl.when((pl.program_id(0) == 0) & (pl.program_id(1) == 0))
-        def _():
-            for spot in range(group):
-                right_ref[spot * rows : (spot + 1) * rows, :] = refs[group + spot][...]
-
-        for spot in range(group):
-            left_ref[:, spot * rows : (spot + 1) * rows] = refs[spot][...]
-        value = dot(left_ref[...], right_ref[...], 1, 0).astype(jnp.bfloat16)
-
-        @pl.when(pl.program_id(0) == 0)
-        def _():
-            other_ref[0] = value
-
-        @pl.when(pl.program_id(0) == 1)
-        def _():
-            mine_ref[0] = value
-
-    def left_map(side, chunk, core_ref):
-        return (2 * chunk + jnp.where(side == 0, 1 - core_ref[0], core_ref[0]), 0)
-
-    shape = jax.ShapeDtypeStruct((chunks, tile, model), jnp.bfloat16)
+        pair_ref, refs = refs[0], refs[1:]
+        back_refs, refs = refs[:hops], refs[hops:]
+        (
+            raw_ref, cos_ref, sin_ref, key_gain_ref, normed_ref, query_ref, weight_ref, x_ref, gain_ref, resid_ref,
+            attended_ref, mixed_ref, refs,
+        ) = *refs[:12], refs[12:]
+        gain_refs, refs = refs[:count], refs[count:]
+        other_ref, mine_ref, grad_in_ref, rows_ref = refs
+        pair = pair_ref[...] + sum(ref[...].astype(jnp.float32) for ref in back_refs)
+        first = pair[:, : size // 2]
+        second = pair[:, size // 2 : size]
+        turned = jnp.concatenate(
+            [
+                first * cos_ref[...] + second * sin_ref[...],
+                second * cos_ref[...] - first * sin_ref[...],
+            ],
+            axis=-1,
+        )
+        pulled, key_rows = norm_pull(raw_ref[...], key_gain_ref[...].astype(jnp.float32), turned)
+        grad_key = pulled.astype(jnp.bfloat16)
+        grad_value = pair[:, size:].astype(jnp.bfloat16)
+        grad_normed = (
+            dot(query_ref[...], weight_ref[:, :inner], 1, 1)
+            + dot(grad_key, weight_ref[:, inner:half], 1, 1)
+            + dot(grad_value, weight_ref[:, half:], 1, 1)
+        )
+        pulled, in_rows = norm_pull(
+            x_ref[...].astype(jnp.float32), gain_ref[...].astype(jnp.float32), grad_normed
+        )
+        grad_in_ref[...] = resid_ref[...] + pulled
+        rows_ref[...] = jnp.zeros_like(rows_ref)
+        rows_ref[0:1, :model] = jnp.sum(in_rows, axis=0, keepdims=True)
+        rows_ref[1:2, :size] = jnp.sum(key_rows, axis=0, keepdims=True)
+        for spot in range(count):
+            rows_ref[2 + spot : 3 + spot, : gain_refs[spot].shape[1]] = gain_refs[spot][...].astype(
+                jnp.float32
+            )
+        gains = rows_ref[...].astype(jnp.bfloat16)
+
+        def write(ref, side):
+            pieces = (
+                [(normed_ref, query_ref[...], 0, inner), (normed_ref, grad_key, inner, half)]
+                if side == 0
+                else [(normed_ref, grad_value, 0, size), (attended_ref, mixed_ref[...], size, half)]
+            )
+            for left, right, begin, end in pieces:
+                value = dot(left[...], right, 0, 0).astype(jnp.bfloat16)
+                for owner in range(group):
+                    ref[owner, :own_rows, begin:end] = value[owner * own_rows : (owner + 1) * own_rows]
+            for owner in range(group):
+                ref[owner, own_rows:, :] = gains
+
+        for core in range(2):
+
+            @pl.when(core_ref[0] == core)
+            def _():
+                write(other_ref, 1 - core)
+                write(mine_ref, core)
+
+    def whole(array):
+        return pl.BlockSpec(array.shape, lambda i, core_ref: (0,) * len(array.shape))
+
+    arrays = [
+        own_pair, *backs, qkv, cosine, sine, gain_key[None, :], normed_in, grad_query, w_qkv, hidden_in,
+        gain_in[None, :], grad_resid, grad_attended, mixed, *gain_grads,
+    ]
+    in_specs = [whole(array) for array in arrays]
+    in_specs[1 + hops] = pl.BlockSpec((rows, size), lambda i, core_ref: (0, inner // size))
+    shape = jax.ShapeDtypeStruct((group, own_rows + 16, half), jnp.bfloat16)
+    grad_in = jax.ShapeDtypeStruct((rows, model), jnp.float32)
     return pl.pallas_call(
         kernel,
         grid_spec=pltpu.PrefetchScalarGridSpec(
             num_scalar_prefetch=1,
-            grid=(2, chunks),
-            in_specs=[pl.BlockSpec((tile, rows), left_map)] * group
-            + [pl.BlockSpec((rows, model), lambda side, chunk, core_ref: (0, 0))] * group,
+            grid=(1,),
+            in_specs=in_specs,
+            out_specs=[whole(shape), whole(shape), whole(grad_in)],
+            scratch_shapes=[pltpu.VMEM((16, half), jnp.float32)],
+        ),
+        out_shape=[shape, shape, grad_in],
+        compiler_params=params(),
+        name="input_backward",
+    )(scalar(lax.axis_index("replica") % 2), *arrays)
+
+
+def chunks_of(units):
+    return 2 if units % 64 == 0 else 1
+
+
+def weight_grad(sets, rights):
+    group = len(rights)
+    count = len(sets)
+    units, rows = sets[0][0].shape
+    model = rights[0].shape[1]
+    chunks = chunks_of(units)
+    tile = units // (2 * chunks)
+
+    def kernel(core_ref, *refs):
+        right_refs, left_refs = refs[:group], refs[group:-4]
+        other_ref, mine_ref, left_ref, right_ref = refs[-4:]
+
+        @pl.when((pl.program_id(0) == 0) & (pl.program_id(1) == 0))
+        def _():
+            for spot in range(group):
+                right_ref[spot * rows : (spot + 1) * rows, :] = right_refs[spot][...]
+
+        for index in range(count):
+
+            @pl.when(pl.program_id(1) == index)
+            def _():
+                for chunk in range(chunks):
+                    for spot in range(group):
+                        left_ref[
+                            chunk * tile : (chunk + 1) * tile, spot * rows : (spot + 1) * rows
+                        ] = left_refs[(index * chunks + chunk) * group + spot][...]
+
+        value = dot(left_ref[...], right_ref[...], 1, 0).astype(jnp.bfloat16)
+
+        @pl.when(pl.program_id(0) == 0)
+        def _():
+            for chunk in range(chunks):
+                other_ref[chunk] = value[chunk * tile : (chunk + 1) * tile]
+
+        @pl.when(pl.program_id(0) == 1)
+        def _():
+            for chunk in range(chunks):
+                mine_ref[chunk] = value[chunk * tile : (chunk + 1) * tile]
+
+    def left_spec(chunk):
+        def index(side, spot, core_ref):
+            return (2 * chunk + jnp.where(side == 0, 1 - core_ref[0], core_ref[0]), 0)
+
+        return pl.BlockSpec((tile, rows), index)
+
+    shape = jax.ShapeDtypeStruct((count * chunks, tile, model), jnp.bfloat16)
+    block = (chunks, tile, model)
+    return pl.pallas_call(
+        kernel,
+        grid_spec=pltpu.PrefetchScalarGridSpec(
+            num_scalar_prefetch=1,
+            grid=(2, count),
+            in_specs=[pl.BlockSpec((rows, model), lambda side, spot, core_ref: (0, 0))] * group
+            + [left_spec(chunk) for _ in range(count) for chunk in range(chunks) for _ in range(group)],
             out_specs=[
                 pl.BlockSpec(
-                    (1, tile, model),
-                    lambda side, chunk, core_ref: (jnp.where(side == 0, chunk, chunks - 1), 0, 0),
+                    block, lambda side, spot, core_ref: (jnp.where(side == 0, spot, count - 1), 0, 0)
                 ),
-                pl.BlockSpec(
-                    (1, tile, model),
-                    lambda side, chunk, core_ref: (jnp.where(side == 0, 0, chunk), 0, 0),
-                ),
+                pl.BlockSpec(block, lambda side, spot, core_ref: (jnp.where(side == 0, 0, spot), 0, 0)),
             ],
             scratch_shapes=[
-                pltpu.VMEM((tile, group * rows), jnp.bfloat16),
+                pltpu.VMEM((chunks * tile, group * rows), jnp.bfloat16),
                 pltpu.VMEM((group * rows, model), jnp.bfloat16),
             ],
         ),
         out_shape=[shape, shape],
         compiler_params=params(),
         name="weight_grad",
-    )(core, *lefts, *rights)
+    )(
+        scalar(lax.axis_index("replica") % 2),
+        *rights,
+        *[left for lefts in sets for _ in range(chunks) for left in lefts],
+    )
 
 
 def allowed_mask(query_segs_ref, key_segs_ref, rows, width):
@@ -404,9 +640,12 @@
             states = []
             for spot, (_, _, terms, last) in enumerate(plan):
                 value = inputs[terms[0]][...]
-                if len(terms) == 2:
+                if len(terms) > 1:
                     far = inputs[terms[1]][...]
-                    total = (value.astype(jnp.float32) + far.astype(jnp.float32)).astype(jnp.bfloat16)
+                    total = value.astype(jnp.float32)
+                    for term in terms[1:]:
+                        total = total + inputs[term][...].astype(jnp.float32)
+                    total = total.astype(jnp.bfloat16)
                     if last is None:
                         value = total
                     elif last <= outer:
@@ -469,6 +708,9 @@
             self.moving.append((name, block, step, received[index]))
         return outs[-1]
 
+    def arrived(self):
+        return [far for _, _, _, far in self.moving]
+
     def finished(self, name):
         while name not in self.done:
             self.advance([])
@@ -516,14 +758,6 @@
     )(core, *mines, *others)
 
 
-def halves(block, axis):
-    core = lax.axis_index("replica") % 2
-    half = block.shape[axis] // 2
-    mine = lax.dynamic_slice_in_dim(block, core * half, half, axis)
-    other = lax.dynamic_slice_in_dim(block, (1 - core) * half, half, axis)
-    return mine, other
-
-
 def joined(mine, other, axis):
     core = lax.axis_index("replica") % 2
     return jnp.where(
@@ -533,23 +767,8 @@
     )
 
 
-def core_sum(block, axis):
-    mine, other = halves(block, axis)
-    return added(mine, swapped(other, "replica", 1))
-
-
 def core_join(block, axis):
     return joined(block, swapped(block, "replica", 1), axis)
-
-
-def owner_part(blocks):
-    rank = lax.axis_index("fsdp")
-    part = core_sum(blocks, 1)
-    total = lax.dynamic_index_in_dim(part, rank, 0, keepdims=False).astype(jnp.float32)
-    for mask in range(1, blocks.shape[0]):
-        far = swapped(lax.dynamic_index_in_dim(part, rank ^ mask, 0, keepdims=False), "fsdp", mask)
-        total = total + far.astype(jnp.float32)
-    return lax.optimization_barrier(total.astype(jnp.bfloat16))
 
 
 def fetched(block):
@@ -629,20 +848,17 @@
     scale = head_size ** (-0.5)
     qkv_weights = (query_weight, key_weight, value_weight)
     wide = sum(weight.shape[1] for weight in qkv_weights)
-    sizes = [own_model] * 4 + [own_head] * 2
-    gains = jnp.concatenate([norm_in, norm_attn, norm_ffn, norm_out, query_gain, key_gain])
-    gains = jnp.pad(gains[None, :], ((0, 15), (0, wide - sum(sizes))))
-    got, peers = fetched(packed(qkv_weights, gains))
+    gains = (norm_in, norm_attn, norm_ffn, norm_out, query_gain, key_gain)
+    block = packed(qkv_weights, gains)
+    got, peers = fetched(block)
     w_qkv = unpacked(qkv_weights, got, peers)
-    gain_stack = jnp.stack([gains[0]] + [part[-16] for part in got])
-    gain_rows = [
-        lax.dynamic_index_in_dim(gain_stack, rank ^ i, 0, keepdims=False) for i in range(group)
-    ]
+    gain_stack = jnp.stack([part[-16:, :own_model] for part in [block] + got])
+    gain_rows = jnp.stack(
+        [lax.dynamic_index_in_dim(gain_stack, rank ^ i, 0, keepdims=False) for i in range(group)], axis=1
+    )
+    gain_in, gain_attn, gain_ffn, gain_out = (gain_rows[i].reshape(-1) for i in range(4))
+    gain_query, gain_key = (gain_rows[i, :, :own_head].reshape(-1) for i in (4, 5))
     got, peers = fetched(after(packed([out_weight]), w_qkv))
-    spots = [sum(sizes[:i]) for i in range(7)]
-    gain_in, gain_attn, gain_ffn, gain_out, gain_query, gain_key = (
-        jnp.concatenate([row[spots[i] : spots[i + 1]] for row in gain_rows]) for i in range(6)
-    )
     residual_in = hidden_in.astype(jnp.float32)
     normed_in = normed(residual_in, gain_in).astype(jnp.bfloat16)
     qkv = jnp.dot(normed_in, w_qkv, preferred_element_type=jnp.float32)
@@ -692,28 +908,43 @@
     units = gate_weight.shape[0]
     lines = [Line(), Line()]
 
-    def fresh(name, other, mine):
+    def fresh(names, other, mine):
         far = swapped(other, "replica", 1)
-        return [(key, [(mine, key[1]), (far, key[1])]) for key in line_names(name, units)]
+        keys = [key for name in names for key in line_names(name, units)]
+        return [(key, [(mine, spot), (far, spot)]) for spot, key in enumerate(keys)]
 
     grad_gates, grad_uppers, returned = {}, {}, {}
     early = group // 2
-    for mask in range(group):
-        if mask == early:
-            pieces[mask] = after(pieces[mask], part)
-            waiting = fresh("down", *weight_grad(hiddens, pieces))
-            pieces[mask] = lines[0].advance([waiting.pop(0)], pieces[mask])
-        if mask == early + 1 and waiting:
-            pieces[mask] = lines[1].advance([waiting.pop(0)], pieces[mask])
+    for mask in range(early):
         grad_gates[mask], grad_uppers[mask], part = ffn_backward(
             pieces[mask], gate_weight, up_weight, down_weight, slopes[mask], acts[mask]
         )
-        if mask + 1 < early:
-            pieces[mask + 1] = after(pieces[mask + 1], part)
+        pieces[mask + 1] = after(pieces[mask + 1], part)
         returned[mask] = swapped(part, "fsdp", mask) if mask else part
-    waiting = []
-    waiting += fresh("gate", *weight_grad([grad_gates[i] for i in range(group)], ffn_blocks))
-    waiting += fresh("up", *weight_grad([grad_uppers[i] for i in range(group)], ffn_blocks))
+    waiting = fresh(["down"], *weight_grad([hiddens], pieces))
+    for mask in range(1, early):
+        pieces[early] = after(pieces[early], returned[mask])
+    pieces[early] = lines[0].advance([waiting.pop(0)], pieces[early])
+    late = range(early, group)
+    gate_parts, upper_parts, parts = ffn_backward_blocks(
+        [pieces[mask] for mask in late],
+        gate_weight,
+        up_weight,
+        down_weight,
+        [slopes[mask] for mask in late],
+        [acts[mask] for mask in late],
+    )
+    for spot, mask in enumerate(late):
+        grad_gates[mask], grad_uppers[mask] = gate_parts[spot], upper_parts[spot]
+        returned[mask] = swapped(parts[spot], "fsdp", mask)
+    if waiting:
+        grad_gates[early] = lines[1].advance([waiting.pop(0)], grad_gates[early])
+    grad_gates[0] = after(grad_gates[0], *lines[0].arrived())
+    other, mine = weight_grad(
+        [[grad_gates[i] for i in range(group)], [grad_uppers[i] for i in range(group)]], ffn_blocks
+    )
+    other = after(other, *lines[1].arrived(), *[returned[mask] for mask in late])
+    waiting = fresh(["gate", "up"], other, mine)
 
     def advance(spot, gate=None):
         ready = [entry for entry in waiting if entry[0][1] == spot][:1]
@@ -721,71 +952,69 @@
             waiting.remove(entry)
         return lines[spot].advance(ready, gate)
 
-    returned[0] = advance(0, returned[0])
-    grad_ffn_in = sum(returned[i].astype(jnp.float32) for i in range(group))
-    grad_resid_part, grad_gain_ffn = norm_back(resid, gain_ffn, grad_ffn_in)
-    grad_resid = grad_result + grad_resid_part
-    grad_attended, grad_gain_attn = norm_back(attended, gain_attn, grad_resid)
-    grad_attended_low = advance(1, grad_attended.astype(jnp.bfloat16))
-    grad_wout = contract(grad_attended_low, mixed, 0, 0).astype(jnp.bfloat16)
-    grad_mixed = jnp.dot(grad_attended_low, w_out, preferred_element_type=jnp.float32).astype(
-        jnp.bfloat16
-    )
+    grad_resid, grad_attended_low, grad_mixed, grad_gain_ffn, grad_gain_attn = resid_backward(
+        [returned[mask] for mask in range(group)], resid, attended, out_grad, gain_ffn, gain_attn, w_out
+    )
+    grad_mixed = advance(0, grad_mixed)
     grad_query_low, grad_gain_query, grad_far, grad_pair = attention_backward(
         *attention_args, query_new, grad_mixed, heads
     )
-    grad_gain_query = grad_gain_query[0]
-    grad_far = advance(0, grad_far)
+    grad_far = advance(1, grad_far)
+    backs = []
     for step in range(1, hops + 1):
-        lower = (hops - step) * rows
-        back = passed_along(grad_far[lower : lower + rows], "fsdp", -step)
-        grad_pair = grad_pair + back.astype(jnp.float32)
-    grad_pair = advance(1, grad_pair)
-    grad_key = grad_pair[:, :head_size]
-    grad_value_low = grad_pair[:, head_size:].astype(jnp.bfloat16)
-    _, pull_key = jax.vjp(lambda raw, gain: head_post(raw, gain, cosine, sine), key_raw, gain_key)
-    grad_key_raw, grad_gain_key = pull_key(grad_key)
-    grad_key_low = grad_key_raw.astype(jnp.bfloat16)
-    grad_qkv = jnp.concatenate([grad_query_low, grad_key_low, grad_value_low], axis=1)
-    grad_wqkv = contract(normed_in, grad_qkv, 0, 0).astype(jnp.bfloat16)
-    grad_normed_in = contract(grad_qkv, w_qkv, 1, 1)
-    grad_input_part, grad_gain_in = norm_back(residual_in, gain_in, grad_normed_in)
-    grad_in = grad_resid + grad_input_part
-    gain_grads = jnp.concatenate(
-        [
-            grad.astype(jnp.bfloat16).reshape(group, -1)
-            for grad in (
-                grad_gain_in,
-                grad_gain_attn,
-                grad_gain_ffn,
-                grad_gain_out,
-                grad_gain_query,
-                grad_gain_key,
-            )
-        ],
-        axis=1,
-    )
-    gain_grads = jnp.pad(gain_grads[:, None, :], ((0, 0), (0, 31), (0, wide - sum(sizes))))
-    grad_weights = jnp.concatenate([grad_wqkv, grad_wout], axis=1).reshape(group, own_model, -1)
-    gain_grads = jnp.pad(gain_grads, ((0, 0), (0, 0), (0, grad_wout.shape[1])))
-    weights_part = owner_part(jnp.concatenate([grad_weights, gain_grads], axis=1))
+        grad_far = passed_along(grad_far, "fsdp", -1)
+        backs.append(grad_far[-rows:])
+        grad_far = grad_far[:-rows]
+    grad_pair = advance(0, grad_pair)
+    other, mine, grad_in = input_backward(
+        grad_pair,
+        backs,
+        qkv,
+        cosine,
+        sine,
+        gain_key,
+        normed_in,
+        grad_query_low,
+        w_qkv,
+        hidden_in,
+        gain_in,
+        grad_resid,
+        grad_attended_low,
+        mixed,
+        [grad_gain_attn, grad_gain_ffn, grad_gain_out[None, :], grad_gain_query],
+        group,
+    )
+    other = advance(1, other)
+    chip = added(mine, swapped(other, "replica", 1))
+    owned = lax.psum_scatter(chip, "fsdp", scatter_dimension=0, tiled=True)[0]
+    places = lax.axis_size("replica") // 2
+    cores = [[2 * place + core for place in range(places)] for core in range(2)]
+    owned = lax.psum(owned, "replica", axis_index_groups=cores)
     advance(0)
     advance(1)
-    lines[0].advance([("weights", [weights_part])])
-    lines[1].advance([])
+    advance(0)
+    advance(1)
+    while waiting:
+        advance(0)
     grad_down = whole_grad(lines, "down", units)
     grad_down = lines[0].advance([], grad_down)
     grad_gate_w = whole_grad(lines, "gate", units)
     grad_gate_w = lines[1].advance([], grad_gate_w)
     grad_up_w = whole_grad(lines, "up", units)
-    owned = core_join(lines[0].finished("weights"), 0).astype(jnp.float32)
-    owned_out = owned[:own_model, wide:]
-    owned_query = owned[:own_model, : heads * head_size]
-    owned_key = owned[:own_model, heads * head_size : (heads + 1) * head_size]
-    owned_value = owned[:own_model, (heads + 1) * head_size : wide]
-    owned_gain_in, owned_gain_attn, owned_gain_ffn, owned_gain_out, owned_gain_query, owned_gain_key = (
-        owned[own_model, spots[i] : spots[i + 1]] for i in range(6)
-    )
+    owned = core_join(owned, 1).astype(jnp.float32)
+    inner = heads * head_size
+    columns = [0, inner, inner + head_size, inner + 2 * head_size, wide + inner]
+    owned_query, owned_key, owned_value, owned_out = (
+        owned[:own_model, columns[i] : columns[i + 1]] for i in range(4)
+    )
+
+    def owned_gain(row, size):
+        return lax.dynamic_slice_in_dim(owned[own_model + row], rank * size, size, 0)
+
+    owned_gain_in, owned_gain_attn, owned_gain_ffn, owned_gain_out = (
+        owned_gain(row, own_model) for row in (0, 2, 3, 4)
+    )
+    owned_gain_key, owned_gain_query = (owned_gain(row, own_head) for row in (1, 5))
     return (
         hidden_out,
         grad_in,

time: 550 us -> 573 us (1.042)
  waiting for transfers between devices: 173 us -> 237 us
  matrix products: 76.6 us -> 46.6 us
  starting transfers between devices: 86.4 us -> 60.2 us
  Pallas kernels: 129 us -> 153 us
  other arithmetic: 30.1 us -> 12.9 us
  between operations: 2.55 us -> 15.6 us
    ppermute x38 -> x34, waiting for transfers between devices: 61.8 us -> 107 us  [swapped(): return lax.ppermute(block, axis, route)]
    pallas_call x0 -> x3, Pallas kernels: none -> 31 us  [the longest x1 14.1 us: ffn_backward_blocks(): pl.pallas_call(kernel, grid=(steps,), out_shape=[kept] * (2 * count) + [j...]
    dot_general x28 -> x19, matrix products: 70.6 us -> 44.3 us  [contract(): lax.dot_general(left, right, (((left_dim,), (right_dim,)), ((), ())), pre...]
    ppermute x19 -> x16, waiting for transfers between devices: 99.1 us -> 119 us  [exchanged(): return lax.ppermute(block, 'replica', route)]
    ppermute x19 -> x16, starting transfers between devices: 47 us -> 27.3 us  [exchanged(): return lax.ppermute(block, 'replica', route)]
    concatenate x7 -> x0, local copies, waits for them, and re-layouts: 8.9 us -> none  [the longest x1 4.24 us: per_device(): jnp.concatenate([norm_in, norm_attn, norm_ffn, norm_out, query_gain, key_...]
    reduce_sum x4 -> x1, other arithmetic: 7.49 us -> 0.4 us  [normed(): value * lax.rsqrt(jnp.mean(value * value, axis=-1, keepdims=True) + EPS)]
    ppermute x38 -> x34, starting transfers between devices: 30.9 us -> 24.3 us  [swapped(): return lax.ppermute(block, axis, route)]
  transfers between devices with their start and end apart: 61 -> 56, of which waited for: 23 -> 28; matrix products, arithmetic and copies ran while one was open for 18% -> 10% of each run, Pallas kernels for 19% -> 19%
where the time goes in v6:
time: 573 us; the launch traced here: 567 us
  waiting for transfers between devices  237 us (41%)
  Pallas kernels  153 us (27%)
  starting transfers between devices  60.2 us (11%)
  matrix products  46.6 us (8%)
  local copies, waits for them, and re-layouts  41.1 us (7%)
  between operations  15.6 us (3%)
  other arithmetic  12.9 us (2%)
    ppermute x16, waiting for transfers between devices, exchanged(): return lax.ppermute(block, 'replica', route)  119 us
    ppermute x34, waiting for transfers between devices, swapped(): return lax.ppermute(block, axis, route)  107 us
    pallas_call x12, Pallas kernels, advance(): pl.pallas_call(kernel, grid_spec=pltpu.PrefetchScalarGridSpec(num_scalar_...  50.8 us
    dot_general x19, matrix products, contract(): lax.dot_general(left, right, (((left_dim,), (right_dim,)), ((), ())), pre...  44.3 us
    pallas_call x2, Pallas kernels, weight_grad(): pl.pallas_call(kernel, grid_spec=pltpu.PrefetchScalarGridSpec(num_scalar_...  27.9 us
    ppermute x16, starting transfers between devices, exchanged(): return lax.ppermute(block, 'replica', route)  27.3 us
    ppermute x34, starting transfers between devices, swapped(): return lax.ppermute(block, axis, route)  24.3 us
    unnamed x168, local copies, waits for them, and re-layouts  21.8 us
  transfers between devices with their start and end apart: 56, of which 28 were waited for; matrix products, arithmetic and copies ran while one was open for 10% of the time, Pallas kernels for 19%

profile of v6, /device:TPU:0, one launch (start us, length us, event | category | flops | bytes accessed | tf_op | source)
XLA Modules:
  0.0 567.0 jit_solution(9422007964984021646)
XLA Ops:
  22.7 7.8 %collective-permute-done.2.refs_5_ = bf16[160,1536]{1,0:T(8,128)(2,1)S(1)} collective-permute-done((bf16[160,1536]{1,0:T(8,128)(2,1)}, bf16[160,1536]{1,0:T(8,128)(2,1)S(1)}, u32[]{:S(2)}, u32[]{:S(2)}) %collective-permute-start.2) | collective-permute-done | bytes 491552 | tf_op jit(solution)/shard_map/ppermute | solution.py:17
  30.5 9.7 %collective-permute-done.1.refs_4_ = bf16[160,1536]{1,0:T(8,128)(2,1)S(1)} collective-permute-done((bf16[160,1536]{1,0:T(8,128)(2,1)}, bf16[160,1536]{1,0:T(8,128)(2,1)S(1)}, u32[]{:S(2)}, u32[]{:S(2)}) %collective-permute-start.1) | collective-permute-done | bytes 491552 | tf_op jit(solution)/shard_map/ppermute | solution.py:17
  72.6 6.5 %collective-permute-done.6 = bf16[256,512]{1,0:T(8,128)(2,1)S(1)} collective-permute-done((bf16[256,512]{1,0:T(8,128)(2,1)S(1)}, bf16[256,512]{1,0:T(8,128)(2,1)S(1)}, u32[]{:S(2)}, u32[]{:S(2)}) %collective-permute-start.6) | collective-permute-done | bytes 262176 | tf_op jit(solution)/shard_map/ppermute | solution.py:782
  80.0 5.9 %attention_forward.1 = (bf16[256,1024]{1,0:T(8,128)(2,1)}, bf16[256,1024]{1,0:T(8,128)(2,1)}) custom-call(f32[256,1536]{1,0:T(8,128)} %copy-done.3, bf16[1,256]{1,0:T(2,128)(2,1)} %broadcast_in_dim_reshape_squeeze.2.gain_ref, f32[256,128]{1,0:T(8,128)} %get-tuple-element.181.cos_ref.refs_4_, f32[256,128]{1,0:T(8,128)} %get-tuple-element.180.sin_ref.refs_5_, ...), custom_call_target="tpu_custom_call" | custom-call | tf_op jit(solution)/shard_map/attention_forward/pallas_call | solution.py:497
  99.1 24.5 %collective-permute-done.16.refs_2_ = bf16[256,1152]{1,0:T(8,128)(2,1)S(1)} collective-permute-done((bf16[256,1152]{1,0:T(8,128)(2,1)S(1)}, bf16[256,1152]{1,0:T(8,128)(2,1)S(1)}, u32[]{:S(2)}, u32[]{:S(2)}) %collective-permute-start.16) | collective-permute-done | bytes 589856 | tf_op jit(solution)/shard_map/ppermute | solution.py:17
  151.7 7.9 %collective-permute-done.17 = bf16[256,1152]{1,0:T(8,128)(2,1)S(1)} collective-permute-done((bf16[256,1152]{1,0:T(8,128)(2,1)S(1)}, bf16[256,1152]{1,0:T(8,128)(2,1)S(1)}, u32[]{:S(2)}, u32[]{:S(2)}) %collective-permute-start.17) | collective-permute-done | bytes 589856 | tf_op jit(solution)/shard_map/ppermute | solution.py:17
  159.6 8.1 %collective-permute-done.15 = bf16[256,1152]{1,0:T(8,128)(2,1)S(1)} collective-permute-done((bf16[256,1152]{1,0:T(8,128)(2,1)S(1)}, bf16[256,1152]{1,0:T(8,128)(2,1)S(1)}, u32[]{:S(2)}, u32[]{:S(2)}) %collective-permute-start.15) | collective-permute-done | bytes 589856 | tf_op jit(solution)/shard_map/ppermute | solution.py:17
  181.9 15.8 %collective-permute-done.20.refs_0_ = bf16[256,1152]{1,0:T(8,128)(2,1)S(1)} collective-permute-done((bf16[256,1152]{1,0:T(8,128)(2,1)}, bf16[256,1152]{1,0:T(8,128)(2,1)S(1)}, u32[]{:S(2)}, u32[]{:S(2)}) %collective-permute-start.20) | collective-permute-done | bytes 589856 | tf_op jit(solution)/shard_map/ppermute | solution.py:17
  198.6 5.9 %multiply_convert_fusion.2 = (bf16[1728,256]{1,0:T(8,128)(2,1)S(1)}, bf16[1728,256]{1,0:T(8,128)(2,1)S(1)}) fusion(f32[1728,256]{1,0:T(8,128)} %copy-done.83, f32[1728,256]{1,0:T(8,128)} %get-tuple-element.187, bf16[256,1152]{1,0:T(8,128)(2,1)} %after.7.refs_1_, bf16[1728,1152]{1,0:T(8,128)(2,1)} %refs_4_.1), kind=kOutput, calls=%fused_computation.22 | convolution fusion | flops 1030717440 | bytes 9879552 | tf_op jit(solution)/shard_map/dot_general | solution.py:786
  211.2 10.1 %weight_grad.2 = (bf16[2,432,1152]{2,1,0:T(8,128)(2,1)}, bf16[2,432,1152]{2,1,0:T(8,128)(2,1)}) custom-call(s32[1]{0:T(128)} %bitcast.core_ref, bf16[256,1152]{1,0:T(8,128)(2,1)} %get-tuple-element.165.refs_0_, bf16[256,1152]{1,0:T(8,128)(2,1)} %after.7.refs_1_, bf16[256,1152]{1,0:T(8,128)(2,1)} %after.8.refs_2_.refs_0_, bf16[256,1152]{1,0:T(8,128)(2,1)} %copy-done.25, ...), custom_call_target="tpu_custom_call" | custom-call | tf_op jit(solution)/shard_map/weight_grad/pallas_call | solution.py:426
  221.9 15.1 %collective-permute-done.24.refs_1_ = bf16[256,1152]{1,0:T(8,128)(2,1)S(1)} collective-permute-done((bf16[256,1152]{1,0:T(8,128)(2,1)S(1)}, bf16[256,1152]{1,0:T(8,128)(2,1)S(1)}, u32[]{:S(2)}, u32[]{:S(2)}) %collective-permute-start.24) | collective-permute-done | bytes 589856 | tf_op jit(solution)/shard_map/ppermute | solution.py:17
  246.1 14.1 %ffn_backward.1 = (bf16[1728,256]{1,0:T(8,128)(2,1)}, bf16[1728,256]{1,0:T(8,128)(2,1)}, bf16[1728,256]{1,0:T(8,128)(2,1)}, bf16[1728,256]{1,0:T(8,128)(2,1)}, b...) custom-call(bf16[256,1152]{1,0:T(8,128)(2,1)} %get-tuple-element.77.refs_0_, bf16[256,1152]{1,0:T(8,128)(2,1)} %copy-done.25, ...), custom_call_target="tpu_custom_call" | custom-call | tf_op jit(solution)/shard_map/ffn_backward/pallas_call | solution.py:204
  269.7 17.9 %weight_grad.3 = (bf16[4,432,1152]{2,1,0:T(8,128)(2,1)}, bf16[4,432,1152]{2,1,0:T(8,128)(2,1)}) custom-call(s32[1]{0:T(128)} %bitcast.core_ref, bf16[256,1152]{1,0:T(8,128)(2,1)} %copy-done.26, bf16[256,1152]{1,0:T(8,128)(2,1)} %copy-done.53, bf16[256,1152]{1,0:T(8,128)(2,1)} %copy-done.51, bf16[256,1152]{1,0:T(8,128)(2,1)} %copy-done.52, ...), custom_call_target="tpu_custom_call" | custom-call | tf_op jit(solution)/shard_map/weight_grad/pallas_call | solution.py:426
  295.7 6.4 %resid_backward.1 = (f32[256,1152]{1,0:T(8,128)}, bf16[256,1152]{1,0:T(8,128)(2,1)}, bf16[256,1024]{1,0:T(8,128)(2,1)}, f32[1,1152]{1,0:T(1,128)}, f32[1,1152]{1,0:T(1,128)}) custom-call(bf16[256,1152]{1,0:T(8,128)(2,1)} %fusion.1.refs_1_.refs_0_, bf16[256,1152]{1,0:T(8,128)(2,1)} %copy-done.27, bf16[256,1152]{1,0:T(8,128)(2,1)} %copy-done.29, ...), custom_call_target="tpu_custom_call" | custom-call | tf_op jit(solution)/shard_map/resid_backward/pallas_call | solution.py:260
  306.4 8.9 %attention_backward.1 = (bf16[256,1024]{1,0:T(8,128)(2,1)}, f32[1,256]{1,0:T(1,128)}, bf16[512,512]{1,0:T(8,128)(2,1)}, f32[256,512]{1,0:T(8,128)}) custom-call(f32[256,1536]{1,0:T(8,128)} %copy-done.3, bf16[1,256]{1,0:T(2,128)(2,1)} %broadcast_in_dim_reshape_squeeze.2.gain_ref, f32[256,128]{1,0:T(8,128)} %get-tuple-element.181.cos_ref.refs_4_, ...), custom_call_target="tpu_custom_call" | custom-call | tf_op jit(solution)/shard_map/attention_backward/pallas_call | solution.py:571
  321.7 5.2 collective-permute-start.31
  339.4 9.0 %collective-permute-done.31.refs_3_ = bf16[432,1152]{1,0:T(8,128)(2,1)} collective-permute-done((bf16[432,1152]{1,0:T(8,128)(2,1)S(1)}, bf16[432,1152]{1,0:T(8,128)(2,1)}, u32[]{:S(2)}, u32[]{:S(2)}) %collective-permute-start.31) | collective-permute-done | bytes 995360 | tf_op jit(solution)/shard_map/ppermute | solution.py:596
  348.4 5.5 line_step.15
  354.6 10.4 %input_backward.1 = (bf16[4,304,1280]{2,1,0:T(8,128)(2,1)}, bf16[4,304,1280]{2,1,0:T(8,128)(2,1)}, f32[256,1152]{1,0:T(8,128)}) custom-call(s32[1]{0:T(128)} %bitcast.core_ref, f32[256,512]{1,0:T(8,128)} %get-tuple-element.94.refs_0_, bf16[256,512]{1,0:T(8,128)(2,1)} %get-tuple-element.168.refs_1_, bf16[256,512]{1,0:T(8,128)(2,1)} %copy-done.64, ...), custom_call_target="tpu_custom_call" | custom-call | tf_op jit(solution)/shard_map/input_backward/pallas_call | solution.py:360
  368.3 5.9 %line_step.17 = (bf16[432,1152]{1,0:T(8,128)(2,1)}, bf16[432,1152]{1,0:T(8,128)(2,1)}, bf16[432,1152]{1,0:T(8,128)(2,1)}, bf16[432,1152]{1,0:T(8,128)(2,1)}, bf16[4,304,1280]{2,1,0:T(8,128)(2,1)}) custom-call(s32[1]{0:T(128)} %bitcast.21.place_ref, bf16[432,1152]{1,0:T(8,128)(2,1)} %get-tuple-element.105.refs_0_, ...), custom_call_target="tpu_custom_call", output_to_operand_aliasing={{4}: (7, {})} | custom-call | tf_op jit(solution)/shard_map/line_step/pallas_call | solution.py:681
  374.2 5.8 %collective-permute-done.36 = bf16[4,304,1280]{2,1,0:T(8,128)(2,1)S(1)} collective-permute-done((bf16[4,304,1280]{2,1,0:T(8,128)(2,1)}, bf16[4,304,1280]{2,1,0:T(8,128)(2,1)S(1)}, u32[]{:S(2)}, u32[]{:S(2)}) %collective-permute-start.36) | collective-permute-done | bytes 3112992 | tf_op jit(solution)/shard_map/ppermute | solution.py:17
  389.6 19.3 %collective-permute-done.43.refs_1_ = bf16[432,1152]{1,0:T(8,128)(2,1)S(1)} collective-permute-done((bf16[432,1152]{1,0:T(8,128)(2,1)S(1)}, bf16[432,1152]{1,0:T(8,128)(2,1)S(1)}, u32[]{:S(2)}, u32[]{:S(2)}) %collective-permute-start.43) | collective-permute-done | bytes 995360 | tf_op jit(solution)/shard_map/ppermute | solution.py:596
  410.2 4.8 line_step.20
  417.1 13.2 %collective-permute-done.38.refs_1_ = bf16[432,1152]{1,0:T(8,128)(2,1)S(1)} collective-permute-done((bf16[432,1152]{1,0:T(8,128)(2,1)}, bf16[432,1152]{1,0:T(8,128)(2,1)S(1)}, u32[]{:S(2)}, u32[]{:S(2)}) %collective-permute-start.38) | collective-permute-done | bytes 995360 | tf_op jit(solution)/shard_map/ppermute | solution.py:596
  431.5 4.9 line_step.18
  438.5 13.1 %collective-permute-done.45.refs_1_ = bf16[432,1152]{1,0:T(8,128)(2,1)S(1)} collective-permute-done((bf16[432,1152]{1,0:T(8,128)(2,1)}, bf16[432,1152]{1,0:T(8,128)(2,1)S(1)}, u32[]{:S(2)}, u32[]{:S(2)}) %collective-permute-start.45) | collective-permute-done | bytes 995360 | tf_op jit(solution)/shard_map/ppermute | solution.py:596
  458.9 14.0 %collective-permute-done.40.refs_1_ = bf16[432,1152]{1,0:T(8,128)(2,1)S(1)} collective-permute-done((bf16[432,1152]{1,0:T(8,128)(2,1)}, bf16[432,1152]{1,0:T(8,128)(2,1)S(1)}, u32[]{:S(2)}, u32[]{:S(2)}) %collective-permute-start.40) | collective-permute-done | bytes 995360 | tf_op jit(solution)/shard_map/ppermute | solution.py:596
  480.8 5.7 whole_grad.4.refs_2_
  486.4 16.4 %collective-permute-done.49.refs_1_ = bf16[432,1152]{1,0:T(8,128)(2,1)} collective-permute-done((bf16[432,1152]{1,0:T(8,128)(2,1)}, bf16[432,1152]{1,0:T(8,128)(2,1)}, u32[]{:S(2)}, u32[]{:S(2)}) %collective-permute-start.49) | collective-permute-done | bytes 995360 | tf_op jit(solution)/shard_map/ppermute | solution.py:596
  506.1 5.7 %whole_grad.3.refs_2_ = f32[1728,1152]{1,0:T(8,128)} custom-call(s32[1]{0:T(128)} %bitcast.core_ref, bf16[432,1152]{1,0:T(8,128)(2,1)} %get-tuple-element.122.refs_0_, bf16[432,1152]{1,0:T(8,128)(2,1)} %get-tuple-element.123.refs_1_, bf16[432,1152]{1,0:T(8,128)(2,1)} %collective-permute-done.47.refs_2_, bf16[432,1152]{1,0:T(8,128)(2,1)} %collective-permute-done.48.refs_3_), custom_call_target="tpu_custom_call" | custom-call | tf_op jit(solution)/shard_map/whole_grad/pallas_call | solution.py:747
  511.8 28.5 %collective-permute-done.42.refs_1_ = bf16[432,1152]{1,0:T(8,128)(2,1)} collective-permute-done((bf16[432,1152]{1,0:T(8,128)(2,1)}, bf16[432,1152]{1,0:T(8,128)(2,1)}, u32[]{:S(2)}, u32[]{:S(2)}) %collective-permute-start.42) | collective-permute-done | bytes 995360 | tf_op jit(solution)/shard_map/ppermute | solution.py:596
  547.3 5.6 whole_grad.5
  (365 shorter events, 213.9 us)
Async XLA Ops:
  7.2 473.5 %reduce-scatter.4.cloned.1.call-start = ((), (), s32[]{:S(2)}) async-start(), calls=%async_computation.2 | async-start | bytes 3891200
  18.2 22.0 %collective-permute-start.1 = (bf16[160,1536]{1,0:T(8,128)(2,1)}, bf16[160,1536]{1,0:T(8,128)(2,1)S(1)}, u32[]{:S(2)}, u32[]{:S(2)}) collective-permute-start(bf16[160,1536]{1,0:T(8,128)(2,1)} %pack.2), channel_id=1, source_target_pairs={{0,2},{1,3},{2,0},{3,1},{4,6},{5,7},{6,4},{7,5},{8,10},{9,11},{10,... | collective-permute-start | bytes 1474568 | tf_op jit(solution)/shard_map/ppermute | solution.py:17
  95.0 28.6 %collective-permute-start.16 = (bf16[256,1152]{1,0:T(8,128)(2,1)S(1)}, bf16[256,1152]{1,0:T(8,128)(2,1)S(1)}, u32[]{:S(2)}, u32[]{:S(2)}) collective-permute-start(bf16[256,1152]{1,0:T(8,128)(2,1)S(1)} %multiply_convert_fusion.12.refs_0_), channel_id=1, source_target_pairs={{0,2},{1,3},{2,0},{3,1},{4,6},{5,7},{6,4},{7,5},{8,10},{9,11},{10,... | collective-permute-start | bytes 1769480 | tf_op jit(solution)/shard_map/ppermute | solution.py:17
  97.6 36.4 %collective-permute-start.18 = (bf16[256,1152]{1,0:T(8,128)(2,1)S(1)}, bf16[256,1152]{1,0:T(8,128)(2,1)S(1)}, u32[]{:S(2)}, u32[]{:S(2)}) collective-permute-start(bf16[256,1152]{1,0:T(8,128)(2,1)S(1)} %multiply_convert_fusion.12.refs_0_), channel_id=1, source_target_pairs={{0,3},{1,2},{2,1},{3,0},{4,7},{5,6},{6,5},{7,4},{8,11},{9,10},{10,... | collective-permute-start | bytes 1769480 | tf_op jit(solution)/shard_map/ppermute | solution.py:17
  97.7 42.6 %collective-permute-start.14 = (bf16[256,1152]{1,0:T(8,128)(2,1)S(1)}, bf16[256,1152]{1,0:T(8,128)(2,1)S(1)}, u32[]{:S(2)}, u32[]{:S(2)}) collective-permute-start(bf16[256,1152]{1,0:T(8,128)(2,1)S(1)} %multiply_convert_fusion.12.refs_0_), channel_id=1, source_target_pairs={{0,1},{1,0},{2,3},{3,2},{4,5},{5,4},{6,7},{7,6},{8,9},{9,8},{10,11... | collective-permute-start | bytes 1769480 | tf_op jit(solution)/shard_map/ppermute | solution.py:17
  132.2 27.4 %collective-permute-start.17 = (bf16[256,1152]{1,0:T(8,128)(2,1)S(1)}, bf16[256,1152]{1,0:T(8,128)(2,1)S(1)}, u32[]{:S(2)}, u32[]{:S(2)}) collective-permute-start(bf16[256,1152]{1,0:T(8,128)(2,1)S(1)} %convolution_convert_fusion.1), channel_id=1, source_target_pairs={{0,2},{1,3},{2,0},{3,1},{4,6},{5,7},{6,4},{7,5},{8,10},{9,11},{10,... | collective-permute-start | bytes 1769480 | tf_op jit(solution)/shard_map/ppermute | solution.py:17
  171.4 38.9 %collective-permute-start.22 = (bf16[256,1152]{1,0:T(8,128)(2,1)}, bf16[256,1152]{1,0:T(8,128)(2,1)S(1)}, u32[]{:S(2)}, u32[]{:S(2)}) collective-permute-start(bf16[256,1152]{1,0:T(8,128)(2,1)} %get-tuple-element.165.refs_0_), channel_id=1, source_target_pairs={{0,3},{1,2},{2,1},{3,0},{4,7},{5,6},{6,5},{7,4},{8,11},{9,10},{10,... | collective-permute-start | bytes 1769480 | tf_op jit(solution)/shard_map/ppermute | solution.py:17
  171.7 37.8 %collective-permute-start.21 = (bf16[256,1152]{1,0:T(8,128)(2,1)}, bf16[256,1152]{1,0:T(8,128)(2,1)S(1)}, u32[]{:S(2)}, u32[]{:S(2)}) collective-permute-start(bf16[256,1152]{1,0:T(8,128)(2,1)} %get-tuple-element.165.refs_0_), channel_id=1, source_target_pairs={{0,2},{1,3},{2,0},{3,1},{4,6},{5,7},{6,4},{7,5},{8,10},{9,11},{10,... | collective-permute-start | bytes 1769480 | tf_op jit(solution)/shard_map/ppermute | solution.py:17
  172.4 25.3 %collective-permute-start.20 = (bf16[256,1152]{1,0:T(8,128)(2,1)}, bf16[256,1152]{1,0:T(8,128)(2,1)S(1)}, u32[]{:S(2)}, u32[]{:S(2)}) collective-permute-start(bf16[256,1152]{1,0:T(8,128)(2,1)} %get-tuple-element.165.refs_0_), channel_id=1, source_target_pairs={{0,1},{1,0},{2,3},{3,2},{4,5},{5,4},{6,7},{7,6},{8,9},{9,8},{10,11... | collective-permute-start | bytes 1769480 | tf_op jit(solution)/shard_map/ppermute | solution.py:17
  242.5 26.2 %collective-permute-start.25 = (bf16[432,1152]{1,0:T(8,128)(2,1)}, bf16[432,1152]{1,0:T(8,128)(2,1)S(1)}, u32[]{:S(2)}, u32[]{:S(2)}) collective-permute-start(bf16[432,1152]{1,0:T(8,128)(2,1)} %get-tuple-element.76.refs_0_), channel_id=1, source_target_pairs={{0,8},{4,12},{24,16},{28,20},{1,9},{5,13},{25,17},{29,21},{2,10},{... | collective-permute-start | bytes 2985992 | tf_op jit(solution)/shard_map/ppermute | solution.py:596
  263.5 28.9 %collective-permute-start.26 = (bf16[432,1152]{1,0:T(8,128)(2,1)}, bf16[432,1152]{1,0:T(8,128)(2,1)S(1)}, u32[]{:S(2)}, u32[]{:S(2)}) collective-permute-start(bf16[432,1152]{1,0:T(8,128)(2,1)} %get-tuple-element.85.refs_0_), channel_id=1, source_target_pairs={{0,8},{4,12},{24,16},{28,20},{1,9},{5,13},{25,17},{29,21},{2,10},{... | collective-permute-start | bytes 2985992 | tf_op jit(solution)/shard_map/ppermute | solution.py:596
  264.8 27.5 %collective-permute-start.27 = (bf16[256,1152]{1,0:T(8,128)(2,1)}, bf16[256,1152]{1,0:T(8,128)(2,1)S(1)}, u32[]{:S(2)}, u32[]{:S(2)}) collective-permute-start(bf16[256,1152]{1,0:T(8,128)(2,1)} %get-tuple-element.86), channel_id=1, source_target_pairs={{0,2},{1,3},{2,0},{3,1},{4,6},{5,7},{6,4},{7,5},{8,10},{9,11},{10,... | collective-permute-start | bytes 1769480 | tf_op jit(solution)/shard_map/ppermute | solution.py:17
  266.4 25.9 %collective-permute-start.28 = (bf16[256,1152]{1,0:T(8,128)(2,1)}, bf16[256,1152]{1,0:T(8,128)(2,1)S(1)}, u32[]{:S(2)}, u32[]{:S(2)}) collective-permute-start(bf16[256,1152]{1,0:T(8,128)(2,1)} %get-tuple-element.87), channel_id=1, source_target_pairs={{0,3},{1,2},{2,1},{3,0},{4,7},{5,6},{6,5},{7,4},{8,11},{9,10},{10,... | collective-permute-start | bytes 1769480 | tf_op jit(solution)/shard_map/ppermute | solution.py:17
  321.7 26.7 %collective-permute-start.31 = (bf16[432,1152]{1,0:T(8,128)(2,1)S(1)}, bf16[432,1152]{1,0:T(8,128)(2,1)}, u32[]{:S(2)}, u32[]{:S(2)}) collective-permute-start(bf16[432,1152]{1,0:T(8,128)(2,1)S(1)} %copy-done.33), channel_id=1, source_target_pairs={{0,8},{4,12},{24,16},{28,20},{1,9},{5,13},{25,17},{29,21},{2,10},{... | collective-permute-start | bytes 2985992 | tf_op jit(solution)/shard_map/ppermute | solution.py:596
  326.9 38.2 %collective-permute-start.34 = (bf16[432,1152]{1,0:T(8,128)(2,1)}, bf16[432,1152]{1,0:T(8,128)(2,1)}, u32[]{:S(2)}, u32[]{:S(2)}) collective-permute-start(bf16[432,1152]{1,0:T(8,128)(2,1)} %get-tuple-element.105.refs_0_), channel_id=1, source_target_pairs={{8,16},{12,20},{16,8},{20,12},{9,17},{13,21},{17,9},{21,13},{10,18... | collective-permute-start | bytes 2985992 | tf_op jit(solution)/shard_map/ppermute | solution.py:596
  328.5 39.8 %collective-permute-start.35 = (bf16[432,1152]{1,0:T(8,128)(2,1)}, bf16[432,1152]{1,0:T(8,128)(2,1)}, u32[]{:S(2)}, u32[]{:S(2)}) collective-permute-start(bf16[432,1152]{1,0:T(8,128)(2,1)} %get-tuple-element.106.refs_2_), channel_id=1, source_target_pairs={{0,8},{4,12},{24,16},{28,20},{1,9},{5,13},{25,17},{29,21},{2,10},{... | collective-permute-start | bytes 2985992 | tf_op jit(solution)/shard_map/ppermute | solution.py:596
  382.5 161.1 %all-reduce.4.cloned.1.call-start = ((), (), s32[]{:S(2)}) async-start(), calls=%async_computation.1 | async-start | bytes 1556480 | tf_op jit(solution)/shard_map/psum | solution.py:992
  383.7 25.3 %collective-permute-start.43 = (bf16[432,1152]{1,0:T(8,128)(2,1)S(1)}, bf16[432,1152]{1,0:T(8,128)(2,1)S(1)}, u32[]{:S(2)}, u32[]{:S(2)}) collective-permute-start(bf16[432,1152]{1,0:T(8,128)(2,1)S(1)} %copy-done.82), channel_id=1, source_target_pairs={{0,8},{4,12},{24,16},{28,20},{8,0},{12,4},{16,24},{20,28},{1,9},{5... | collective-permute-start | bytes 2985992 | tf_op jit(solution)/shard_map/ppermute | solution.py:596
  386.2 22.8 %collective-permute-start.44 = (bf16[432,1152]{1,0:T(8,128)(2,1)S(1)}, bf16[432,1152]{1,0:T(8,128)(2,1)S(1)}, u32[]{:S(2)}, u32[]{:S(2)}) collective-permute-start(bf16[432,1152]{1,0:T(8,128)(2,1)S(1)} %copy-done.36), channel_id=1, source_target_pairs={{8,16},{12,20},{16,8},{20,12},{9,17},{13,21},{17,9},{21,13},{10,18... | collective-permute-start | bytes 2985992 | tf_op jit(solution)/shard_map/ppermute | solution.py:596
  386.9 43.4 %collective-permute-start.38 = (bf16[432,1152]{1,0:T(8,128)(2,1)}, bf16[432,1152]{1,0:T(8,128)(2,1)S(1)}, u32[]{:S(2)}, u32[]{:S(2)}) collective-permute-start(bf16[432,1152]{1,0:T(8,128)(2,1)} %get-tuple-element.110), channel_id=1, source_target_pairs={{0,8},{4,12},{24,16},{28,20},{8,0},{12,4},{16,24},{20,28},{1,9},{5... | collective-permute-start | bytes 2985992 | tf_op jit(solution)/shard_map/ppermute | solution.py:596
  388.9 41.4 %collective-permute-start.39 = (bf16[432,1152]{1,0:T(8,128)(2,1)S(1)}, bf16[432,1152]{1,0:T(8,128)(2,1)S(1)}, u32[]{:S(2)}, u32[]{:S(2)}) collective-permute-start(bf16[432,1152]{1,0:T(8,128)(2,1)S(1)} %copy-done.37), channel_id=1, source_target_pairs={{8,16},{12,20},{16,8},{20,12},{9,17},{13,21},{17,9},{21,13},{10,18... | collective-permute-start | bytes 2985992 | tf_op jit(solution)/shard_map/ppermute | solution.py:596
  415.0 36.6 %collective-permute-start.45 = (bf16[432,1152]{1,0:T(8,128)(2,1)}, bf16[432,1152]{1,0:T(8,128)(2,1)S(1)}, u32[]{:S(2)}, u32[]{:S(2)}) collective-permute-start(bf16[432,1152]{1,0:T(8,128)(2,1)} %get-tuple-element.120.refs_0_), channel_id=1, source_target_pairs={{8,0},{12,4},{16,24},{20,28},{9,1},{13,5},{17,25},{21,29},{10,2},{... | collective-permute-start | bytes 2985992 | tf_op jit(solution)/shard_map/ppermute | solution.py:596
  416.3 35.3 %collective-permute-start.46 = (bf16[432,1152]{1,0:T(8,128)(2,1)}, bf16[432,1152]{1,0:T(8,128)(2,1)S(1)}, u32[]{:S(2)}, u32[]{:S(2)}) collective-permute-start(bf16[432,1152]{1,0:T(8,128)(2,1)} %get-tuple-element.121.refs_2_), channel_id=1, source_target_pairs={{8,16},{12,20},{16,8},{20,12},{9,17},{13,21},{17,9},{21,13},{10,18... | collective-permute-start | bytes 2985992 | tf_op jit(solution)/shard_map/ppermute | solution.py:596
  436.4 36.5 %collective-permute-start.40 = (bf16[432,1152]{1,0:T(8,128)(2,1)}, bf16[432,1152]{1,0:T(8,128)(2,1)S(1)}, u32[]{:S(2)}, u32[]{:S(2)}) collective-permute-start(bf16[432,1152]{1,0:T(8,128)(2,1)} %get-tuple-element.113.refs_0_), channel_id=1, source_target_pairs={{8,0},{12,4},{16,24},{20,28},{9,1},{13,5},{17,25},{21,29},{10,2},{... | collective-permute-start | bytes 2985992 | tf_op jit(solution)/shard_map/ppermute | solution.py:596
  437.7 35.2 %collective-permute-start.41 = (bf16[432,1152]{1,0:T(8,128)(2,1)}, bf16[432,1152]{1,0:T(8,128)(2,1)S(1)}, u32[]{:S(2)}, u32[]{:S(2)}) collective-permute-start(bf16[432,1152]{1,0:T(8,128)(2,1)} %get-tuple-element.114.refs_2_), channel_id=1, source_target_pairs={{8,16},{12,20},{16,8},{20,12},{9,17},{13,21},{17,9},{21,13},{10,18... | collective-permute-start | bytes 2985992 | tf_op jit(solution)/shard_map/ppermute | solution.py:596
  438.4 41.0 %collective-permute-start.51 = (bf16[432,1152]{1,0:T(8,128)(2,1)}, bf16[432,1152]{1,0:T(8,128)(2,1)S(1)}, u32[]{:S(2)}, u32[]{:S(2)}) collective-permute-start(bf16[432,1152]{1,0:T(8,128)(2,1)} %get-tuple-element.127.refs_1_), channel_id=1, source_target_pairs={{0,4},{4,0},{8,12},{12,8},{16,20},{20,16},{24,28},{28,24},{1,5},{5... | collective-permute-start | bytes 2985992 | tf_op jit(solution)/shard_map/ppermute | solution.py:17
  451.6 29.1 %collective-permute-start.50 = (bf16[432,1152]{1,0:T(8,128)(2,1)S(1)}, bf16[432,1152]{1,0:T(8,128)(2,1)}, u32[]{:S(2)}, u32[]{:S(2)}) collective-permute-start(bf16[432,1152]{1,0:T(8,128)(2,1)S(1)} %copy-done.35), channel_id=1, source_target_pairs={{0,4},{4,0},{8,12},{12,8},{16,20},{20,16},{24,28},{28,24},{1,5},{5... | collective-permute-start | bytes 2985992 | tf_op jit(solution)/shard_map/ppermute | solution.py:17
  457.5 45.3 %collective-permute-start.49 = (bf16[432,1152]{1,0:T(8,128)(2,1)}, bf16[432,1152]{1,0:T(8,128)(2,1)}, u32[]{:S(2)}, u32[]{:S(2)}) collective-permute-start(bf16[432,1152]{1,0:T(8,128)(2,1)} %get-tuple-element.125.refs_0_), channel_id=1, source_target_pairs={{8,0},{12,4},{16,24},{20,28},{9,1},{13,5},{17,25},{21,29},{10,2},{... | collective-permute-start | bytes 2985992 | tf_op jit(solution)/shard_map/ppermute | solution.py:596
  478.9 27.2 %collective-permute-start.48 = (bf16[432,1152]{1,0:T(8,128)(2,1)}, bf16[432,1152]{1,0:T(8,128)(2,1)}, u32[]{:S(2)}, u32[]{:S(2)}) collective-permute-start(bf16[432,1152]{1,0:T(8,128)(2,1)} %get-tuple-element.123.refs_1_), channel_id=1, source_target_pairs={{0,4},{4,0},{8,12},{12,8},{16,20},{20,16},{24,28},{28,24},{1,5},{5... | collective-permute-start | bytes 2985992 | tf_op jit(solution)/shard_map/ppermute | solution.py:17
  478.9 27.2 %collective-permute-start.47 = (bf16[432,1152]{1,0:T(8,128)(2,1)S(1)}, bf16[432,1152]{1,0:T(8,128)(2,1)}, u32[]{:S(2)}, u32[]{:S(2)}) collective-permute-start(bf16[432,1152]{1,0:T(8,128)(2,1)S(1)} %copy-done.38), channel_id=1, source_target_pairs={{0,4},{4,0},{8,12},{12,8},{16,20},{20,16},{24,28},{28,24},{1,5},{5... | collective-permute-start | bytes 2985992 | tf_op jit(solution)/shard_map/ppermute | solution.py:17
  479.4 60.9 %collective-permute-start.42 = (bf16[432,1152]{1,0:T(8,128)(2,1)}, bf16[432,1152]{1,0:T(8,128)(2,1)}, u32[]{:S(2)}, u32[]{:S(2)}) collective-permute-start(bf16[432,1152]{1,0:T(8,128)(2,1)} %get-tuple-element.115.refs_0_), channel_id=1, source_target_pairs={{8,0},{12,4},{16,24},{20,28},{9,1},{13,5},{17,25},{21,29},{10,2},{... | collective-permute-start | bytes 2985992 | tf_op jit(solution)/shard_map/ppermute | solution.py:596
  506.1 38.0 %collective-permute-start.52 = (bf16[432,1152]{1,0:T(8,128)(2,1)}, bf16[432,1152]{1,0:T(8,128)(2,1)S(1)}, u32[]{:S(2)}, u32[]{:S(2)}) collective-permute-start(bf16[432,1152]{1,0:T(8,128)(2,1)} %get-tuple-element.128.refs_0_), channel_id=1, source_target_pairs={{0,4},{4,0},{8,12},{12,8},{16,20},{20,16},{24,28},{28,24},{1,5},{5... | collective-permute-start | bytes 2985992 | tf_op jit(solution)/shard_map/ppermute | solution.py:17
  (108 other events, 865.3 us)
Sparse Core Ops, SparseCore 0:
  382.6 44.7 reduce-scatter.3
  480.9 57.4 all-reduce.3

commit v7 on v6

--- a/solution.py
+++ b/solution.py
@@ -51,40 +51,33 @@
     return value.astype(jnp.int32).reshape(1)
 
 
-def packed(weights, gains=()):
+def packed(weights):
     half = weights[0].shape[0] // 2
     wide = sum(weight.shape[1] for weight in weights)
-    below = 16 if gains else 0
 
     def kernel(core_ref, *refs):
         out_ref = refs[-1]
-        if gains:
-            out_ref[half:, :] = jnp.zeros((below, wide), jnp.bfloat16)
-        for spot in range(len(gains)):
-            ref = refs[len(weights) + spot]
-            out_ref[half + spot : half + spot + 1, : ref.shape[1]] = ref[...]
         for side in range(2):
 
             @pl.when(core_ref[0] == side)
             def _():
                 at = 0
-                for ref in refs[: len(weights)]:
-                    out_ref[:half, at : at + ref.shape[1]] = ref[side * half : (side + 1) * half, :]
+                for ref in refs[:-1]:
+                    out_ref[:, at : at + ref.shape[1]] = ref[side * half : (side + 1) * half, :]
                     at += ref.shape[1]
 
-    arrays = list(weights) + [gain[None, :] for gain in gains]
     return pl.pallas_call(
         kernel,
         grid_spec=pltpu.PrefetchScalarGridSpec(
             num_scalar_prefetch=1,
             grid=(1,),
-            in_specs=[pl.BlockSpec(array.shape, lambda i, core_ref: (0, 0)) for array in arrays],
-            out_specs=pl.BlockSpec((half + below, wide), lambda i, core_ref: (0, 0)),
+            in_specs=[pl.BlockSpec(weight.shape, lambda i, core_ref: (0, 0)) for weight in weights],
+            out_specs=pl.BlockSpec((half, wide), lambda i, core_ref: (0, 0)),
         ),
-        out_shape=jax.ShapeDtypeStruct((half + below, wide), jnp.bfloat16),
+        out_shape=jax.ShapeDtypeStruct((half, wide), jnp.bfloat16),
         compiler_params=params(),
         name="pack",
-    )(scalar(lax.axis_index("replica") % 2), *arrays)
+    )(scalar(lax.axis_index("replica") % 2), *weights)
 
 
 def unpacked(weights, got, peers):
@@ -776,6 +769,18 @@
     return got, [swapped(part, "replica", 1) for part in got]
 
 
+def gathered(block):
+    group = lax.axis_size("fsdp")
+    blocks, near = [block] + [None] * (group - 1), []
+    for ring in range(1, group.bit_length()):
+        masks = [mask for mask in range(1, group) if bin(mask).count("1") == ring]
+        source = after(block, *near) if near else block
+        near = [swapped(source, "fsdp", mask) for mask in masks]
+        for mask, far in zip(masks, near):
+            blocks[mask] = far
+    return blocks
+
+
 def passed_along(block, axis, distance):
     devices = range(lax.axis_size(axis))
     route = [(i - distance, i) for i in devices if i - distance in devices]
@@ -848,11 +853,15 @@
     scale = head_size ** (-0.5)
     qkv_weights = (query_weight, key_weight, value_weight)
     wide = sum(weight.shape[1] for weight in qkv_weights)
-    gains = (norm_in, norm_attn, norm_ffn, norm_out, query_gain, key_gain)
-    block = packed(qkv_weights, gains)
-    got, peers = fetched(block)
+    got, peers = fetched(packed(qkv_weights))
+    gains = jnp.stack(
+        [
+            jnp.pad(gain, (0, own_model - gain.shape[0]))
+            for gain in (norm_in, norm_attn, norm_ffn, norm_out, query_gain, key_gain)
+        ]
+    )
+    gain_stack = jnp.stack([gains] + [swapped(gains, "fsdp", mask) for mask in masks])
     w_qkv = unpacked(qkv_weights, got, peers)
-    gain_stack = jnp.stack([part[-16:, :own_model] for part in [block] + got])
     gain_rows = jnp.stack(
         [lax.dynamic_index_in_dim(gain_stack, rank ^ i, 0, keepdims=False) for i in range(group)], axis=1
     )
@@ -889,22 +898,27 @@
     attended = contract(mixed, w_out, 1, 1)
     resid = residual_in + normed(attended, gain_attn)
     ffn_in = normed(resid, gain_ffn).astype(jnp.bfloat16)
-    ffn_blocks = [ffn_in] + [swapped(ffn_in, "fsdp", mask) for mask in masks]
-    hiddens, slopes, acts, parts = [], [], [], []
-    for mask in range(group):
-        hidden, slope, act, part = ffn_forward(ffn_blocks[mask], gate_weight, up_weight, down_weight)
-        parts.append(part)
-        hiddens.append(hidden)
-        slopes.append(slope)
-        acts.append(act)
-    parts = parts[:1] + [swapped(parts[mask], "fsdp", mask) for mask in masks]
-    branch = sum(part.astype(jnp.float32) for part in parts)
+    ffn_blocks = gathered(ffn_in)
+    hiddens, slopes, acts, parts = {}, {}, {}, {}
+    rings = sorted(range(group), key=lambda mask: (bin(mask).count("1"), mask))
+    last = None
+    for mask in rings[1:] + [0]:
+        if last is not None:
+            ffn_blocks[mask] = after(ffn_blocks[mask], parts[last])
+        hiddens[mask], slopes[mask], acts[mask], parts[mask] = ffn_forward(
+            ffn_blocks[mask], gate_weight, up_weight, down_weight
+        )
+        last = mask
+    branch = sum(
+        (swapped(parts[mask], "fsdp", mask) if mask else parts[mask]).astype(jnp.float32)
+        for mask in range(group)
+    )
     result = resid + normed(branch, gain_out)
     hidden_out = result.astype(jnp.bfloat16)
     grad_result = out_grad.astype(jnp.float32)
     grad_branch, grad_gain_out = norm_back(branch, gain_out, grad_result)
     grad_branch_low = grad_branch.astype(jnp.bfloat16)
-    pieces = [grad_branch_low] + [swapped(grad_branch_low, "fsdp", mask) for mask in masks]
+    pieces = gathered(grad_branch_low)
     units = gate_weight.shape[0]
     lines = [Line(), Line()]
 
@@ -914,36 +928,32 @@
         return [(key, [(mine, spot), (far, spot)]) for spot, key in enumerate(keys)]
 
     grad_gates, grad_uppers, returned = {}, {}, {}
-    early = group // 2
-    for mask in range(early):
+    final = rings[-1]
+    last = None
+    for mask in rings[:-1]:
+        if last is not None:
+            pieces[mask] = after(pieces[mask], part)
         grad_gates[mask], grad_uppers[mask], part = ffn_backward(
             pieces[mask], gate_weight, up_weight, down_weight, slopes[mask], acts[mask]
         )
-        pieces[mask + 1] = after(pieces[mask + 1], part)
         returned[mask] = swapped(part, "fsdp", mask) if mask else part
-    waiting = fresh(["down"], *weight_grad([hiddens], pieces))
-    for mask in range(1, early):
-        pieces[early] = after(pieces[early], returned[mask])
-    pieces[early] = lines[0].advance([waiting.pop(0)], pieces[early])
-    late = range(early, group)
+        last = mask
+    pieces[final] = after(pieces[final], part)
+    waiting = fresh(
+        ["down"], *weight_grad([[hiddens[i] for i in range(group)]], [pieces[i] for i in range(group)])
+    )
     gate_parts, upper_parts, parts = ffn_backward_blocks(
-        [pieces[mask] for mask in late],
-        gate_weight,
-        up_weight,
-        down_weight,
-        [slopes[mask] for mask in late],
-        [acts[mask] for mask in late],
-    )
-    for spot, mask in enumerate(late):
-        grad_gates[mask], grad_uppers[mask] = gate_parts[spot], upper_parts[spot]
-        returned[mask] = swapped(parts[spot], "fsdp", mask)
-    if waiting:
-        grad_gates[early] = lines[1].advance([waiting.pop(0)], grad_gates[early])
-    grad_gates[0] = after(grad_gates[0], *lines[0].arrived())
+        [pieces[final]], gate_weight, up_weight, down_weight, [slopes[final]], [acts[final]]
+    )
+    grad_gates[final], grad_uppers[final] = gate_parts[0], upper_parts[0]
+    returned[final] = swapped(parts[0], "fsdp", final)
+    grad_gates[final] = after(grad_gates[final], *[returned[mask] for mask in rings[1:-1]])
+    grad_gates[final] = lines[0].advance([waiting.pop(0)], grad_gates[final])
     other, mine = weight_grad(
         [[grad_gates[i] for i in range(group)], [grad_uppers[i] for i in range(group)]], ffn_blocks
     )
-    other = after(other, *lines[1].arrived(), *[returned[mask] for mask in late])
+    other = after(other, *lines[0].arrived(), returned[final])
+    other = lines[1].advance([waiting.pop(0)] if waiting else [], other)
     waiting = fresh(["gate", "up"], other, mine)
 
     def advance(spot, gate=None):
@@ -962,6 +972,8 @@
     grad_far = advance(1, grad_far)
     backs = []
     for step in range(1, hops + 1):
+        if step == 2:
+            grad_far = after(grad_far, *lines[0].arrived())
         grad_far = passed_along(grad_far, "fsdp", -1)
         backs.append(grad_far[-rows:])
         grad_far = grad_far[:-rows]
@@ -984,24 +996,21 @@
         [grad_gain_attn, grad_gain_ffn, grad_gain_out[None, :], grad_gain_query],
         group,
     )
-    other = advance(1, other)
+    other = advance(1, after(other, *lines[0].arrived()))
     chip = added(mine, swapped(other, "replica", 1))
     owned = lax.psum_scatter(chip, "fsdp", scatter_dimension=0, tiled=True)[0]
-    places = lax.axis_size("replica") // 2
-    cores = [[2 * place + core for place in range(places)] for core in range(2)]
-    owned = lax.psum(owned, "replica", axis_index_groups=cores)
-    advance(0)
-    advance(1)
     advance(0)
     advance(1)
     while waiting:
         advance(0)
+    lines[0].advance([("weights", [owned])])
+    advance(1)
     grad_down = whole_grad(lines, "down", units)
     grad_down = lines[0].advance([], grad_down)
     grad_gate_w = whole_grad(lines, "gate", units)
     grad_gate_w = lines[1].advance([], grad_gate_w)
     grad_up_w = whole_grad(lines, "up", units)
-    owned = core_join(owned, 1).astype(jnp.float32)
+    owned = core_join(lines[0].finished("weights"), 1).astype(jnp.float32)
     inner = heads * head_size
     columns = [0, inner, inner + head_size, inner + 2 * head_size, wide + inner]
     owned_query, owned_key, owned_value, owned_out = (

time: 573 us -> 557 us (0.972)
  waiting for transfers between devices: 237 us -> 173 us
  matrix products: 46.6 us -> 65.1 us
  starting transfers between devices: 60.2 us -> 78.6 us
  local copies, waits for them, and re-layouts: 41.1 us -> 48.8 us
    ppermute x34 -> x37, waiting for transfers between devices: 107 us -> 54.3 us  [swapped(): return lax.ppermute(block, axis, route)]
    dot_general x19 -> x22, matrix products: 44.3 us -> 62.9 us  [contract(): lax.dot_general(left, right, (((left_dim,), (right_dim,)), ((), ())), pre...]
    ppermute x16 -> x19, starting transfers between devices: 27.3 us -> 44.5 us  [exchanged(): return lax.ppermute(block, 'replica', route)]
    ppermute x16 -> x19, waiting for transfers between devices: 119 us -> 106 us  [exchanged(): return lax.ppermute(block, 'replica', route)]
    unnamed x168 -> x204, local copies, waits for them, and re-layouts: 21.8 us -> 32.9 us
    pallas_call x12 -> x14, Pallas kernels: 50.8 us -> 56.1 us  [advance(): pl.pallas_call(kernel, grid_spec=pltpu.PrefetchScalarGridSpec(num_scalar_...]
    ppermute x34 -> x37, starting transfers between devices: 24.3 us -> 25.4 us  [swapped(): return lax.ppermute(block, axis, route)]
  transfers between devices with their start and end apart: 56 -> 61, of which waited for: 28 -> 28; matrix products, arithmetic and copies ran while one was open for 10% -> 14% of each run, Pallas kernels for 19% -> 23%
where the time goes in v7:
time: 557 us; the launch traced here: 550 us
  waiting for transfers between devices  173 us (31%)
  Pallas kernels  156 us (28%)
  starting transfers between devices  78.6 us (14%)
  matrix products  65.1 us (12%)
  local copies, waits for them, and re-layouts  48.8 us (9%)
  between operations  15.7 us (3%)
  other arithmetic  12.7 us (2%)
    ppermute x19, waiting for transfers between devices, exchanged(): return lax.ppermute(block, 'replica', route)  106 us
    dot_general x22, matrix products, contract(): lax.dot_general(left, right, (((left_dim,), (right_dim,)), ((), ())), pre...  62.9 us
    pallas_call x14, Pallas kernels, advance(): pl.pallas_call(kernel, grid_spec=pltpu.PrefetchScalarGridSpec(num_scalar_...  56.1 us
    ppermute x37, waiting for transfers between devices, swapped(): return lax.ppermute(block, axis, route)  54.3 us
    ppermute x19, starting transfers between devices, exchanged(): return lax.ppermute(block, 'replica', route)  44.5 us
    unnamed x204, local copies, waits for them, and re-layouts  32.9 us
    pallas_call x2, Pallas kernels, weight_grad(): pl.pallas_call(kernel, grid_spec=pltpu.PrefetchScalarGridSpec(num_scalar_...  27.7 us
    ppermute x37, starting transfers between devices, swapped(): return lax.ppermute(block, axis, route)  25.4 us
  transfers between devices with their start and end apart: 61, of which 28 were waited for; matrix products, arithmetic and copies ran while one was open for 14% of the time, Pallas kernels for 23%

profile of v7, /device:TPU:0, one launch (start us, length us, event | category | flops | bytes accessed | tf_op | source)
XLA Modules:
  0.0 549.9 jit_solution(2688431649964519345)
XLA Ops:
  27.2 5.0 collective-permute-done.5.refs_5_
  32.2 7.7 %collective-permute-done.4.refs_4_ = bf16[144,1536]{1,0:T(8,128)(2,1)S(1)} collective-permute-done((bf16[144,1536]{1,0:T(8,128)(2,1)}, bf16[144,1536]{1,0:T(8,128)(2,1)S(1)}, u32[]{:S(2)}, u32[]{:S(2)}) %collective-permute-start.4) | collective-permute-done | bytes 442400 | tf_op jit(solution)/shard_map/ppermute | solution.py:17
  67.9 6.4 %collective-permute-done.9 = bf16[256,512]{1,0:T(8,128)(2,1)S(1)} collective-permute-done((bf16[256,512]{1,0:T(8,128)(2,1)S(1)}, bf16[256,512]{1,0:T(8,128)(2,1)S(1)}, u32[]{:S(2)}, u32[]{:S(2)}) %collective-permute-start.9) | collective-permute-done | bytes 262176 | tf_op jit(solution)/shard_map/ppermute | solution.py:787
  75.3 5.9 %attention_forward.1 = (bf16[256,1024]{1,0:T(8,128)(2,1)}, bf16[256,1024]{1,0:T(8,128)(2,1)}) custom-call(f32[256,1536]{1,0:T(8,128)} %copy-done.6, bf16[1,256]{1,0:T(2,128)(2,1)} %broadcast_in_dim_reshape_squeeze.2.gain_ref, f32[256,128]{1,0:T(8,128)} %get-tuple-element.175.cos_ref.refs_4_, f32[256,128]{1,0:T(8,128)} %get-tuple-element.174.sin_ref.refs_5_, ...), custom_call_target="tpu_custom_call" | custom-call | tf_op jit(solution)/shard_map/attention_forward/pallas_call | solution.py:490
  93.7 12.6 %collective-permute-done.18.refs_2_.refs_0_ = bf16[256,1152]{1,0:T(8,128)(2,1)S(1)} collective-permute-done((bf16[256,1152]{1,0:T(8,128)(2,1)S(1)}, bf16[256,1152]{1,0:T(8,128)(2,1)S(1)}, u32[]{:S(2)}, u32[]{:S(2)}) %collective-permute-start.18) | collective-permute-done | bytes 589856 | tf_op jit(solution)/shard_map/ppermute | solution.py:17
  148.4 8.3 %collective-permute-done.21 = bf16[256,1152]{1,0:T(8,128)(2,1)} collective-permute-done((bf16[256,1152]{1,0:T(8,128)(2,1)}, bf16[256,1152]{1,0:T(8,128)(2,1)}, u32[]{:S(2)}, u32[]{:S(2)}) %collective-permute-start.21) | collective-permute-done | bytes 589856 | tf_op jit(solution)/shard_map/ppermute | solution.py:17
  176.6 5.9 %multiply_convert_fusion.4 = (bf16[1728,256]{1,0:T(8,128)(2,1)S(1)}, bf16[1728,256]{1,0:T(8,128)(2,1)S(1)}) fusion(f32[1728,256]{1,0:T(8,128)} %copy-done.100, f32[1728,256]{1,0:T(8,128)} %get-tuple-element.179, bf16[256,1152]{1,0:T(8,128)(2,1)} %after.18.refs_1_, bf16[1728,1152]{1,0:T(8,128)(2,1)} %refs_3_.1), kind=kOutput, calls=%fused_computation.27 | convolution fusion | flops 1030717440 | bytes 9879552 | tf_op jit(solution)/shard_map/dot_general | solution.py:791
  187.6 5.7 %multiply_convert_fusion.1 = (bf16[1728,256]{1,0:T(8,128)(2,1)S(1)}, bf16[1728,256]{1,0:T(8,128)(2,1)S(1)}) fusion(f32[1728,256]{1,0:T(8,128)} %copy-done.99, f32[1728,256]{1,0:T(8,128)} %get-tuple-element.181, bf16[256,1152]{1,0:T(8,128)(2,1)} %after.19.refs_2_, bf16[1728,1152]{1,0:T(8,128)(2,1)} %refs_3_.1), kind=kOutput, calls=%fused_computation.24 | convolution fusion | flops 1030717440 | bytes 9879552 | tf_op jit(solution)/shard_map/dot_general | solution.py:791
  199.1 10.0 %weight_grad.2 = (bf16[2,432,1152]{2,1,0:T(8,128)(2,1)}, bf16[2,432,1152]{2,1,0:T(8,128)(2,1)}) custom-call(s32[1]{0:T(128)} %bitcast.8.core_ref, bf16[256,1152]{1,0:T(8,128)(2,1)} %copy-done.14, bf16[256,1152]{1,0:T(8,128)(2,1)} %after.18.refs_1_, bf16[256,1152]{1,0:T(8,128)(2,1)} %after.19.refs_2_, bf16[256,1152]{1,0:T(8,128)(2,1)} %after.21.refs_3_.refs_0_, ...), custom_call_target="tpu_custom_call" | custom-call | tf_op jit(solution)/shard_map/weight_grad/pallas_call | solution.py:419
  211.7 11.6 %ffn_backward.1 = (bf16[1728,256]{1,0:T(8,128)(2,1)}, bf16[1728,256]{1,0:T(8,128)(2,1)}, bf16[256,1152]{1,0:T(8,128)(2,1)}) custom-call(bf16[256,1152]{1,0:T(8,128)(2,1)} %after.21.refs_3_.refs_0_, bf16[1728,1152]{1,0:T(8,128)(2,1)} %refs_1_.5, bf16[1728,1152]{1,0:T(8,128)(2,1)} %refs_2_.5, bf16[1728,1152]{1,0:T(8,128)(2,1)} %refs_3_.1, ...), custom_call_target="tpu_custom_call" | custom-call | tf_op jit(solution)/shard_map/ffn_backward/pallas_call | solution.py:197
  236.7 17.7 %weight_grad.3 = (bf16[4,432,1152]{2,1,0:T(8,128)(2,1)}, bf16[4,432,1152]{2,1,0:T(8,128)(2,1)}) custom-call(s32[1]{0:T(128)} %bitcast.8.core_ref, bf16[256,1152]{1,0:T(8,128)(2,1)} %after.17.refs_0_, bf16[256,1152]{1,0:T(8,128)(2,1)} %copy-done.49, bf16[256,1152]{1,0:T(8,128)(2,1)} %after.15.refs_2_, bf16[256,1152]{1,0:T(8,128)(2,1)} %after.16.refs_3_, ...), custom_call_target="tpu_custom_call" | custom-call | tf_op jit(solution)/shard_map/weight_grad/pallas_call | solution.py:419
  266.8 6.4 %resid_backward.1 = (f32[256,1152]{1,0:T(8,128)}, bf16[256,1152]{1,0:T(8,128)(2,1)}, bf16[256,1024]{1,0:T(8,128)(2,1)}, f32[1,1152]{1,0:T(1,128)}, f32[1,1152]{1,0:T(1,128)}) custom-call(bf16[256,1152]{1,0:T(8,128)(2,1)} %fusion.1.refs_1_.refs_0_, bf16[256,1152]{1,0:T(8,128)(2,1)} %copy-done.51, bf16[256,1152]{1,0:T(8,128)(2,1)} %copy-done.52, ...), custom_call_target="tpu_custom_call" | custom-call | tf_op jit(solution)/shard_map/resid_backward/pallas_call | solution.py:253
  282.2 8.9 %attention_backward.1 = (bf16[256,1024]{1,0:T(8,128)(2,1)}, f32[1,256]{1,0:T(1,128)}, bf16[512,512]{1,0:T(8,128)(2,1)}, f32[256,512]{1,0:T(8,128)}) custom-call(f32[256,1536]{1,0:T(8,128)} %copy-done.6, bf16[1,256]{1,0:T(2,128)(2,1)} %broadcast_in_dim_reshape_squeeze.2.gain_ref, f32[256,128]{1,0:T(8,128)} %get-tuple-element.175.cos_ref.refs_4_, ...), custom_call_target="tpu_custom_call" | custom-call | tf_op jit(solution)/shard_map/attention_backward/pallas_call | solution.py:564
  297.6 11.3 %collective-permute-done.33.refs_3_.refs_2_ = bf16[432,1152]{1,0:T(8,128)(2,1)S(1)} collective-permute-done((bf16[432,1152]{1,0:T(8,128)(2,1)}, bf16[432,1152]{1,0:T(8,128)(2,1)S(1)}, u32[]{:S(2)}, u32[]{:S(2)}) %collective-permute-start.33) | collective-permute-done | bytes 995360 | tf_op jit(solution)/shard_map/ppermute | solution.py:589
  309.8 5.6 %line_step.17 = (bf16[432,1152]{1,0:T(8,128)(2,1)}, bf16[432,1152]{1,0:T(8,128)(2,1)}, bf16[432,1152]{1,0:T(8,128)(2,1)}, bf16[432,1152]{1,0:T(8,128)(2,1)}, f32[256,512]{1,0:T(8,128)}) custom-call(s32[1]{0:T(128)} %bitcast.19.place_ref, bf16[432,1152]{1,0:T(8,128)(2,1)} %get-tuple-element.84.refs_0_, ...), custom_call_target="tpu_custom_call", output_to_operand_aliasing={{4}: (7, {})} | custom-call | tf_op jit(solution)/shard_map/line_step/pallas_call | solution.py:674
  320.2 6.4 %collective-permute-start.42 = (bf16[432,1152]{1,0:T(8,128)(2,1)}, bf16[432,1152]{1,0:T(8,128)(2,1)}, u32[]{:S(2)}, u32[]{:S(2)}) collective-permute-start(bf16[432,1152]{1,0:T(8,128)(2,1)} %get-tuple-element.108.refs_2_), channel_id=1, source_target_pairs={{0,8},{4,12},{24,16},{28,20},{1,9},{5,13},{25,17},{29,21},{2,10},{... | collective-permute-start | bytes 2985992 | tf_op jit(solution)/shard_map/ppermute | solution.py:589
  330.6 6.0 %collective-permute-done.36.refs_2_ = bf16[256,512]{1,0:T(8,128)(2,1)S(1)} collective-permute-done((bf16[256,512]{1,0:T(8,128)(2,1)}, bf16[256,512]{1,0:T(8,128)(2,1)S(1)}, u32[]{:S(2)}, u32[]{:S(2)}) %collective-permute-start.36) | collective-permute-done | bytes 262176 | tf_op jit(solution)/shard_map/ppermute | solution.py:787
  337.3 10.5 %input_backward.1 = (bf16[4,304,1280]{2,1,0:T(8,128)(2,1)}, bf16[4,304,1280]{2,1,0:T(8,128)(2,1)}, f32[256,1152]{1,0:T(8,128)}) custom-call(s32[1]{0:T(128)} %bitcast.8.core_ref, f32[256,512]{1,0:T(8,128)} %get-tuple-element.89.refs_0_, bf16[256,512]{1,0:T(8,128)(2,1)} %get-tuple-element.166.refs_1_, bf16[256,512]{1,0:T(8,128)(2,1)} %copy-done.87, ...), custom_call_target="tpu_custom_call" | custom-call | tf_op jit(solution)/shard_map/input_backward/pallas_call | solution.py:353
  349.0 11.5 %collective-permute-done.42.refs_3_ = bf16[432,1152]{1,0:T(8,128)(2,1)} collective-permute-done((bf16[432,1152]{1,0:T(8,128)(2,1)}, bf16[432,1152]{1,0:T(8,128)(2,1)}, u32[]{:S(2)}, u32[]{:S(2)}) %collective-permute-start.42) | collective-permute-done | bytes 995360 | tf_op jit(solution)/shard_map/ppermute | solution.py:589
  360.6 5.9 %line_step.20 = (bf16[432,1152]{1,0:T(8,128)(2,1)}, bf16[432,1152]{1,0:T(8,128)(2,1)}, bf16[432,1152]{1,0:T(8,128)(2,1)}, bf16[432,1152]{1,0:T(8,128)(2,1)}, bf16[4,304,1280]{2,1,0:T(8,128)(2,1)}) custom-call(s32[1]{0:T(128)} %bitcast.19.place_ref, bf16[432,1152]{1,0:T(8,128)(2,1)} %get-tuple-element.107.refs_0_, ...), custom_call_target="tpu_custom_call", output_to_operand_aliasing={{4}: (7, {})} | custom-call | tf_op jit(solution)/shard_map/line_step/pallas_call | solution.py:674
  366.5 5.8 %collective-permute-done.43 = bf16[4,304,1280]{2,1,0:T(8,128)(2,1)S(1)} collective-permute-done((bf16[4,304,1280]{2,1,0:T(8,128)(2,1)}, bf16[4,304,1280]{2,1,0:T(8,128)(2,1)S(1)}, u32[]{:S(2)}, u32[]{:S(2)}) %collective-permute-start.43) | collective-permute-done | bytes 3112992 | tf_op jit(solution)/shard_map/ppermute | solution.py:17
  380.0 5.0 line_step.19
  387.9 14.3 %collective-permute-done.46.refs_1_ = bf16[432,1152]{1,0:T(8,128)(2,1)S(1)} collective-permute-done((bf16[432,1152]{1,0:T(8,128)(2,1)}, bf16[432,1152]{1,0:T(8,128)(2,1)S(1)}, u32[]{:S(2)}, u32[]{:S(2)}) %collective-permute-start.46) | collective-permute-done | bytes 995360 | tf_op jit(solution)/shard_map/ppermute | solution.py:589
  408.3 14.8 %collective-permute-done.39.refs_1_ = bf16[432,1152]{1,0:T(8,128)(2,1)S(1)} collective-permute-done((bf16[432,1152]{1,0:T(8,128)(2,1)}, bf16[432,1152]{1,0:T(8,128)(2,1)S(1)}, u32[]{:S(2)}, u32[]{:S(2)}) %collective-permute-start.39) | collective-permute-done | bytes 995360 | tf_op jit(solution)/shard_map/ppermute | solution.py:589
  429.7 5.7 %collective-permute-start.45 = (bf16[304,1280]{1,0:T(8,128)(2,1)}, bf16[304,1280]{1,0:T(8,128)(2,1)S(1)}, u32[]{:S(2)}, u32[]{:S(2)}) collective-permute-start(bf16[304,1280]{1,0:T(8,128)(2,1)} %get-tuple-element.112.refs_2_), channel_id=1, source_target_pairs={{0,8},{4,12},{24,16},{28,20},{1,9},{5,13},{25,17},{29,21},{2,10},{... | collective-permute-start | bytes 2334728 | tf_op jit(solution)/shard_map/ppermute | solution.py:589
  438.6 5.6 %whole_grad.3.refs_4_ = f32[1728,1152]{1,0:T(8,128)} custom-call(s32[1]{0:T(128)} %bitcast.8.core_ref, bf16[432,1152]{1,0:T(8,128)(2,1)} %get-tuple-element.113.refs_0_, bf16[432,1152]{1,0:T(8,128)(2,1)} %get-tuple-element.118.refs_1_, bf16[432,1152]{1,0:T(8,128)(2,1)} %copy-done.59, bf16[432,1152]{1,0:T(8,128)(2,1)} %copy-done.61), custom_call_target="tpu_custom_call" | custom-call | tf_op jit(solution)/shard_map/whole_grad/pallas_call | solution.py:740
  444.2 7.5 %collective-permute-done.45.refs_3_ = bf16[304,1280]{1,0:T(8,128)(2,1)S(1)} collective-permute-done((bf16[304,1280]{1,0:T(8,128)(2,1)}, bf16[304,1280]{1,0:T(8,128)(2,1)S(1)}, u32[]{:S(2)}, u32[]{:S(2)}) %collective-permute-start.45) | collective-permute-done | bytes 778272 | tf_op jit(solution)/shard_map/ppermute | solution.py:589
  461.6 14.8 %collective-permute-done.53.refs_1_ = bf16[432,1152]{1,0:T(8,128)(2,1)S(1)} collective-permute-done((bf16[432,1152]{1,0:T(8,128)(2,1)S(1)}, bf16[432,1152]{1,0:T(8,128)(2,1)S(1)}, u32[]{:S(2)}, u32[]{:S(2)}) %collective-permute-start.53) | collective-permute-done | bytes 995360 | tf_op jit(solution)/shard_map/ppermute | solution.py:589
  490.7 5.6 %whole_grad.4.refs_2_ = f32[1728,1152]{1,0:T(8,128)} custom-call(s32[1]{0:T(128)} %bitcast.8.core_ref, bf16[432,1152]{1,0:T(8,128)(2,1)} %get-tuple-element.123.refs_0_, bf16[432,1152]{1,0:T(8,128)(2,1)} %get-tuple-element.124.refs_1_, bf16[432,1152]{1,0:T(8,128)(2,1)} %copy-done.68, bf16[432,1152]{1,0:T(8,128)(2,1)} %copy-done.66), custom_call_target="tpu_custom_call" | custom-call | tf_op jit(solution)/shard_map/whole_grad/pallas_call | solution.py:740
  496.3 13.5 %collective-permute-done.55.refs_1_ = bf16[432,1152]{1,0:T(8,128)(2,1)S(1)} collective-permute-done((bf16[432,1152]{1,0:T(8,128)(2,1)}, bf16[432,1152]{1,0:T(8,128)(2,1)S(1)}, u32[]{:S(2)}, u32[]{:S(2)}) %collective-permute-start.55) | collective-permute-done | bytes 995360 | tf_op jit(solution)/shard_map/ppermute | solution.py:589
  514.5 11.1 %collective-permute-done.51.refs_1_ = bf16[304,1280]{1,0:T(8,128)(2,1)S(1)} collective-permute-done((bf16[304,1280]{1,0:T(8,128)(2,1)}, bf16[304,1280]{1,0:T(8,128)(2,1)S(1)}, u32[]{:S(2)}, u32[]{:S(2)}) %collective-permute-start.51) | collective-permute-done | bytes 778272 | tf_op jit(solution)/shard_map/ppermute | solution.py:589
  530.7 5.6 %whole_grad.5 = f32[1728,1152]{1,0:T(8,128)} custom-call(s32[1]{0:T(128)} %bitcast.8.core_ref, bf16[432,1152]{1,0:T(8,128)(2,1)} %get-tuple-element.126.refs_0_, bf16[432,1152]{1,0:T(8,128)(2,1)} %get-tuple-element.127.refs_1_, bf16[432,1152]{1,0:T(8,128)(2,1)} %copy-done.64, bf16[432,1152]{1,0:T(8,128)(2,1)} %copy-done.62), custom_call_target="tpu_custom_call" | custom-call | tf_op jit(solution)/shard_map/whole_grad/pallas_call | solution.py:740
  (419 shorter events, 255.9 us)
Async XLA Ops:
  7.2 415.9 %reduce-scatter.4.cloned.1.call-start = ((), (), s32[]{:S(2)}) async-start(), calls=%async_computation.1 | async-start | bytes 3891200
  20.8 19.1 %collective-permute-start.4 = (bf16[144,1536]{1,0:T(8,128)(2,1)}, bf16[144,1536]{1,0:T(8,128)(2,1)S(1)}, u32[]{:S(2)}, u32[]{:S(2)}) collective-permute-start(bf16[144,1536]{1,0:T(8,128)(2,1)} %pack.2), channel_id=1, source_target_pairs={{0,2},{1,3},{2,0},{3,1},{4,6},{5,7},{6,4},{7,5},{8,10},{9,11},{10,... | collective-permute-start | bytes 1327112 | tf_op jit(solution)/shard_map/ppermute | solution.py:17
  61.0 20.2 %collective-permute-start.16 = (bf16[144,1024]{1,0:T(8,128)(2,1)}, bf16[144,1024]{1,0:T(8,128)(2,1)S(1)}, u32[]{:S(2)}, u32[]{:S(2)}) collective-permute-start(bf16[144,1024]{1,0:T(8,128)(2,1)} %collective-permute-done.13.refs_3_), channel_id=1, source_target_pairs={{0,4},{4,0},{8,12},{12,8},{16,20},{20,16},{24,28},{28,24},{1,5},{5... | collective-permute-start | bytes 884744 | tf_op jit(solution)/shard_map/ppermute | solution.py:17
  64.0 17.2 %collective-permute-start.15 = (bf16[144,1024]{1,0:T(8,128)(2,1)}, bf16[144,1024]{1,0:T(8,128)(2,1)S(1)}, u32[]{:S(2)}, u32[]{:S(2)}) collective-permute-start(bf16[144,1024]{1,0:T(8,128)(2,1)} %collective-permute-done.12.refs_2_), channel_id=1, source_target_pairs={{0,4},{4,0},{8,12},{12,8},{16,20},{20,16},{24,28},{28,24},{1,5},{5... | collective-permute-start | bytes 884744 | tf_op jit(solution)/shard_map/ppermute | solution.py:17
  108.6 22.1 %collective-permute-start.19 = (bf16[256,1152]{1,0:T(8,128)(2,1)}, bf16[256,1152]{1,0:T(8,128)(2,1)S(1)}, u32[]{:S(2)}, u32[]{:S(2)}) collective-permute-start(bf16[256,1152]{1,0:T(8,128)(2,1)} %after.14), channel_id=1, source_target_pairs={{0,3},{1,2},{2,1},{3,0},{4,7},{5,6},{6,5},{7,4},{8,11},{9,10},{10,... | collective-permute-start | bytes 1769480 | tf_op jit(solution)/shard_map/ppermute | solution.py:17
  118.0 30.3 %collective-permute-start.20 = (bf16[256,1152]{1,0:T(8,128)(2,1)}, bf16[256,1152]{1,0:T(8,128)(2,1)S(1)}, u32[]{:S(2)}, u32[]{:S(2)}) collective-permute-start(bf16[256,1152]{1,0:T(8,128)(2,1)} %convolution_convert_fusion.3.refs_1_), channel_id=1, source_target_pairs={{0,1},{1,0},{2,3},{3,2},{4,5},{5,4},{6,7},{7,6},{8,9},{9,8},{10,11... | collective-permute-start | bytes 1769480 | tf_op jit(solution)/shard_map/ppermute | solution.py:17
  129.8 26.8 %collective-permute-start.21 = (bf16[256,1152]{1,0:T(8,128)(2,1)}, bf16[256,1152]{1,0:T(8,128)(2,1)}, u32[]{:S(2)}, u32[]{:S(2)}) collective-permute-start(bf16[256,1152]{1,0:T(8,128)(2,1)} %convolution_convert_fusion.2.refs_1_), channel_id=1, source_target_pairs={{0,2},{1,3},{2,0},{3,1},{4,6},{5,7},{6,4},{7,5},{8,10},{9,11},{10,... | collective-permute-start | bytes 1769480 | tf_op jit(solution)/shard_map/ppermute | solution.py:17
  175.6 22.7 %collective-permute-start.25 = (bf16[256,1152]{1,0:T(8,128)(2,1)}, bf16[256,1152]{1,0:T(8,128)(2,1)S(1)}, u32[]{:S(2)}, u32[]{:S(2)}) collective-permute-start(bf16[256,1152]{1,0:T(8,128)(2,1)} %after.20), channel_id=1, source_target_pairs={{0,3},{1,2},{2,1},{3,0},{4,7},{5,6},{6,5},{7,4},{8,11},{9,10},{10,... | collective-permute-start | bytes 1769480 | tf_op jit(solution)/shard_map/ppermute | solution.py:17
  209.2 18.1 %collective-permute-start.26 = (bf16[2,432,1152]{2,1,0:T(8,128)(2,1)}, bf16[2,432,1152]{2,1,0:T(8,128)(2,1)S(1)}, u32[]{:S(2)}, u32[]{:S(2)}) collective-permute-start(bf16[2,432,1152]{2,1,0:T(8,128)(2,1)} %get-tuple-element.74), channel_id=1, source_target_pairs={{0,4},{4,0},{8,12},{12,8},{16,20},{20,16},{24,28},{28,24},{1,5},{5... | collective-permute-start | bytes 5971976 | tf_op jit(solution)/shard_map/ppermute | solution.py:17
  232.0 24.7 %collective-permute-start.29 = (bf16[432,1152]{1,0:T(8,128)(2,1)}, bf16[432,1152]{1,0:T(8,128)(2,1)S(1)}, u32[]{:S(2)}, u32[]{:S(2)}) collective-permute-start(bf16[432,1152]{1,0:T(8,128)(2,1)} %get-tuple-element.76.refs_0_), channel_id=1, source_target_pairs={{0,8},{4,12},{24,16},{28,20},{1,9},{5,13},{25,17},{29,21},{2,10},{... | collective-permute-start | bytes 2985992 | tf_op jit(solution)/shard_map/ppermute | solution.py:589
  235.7 18.6 %collective-permute-start.30 = (bf16[256,1152]{1,0:T(8,128)(2,1)S(1)}, bf16[256,1152]{1,0:T(8,128)(2,1)S(1)}, u32[]{:S(2)}, u32[]{:S(2)}) collective-permute-start(bf16[256,1152]{1,0:T(8,128)(2,1)S(1)} %copy-done.98), channel_id=1, source_target_pairs={{0,3},{1,2},{2,1},{3,0},{4,7},{5,6},{6,5},{7,4},{8,11},{9,10},{10,... | collective-permute-start | bytes 1769480 | tf_op jit(solution)/shard_map/ppermute | solution.py:17
  261.0 30.1 %collective-permute-start.34 = (bf16[432,1152]{1,0:T(8,128)(2,1)}, bf16[432,1152]{1,0:T(8,128)(2,1)S(1)}, u32[]{:S(2)}, u32[]{:S(2)}) collective-permute-start(bf16[432,1152]{1,0:T(8,128)(2,1)} %get-tuple-element.90.refs_0_), channel_id=1, source_target_pairs={{0,8},{4,12},{24,16},{28,20},{1,9},{5,13},{25,17},{29,21},{2,10},{... | collective-permute-start | bytes 2985992 | tf_op jit(solution)/shard_map/ppermute | solution.py:589
  277.4 20.2 %collective-permute-start.32 = (bf16[432,1152]{1,0:T(8,128)(2,1)}, bf16[432,1152]{1,0:T(8,128)(2,1)S(1)}, u32[]{:S(2)}, u32[]{:S(2)}) collective-permute-start(bf16[432,1152]{1,0:T(8,128)(2,1)} %get-tuple-element.84.refs_0_), channel_id=1, source_target_pairs={{8,16},{12,20},{16,8},{20,12},{9,17},{13,21},{17,9},{21,13},{10,18... | collective-permute-start | bytes 2985992 | tf_op jit(solution)/shard_map/ppermute | solution.py:589
  278.1 30.7 %collective-permute-start.33 = (bf16[432,1152]{1,0:T(8,128)(2,1)}, bf16[432,1152]{1,0:T(8,128)(2,1)S(1)}, u32[]{:S(2)}, u32[]{:S(2)}) collective-permute-start(bf16[432,1152]{1,0:T(8,128)(2,1)} %get-tuple-element.85.refs_2_), channel_id=1, source_target_pairs={{0,8},{4,12},{24,16},{28,20},{1,9},{5,13},{25,17},{29,21},{2,10},{... | collective-permute-start | bytes 2985992 | tf_op jit(solution)/shard_map/ppermute | solution.py:589
  296.3 30.3 %collective-permute-start.35 = (bf16[512,512]{1,0:T(8,128)(2,1)}, bf16[512,512]{1,0:T(8,128)(2,1)S(1)}, u32[]{:S(2)}, u32[]{:S(2)}) collective-permute-start(bf16[512,512]{1,0:T(8,128)(2,1)} %get-tuple-element.92), channel_id=1, source_target_pairs={{1,0},{2,1},{3,2},{5,4},{6,5},{7,6},{9,8},{10,9},{11,10},{13,12},{... | collective-permute-start | bytes 1572872 | tf_op jit(solution)/shard_map/ppermute | solution.py:787
  315.4 32.4 %collective-permute-start.37 = (bf16[432,1152]{1,0:T(8,128)(2,1)}, bf16[432,1152]{1,0:T(8,128)(2,1)S(1)}, u32[]{:S(2)}, u32[]{:S(2)}) collective-permute-start(bf16[432,1152]{1,0:T(8,128)(2,1)} %get-tuple-element.101), channel_id=1, source_target_pairs={{0,8},{4,12},{24,16},{28,20},{8,0},{12,4},{16,24},{20,28},{1,9},{5... | collective-permute-start | bytes 2985992 | tf_op jit(solution)/shard_map/ppermute | solution.py:589
  317.8 30.0 %collective-permute-start.38 = (bf16[432,1152]{1,0:T(8,128)(2,1)}, bf16[432,1152]{1,0:T(8,128)(2,1)S(1)}, u32[]{:S(2)}, u32[]{:S(2)}) collective-permute-start(bf16[432,1152]{1,0:T(8,128)(2,1)} %get-tuple-element.102.refs_2_), channel_id=1, source_target_pairs={{8,16},{12,20},{16,8},{20,12},{9,17},{13,21},{17,9},{21,13},{10,18... | collective-permute-start | bytes 2985992 | tf_op jit(solution)/shard_map/ppermute | solution.py:589
  318.5 30.6 %collective-permute-start.41 = (bf16[432,1152]{1,0:T(8,128)(2,1)S(1)}, bf16[432,1152]{1,0:T(8,128)(2,1)}, u32[]{:S(2)}, u32[]{:S(2)}) collective-permute-start(bf16[432,1152]{1,0:T(8,128)(2,1)S(1)} %copy-done.73), channel_id=1, source_target_pairs={{8,16},{12,20},{16,8},{20,12},{9,17},{13,21},{17,9},{21,13},{10,18... | collective-permute-start | bytes 2985992 | tf_op jit(solution)/shard_map/ppermute | solution.py:589
  320.2 40.4 %collective-permute-start.42 = (bf16[432,1152]{1,0:T(8,128)(2,1)}, bf16[432,1152]{1,0:T(8,128)(2,1)}, u32[]{:S(2)}, u32[]{:S(2)}) collective-permute-start(bf16[432,1152]{1,0:T(8,128)(2,1)} %get-tuple-element.108.refs_2_), channel_id=1, source_target_pairs={{0,8},{4,12},{24,16},{28,20},{1,9},{5,13},{25,17},{29,21},{2,10},{... | collective-permute-start | bytes 2985992 | tf_op jit(solution)/shard_map/ppermute | solution.py:589
  374.8 27.5 %collective-permute-start.46 = (bf16[432,1152]{1,0:T(8,128)(2,1)}, bf16[432,1152]{1,0:T(8,128)(2,1)S(1)}, u32[]{:S(2)}, u32[]{:S(2)}) collective-permute-start(bf16[432,1152]{1,0:T(8,128)(2,1)} %get-tuple-element.115), channel_id=1, source_target_pairs={{0,8},{4,12},{24,16},{28,20},{8,0},{12,4},{16,24},{20,28},{1,9},{5... | collective-permute-start | bytes 2985992 | tf_op jit(solution)/shard_map/ppermute | solution.py:589
  379.2 23.0 %collective-permute-start.47 = (bf16[432,1152]{1,0:T(8,128)(2,1)S(1)}, bf16[432,1152]{1,0:T(8,128)(2,1)S(1)}, u32[]{:S(2)}, u32[]{:S(2)}) collective-permute-start(bf16[432,1152]{1,0:T(8,128)(2,1)S(1)} %copy-done.57), channel_id=1, source_target_pairs={{8,16},{12,20},{16,8},{20,12},{9,17},{13,21},{17,9},{21,13},{10,18... | collective-permute-start | bytes 2985992 | tf_op jit(solution)/shard_map/ppermute | solution.py:589
  385.0 38.1 %collective-permute-start.39 = (bf16[432,1152]{1,0:T(8,128)(2,1)}, bf16[432,1152]{1,0:T(8,128)(2,1)S(1)}, u32[]{:S(2)}, u32[]{:S(2)}) collective-permute-start(bf16[432,1152]{1,0:T(8,128)(2,1)} %get-tuple-element.104.refs_0_), channel_id=1, source_target_pairs={{8,0},{12,4},{16,24},{20,28},{9,1},{13,5},{17,25},{21,29},{10,2},{... | collective-permute-start | bytes 2985992 | tf_op jit(solution)/shard_map/ppermute | solution.py:589
  386.2 36.8 %collective-permute-start.40 = (bf16[432,1152]{1,0:T(8,128)(2,1)}, bf16[432,1152]{1,0:T(8,128)(2,1)}, u32[]{:S(2)}, u32[]{:S(2)}) collective-permute-start(bf16[432,1152]{1,0:T(8,128)(2,1)} %get-tuple-element.105.refs_2_), channel_id=1, source_target_pairs={{8,16},{12,20},{16,8},{20,12},{9,17},{13,21},{17,9},{21,13},{10,18... | collective-permute-start | bytes 2985992 | tf_op jit(solution)/shard_map/ppermute | solution.py:589
  387.9 48.8 %collective-permute-start.48 = (bf16[432,1152]{1,0:T(8,128)(2,1)}, bf16[432,1152]{1,0:T(8,128)(2,1)S(1)}, u32[]{:S(2)}, u32[]{:S(2)}) collective-permute-start(bf16[432,1152]{1,0:T(8,128)(2,1)} %get-tuple-element.113.refs_0_), channel_id=1, source_target_pairs={{0,4},{4,0},{8,12},{12,8},{16,20},{20,16},{24,28},{28,24},{1,5},{5... | collective-permute-start | bytes 2985992 | tf_op jit(solution)/shard_map/ppermute | solution.py:17
  408.3 29.1 %collective-permute-start.49 = (bf16[432,1152]{1,0:T(8,128)(2,1)}, bf16[432,1152]{1,0:T(8,128)(2,1)S(1)}, u32[]{:S(2)}, u32[]{:S(2)}) collective-permute-start(bf16[432,1152]{1,0:T(8,128)(2,1)} %get-tuple-element.118.refs_1_), channel_id=1, source_target_pairs={{0,4},{4,0},{8,12},{12,8},{16,20},{20,16},{24,28},{28,24},{1,5},{5... | collective-permute-start | bytes 2985992 | tf_op jit(solution)/shard_map/ppermute | solution.py:17
  428.4 28.1 %collective-permute-start.44 = (bf16[432,1152]{1,0:T(8,128)(2,1)}, bf16[432,1152]{1,0:T(8,128)(2,1)S(1)}, u32[]{:S(2)}, u32[]{:S(2)}) collective-permute-start(bf16[432,1152]{1,0:T(8,128)(2,1)} %get-tuple-element.111.refs_0_), channel_id=1, source_target_pairs={{8,0},{12,4},{16,24},{20,28},{9,1},{13,5},{17,25},{21,29},{10,2},{... | collective-permute-start | bytes 2985992 | tf_op jit(solution)/shard_map/ppermute | solution.py:589
  429.7 22.1 %collective-permute-start.45 = (bf16[304,1280]{1,0:T(8,128)(2,1)}, bf16[304,1280]{1,0:T(8,128)(2,1)S(1)}, u32[]{:S(2)}, u32[]{:S(2)}) collective-permute-start(bf16[304,1280]{1,0:T(8,128)(2,1)} %get-tuple-element.112.refs_2_), channel_id=1, source_target_pairs={{0,8},{4,12},{24,16},{28,20},{1,9},{5,13},{25,17},{29,21},{2,10},{... | collective-permute-start | bytes 2334728 | tf_op jit(solution)/shard_map/ppermute | solution.py:589
  435.4 41.0 %collective-permute-start.53 = (bf16[432,1152]{1,0:T(8,128)(2,1)S(1)}, bf16[432,1152]{1,0:T(8,128)(2,1)S(1)}, u32[]{:S(2)}, u32[]{:S(2)}) collective-permute-start(bf16[432,1152]{1,0:T(8,128)(2,1)S(1)} %copy-done.69), channel_id=1, source_target_pairs={{8,0},{12,4},{16,24},{20,28},{9,1},{13,5},{17,25},{21,29},{10,2},{... | collective-permute-start | bytes 2985992 | tf_op jit(solution)/shard_map/ppermute | solution.py:589
  436.7 39.6 %collective-permute-start.54 = (bf16[432,1152]{1,0:T(8,128)(2,1)S(1)}, bf16[432,1152]{1,0:T(8,128)(2,1)S(1)}, u32[]{:S(2)}, u32[]{:S(2)}) collective-permute-start(bf16[432,1152]{1,0:T(8,128)(2,1)S(1)} %copy-done.70), channel_id=1, source_target_pairs={{8,16},{12,20},{16,8},{20,12},{9,17},{13,21},{17,9},{21,13},{10,18... | collective-permute-start | bytes 2985992 | tf_op jit(solution)/shard_map/ppermute | solution.py:589
  460.7 23.4 %collective-permute-start.50 = (bf16[304,1280]{1,0:T(8,128)(2,1)}, bf16[304,1280]{1,0:T(8,128)(2,1)S(1)}, u32[]{:S(2)}, u32[]{:S(2)}) collective-permute-start(bf16[304,1280]{1,0:T(8,128)(2,1)} %get-tuple-element.119.refs_0_), channel_id=1, source_target_pairs={{8,16},{12,20},{16,8},{20,12},{9,17},{13,21},{17,9},{21,13},{10,18... | collective-permute-start | bytes 2334728 | tf_op jit(solution)/shard_map/ppermute | solution.py:589
  482.8 27.0 %collective-permute-start.55 = (bf16[432,1152]{1,0:T(8,128)(2,1)}, bf16[432,1152]{1,0:T(8,128)(2,1)S(1)}, u32[]{:S(2)}, u32[]{:S(2)}) collective-permute-start(bf16[432,1152]{1,0:T(8,128)(2,1)} %get-tuple-element.122.refs_0_), channel_id=1, source_target_pairs={{8,0},{12,4},{16,24},{20,28},{9,1},{13,5},{17,25},{21,29},{10,2},{... | collective-permute-start | bytes 2985992 | tf_op jit(solution)/shard_map/ppermute | solution.py:589
  487.5 38.1 %collective-permute-start.51 = (bf16[304,1280]{1,0:T(8,128)(2,1)}, bf16[304,1280]{1,0:T(8,128)(2,1)S(1)}, u32[]{:S(2)}, u32[]{:S(2)}) collective-permute-start(bf16[304,1280]{1,0:T(8,128)(2,1)} %line_step.24.refs_0_), channel_id=1, source_target_pairs={{8,0},{12,4},{16,24},{20,28},{9,1},{13,5},{17,25},{21,29},{10,2},{... | collective-permute-start | bytes 2334728 | tf_op jit(solution)/shard_map/ppermute | solution.py:589
  (130 other events, 831.3 us)
Sparse Core Ops, SparseCore 0:
  374.9 45.4 reduce-scatter.3

commit v8 on v7

--- a/solution.py
+++ b/solution.py
@@ -22,11 +22,8 @@
     return lax.optimization_barrier(total.astype(jnp.bfloat16))
 
 
-VMEM_LIMIT = 56 * 1024 * 1024
-
-
-def params(*semantics):
-    return pltpu.CompilerParams(vmem_limit_bytes=VMEM_LIMIT)
+def params(mebibytes=48):
+    return pltpu.CompilerParams(vmem_limit_bytes=mebibytes * 1024 * 1024)
 
 
 def dot(left, right, left_dim, right_dim):
@@ -43,6 +40,7 @@
         in_specs=[place] * (1 + len(others)),
         out_specs=place,
         input_output_aliases={0: 0},
+        compiler_params=params(1),
         name="after",
     )(array, *others)
 
@@ -75,7 +73,7 @@
             out_specs=pl.BlockSpec((half, wide), lambda i, core_ref: (0, 0)),
         ),
         out_shape=jax.ShapeDtypeStruct((half, wide), jnp.bfloat16),
-        compiler_params=params(),
+        compiler_params=params(16),
         name="pack",
     )(scalar(lax.axis_index("replica") % 2), *weights)
 
@@ -116,7 +114,7 @@
             out_specs=pl.BlockSpec((rows, wide), lambda i, *refs: (i, 0)),
         ),
         out_shape=jax.ShapeDtypeStruct((group * rows, wide), jnp.bfloat16),
-        compiler_params=params(),
+        compiler_params=params(24),
         name="unpack",
     )(scalar(lax.axis_index("replica") % 2), scalar(lax.axis_index("fsdp")), *arrays)
 
@@ -262,7 +260,7 @@
             jax.ShapeDtypeStruct((1, model), jnp.float32),
             jax.ShapeDtypeStruct((1, model), jnp.float32),
         ],
-        compiler_params=params(),
+        compiler_params=params(32),
         name="resid_backward",
     )(*parts, resid, attended, out_grad, gain_ffn[None, :], gain_attn[None, :], w_out)
 
@@ -365,6 +363,69 @@
     )(scalar(lax.axis_index("replica") % 2), *arrays)
 
 
+def owner_parts(other, mine):
+    group, height, wide = mine.shape
+    far = swapped(other, "replica", 1)
+
+    def kernel(rank_ref, mine_ref, far_ref, *outs):
+        total = mine_ref[...].astype(jnp.float32) + far_ref[...].astype(jnp.float32)
+        for mask in range(group):
+
+            @pl.when(pl.program_id(0) == mask)
+            def _():
+                outs[mask][...] = total.astype(jnp.bfloat16)
+
+    block = pl.BlockSpec((None, height, wide), lambda i, rank_ref: (rank_ref[0] ^ i, 0, 0))
+    parts = pl.pallas_call(
+        kernel,
+        grid_spec=pltpu.PrefetchScalarGridSpec(
+            num_scalar_prefetch=1,
+            grid=(group,),
+            in_specs=[block, block],
+            out_specs=[pl.BlockSpec((height, wide), lambda i, rank_ref: (0, 0))] * group,
+        ),
+        out_shape=[jax.ShapeDtypeStruct((height, wide), jnp.bfloat16)] * group,
+        compiler_params=params(16),
+        name="owner_parts",
+    )(scalar(lax.axis_index("fsdp")), mine, far)
+    return [parts[0]] + [swapped(parts[mask], "fsdp", mask) for mask in range(1, group)]
+
+
+def weight_grad_whole(lefts, rights):
+    group = len(rights)
+    units, rows = lefts[0].shape
+    model = rights[0].shape[1]
+    tile = tile_of(units, 432)
+
+    def kernel(*refs):
+        right_refs, left_refs = refs[:group], refs[group : 2 * group]
+        out_ref, left_ref, right_ref = refs[2 * group :]
+
+        @pl.when(pl.program_id(0) == 0)
+        def _():
+            for spot in range(group):
+                right_ref[spot * rows : (spot + 1) * rows, :] = right_refs[spot][...]
+
+        for spot in range(group):
+            left_ref[:, spot * rows : (spot + 1) * rows] = left_refs[spot][...]
+        out_ref[...] = dot(left_ref[...], right_ref[...], 1, 0).astype(jnp.bfloat16)
+
+    return pl.pallas_call(
+        kernel,
+        grid=(units // tile,),
+        in_specs=[pl.BlockSpec((rows, model), lambda i: (0, 0))] * group
+        + [pl.BlockSpec((tile, rows), lambda i: (i, 0))] * group,
+        out_specs=pl.BlockSpec((tile, model), lambda i: (i, 0)),
+        out_shape=jax.ShapeDtypeStruct((units, model), jnp.bfloat16),
+        scratch_shapes=[
+            pltpu.VMEM((tile, group * rows), jnp.bfloat16),
+            pltpu.VMEM((group * rows, model), jnp.bfloat16),
+        ],
+        compiler_params=params(32),
+        name="weight_grad",
+    )(*rights, *lefts)
+
+
 def chunks_of(units):
     return 2 if units % 64 == 0 else 1
 
@@ -493,7 +554,7 @@
         in_specs=common,
         out_specs=[head, head],
         out_shape=[shape, shape],
-        compiler_params=params(),
+        compiler_params=params(32),
         name="attention_forward",
     )(qkv, gain, cosine, sine, pairs, query_segs, key_segs)
 
@@ -573,7 +634,7 @@
             jax.ShapeDtypeStruct((rows, 2 * size), jnp.float32),
         ],
         scratch_shapes=[pltpu.VMEM((width, 2 * size), jnp.float32)],
-        compiler_params=params(),
+        compiler_params=params(32),
         name="attention_backward",
     )(qkv, gain, cosine, sine, pairs, query_segs, key_segs, query, grad_mixed)
 
@@ -678,7 +739,7 @@
             ),
             out_shape=out_shape,
             input_output_aliases=aliases,
-            compiler_params=params(),
+            compiler_params=params(32),
             name="line_step",
         )(place, *arrays)
         received = {}
@@ -714,9 +775,9 @@
     return [(name, chunk) for chunk in range(chunks_of(units))]
 
 
-def whole_grad(lines, name, units, dtype=jnp.float32):
+def whole_grad(line, name, units, dtype=jnp.float32):
     names = line_names(name, units)
-    mines = [lines[chunk[1]].finished(chunk) for chunk in names]
+    mines = [line.finished(chunk) for chunk in names]
     others = [swapped(mine, "replica", 1) for mine in mines]
     chunks = len(mines)
     tile, model = mines[0].shape
@@ -746,7 +807,7 @@
             out_specs=pl.BlockSpec((tile, model), lambda chunk, side, core_ref: (2 * chunk + side, 0)),
         ),
         out_shape=jax.ShapeDtypeStruct((units, model), dtype),
-        compiler_params=params(),
+        compiler_params=params(24),
         name="whole_grad",
     )(core, *mines, *others)
 
@@ -853,13 +914,15 @@
     scale = head_size ** (-0.5)
     qkv_weights = (query_weight, key_weight, value_weight)
     wide = sum(weight.shape[1] for weight in qkv_weights)
-    got, peers = fetched(packed(qkv_weights))
+    qkv_block = packed(qkv_weights)
+    got, peers = fetched(qkv_block)
     gains = jnp.stack(
         [
             jnp.pad(gain, (0, own_model - gain.shape[0]))
             for gain in (norm_in, norm_attn, norm_ffn, norm_out, query_gain, key_gain)
         ]
     )
+    gains = after(gains, qkv_block)
     gain_stack = jnp.stack([gains] + [swapped(gains, "fsdp", mask) for mask in masks])
     w_qkv = unpacked(qkv_weights, got, peers)
     gain_rows = jnp.stack(
@@ -867,7 +930,6 @@
     )
     gain_in, gain_attn, gain_ffn, gain_out = (gain_rows[i].reshape(-1) for i in range(4))
     gain_query, gain_key = (gain_rows[i, :, :own_head].reshape(-1) for i in (4, 5))
-    got, peers = fetched(after(packed([out_weight]), w_qkv))
     residual_in = hidden_in.astype(jnp.float32)
     normed_in = normed(residual_in, gain_in).astype(jnp.bfloat16)
     qkv = jnp.dot(normed_in, w_qkv, preferred_element_type=jnp.float32)
@@ -876,10 +938,12 @@
     cosine, sine = tables(positions, head_size // 2)
     key_new = head_post(key_raw, gain_key, cosine, sine).astype(jnp.bfloat16)
     pair_new = jnp.concatenate([key_new, value_new], axis=1)
+    got, peers = fetched(after(packed([out_weight]), pair_new))
+    w_out = unpacked([out_weight], got, peers)
     parts = [pair_new]
     for step in range(1, hops + 1):
         parts.insert(0, passed_along(pair_new, "fsdp", step))
-    pairs = jnp.concatenate(parts, axis=0)
+    pairs = after(jnp.concatenate(parts, axis=0), w_out)
     width = pairs.shape[0]
     seg_padded = jnp.concatenate([jnp.full((hops * rows,), -1, jnp.int32), segments], axis=0)
     key_segs = lax.dynamic_slice_in_dim(seg_padded, rank * rows, width, 0)
@@ -894,7 +958,6 @@
         key_segs[None, :],
     )
     query_new, mixed = attention_forward(*attention_args, heads)
-    w_out = unpacked([out_weight], got, peers)
     attended = contract(mixed, w_out, 1, 1)
     resid = residual_in + normed(attended, gain_attn)
     ffn_in = normed(resid, gain_ffn).astype(jnp.bfloat16)
@@ -920,7 +983,7 @@
     grad_branch_low = grad_branch.astype(jnp.bfloat16)
     pieces = gathered(grad_branch_low)
     units = gate_weight.shape[0]
-    lines = [Line(), Line()]
+    line = Line()
 
     def fresh(names, other, mine):
         far = swapped(other, "replica", 1)
@@ -939,45 +1002,39 @@
         returned[mask] = swapped(part, "fsdp", mask) if mask else part
         last = mask
     pieces[final] = after(pieces[final], part)
-    waiting = fresh(
-        ["down"], *weight_grad([[hiddens[i] for i in range(group)]], [pieces[i] for i in range(group)])
-    )
+    grad_down = weight_grad_whole(
+        [hiddens[i] for i in range(group)], [pieces[i] for i in range(group)]
+    )
+    pieces[final] = after(pieces[final], grad_down)
+    grad_down = lax.psum(grad_down, "replica").astype(jnp.float32)
     gate_parts, upper_parts, parts = ffn_backward_blocks(
         [pieces[final]], gate_weight, up_weight, down_weight, [slopes[final]], [acts[final]]
     )
     grad_gates[final], grad_uppers[final] = gate_parts[0], upper_parts[0]
     returned[final] = swapped(parts[0], "fsdp", final)
     grad_gates[final] = after(grad_gates[final], *[returned[mask] for mask in rings[1:-1]])
-    grad_gates[final] = lines[0].advance([waiting.pop(0)], grad_gates[final])
     other, mine = weight_grad(
         [[grad_gates[i] for i in range(group)], [grad_uppers[i] for i in range(group)]], ffn_blocks
     )
-    other = after(other, *lines[0].arrived(), returned[final])
-    other = lines[1].advance([waiting.pop(0)] if waiting else [], other)
+    other = after(other, returned[final])
     waiting = fresh(["gate", "up"], other, mine)
 
-    def advance(spot, gate=None):
-        ready = [entry for entry in waiting if entry[0][1] == spot][:1]
-        for entry in ready:
-            waiting.remove(entry)
-        return lines[spot].advance(ready, gate)
+    def advance(gate=None):
+        return line.advance([waiting.pop(0)] if waiting else [], gate)
 
     grad_resid, grad_attended_low, grad_mixed, grad_gain_ffn, grad_gain_attn = resid_backward(
         [returned[mask] for mask in range(group)], resid, attended, out_grad, gain_ffn, gain_attn, w_out
     )
-    grad_mixed = advance(0, grad_mixed)
+    grad_mixed = advance(grad_mixed)
     grad_query_low, grad_gain_query, grad_far, grad_pair = attention_backward(
         *attention_args, query_new, grad_mixed, heads
     )
-    grad_far = advance(1, grad_far)
     backs = []
     for step in range(1, hops + 1):
-        if step == 2:
-            grad_far = after(grad_far, *lines[0].arrived())
         grad_far = passed_along(grad_far, "fsdp", -1)
         backs.append(grad_far[-rows:])
         grad_far = grad_far[:-rows]
-    grad_pair = advance(0, grad_pair)
+    grad_pair = advance(grad_pair)
     other, mine, grad_in = input_backward(
         grad_pair,
         backs,
@@ -996,21 +1053,15 @@
         [grad_gain_attn, grad_gain_ffn, grad_gain_out[None, :], grad_gain_query],
         group,
     )
-    other = advance(1, after(other, *lines[0].arrived()))
-    chip = added(mine, swapped(other, "replica", 1))
-    owned = lax.psum_scatter(chip, "fsdp", scatter_dimension=0, tiled=True)[0]
-    advance(0)
-    advance(1)
+    other = advance(other)
+    weight_parts = owner_parts(other, mine)
     while waiting:
-        advance(0)
-    lines[0].advance([("weights", [owned])])
-    advance(1)
-    grad_down = whole_grad(lines, "down", units)
-    grad_down = lines[0].advance([], grad_down)
-    grad_gate_w = whole_grad(lines, "gate", units)
-    grad_gate_w = lines[1].advance([], grad_gate_w)
-    grad_up_w = whole_grad(lines, "up", units)
-    owned = core_join(lines[0].finished("weights"), 1).astype(jnp.float32)
+        weight_parts[0] = advance(weight_parts[0])
+    line.advance([("weights", weight_parts)])
+    grad_gate_w = whole_grad(line, "gate", units)
+    grad_gate_w = line.advance([], grad_gate_w)
+    grad_up_w = whole_grad(line, "up", units)
+    owned = core_join(line.finished("weights"), 1).astype(jnp.float32)
     inner = heads * head_size
     columns = [0, inner, inner + head_size, inner + 2 * head_size, wide + inner]
     owned_query, owned_key, owned_value, owned_out = (

time: 557 us -> 569 us (1.022)
  waiting for transfers between devices: 173 us -> 268 us
  Pallas kernels: 156 us -> 83.4 us
  matrix products: 65.1 us -> 44.3 us
  local copies, waits for them, and re-layouts: 48.8 us -> 61.8 us
    psum x0 -> x1, waiting for transfers between devices: none -> 46.2 us  [per_device(): grad_down = lax.psum(grad_down, 'replica').astype(jnp.float32)]
    pallas_call x14 -> x8, Pallas kernels: 56.1 us -> 15.8 us  [advance(): pl.pallas_call(kernel, grid_spec=pltpu.PrefetchScalarGridSpec(num_scalar_...]
    ppermute x37, waiting for transfers between devices: 54.3 us -> 92.2 us  [swapped(): return lax.ppermute(block, axis, route)]
    dot_general x22, matrix products: 62.9 us -> 43.1 us  [contract(): lax.dot_general(left, right, (((left_dim,), (right_dim,)), ((), ())), pre...]
    ppermute x19 -> x13, starting transfers between devices: 44.5 us -> 30.1 us  [exchanged(): return lax.ppermute(block, 'replica', route)]
    unnamed x204 -> x208, local copies, waits for them, and re-layouts: 32.9 us -> 46.6 us
    ppermute x19 -> x13, waiting for transfers between devices: 106 us -> 119 us  [exchanged(): return lax.ppermute(block, 'replica', route)]
    pallas_call x2 -> x1, Pallas kernels: 27.7 us -> 16.2 us  [weight_grad(): pl.pallas_call(kernel, grid_spec=pltpu.PrefetchScalarGridSpec(num_scalar_...]
  transfers between devices with their start and end apart: 61 -> 55, of which waited for: 28 -> 21; matrix products, arithmetic and copies ran while one was open for 14% -> 11% of each run, Pallas kernels for 23% -> 12%
where the time goes in v8:
time: 569 us; the launch traced here: 562 us
  waiting for transfers between devices  268 us (47%)
  Pallas kernels  83.4 us (15%)
  starting transfers between devices  74.8 us (13%)
  local copies, waits for them, and re-layouts  61.8 us (11%)
  matrix products  44.3 us (8%)
  between operations  15.9 us (3%)
  other arithmetic  14.3 us (3%)
    ppermute x13, waiting for transfers between devices, exchanged(): return lax.ppermute(block, 'replica', route)  119 us
    ppermute x37, waiting for transfers between devices, swapped(): return lax.ppermute(block, axis, route)  92.2 us
    unnamed x208, local copies, waits for them, and re-layouts  46.6 us
    psum x1, waiting for transfers between devices, per_device(): grad_down = lax.psum(grad_down, 'replica').astype(jnp.float32)  46.2 us
    dot_general x22, matrix products, contract(): lax.dot_general(left, right, (((left_dim,), (right_dim,)), ((), ())), pre...  43.1 us
    ppermute x37, starting transfers between devices, swapped(): return lax.ppermute(block, axis, route)  34.8 us
    ppermute x13, starting transfers between devices, exchanged(): return lax.ppermute(block, 'replica', route)  30.1 us
    pallas_call x1, Pallas kernels, weight_grad(): pl.pallas_call(kernel, grid_spec=pltpu.PrefetchScalarGridSpec(num_scalar_...  16.2 us
  transfers between devices with their start and end apart: 55, of which 21 were waited for; matrix products, arithmetic and copies ran while one was open for 11% of the time, Pallas kernels for 12%

profile of v8, /device:TPU:0, one launch (start us, length us, event | category | flops | bytes accessed | tf_op | source)
XLA Modules:
  0.0 562.4 jit_solution(10224609536516134401)
XLA Ops:
  28.4 7.6 %collective-permute-done.5.refs_5_ = bf16[144,1536]{1,0:T(8,128)(2,1)} collective-permute-done((bf16[144,1536]{1,0:T(8,128)(2,1)S(1)}, bf16[144,1536]{1,0:T(8,128)(2,1)}, u32[]{:S(2)}, u32[]{:S(2)}) %collective-permute-start.5) | collective-permute-done | bytes 442400 | tf_op jit(solution)/shard_map/ppermute | solution.py:17
  47.2 4.0 collective-permute-start.10
  54.6 11.2 %collective-permute-done.12.refs_2_ = bf16[144,1024]{1,0:T(8,128)(2,1)S(1)} collective-permute-done((bf16[144,1024]{1,0:T(8,128)(2,1)S(1)}, bf16[144,1024]{1,0:T(8,128)(2,1)S(1)}, u32[]{:S(2)}, u32[]{:S(2)}) %collective-permute-start.12) | collective-permute-done | bytes 294944 | tf_op jit(solution)/shard_map/ppermute | solution.py:17
  81.6 4.2 attention_forward.1
  93.1 10.3 %collective-permute-done.17.refs_1_ = bf16[256,1152]{1,0:T(8,128)(2,1)} collective-permute-done((bf16[256,1152]{1,0:T(8,128)(2,1)}, bf16[256,1152]{1,0:T(8,128)(2,1)}, u32[]{:S(2)}, u32[]{:S(2)}) %collective-permute-start.17) | collective-permute-done | bytes 589856 | tf_op jit(solution)/shard_map/ppermute | solution.py:17
  107.1 3.7 convolution_bitcast_fusion.10
  134.6 13.1 %collective-permute-done.21 = bf16[256,1152]{1,0:T(8,128)(2,1)S(1)} collective-permute-done((bf16[256,1152]{1,0:T(8,128)(2,1)S(1)}, bf16[256,1152]{1,0:T(8,128)(2,1)S(1)}, u32[]{:S(2)}, u32[]{:S(2)}) %collective-permute-start.21) | collective-permute-done | bytes 589856 | tf_op jit(solution)/shard_map/ppermute | solution.py:17
  159.0 4.1 collective-permute-done.23.refs_0_.refs_1_
  163.1 6.1 %collective-permute-done.24.refs_0_.refs_2_ = bf16[256,1152]{1,0:T(8,128)(2,1)S(1)} collective-permute-done((bf16[256,1152]{1,0:T(8,128)(2,1)S(1)}, bf16[256,1152]{1,0:T(8,128)(2,1)S(1)}, u32[]{:S(2)}, u32[]{:S(2)}) %collective-permute-start.24) | collective-permute-done | bytes 589856 | tf_op jit(solution)/shard_map/ppermute | solution.py:17
  184.7 5.5 weight_grad.2.refs_1_
  200.4 10.0 %ffn_backward.1 = (bf16[1728,256]{1,0:T(8,128)(2,1)S(1)}, bf16[1728,256]{1,0:T(8,128)(2,1)S(1)}, bf16[256,1152]{1,0:T(8,128)(2,1)S(1)}) custom-call(bf16[256,1152]{1,0:T(8,128)(2,1)S(1)} %copy-done.15, bf16[1728,1152]{1,0:T(8,128)(2,1)} %refs_1_.5, bf16[1728,1152]{1,0:T(8,128)(2,1)} %refs_2_.5, bf16[1728,1152]{1,0:T(8,128)(2,1)} %refs_3_.1, ...), custom_call_target="tpu_custom_call" | custom-call | tf_op jit(solution)/shard_map/ffn_backward/pallas_call | solution.py:195
  212.5 16.2 %weight_grad.3 = (bf16[4,432,1152]{2,1,0:T(8,128)(2,1)}, bf16[4,432,1152]{2,1,0:T(8,128)(2,1)}) custom-call(s32[1]{0:T(128)} %bitcast.core_ref, bf16[256,1152]{1,0:T(8,128)(2,1)S(1)} %copy-done.22, bf16[256,1152]{1,0:T(8,128)(2,1)} %collective-permute-done.17.refs_1_, bf16[256,1152]{1,0:T(8,128)(2,1)} %after.18.refs_2_, bf16[256,1152]{1,0:T(8,128)(2,1)S(1)} %copy-done.39, ...), custom_call_target="tpu_custom_call" | custom-call | tf_op jit(solution)/shard_map/weight_grad/pallas_call | solution.py:480
  241.9 3.6 resid_backward.1
  254.3 6.6 %attention_backward.1 = (bf16[256,1024]{1,0:T(8,128)(2,1)S(1)}, f32[1,256]{1,0:T(1,128)S(1)}, bf16[512,512]{1,0:T(8,128)(2,1)S(1)}, f32[256,512]{1,0:T(8,128)S(1)}) custom-call(f32[256,1536]{1,0:T(8,128)S(1)} %copy-done.6, bf16[1,256]{1,0:T(2,128)(2,1)S(1)} %broadcast_in_dim_reshape_squeeze.2.gain_ref, f32[256,128]{1,0:T(8,128)S(1)} %copy-done.48, ...), custom_call_target="tpu_custom_call" | custom-call | tf_op jit(solution)/shard_map/attention_backward/pallas_call | solution.py:625
  262.9 13.2 %collective-permute-done.30.refs_1_ = bf16[432,1152]{1,0:T(8,128)(2,1)S(1)} collective-permute-done((bf16[432,1152]{1,0:T(8,128)(2,1)S(1)}, bf16[432,1152]{1,0:T(8,128)(2,1)S(1)}, u32[]{:S(2)}, u32[]{:S(2)}) %collective-permute-start.30) | collective-permute-done | bytes 995360 | tf_op jit(solution)/shard_map/ppermute | solution.py:650
  281.3 7.2 %collective-permute-start.34 = (bf16[432,1152]{1,0:T(8,128)(2,1)}, bf16[432,1152]{1,0:T(8,128)(2,1)}, u32[]{:S(2)}, u32[]{:S(2)}) collective-permute-start(bf16[432,1152]{1,0:T(8,128)(2,1)} %get-tuple-element.85.refs_2_), channel_id=1, source_target_pairs={{0,8},{4,12},{24,16},{28,20},{1,9},{5,13},{25,17},{29,21},{2,10},{... | collective-permute-start | bytes 2985992 | tf_op jit(solution)/shard_map/ppermute | solution.py:650
  290.8 8.1 %collective-permute-done.32.refs_2_ = bf16[256,512]{1,0:T(8,128)(2,1)} collective-permute-done((bf16[256,512]{1,0:T(8,128)(2,1)}, bf16[256,512]{1,0:T(8,128)(2,1)}, u32[]{:S(2)}, u32[]{:S(2)}) %collective-permute-start.32) | collective-permute-done | bytes 262176 | tf_op jit(solution)/shard_map/ppermute | solution.py:848
  301.2 9.1 %input_backward.1 = (bf16[4,304,1280]{2,1,0:T(8,128)(2,1)}, bf16[4,304,1280]{2,1,0:T(8,128)(2,1)}, f32[256,1152]{1,0:T(8,128)}) custom-call(s32[1]{0:T(128)} %bitcast.core_ref, f32[256,512]{1,0:T(8,128)S(1)} %get-tuple-element.75.refs_0_, bf16[256,512]{1,0:T(8,128)(2,1)S(1)} %get-tuple-element.150.refs_1_, bf16[256,512]{1,0:T(8,128)(2,1)} %collective-permute-done.32.refs_2_, ...), custom_call_target="tpu_custom_call" | custom-call | tf_op jit(solution)/shard_map/input_backward/pallas_call | solution.py:351
  312.2 3.7 line_step.10
  317.7 3.9 collective-permute-done.37.far_ref
  323.3 17.1 %collective-permute-done.35.refs_1_ = bf16[432,1152]{1,0:T(8,128)(2,1)S(1)} collective-permute-done((bf16[432,1152]{1,0:T(8,128)(2,1)S(1)}, bf16[432,1152]{1,0:T(8,128)(2,1)S(1)}, u32[]{:S(2)}, u32[]{:S(2)}) %collective-permute-start.35) | collective-permute-done | bytes 995360 | tf_op jit(solution)/shard_map/ppermute | solution.py:650
  343.2 3.7 collective-permute-start.38
  351.1 16.8 %collective-permute-done.40.refs_6_ = bf16[304,1280]{1,0:T(8,128)(2,1)S(1)} collective-permute-done((bf16[304,1280]{1,0:T(8,128)(2,1)S(1)}, bf16[304,1280]{1,0:T(8,128)(2,1)S(1)}, u32[]{:S(2)}, u32[]{:S(2)}) %collective-permute-start.40) | collective-permute-done | bytes 778272 | tf_op jit(solution)/shard_map/ppermute | solution.py:17
  368.0 16.0 %collective-permute-done.41.refs_7_ = bf16[304,1280]{1,0:T(8,128)(2,1)S(1)} collective-permute-done((bf16[304,1280]{1,0:T(8,128)(2,1)S(1)}, bf16[304,1280]{1,0:T(8,128)(2,1)S(1)}, u32[]{:S(2)}, u32[]{:S(2)}) %collective-permute-start.41) | collective-permute-done | bytes 778272 | tf_op jit(solution)/shard_map/ppermute | solution.py:17
  387.3 6.4 %collective-permute-start.45 = (bf16[304,1280]{1,0:T(8,128)(2,1)S(1)}, bf16[304,1280]{1,0:T(8,128)(2,1)S(1)}, u32[]{:S(2)}, u32[]{:S(2)}) collective-permute-start(bf16[304,1280]{1,0:T(8,128)(2,1)S(1)} %get-tuple-element.104.refs_4_), channel_id=1, source_target_pairs={{0,8},{4,12},{24,16},{28,20},{1,9},{5,13},{25,17},{29,21},{2,10},{... | collective-permute-start | bytes 2334728 | tf_op jit(solution)/shard_map/ppermute | solution.py:650
  393.7 3.6 whole_grad.2.refs_6_
  397.3 13.4 %collective-permute-done.45.refs_5_ = bf16[304,1280]{1,0:T(8,128)(2,1)S(1)} collective-permute-done((bf16[304,1280]{1,0:T(8,128)(2,1)S(1)}, bf16[304,1280]{1,0:T(8,128)(2,1)S(1)}, u32[]{:S(2)}, u32[]{:S(2)}) %collective-permute-start.45) | collective-permute-done | bytes 778272 | tf_op jit(solution)/shard_map/ppermute | solution.py:650
  414.3 39.1 %collective-permute-done.48.refs_1_ = bf16[432,1152]{1,0:T(8,128)(2,1)} collective-permute-done((bf16[432,1152]{1,0:T(8,128)(2,1)S(1)}, bf16[432,1152]{1,0:T(8,128)(2,1)}, u32[]{:S(2)}, u32[]{:S(2)}) %collective-permute-start.48) | collective-permute-done | bytes 995360 | tf_op jit(solution)/shard_map/ppermute | solution.py:650
  458.1 34.9 %collective-permute-done.50.refs_1_ = bf16[304,1280]{1,0:T(8,128)(2,1)S(1)} collective-permute-done((bf16[304,1280]{1,0:T(8,128)(2,1)S(1)}, bf16[304,1280]{1,0:T(8,128)(2,1)S(1)}, u32[]{:S(2)}, u32[]{:S(2)}) %collective-permute-start.50) | collective-permute-done | bytes 778272 | tf_op jit(solution)/shard_map/ppermute | solution.py:650
  493.1 46.2 %all-reduce.5.cloned.1.call-done = bf16[1728,1152]{1,0:T(8,128)(2,1)} async-done(((bf16[1728,1152]{1,0:T(8,128)(2,1)}), bf16[1728,1152]{1,0:T(8,128)(2,1)}) %all-reduce.5.cloned.1.call-update) | async-done | bytes 3981328 | tf_op jit(solution)/shard_map/psum | solution.py:1009
  539.3 5.9 %convert_element_type.256 = f32[1728,1152]{1,0:T(8,128)} convert(bf16[1728,1152]{1,0:T(8,128)(2,1)} %all-reduce.5.cloned.1.call-done) | non-fusion elementwise | flops 1990656 | bytes 11943936 | tf_op jit(solution)/shard_map/convert_element_type | solution.py:1009
  545.2 5.0 whole_grad.3
  (406 shorter events, 187.1 us)
Async XLA Ops:
  45.1 20.7 %collective-permute-start.12 = (bf16[144,1024]{1,0:T(8,128)(2,1)S(1)}, bf16[144,1024]{1,0:T(8,128)(2,1)S(1)}, u32[]{:S(2)}, u32[]{:S(2)}) collective-permute-start(bf16[144,1024]{1,0:T(8,128)(2,1)S(1)} %after.15), channel_id=1, source_target_pairs={{0,2},{1,3},{2,0},{3,1},{4,6},{5,7},{6,4},{7,5},{8,10},{9,11},{10,... | collective-permute-start | bytes 884744 | tf_op jit(solution)/shard_map/ppermute | solution.py:17
  46.6 19.2 %collective-permute-start.13 = (bf16[144,1024]{1,0:T(8,128)(2,1)S(1)}, bf16[144,1024]{1,0:T(8,128)(2,1)S(1)}, u32[]{:S(2)}, u32[]{:S(2)}) collective-permute-start(bf16[144,1024]{1,0:T(8,128)(2,1)S(1)} %after.15), channel_id=1, source_target_pairs={{0,3},{1,2},{2,1},{3,0},{4,7},{5,6},{6,5},{7,4},{8,11},{9,10},{10,... | collective-permute-start | bytes 884744 | tf_op jit(solution)/shard_map/ppermute | solution.py:17
  47.2 20.3 %collective-permute-start.10 = (bf16[256,512]{1,0:T(8,128)(2,1)S(1)}, bf16[256,512]{1,0:T(8,128)(2,1)}, u32[]{:S(2)}, u32[]{:S(2)}) collective-permute-start(bf16[256,512]{1,0:T(8,128)(2,1)S(1)} %pad_maximum_fusion.refs_1_), channel_id=1, source_target_pairs={{0,1},{1,2},{2,3},{4,5},{5,6},{6,7},{8,9},{9,10},{10,11},{12,13},{... | collective-permute-start | bytes 786440 | tf_op jit(solution)/shard_map/ppermute | solution.py:848
  51.2 19.2 %collective-permute-start.9 = (bf16[256,512]{1,0:T(8,128)(2,1)S(1)}, bf16[256,512]{1,0:T(8,128)(2,1)}, u32[]{:S(2)}, u32[]{:S(2)}) collective-permute-start(bf16[256,512]{1,0:T(8,128)(2,1)S(1)} %pad_maximum_fusion.refs_1_), channel_id=1, source_target_pairs={{0,2},{1,3},{4,6},{5,7},{8,10},{9,11},{12,14},{13,15},{16,18},{17,... | collective-permute-start | bytes 786440 | tf_op jit(solution)/shard_map/ppermute | solution.py:848
  104.2 18.3 %collective-permute-start.19 = (bf16[256,1152]{1,0:T(8,128)(2,1)}, bf16[256,1152]{1,0:T(8,128)(2,1)S(1)}, u32[]{:S(2)}, u32[]{:S(2)}) collective-permute-start(bf16[256,1152]{1,0:T(8,128)(2,1)} %after.17), channel_id=1, source_target_pairs={{0,3},{1,2},{2,1},{3,0},{4,7},{5,6},{6,5},{7,4},{8,11},{9,10},{10,... | collective-permute-start | bytes 1769480 | tf_op jit(solution)/shard_map/ppermute | solution.py:17
  115.0 32.7 %collective-permute-start.20 = (bf16[256,1152]{1,0:T(8,128)(2,1)S(1)}, bf16[256,1152]{1,0:T(8,128)(2,1)S(1)}, u32[]{:S(2)}, u32[]{:S(2)}) collective-permute-start(bf16[256,1152]{1,0:T(8,128)(2,1)S(1)} %convolution_convert_fusion.3.refs_1_), channel_id=1, source_target_pairs={{0,1},{1,0},{2,3},{3,2},{4,5},{5,4},{6,7},{7,6},{8,9},{9,8},{10,11... | collective-permute-start | bytes 1769480 | tf_op jit(solution)/shard_map/ppermute | solution.py:17
  122.1 25.6 %collective-permute-start.21 = (bf16[256,1152]{1,0:T(8,128)(2,1)S(1)}, bf16[256,1152]{1,0:T(8,128)(2,1)S(1)}, u32[]{:S(2)}, u32[]{:S(2)}) collective-permute-start(bf16[256,1152]{1,0:T(8,128)(2,1)S(1)} %convolution_convert_fusion.2.refs_1_), channel_id=1, source_target_pairs={{0,2},{1,3},{2,0},{3,1},{4,6},{5,7},{6,4},{7,5},{8,10},{9,11},{10,... | collective-permute-start | bytes 1769480 | tf_op jit(solution)/shard_map/ppermute | solution.py:17
  129.1 18.6 %collective-permute-start.22 = (bf16[256,1152]{1,0:T(8,128)(2,1)S(1)}, bf16[256,1152]{1,0:T(8,128)(2,1)S(1)}, u32[]{:S(2)}, u32[]{:S(2)}) collective-permute-start(bf16[256,1152]{1,0:T(8,128)(2,1)S(1)} %convolution_convert_fusion.1.refs_1_), channel_id=1, source_target_pairs={{0,3},{1,2},{2,1},{3,0},{4,7},{5,6},{6,5},{7,4},{8,11},{9,10},{10,... | collective-permute-start | bytes 1769480 | tf_op jit(solution)/shard_map/ppermute | solution.py:17
  175.3 35.8 %collective-permute-start.26 = (bf16[256,1152]{1,0:T(8,128)(2,1)}, bf16[256,1152]{1,0:T(8,128)(2,1)}, u32[]{:S(2)}, u32[]{:S(2)}) collective-permute-start(bf16[256,1152]{1,0:T(8,128)(2,1)} %fusion.2.refs_1_), channel_id=1, source_target_pairs={{0,1},{1,0},{2,3},{3,2},{4,5},{5,4},{6,7},{7,6},{8,9},{9,8},{10,11... | collective-permute-start | bytes 1769480 | tf_op jit(solution)/shard_map/ppermute | solution.py:17
  183.8 27.4 %collective-permute-start.27 = (bf16[256,1152]{1,0:T(8,128)(2,1)}, bf16[256,1152]{1,0:T(8,128)(2,1)}, u32[]{:S(2)}, u32[]{:S(2)}) collective-permute-start(bf16[256,1152]{1,0:T(8,128)(2,1)} %fusion.3.refs_1_), channel_id=1, source_target_pairs={{0,2},{1,3},{2,0},{3,1},{4,6},{5,7},{6,4},{7,5},{8,10},{9,11},{10,... | collective-permute-start | bytes 1769480 | tf_op jit(solution)/shard_map/ppermute | solution.py:17
  197.0 342.3 %all-reduce.5.cloned.1.call-start = ((), (), s32[]{:S(2)}) async-start(), calls=%async_computation | async-start | bytes 7962624 | tf_op jit(solution)/shard_map/psum | solution.py:1009
  210.5 18.3 %collective-permute-start.28 = (bf16[256,1152]{1,0:T(8,128)(2,1)S(1)}, bf16[256,1152]{1,0:T(8,128)(2,1)S(1)}, u32[]{:S(2)}, u32[]{:S(2)}) collective-permute-start(bf16[256,1152]{1,0:T(8,128)(2,1)S(1)} %get-tuple-element.69), channel_id=1, source_target_pairs={{0,3},{1,2},{2,1},{3,0},{4,7},{5,6},{6,5},{7,4},{8,11},{9,10},{10,... | collective-permute-start | bytes 1769480 | tf_op jit(solution)/shard_map/ppermute | solution.py:17
  250.9 25.2 %collective-permute-start.30 = (bf16[432,1152]{1,0:T(8,128)(2,1)S(1)}, bf16[432,1152]{1,0:T(8,128)(2,1)S(1)}, u32[]{:S(2)}, u32[]{:S(2)}) collective-permute-start(bf16[432,1152]{1,0:T(8,128)(2,1)S(1)} %get-tuple-element.71.refs_0_), channel_id=1, source_target_pairs={{0,8},{4,12},{24,16},{28,20},{1,9},{5,13},{25,17},{29,21},{2,10},{... | collective-permute-start | bytes 2985992 | tf_op jit(solution)/shard_map/ppermute | solution.py:650
  261.6 26.9 %collective-permute-start.31 = (bf16[512,512]{1,0:T(8,128)(2,1)S(1)}, bf16[512,512]{1,0:T(8,128)(2,1)S(1)}, u32[]{:S(2)}, u32[]{:S(2)}) collective-permute-start(bf16[512,512]{1,0:T(8,128)(2,1)S(1)} %get-tuple-element.76), channel_id=1, source_target_pairs={{1,0},{2,1},{3,2},{5,4},{6,5},{7,6},{9,8},{10,9},{11,10},{13,12},{... | collective-permute-start | bytes 1572872 | tf_op jit(solution)/shard_map/ppermute | solution.py:848
  279.7 30.6 %collective-permute-start.33 = (bf16[432,1152]{1,0:T(8,128)(2,1)}, bf16[432,1152]{1,0:T(8,128)(2,1)}, u32[]{:S(2)}, u32[]{:S(2)}) collective-permute-start(bf16[432,1152]{1,0:T(8,128)(2,1)} %get-tuple-element.84.refs_0_), channel_id=1, source_target_pairs={{8,16},{12,20},{16,8},{20,12},{9,17},{13,21},{17,9},{21,13},{10,18... | collective-permute-start | bytes 2985992 | tf_op jit(solution)/shard_map/ppermute | solution.py:650
  281.3 29.0 %collective-permute-start.34 = (bf16[432,1152]{1,0:T(8,128)(2,1)}, bf16[432,1152]{1,0:T(8,128)(2,1)}, u32[]{:S(2)}, u32[]{:S(2)}) collective-permute-start(bf16[432,1152]{1,0:T(8,128)(2,1)} %get-tuple-element.85.refs_2_), channel_id=1, source_target_pairs={{0,8},{4,12},{24,16},{28,20},{1,9},{5,13},{25,17},{29,21},{2,10},{... | collective-permute-start | bytes 2985992 | tf_op jit(solution)/shard_map/ppermute | solution.py:650
  316.0 24.4 %collective-permute-start.35 = (bf16[432,1152]{1,0:T(8,128)(2,1)S(1)}, bf16[432,1152]{1,0:T(8,128)(2,1)S(1)}, u32[]{:S(2)}, u32[]{:S(2)}) collective-permute-start(bf16[432,1152]{1,0:T(8,128)(2,1)S(1)} %get-tuple-element.88), channel_id=1, source_target_pairs={{0,8},{4,12},{24,16},{28,20},{8,0},{12,4},{16,24},{20,28},{1,9},{5... | collective-permute-start | bytes 2985992 | tf_op jit(solution)/shard_map/ppermute | solution.py:650
  317.0 23.4 %collective-permute-start.36 = (bf16[432,1152]{1,0:T(8,128)(2,1)S(1)}, bf16[432,1152]{1,0:T(8,128)(2,1)S(1)}, u32[]{:S(2)}, u32[]{:S(2)}) collective-permute-start(bf16[432,1152]{1,0:T(8,128)(2,1)S(1)} %get-tuple-element.89.refs_2_), channel_id=1, source_target_pairs={{8,16},{12,20},{16,8},{20,12},{9,17},{13,21},{17,9},{21,13},{10,18... | collective-permute-start | bytes 2985992 | tf_op jit(solution)/shard_map/ppermute | solution.py:650
  343.2 40.8 %collective-permute-start.38 = (bf16[432,1152]{1,0:T(8,128)(2,1)S(1)}, bf16[432,1152]{1,0:T(8,128)(2,1)S(1)}, u32[]{:S(2)}, u32[]{:S(2)}) collective-permute-start(bf16[432,1152]{1,0:T(8,128)(2,1)S(1)} %get-tuple-element.95), channel_id=1, source_target_pairs={{0,8},{4,12},{24,16},{28,20},{8,0},{12,4},{16,24},{20,28},{1,9},{5... | collective-permute-start | bytes 2985992 | tf_op jit(solution)/shard_map/ppermute | solution.py:650
  346.9 37.1 %collective-permute-start.39 = (bf16[432,1152]{1,0:T(8,128)(2,1)S(1)}, bf16[432,1152]{1,0:T(8,128)(2,1)S(1)}, u32[]{:S(2)}, u32[]{:S(2)}) collective-permute-start(bf16[432,1152]{1,0:T(8,128)(2,1)S(1)} %get-tuple-element.96.refs_2_), channel_id=1, source_target_pairs={{8,16},{12,20},{16,8},{20,12},{9,17},{13,21},{17,9},{21,13},{10,18... | collective-permute-start | bytes 2985992 | tf_op jit(solution)/shard_map/ppermute | solution.py:650
  347.6 20.4 %collective-permute-start.40 = (bf16[304,1280]{1,0:T(8,128)(2,1)S(1)}, bf16[304,1280]{1,0:T(8,128)(2,1)S(1)}, u32[]{:S(2)}, u32[]{:S(2)}) collective-permute-start(bf16[304,1280]{1,0:T(8,128)(2,1)S(1)} %get-tuple-element.99), channel_id=1, source_target_pairs={{0,1},{1,0},{2,3},{3,2},{4,5},{5,4},{6,7},{7,6},{8,9},{9,8},{10,11... | collective-permute-start | bytes 2334728 | tf_op jit(solution)/shard_map/ppermute | solution.py:17
  349.3 34.7 %collective-permute-start.41 = (bf16[304,1280]{1,0:T(8,128)(2,1)S(1)}, bf16[304,1280]{1,0:T(8,128)(2,1)S(1)}, u32[]{:S(2)}, u32[]{:S(2)}) collective-permute-start(bf16[304,1280]{1,0:T(8,128)(2,1)S(1)} %get-tuple-element.100), channel_id=1, source_target_pairs={{0,2},{1,3},{2,0},{3,1},{4,6},{5,7},{6,4},{7,5},{8,10},{9,11},{10,... | collective-permute-start | bytes 2334728 | tf_op jit(solution)/shard_map/ppermute | solution.py:17
  349.3 34.7 %collective-permute-start.42 = (bf16[304,1280]{1,0:T(8,128)(2,1)S(1)}, bf16[304,1280]{1,0:T(8,128)(2,1)S(1)}, u32[]{:S(2)}, u32[]{:S(2)}) collective-permute-start(bf16[304,1280]{1,0:T(8,128)(2,1)S(1)} %get-tuple-element.101), channel_id=1, source_target_pairs={{0,3},{1,2},{2,1},{3,0},{4,7},{5,6},{6,5},{7,4},{8,11},{9,10},{10,... | collective-permute-start | bytes 2334728 | tf_op jit(solution)/shard_map/ppermute | solution.py:17
  368.0 25.8 %collective-permute-start.46 = (bf16[432,1152]{1,0:T(8,128)(2,1)S(1)}, bf16[432,1152]{1,0:T(8,128)(2,1)S(1)}, u32[]{:S(2)}, u32[]{:S(2)}) collective-permute-start(bf16[432,1152]{1,0:T(8,128)(2,1)S(1)} %get-tuple-element.105.refs_0_), channel_id=1, source_target_pairs={{0,4},{4,0},{8,12},{12,8},{16,20},{20,16},{24,28},{28,24},{1,5},{5... | collective-permute-start | bytes 2985992 | tf_op jit(solution)/shard_map/ppermute | solution.py:17
  385.2 26.3 %collective-permute-start.43 = (bf16[432,1152]{1,0:T(8,128)(2,1)S(1)}, bf16[432,1152]{1,0:T(8,128)(2,1)S(1)}, u32[]{:S(2)}, u32[]{:S(2)}) collective-permute-start(bf16[432,1152]{1,0:T(8,128)(2,1)S(1)} %get-tuple-element.102.refs_0_), channel_id=1, source_target_pairs={{8,0},{12,4},{16,24},{20,28},{9,1},{13,5},{17,25},{21,29},{10,2},{... | collective-permute-start | bytes 2985992 | tf_op jit(solution)/shard_map/ppermute | solution.py:650
  386.5 25.0 %collective-permute-start.44 = (bf16[432,1152]{1,0:T(8,128)(2,1)S(1)}, bf16[432,1152]{1,0:T(8,128)(2,1)S(1)}, u32[]{:S(2)}, u32[]{:S(2)}) collective-permute-start(bf16[432,1152]{1,0:T(8,128)(2,1)S(1)} %get-tuple-element.103.refs_2_), channel_id=1, source_target_pairs={{8,16},{12,20},{16,8},{20,12},{9,17},{13,21},{17,9},{21,13},{10,18... | collective-permute-start | bytes 2985992 | tf_op jit(solution)/shard_map/ppermute | solution.py:650
  387.3 23.4 %collective-permute-start.45 = (bf16[304,1280]{1,0:T(8,128)(2,1)S(1)}, bf16[304,1280]{1,0:T(8,128)(2,1)S(1)}, u32[]{:S(2)}, u32[]{:S(2)}) collective-permute-start(bf16[304,1280]{1,0:T(8,128)(2,1)S(1)} %get-tuple-element.104.refs_4_), channel_id=1, source_target_pairs={{0,8},{4,12},{24,16},{28,20},{1,9},{5,13},{25,17},{29,21},{2,10},{... | collective-permute-start | bytes 2334728 | tf_op jit(solution)/shard_map/ppermute | solution.py:650
  412.3 41.2 %collective-permute-start.48 = (bf16[432,1152]{1,0:T(8,128)(2,1)S(1)}, bf16[432,1152]{1,0:T(8,128)(2,1)}, u32[]{:S(2)}, u32[]{:S(2)}) collective-permute-start(bf16[432,1152]{1,0:T(8,128)(2,1)S(1)} %get-tuple-element.107.refs_0_), channel_id=1, source_target_pairs={{8,0},{12,4},{16,24},{20,28},{9,1},{13,5},{17,25},{21,29},{10,2},{... | collective-permute-start | bytes 2985992 | tf_op jit(solution)/shard_map/ppermute | solution.py:650
  456.2 36.8 %collective-permute-start.50 = (bf16[304,1280]{1,0:T(8,128)(2,1)S(1)}, bf16[304,1280]{1,0:T(8,128)(2,1)S(1)}, u32[]{:S(2)}, u32[]{:S(2)}) collective-permute-start(bf16[304,1280]{1,0:T(8,128)(2,1)S(1)} %get-tuple-element.109.refs_0_), channel_id=1, source_target_pairs={{8,0},{12,4},{16,24},{20,28},{9,1},{13,5},{17,25},{21,29},{10,2},{... | collective-permute-start | bytes 2334728 | tf_op jit(solution)/shard_map/ppermute | solution.py:650
  457.5 87.7 %collective-permute-start.52 = (bf16[432,1152]{1,0:T(8,128)(2,1)S(1)}, bf16[432,1152]{1,0:T(8,128)(2,1)}, u32[]{:S(2)}, u32[]{:S(2)}) collective-permute-start(bf16[432,1152]{1,0:T(8,128)(2,1)S(1)} %get-tuple-element.111.refs_0_), channel_id=1, source_target_pairs={{0,4},{4,0},{8,12},{12,8},{16,20},{20,16},{24,28},{28,24},{1,5},{5... | collective-permute-start | bytes 2985992 | tf_op jit(solution)/shard_map/ppermute | solution.py:17
  457.6 87.6 %collective-permute-start.53 = (bf16[432,1152]{1,0:T(8,128)(2,1)S(1)}, bf16[432,1152]{1,0:T(8,128)(2,1)}, u32[]{:S(2)}, u32[]{:S(2)}) collective-permute-start(bf16[432,1152]{1,0:T(8,128)(2,1)S(1)} %get-tuple-element.112.refs_1_), channel_id=1, source_target_pairs={{0,4},{4,0},{8,12},{12,8},{16,20},{20,16},{24,28},{28,24},{1,5},{5... | collective-permute-start | bytes 2985992 | tf_op jit(solution)/shard_map/ppermute | solution.py:17
  493.1 57.2 %collective-permute-start.51 = (bf16[304,1280]{1,0:T(8,128)(2,1)S(1)}, bf16[304,1280]{1,0:T(8,128)(2,1)S(1)}, u32[]{:S(2)}, u32[]{:S(2)}) collective-permute-start(bf16[304,1280]{1,0:T(8,128)(2,1)S(1)} %line_step.15), channel_id=1, source_target_pairs={{0,4},{4,0},{8,12},{12,8},{16,20},{20,16},{24,28},{28,24},{1,5},{5... | collective-permute-start | bytes 2334728 | tf_op jit(solution)/shard_map/ppermute | solution.py:17
  (126 other events, 954.3 us)
Sparse Core Ops, SparseCore 0:
  414.4 124.8 all-reduce.4

commit v9 on v8

--- a/solution.py
+++ b/solution.py
@@ -389,41 +389,6 @@
         name="owner_parts",
     )(scalar(lax.axis_index("fsdp")), mine, far)
     return [parts[0]] + [swapped(parts[mask], "fsdp", mask) for mask in range(1, group)]
-
-
-def weight_grad_whole(lefts, rights):
-    group = len(rights)
-    units, rows = lefts[0].shape
-    model = rights[0].shape[1]
-    tile = tile_of(units, 432)
-
-    def kernel(*refs):
-        right_refs, left_refs = refs[:group], refs[group : 2 * group]
-        out_ref, left_ref, right_ref = refs[2 * group :]
-
-        @pl.when(pl.program_id(0) == 0)
-        def _():
-            for spot in range(group):
-                right_ref[spot * rows : (spot + 1) * rows, :] = right_refs[spot][...]
-
-        for spot in range(group):
-            left_ref[:, spot * rows : (spot + 1) * rows] = left_refs[spot][...]
-        out_ref[...] = dot(left_ref[...], right_ref[...], 1, 0).astype(jnp.bfloat16)
-
-    return pl.pallas_call(
-        kernel,
-        grid=(units // tile,),
-        in_specs=[pl.BlockSpec((rows, model), lambda i: (0, 0))] * group
-        + [pl.BlockSpec((tile, rows), lambda i: (i, 0))] * group,
-        out_specs=pl.BlockSpec((tile, model), lambda i: (i, 0)),
-        out_shape=jax.ShapeDtypeStruct((units, model), jnp.bfloat16),
-        scratch_shapes=[
-            pltpu.VMEM((tile, group * rows), jnp.bfloat16),
-            pltpu.VMEM((group * rows, model), jnp.bfloat16),
-        ],
-        compiler_params=params(32),
-        name="weight_grad",
-    )(*rights, *lefts)
 
 
 def chunks_of(units):
@@ -922,7 +887,7 @@
             for gain in (norm_in, norm_attn, norm_ffn, norm_out, query_gain, key_gain)
         ]
     )
-    gains = after(gains, qkv_block)
+    gains = after(gains, *[got[mask - 1] for mask in masks if bin(mask).count("1") == 1])
     gain_stack = jnp.stack([gains] + [swapped(gains, "fsdp", mask) for mask in masks])
     w_qkv = unpacked(qkv_weights, got, peers)
     gain_rows = jnp.stack(
@@ -943,7 +908,7 @@
     parts = [pair_new]
     for step in range(1, hops + 1):
         parts.insert(0, passed_along(pair_new, "fsdp", step))
-    pairs = after(jnp.concatenate(parts, axis=0), w_out)
+    pairs = jnp.concatenate(parts, axis=0)
     width = pairs.shape[0]
     seg_padded = jnp.concatenate([jnp.full((hops * rows,), -1, jnp.int32), segments], axis=0)
     key_segs = lax.dynamic_slice_in_dim(seg_padded, rank * rows, width, 0)
@@ -1002,21 +967,21 @@
         returned[mask] = swapped(part, "fsdp", mask) if mask else part
         last = mask
     pieces[final] = after(pieces[final], part)
-    grad_down = weight_grad_whole(
-        [hiddens[i] for i in range(group)], [pieces[i] for i in range(group)]
-    )
-    pieces[final] = after(pieces[final], grad_down)
-    grad_down = lax.psum(grad_down, "replica").astype(jnp.float32)
+    waiting = fresh(
+        ["down"], *weight_grad([[hiddens[i] for i in range(group)]], [pieces[i] for i in range(group)])
+    )
     gate_parts, upper_parts, parts = ffn_backward_blocks(
         [pieces[final]], gate_weight, up_weight, down_weight, [slopes[final]], [acts[final]]
     )
     grad_gates[final], grad_uppers[final] = gate_parts[0], upper_parts[0]
     returned[final] = swapped(parts[0], "fsdp", final)
-    grad_gates[final] = after(grad_gates[final], *[returned[mask] for mask in rings[1:-1]])
+    grad_gates[final] = line.advance(
+        [waiting.pop(0)], after(grad_gates[final], *[returned[mask] for mask in rings[1:-1]])
+    )
     other, mine = weight_grad(
         [[grad_gates[i] for i in range(group)], [grad_uppers[i] for i in range(group)]], ffn_blocks
     )
-    other = after(other, returned[final])
+    other = line.advance([waiting.pop(0)] if waiting else [], after(other, returned[final]))
     waiting = fresh(["gate", "up"], other, mine)
 
     def advance(gate=None):
@@ -1058,6 +1023,8 @@
     while waiting:
         weight_parts[0] = advance(weight_parts[0])
     line.advance([("weights", weight_parts)])
+    grad_down = whole_grad(line, "down", units)
+    grad_down = line.advance([], grad_down)
     grad_gate_w = whole_grad(line, "gate", units)
     grad_gate_w = line.advance([], grad_gate_w)
     grad_up_w = whole_grad(line, "up", units)

time: 569 us -> 479 us (0.84)
  waiting for transfers between devices: 268 us -> 196 us
  local copies, waits for them, and re-layouts: 61.8 us -> 43.8 us
  Pallas kernels: 83.4 us -> 96.8 us
  between operations: 15.9 us -> 2.55 us
  other arithmetic: 14.3 us -> 8.38 us
    psum x1 -> x0, waiting for transfers between devices: 46.2 us -> none  [per_device(): grad_down = lax.psum(grad_down, 'replica').astype(jnp.float32)]
    ppermute x13 -> x17, waiting for transfers between devices: 119 us -> 91.8 us  [exchanged(): return lax.ppermute(block, 'replica', route)]
    unnamed x208 -> x188, local copies, waits for them, and re-layouts: 46.6 us -> 29.5 us
    ppermute x13 -> x17, starting transfers between devices: 30.1 us -> 40 us  [exchanged(): return lax.ppermute(block, 'replica', route)]
    pallas_call x1 -> x2, Pallas kernels: 16.2 us -> 23.9 us  [weight_grad(): pl.pallas_call(kernel, grid_spec=pltpu.PrefetchScalarGridSpec(num_scalar_...]
    pallas_call x8 -> x10, Pallas kernels: 15.8 us -> 21.8 us  [advance(): pl.pallas_call(kernel, grid_spec=pltpu.PrefetchScalarGridSpec(num_scalar_...]
    convert_element_type x1 -> x0, other arithmetic: 5.89 us -> none  [per_device(): grad_down = lax.psum(grad_down, 'replica').astype(jnp.float32)]
    ppermute x37 -> x40, starting transfers between devices: 34.8 us -> 30.1 us  [swapped(): return lax.ppermute(block, axis, route)]
  transfers between devices with their start and end apart: 55 -> 61, of which waited for: 21 -> 28; matrix products, arithmetic and copies ran while one was open for 11% -> 12% of each run, Pallas kernels for 12% -> 15%
where the time goes in v9:
time: 479 us; the launch traced here: 473 us
  waiting for transfers between devices  196 us (41%)
  Pallas kernels  96.8 us (20%)
  starting transfers between devices  80.3 us (17%)
  matrix products  44.6 us (9%)
  local copies, waits for them, and re-layouts  43.8 us (9%)
  other arithmetic  8.38 us (2%)
    ppermute x17, waiting for transfers between devices, exchanged(): return lax.ppermute(block, 'replica', route)  91.8 us
    ppermute x40, waiting for transfers between devices, swapped(): return lax.ppermute(block, axis, route)  89.2 us
    dot_general x22, matrix products, contract(): lax.dot_general(left, right, (((left_dim,), (right_dim,)), ((), ())), pre...  43.4 us
    ppermute x17, starting transfers between devices, exchanged(): return lax.ppermute(block, 'replica', route)  40 us
    ppermute x40, starting transfers between devices, swapped(): return lax.ppermute(block, axis, route)  30.1 us
    unnamed x188, local copies, waits for them, and re-layouts  29.5 us
    pallas_call x2, Pallas kernels, weight_grad(): pl.pallas_call(kernel, grid_spec=pltpu.PrefetchScalarGridSpec(num_scalar_...  23.9 us
    pallas_call x10, Pallas kernels, advance(): pl.pallas_call(kernel, grid_spec=pltpu.PrefetchScalarGridSpec(num_scalar_...  21.8 us
  transfers between devices with their start and end apart: 61, of which 28 were waited for; matrix products, arithmetic and copies ran while one was open for 12% of the time, Pallas kernels for 15%

profile of v9, /device:TPU:0, one launch (start us, length us, event | category | flops | bytes accessed | tf_op | source)
XLA Modules:
  0.0 472.7 jit_solution(4900998321144325002)
XLA Ops:
  12.6 4.3 collective-permute-done.1.refs_2_.refs_4_
  24.1 3.8 collective-permute-done.5.refs_5_
  39.3 4.2 collective-permute-start.10
  46.9 5.2 %collective-permute-done.12.refs_2_ = bf16[144,1024]{1,0:T(8,128)(2,1)} collective-permute-done((bf16[144,1024]{1,0:T(8,128)(2,1)S(1)}, bf16[144,1024]{1,0:T(8,128)(2,1)}, u32[]{:S(2)}, u32[]{:S(2)}) %collective-permute-start.12) | collective-permute-done | bytes 294944 | tf_op jit(solution)/shard_map/ppermute | solution.py:17
  56.9 5.6 %collective-permute-done.9 = bf16[256,512]{1,0:T(8,128)(2,1)} collective-permute-done((bf16[256,512]{1,0:T(8,128)(2,1)S(1)}, bf16[256,512]{1,0:T(8,128)(2,1)}, u32[]{:S(2)}, u32[]{:S(2)}) %collective-permute-start.9) | collective-permute-done | bytes 262176 | tf_op jit(solution)/shard_map/ppermute | solution.py:813
  63.7 4.1 attention_forward.1
  78.3 12.0 %collective-permute-done.18.refs_2_.refs_0_ = bf16[256,1152]{1,0:T(8,128)(2,1)} collective-permute-done((bf16[256,1152]{1,0:T(8,128)(2,1)}, bf16[256,1152]{1,0:T(8,128)(2,1)}, u32[]{:S(2)}, u32[]{:S(2)}) %collective-permute-start.18) | collective-permute-done | bytes 589856 | tf_op jit(solution)/shard_map/ppermute | solution.py:17
  91.8 3.8 convolution_bitcast_fusion.10
  120.3 14.3 %collective-permute-done.21 = bf16[256,1152]{1,0:T(8,128)(2,1)S(1)} collective-permute-done((bf16[256,1152]{1,0:T(8,128)(2,1)S(1)}, bf16[256,1152]{1,0:T(8,128)(2,1)S(1)}, u32[]{:S(2)}, u32[]{:S(2)}) %collective-permute-start.21) | collective-permute-done | bytes 589856 | tf_op jit(solution)/shard_map/ppermute | solution.py:17
  146.0 4.8 %collective-permute-done.24.refs_0_.refs_2_ = bf16[256,1152]{1,0:T(8,128)(2,1)S(1)} collective-permute-done((bf16[256,1152]{1,0:T(8,128)(2,1)S(1)}, bf16[256,1152]{1,0:T(8,128)(2,1)S(1)}, u32[]{:S(2)}, u32[]{:S(2)}) %collective-permute-start.24) | collective-permute-done | bytes 589856 | tf_op jit(solution)/shard_map/ppermute | solution.py:17
  166.3 7.5 %weight_grad.2 = (bf16[2,432,1152]{2,1,0:T(8,128)(2,1)}, bf16[2,432,1152]{2,1,0:T(8,128)(2,1)}) custom-call(s32[1]{0:T(128)} %bitcast.core_ref, bf16[256,1152]{1,0:T(8,128)(2,1)S(1)} %get-tuple-element.177.refs_0_, bf16[256,1152]{1,0:T(8,128)(2,1)S(1)} %after.18.refs_1_, bf16[256,1152]{1,0:T(8,128)(2,1)S(1)} %after.19.refs_2_, ...), custom_call_target="tpu_custom_call" | custom-call | tf_op jit(solution)/shard_map/weight_grad/pallas_call | solution.py:445
  179.7 9.8 %ffn_backward.1 = (bf16[1728,256]{1,0:T(8,128)(2,1)S(1)}, bf16[1728,256]{1,0:T(8,128)(2,1)S(1)}, bf16[256,1152]{1,0:T(8,128)(2,1)S(1)}) custom-call(bf16[256,1152]{1,0:T(8,128)(2,1)S(1)} %copy-done.14, bf16[1728,1152]{1,0:T(8,128)(2,1)} %refs_1_.5, bf16[1728,1152]{1,0:T(8,128)(2,1)} %refs_2_.5, bf16[1728,1152]{1,0:T(8,128)(2,1)} %refs_3_.1, ...), custom_call_target="tpu_custom_call" | custom-call | tf_op jit(solution)/shard_map/ffn_backward/pallas_call | solution.py:195
  198.3 16.5 %weight_grad.3 = (bf16[4,432,1152]{2,1,0:T(8,128)(2,1)}, bf16[4,432,1152]{2,1,0:T(8,128)(2,1)}) custom-call(s32[1]{0:T(128)} %bitcast.core_ref, bf16[256,1152]{1,0:T(8,128)(2,1)S(1)} %copy-done.18, bf16[256,1152]{1,0:T(8,128)(2,1)} %collective-permute-done.17.refs_1_, bf16[256,1152]{1,0:T(8,128)(2,1)} %after.15.refs_2_, bf16[256,1152]{1,0:T(8,128)(2,1)S(1)} %copy-done.33, ...), custom_call_target="tpu_custom_call" | custom-call | tf_op jit(solution)/shard_map/weight_grad/pallas_call | solution.py:445
  223.7 7.2 %collective-permute-start.32 = (bf16[432,1152]{1,0:T(8,128)(2,1)}, bf16[432,1152]{1,0:T(8,128)(2,1)}, u32[]{:S(2)}, u32[]{:S(2)}) collective-permute-start(bf16[432,1152]{1,0:T(8,128)(2,1)} %get-tuple-element.89.refs_2_), channel_id=1, source_target_pairs={{0,8},{4,12},{24,16},{28,20},{1,9},{5,13},{25,17},{29,21},{2,10},{... | collective-permute-start | bytes 2985992 | tf_op jit(solution)/shard_map/ppermute | solution.py:615
  238.8 3.6 resid_backward.1
  245.5 6.4 %collective-permute-done.32.refs_3_ = bf16[432,1152]{1,0:T(8,128)(2,1)} collective-permute-done((bf16[432,1152]{1,0:T(8,128)(2,1)}, bf16[432,1152]{1,0:T(8,128)(2,1)}, u32[]{:S(2)}, u32[]{:S(2)}) %collective-permute-start.32) | collective-permute-done | bytes 995360 | tf_op jit(solution)/shard_map/ppermute | solution.py:615
  252.0 3.7 line_step.12
  259.0 6.6 %attention_backward.1 = (bf16[256,1024]{1,0:T(8,128)(2,1)S(1)}, f32[1,256]{1,0:T(1,128)S(1)}, bf16[512,512]{1,0:T(8,128)(2,1)S(1)}, f32[256,512]{1,0:T(8,128)S(1)}) custom-call(f32[256,1536]{1,0:T(8,128)S(1)} %copy-done.3, bf16[1,256]{1,0:T(2,128)(2,1)S(1)} %broadcast_in_dim_reshape_squeeze.2.gain_ref, f32[256,128]{1,0:T(8,128)S(1)} %copy-done.42, ...), custom_call_target="tpu_custom_call" | custom-call | tf_op jit(solution)/shard_map/attention_backward/pallas_call | solution.py:590
  267.7 12.1 %collective-permute-done.34.refs_1_ = bf16[432,1152]{1,0:T(8,128)(2,1)S(1)} collective-permute-done((bf16[432,1152]{1,0:T(8,128)(2,1)S(1)}, bf16[432,1152]{1,0:T(8,128)(2,1)S(1)}, u32[]{:S(2)}, u32[]{:S(2)}) %collective-permute-start.34) | collective-permute-done | bytes 995360 | tf_op jit(solution)/shard_map/ppermute | solution.py:615
  279.9 3.6 line_step.13
  286.5 3.6 collective-permute-start.38
  294.0 7.1 %collective-permute-done.37.refs_2_ = bf16[256,512]{1,0:T(8,128)(2,1)} collective-permute-done((bf16[256,512]{1,0:T(8,128)(2,1)}, bf16[256,512]{1,0:T(8,128)(2,1)}, u32[]{:S(2)}, u32[]{:S(2)}) %collective-permute-start.37) | collective-permute-done | bytes 262176 | tf_op jit(solution)/shard_map/ppermute | solution.py:813
  303.5 9.1 %input_backward.1 = (bf16[4,304,1280]{2,1,0:T(8,128)(2,1)}, bf16[4,304,1280]{2,1,0:T(8,128)(2,1)}, f32[256,1152]{1,0:T(8,128)}) custom-call(s32[1]{0:T(128)} %bitcast.core_ref, f32[256,512]{1,0:T(8,128)S(1)} %get-tuple-element.100.refs_0_, bf16[256,512]{1,0:T(8,128)(2,1)S(1)} %get-tuple-element.180.refs_1_, ...), custom_call_target="tpu_custom_call" | custom-call | tf_op jit(solution)/shard_map/input_backward/pallas_call | solution.py:351
  326.6 17.5 %collective-permute-done.40.refs_1_ = bf16[432,1152]{1,0:T(8,128)(2,1)S(1)} collective-permute-done((bf16[432,1152]{1,0:T(8,128)(2,1)S(1)}, bf16[432,1152]{1,0:T(8,128)(2,1)S(1)}, u32[]{:S(2)}, u32[]{:S(2)}) %collective-permute-start.40) | collective-permute-done | bytes 995360 | tf_op jit(solution)/shard_map/ppermute | solution.py:615
  346.9 3.7 collective-permute-start.43
  354.9 16.8 %collective-permute-done.45.refs_6_ = bf16[304,1280]{1,0:T(8,128)(2,1)S(1)} collective-permute-done((bf16[304,1280]{1,0:T(8,128)(2,1)S(1)}, bf16[304,1280]{1,0:T(8,128)(2,1)S(1)}, u32[]{:S(2)}, u32[]{:S(2)}) %collective-permute-start.45) | collective-permute-done | bytes 778272 | tf_op jit(solution)/shard_map/ppermute | solution.py:17
  371.7 15.2 %collective-permute-done.46.refs_7_ = bf16[304,1280]{1,0:T(8,128)(2,1)S(1)} collective-permute-done((bf16[304,1280]{1,0:T(8,128)(2,1)S(1)}, bf16[304,1280]{1,0:T(8,128)(2,1)S(1)}, u32[]{:S(2)}, u32[]{:S(2)}) %collective-permute-start.46) | collective-permute-done | bytes 778272 | tf_op jit(solution)/shard_map/ppermute | solution.py:17
  390.2 6.5 %collective-permute-start.50 = (bf16[304,1280]{1,0:T(8,128)(2,1)S(1)}, bf16[304,1280]{1,0:T(8,128)(2,1)S(1)}, u32[]{:S(2)}, u32[]{:S(2)}) collective-permute-start(bf16[304,1280]{1,0:T(8,128)(2,1)S(1)} %get-tuple-element.131.refs_4_), channel_id=1, source_target_pairs={{0,8},{4,12},{24,16},{28,20},{1,9},{5,13},{25,17},{29,21},{2,10},{... | collective-permute-start | bytes 2334728 | tf_op jit(solution)/shard_map/ppermute | solution.py:615
  400.8 12.8 %collective-permute-done.50.refs_5_ = bf16[304,1280]{1,0:T(8,128)(2,1)S(1)} collective-permute-done((bf16[304,1280]{1,0:T(8,128)(2,1)S(1)}, bf16[304,1280]{1,0:T(8,128)(2,1)S(1)}, u32[]{:S(2)}, u32[]{:S(2)}) %collective-permute-start.50) | collective-permute-done | bytes 778272 | tf_op jit(solution)/shard_map/ppermute | solution.py:615
  420.8 21.0 %collective-permute-done.53.refs_1_ = bf16[432,1152]{1,0:T(8,128)(2,1)S(1)} collective-permute-done((bf16[432,1152]{1,0:T(8,128)(2,1)S(1)}, bf16[432,1152]{1,0:T(8,128)(2,1)S(1)}, u32[]{:S(2)}, u32[]{:S(2)}) %collective-permute-start.53) | collective-permute-done | bytes 995360 | tf_op jit(solution)/shard_map/ppermute | solution.py:615
  444.0 18.1 %collective-permute-done.57.refs_1_ = bf16[304,1280]{1,0:T(8,128)(2,1)S(1)} collective-permute-done((bf16[304,1280]{1,0:T(8,128)(2,1)S(1)}, bf16[304,1280]{1,0:T(8,128)(2,1)S(1)}, u32[]{:S(2)}, u32[]{:S(2)}) %collective-permute-start.57) | collective-permute-done | bytes 778272 | tf_op jit(solution)/shard_map/ppermute | solution.py:615
  462.3 5.0 %whole_grad.5 = f32[1728,1152]{1,0:T(8,128)} custom-call(s32[1]{0:T(128)} %bitcast.core_ref, bf16[432,1152]{1,0:T(8,128)(2,1)S(1)} %get-tuple-element.140.refs_0_, bf16[432,1152]{1,0:T(8,128)(2,1)S(1)} %get-tuple-element.141.refs_1_, bf16[432,1152]{1,0:T(8,128)(2,1)} %collective-permute-done.59.refs_2_, bf16[432,1152]{1,0:T(8,128)(2,1)} %collective-permute-done.60.refs_3_), custom_call_target="tpu_custom_call" | custom-call | tf_op jit(solution)/shard_map/whole_grad/pallas_call | solution.py:766
  (397 shorter events, 194.6 us)
Async XLA Ops:
  8.2 19.7 %collective-permute-start.5 = (bf16[144,1536]{1,0:T(8,128)(2,1)S(1)}, bf16[144,1536]{1,0:T(8,128)(2,1)}, u32[]{:S(2)}, u32[]{:S(2)}) collective-permute-start(bf16[144,1536]{1,0:T(8,128)(2,1)S(1)} %pack.2), channel_id=1, source_target_pairs={{0,3},{1,2},{2,1},{3,0},{4,7},{5,6},{6,5},{7,4},{8,11},{9,10},{10,... | collective-permute-start | bytes 1327112 | tf_op jit(solution)/shard_map/ppermute | solution.py:17
  39.3 17.6 %collective-permute-start.10 = (bf16[256,512]{1,0:T(8,128)(2,1)S(1)}, bf16[256,512]{1,0:T(8,128)(2,1)}, u32[]{:S(2)}, u32[]{:S(2)}) collective-permute-start(bf16[256,512]{1,0:T(8,128)(2,1)S(1)} %pad_maximum_fusion.refs_1_), channel_id=1, source_target_pairs={{0,1},{1,2},{2,3},{4,5},{5,6},{6,7},{8,9},{9,10},{10,11},{12,13},{... | collective-permute-start | bytes 786440 | tf_op jit(solution)/shard_map/ppermute | solution.py:813
  43.5 18.9 %collective-permute-start.9 = (bf16[256,512]{1,0:T(8,128)(2,1)S(1)}, bf16[256,512]{1,0:T(8,128)(2,1)}, u32[]{:S(2)}, u32[]{:S(2)}) collective-permute-start(bf16[256,512]{1,0:T(8,128)(2,1)S(1)} %pad_maximum_fusion.refs_1_), channel_id=1, source_target_pairs={{0,2},{1,3},{4,6},{5,7},{8,10},{9,11},{12,14},{13,15},{16,18},{17,... | collective-permute-start | bytes 786440 | tf_op jit(solution)/shard_map/ppermute | solution.py:813
  46.9 20.9 %collective-permute-start.16 = (bf16[144,1024]{1,0:T(8,128)(2,1)S(1)}, bf16[144,1024]{1,0:T(8,128)(2,1)}, u32[]{:S(2)}, u32[]{:S(2)}) collective-permute-start(bf16[144,1024]{1,0:T(8,128)(2,1)S(1)} %collective-permute-done.13.refs_3_), channel_id=1, source_target_pairs={{0,4},{4,0},{8,12},{12,8},{16,20},{20,16},{24,28},{28,24},{1,5},{5... | collective-permute-start | bytes 884744 | tf_op jit(solution)/shard_map/ppermute | solution.py:17
  91.8 18.0 %collective-permute-start.19 = (bf16[256,1152]{1,0:T(8,128)(2,1)}, bf16[256,1152]{1,0:T(8,128)(2,1)S(1)}, u32[]{:S(2)}, u32[]{:S(2)}) collective-permute-start(bf16[256,1152]{1,0:T(8,128)(2,1)} %after.14), channel_id=1, source_target_pairs={{0,3},{1,2},{2,1},{3,0},{4,7},{5,6},{6,5},{7,4},{8,11},{9,10},{10,... | collective-permute-start | bytes 1769480 | tf_op jit(solution)/shard_map/ppermute | solution.py:17
  99.9 20.4 %collective-permute-start.20 = (bf16[256,1152]{1,0:T(8,128)(2,1)S(1)}, bf16[256,1152]{1,0:T(8,128)(2,1)S(1)}, u32[]{:S(2)}, u32[]{:S(2)}) collective-permute-start(bf16[256,1152]{1,0:T(8,128)(2,1)S(1)} %convolution_convert_fusion.3.refs_1_), channel_id=1, source_target_pairs={{0,1},{1,0},{2,3},{3,2},{4,5},{5,4},{6,7},{7,6},{8,9},{9,8},{10,11... | collective-permute-start | bytes 1769480 | tf_op jit(solution)/shard_map/ppermute | solution.py:17
  108.0 26.6 %collective-permute-start.21 = (bf16[256,1152]{1,0:T(8,128)(2,1)S(1)}, bf16[256,1152]{1,0:T(8,128)(2,1)S(1)}, u32[]{:S(2)}, u32[]{:S(2)}) collective-permute-start(bf16[256,1152]{1,0:T(8,128)(2,1)S(1)} %convolution_convert_fusion.2.refs_1_), channel_id=1, source_target_pairs={{0,2},{1,3},{2,0},{3,1},{4,6},{5,7},{6,4},{7,5},{8,10},{9,11},{10,... | collective-permute-start | bytes 1769480 | tf_op jit(solution)/shard_map/ppermute | solution.py:17
  116.4 18.2 %collective-permute-start.22 = (bf16[256,1152]{1,0:T(8,128)(2,1)S(1)}, bf16[256,1152]{1,0:T(8,128)(2,1)S(1)}, u32[]{:S(2)}, u32[]{:S(2)}) collective-permute-start(bf16[256,1152]{1,0:T(8,128)(2,1)S(1)} %convolution_convert_fusion.1.refs_1_), channel_id=1, source_target_pairs={{0,3},{1,2},{2,1},{3,0},{4,7},{5,6},{6,5},{7,4},{8,11},{9,10},{10,... | collective-permute-start | bytes 1769480 | tf_op jit(solution)/shard_map/ppermute | solution.py:17
  193.8 24.9 %collective-permute-start.29 = (bf16[432,1152]{1,0:T(8,128)(2,1)S(1)}, bf16[432,1152]{1,0:T(8,128)(2,1)S(1)}, u32[]{:S(2)}, u32[]{:S(2)}) collective-permute-start(bf16[432,1152]{1,0:T(8,128)(2,1)S(1)} %get-tuple-element.83.refs_0_), channel_id=1, source_target_pairs={{0,8},{4,12},{24,16},{28,20},{1,9},{5,13},{25,17},{29,21},{2,10},{... | collective-permute-start | bytes 2985992 | tf_op jit(solution)/shard_map/ppermute | solution.py:615
  222.1 29.8 %collective-permute-start.33 = (bf16[4,432,1152]{2,1,0:T(8,128)(2,1)}, bf16[4,432,1152]{2,1,0:T(8,128)(2,1)}, u32[]{:S(2)}, u32[]{:S(2)}) collective-permute-start(bf16[4,432,1152]{2,1,0:T(8,128)(2,1)} %get-tuple-element.91), channel_id=1, source_target_pairs={{0,4},{4,0},{8,12},{12,8},{16,20},{20,16},{24,28},{28,24},{1,5},{5... | collective-permute-start | bytes 11943944 | tf_op jit(solution)/shard_map/ppermute | solution.py:17
  222.1 23.4 %collective-permute-start.31 = (bf16[432,1152]{1,0:T(8,128)(2,1)}, bf16[432,1152]{1,0:T(8,128)(2,1)}, u32[]{:S(2)}, u32[]{:S(2)}) collective-permute-start(bf16[432,1152]{1,0:T(8,128)(2,1)} %get-tuple-element.88.refs_0_), channel_id=1, source_target_pairs={{8,16},{12,20},{16,8},{20,12},{9,17},{13,21},{17,9},{21,13},{10,18... | collective-permute-start | bytes 2985992 | tf_op jit(solution)/shard_map/ppermute | solution.py:615
  223.7 28.2 %collective-permute-start.32 = (bf16[432,1152]{1,0:T(8,128)(2,1)}, bf16[432,1152]{1,0:T(8,128)(2,1)}, u32[]{:S(2)}, u32[]{:S(2)}) collective-permute-start(bf16[432,1152]{1,0:T(8,128)(2,1)} %get-tuple-element.89.refs_2_), channel_id=1, source_target_pairs={{0,8},{4,12},{24,16},{28,20},{1,9},{5,13},{25,17},{29,21},{2,10},{... | collective-permute-start | bytes 2985992 | tf_op jit(solution)/shard_map/ppermute | solution.py:615
  255.7 24.1 %collective-permute-start.34 = (bf16[432,1152]{1,0:T(8,128)(2,1)S(1)}, bf16[432,1152]{1,0:T(8,128)(2,1)S(1)}, u32[]{:S(2)}, u32[]{:S(2)}) collective-permute-start(bf16[432,1152]{1,0:T(8,128)(2,1)S(1)} %get-tuple-element.94), channel_id=1, source_target_pairs={{0,8},{4,12},{24,16},{28,20},{8,0},{12,4},{16,24},{20,28},{1,9},{5... | collective-permute-start | bytes 2985992 | tf_op jit(solution)/shard_map/ppermute | solution.py:615
  258.2 21.6 %collective-permute-start.35 = (bf16[432,1152]{1,0:T(8,128)(2,1)S(1)}, bf16[432,1152]{1,0:T(8,128)(2,1)S(1)}, u32[]{:S(2)}, u32[]{:S(2)}) collective-permute-start(bf16[432,1152]{1,0:T(8,128)(2,1)S(1)} %get-tuple-element.95.refs_2_), channel_id=1, source_target_pairs={{8,16},{12,20},{16,8},{20,12},{9,17},{13,21},{17,9},{21,13},{10,18... | collective-permute-start | bytes 2985992 | tf_op jit(solution)/shard_map/ppermute | solution.py:615
  266.4 25.3 %collective-permute-start.36 = (bf16[512,512]{1,0:T(8,128)(2,1)S(1)}, bf16[512,512]{1,0:T(8,128)(2,1)S(1)}, u32[]{:S(2)}, u32[]{:S(2)}) collective-permute-start(bf16[512,512]{1,0:T(8,128)(2,1)S(1)} %get-tuple-element.101), channel_id=1, source_target_pairs={{1,0},{2,1},{3,2},{5,4},{6,5},{7,6},{9,8},{10,9},{11,10},{13,12},{... | collective-permute-start | bytes 1572872 | tf_op jit(solution)/shard_map/ppermute | solution.py:813
  286.5 26.1 %collective-permute-start.38 = (bf16[432,1152]{1,0:T(8,128)(2,1)}, bf16[432,1152]{1,0:T(8,128)(2,1)}, u32[]{:S(2)}, u32[]{:S(2)}) collective-permute-start(bf16[432,1152]{1,0:T(8,128)(2,1)} %get-tuple-element.110), channel_id=1, source_target_pairs={{0,8},{4,12},{24,16},{28,20},{8,0},{12,4},{16,24},{20,28},{1,9},{5... | collective-permute-start | bytes 2985992 | tf_op jit(solution)/shard_map/ppermute | solution.py:615
  290.1 22.5 %collective-permute-start.39 = (bf16[432,1152]{1,0:T(8,128)(2,1)}, bf16[432,1152]{1,0:T(8,128)(2,1)}, u32[]{:S(2)}, u32[]{:S(2)}) collective-permute-start(bf16[432,1152]{1,0:T(8,128)(2,1)} %get-tuple-element.111.refs_2_), channel_id=1, source_target_pairs={{8,16},{12,20},{16,8},{20,12},{9,17},{13,21},{17,9},{21,13},{10,18... | collective-permute-start | bytes 2985992 | tf_op jit(solution)/shard_map/ppermute | solution.py:615
  319.3 24.8 %collective-permute-start.40 = (bf16[432,1152]{1,0:T(8,128)(2,1)S(1)}, bf16[432,1152]{1,0:T(8,128)(2,1)S(1)}, u32[]{:S(2)}, u32[]{:S(2)}) collective-permute-start(bf16[432,1152]{1,0:T(8,128)(2,1)S(1)} %get-tuple-element.115), channel_id=1, source_target_pairs={{0,8},{4,12},{24,16},{28,20},{8,0},{12,4},{16,24},{20,28},{1,9},{5... | collective-permute-start | bytes 2985992 | tf_op jit(solution)/shard_map/ppermute | solution.py:615
  321.5 22.6 %collective-permute-start.41 = (bf16[432,1152]{1,0:T(8,128)(2,1)S(1)}, bf16[432,1152]{1,0:T(8,128)(2,1)S(1)}, u32[]{:S(2)}, u32[]{:S(2)}) collective-permute-start(bf16[432,1152]{1,0:T(8,128)(2,1)S(1)} %get-tuple-element.116.refs_2_), channel_id=1, source_target_pairs={{8,16},{12,20},{16,8},{20,12},{9,17},{13,21},{17,9},{21,13},{10,18... | collective-permute-start | bytes 2985992 | tf_op jit(solution)/shard_map/ppermute | solution.py:615
  346.9 40.0 %collective-permute-start.43 = (bf16[432,1152]{1,0:T(8,128)(2,1)S(1)}, bf16[432,1152]{1,0:T(8,128)(2,1)S(1)}, u32[]{:S(2)}, u32[]{:S(2)}) collective-permute-start(bf16[432,1152]{1,0:T(8,128)(2,1)S(1)} %get-tuple-element.122), channel_id=1, source_target_pairs={{0,8},{4,12},{24,16},{28,20},{8,0},{12,4},{16,24},{20,28},{1,9},{5... | collective-permute-start | bytes 2985992 | tf_op jit(solution)/shard_map/ppermute | solution.py:615
  350.6 36.3 %collective-permute-start.44 = (bf16[432,1152]{1,0:T(8,128)(2,1)S(1)}, bf16[432,1152]{1,0:T(8,128)(2,1)S(1)}, u32[]{:S(2)}, u32[]{:S(2)}) collective-permute-start(bf16[432,1152]{1,0:T(8,128)(2,1)S(1)} %get-tuple-element.123.refs_2_), channel_id=1, source_target_pairs={{8,16},{12,20},{16,8},{20,12},{9,17},{13,21},{17,9},{21,13},{10,18... | collective-permute-start | bytes 2985992 | tf_op jit(solution)/shard_map/ppermute | solution.py:615
  351.4 20.4 %collective-permute-start.45 = (bf16[304,1280]{1,0:T(8,128)(2,1)S(1)}, bf16[304,1280]{1,0:T(8,128)(2,1)S(1)}, u32[]{:S(2)}, u32[]{:S(2)}) collective-permute-start(bf16[304,1280]{1,0:T(8,128)(2,1)S(1)} %get-tuple-element.126), channel_id=1, source_target_pairs={{0,1},{1,0},{2,3},{3,2},{4,5},{5,4},{6,7},{7,6},{8,9},{9,8},{10,11... | collective-permute-start | bytes 2334728 | tf_op jit(solution)/shard_map/ppermute | solution.py:17
  352.2 34.7 %collective-permute-start.46 = (bf16[304,1280]{1,0:T(8,128)(2,1)S(1)}, bf16[304,1280]{1,0:T(8,128)(2,1)S(1)}, u32[]{:S(2)}, u32[]{:S(2)}) collective-permute-start(bf16[304,1280]{1,0:T(8,128)(2,1)S(1)} %get-tuple-element.127), channel_id=1, source_target_pairs={{0,2},{1,3},{2,0},{3,1},{4,6},{5,7},{6,4},{7,5},{8,10},{9,11},{10,... | collective-permute-start | bytes 2334728 | tf_op jit(solution)/shard_map/ppermute | solution.py:17
  352.9 34.1 %collective-permute-start.47 = (bf16[304,1280]{1,0:T(8,128)(2,1)S(1)}, bf16[304,1280]{1,0:T(8,128)(2,1)S(1)}, u32[]{:S(2)}, u32[]{:S(2)}) collective-permute-start(bf16[304,1280]{1,0:T(8,128)(2,1)S(1)} %get-tuple-element.128), channel_id=1, source_target_pairs={{0,3},{1,2},{2,1},{3,0},{4,7},{5,6},{6,5},{7,4},{8,11},{9,10},{10,... | collective-permute-start | bytes 2334728 | tf_op jit(solution)/shard_map/ppermute | solution.py:17
  371.7 24.9 %collective-permute-start.51 = (bf16[432,1152]{1,0:T(8,128)(2,1)S(1)}, bf16[432,1152]{1,0:T(8,128)(2,1)S(1)}, u32[]{:S(2)}, u32[]{:S(2)}) collective-permute-start(bf16[432,1152]{1,0:T(8,128)(2,1)S(1)} %copy-done.52), channel_id=1, source_target_pairs={{0,4},{4,0},{8,12},{12,8},{16,20},{20,16},{24,28},{28,24},{1,5},{5... | collective-permute-start | bytes 2985992 | tf_op jit(solution)/shard_map/ppermute | solution.py:17
  388.2 26.3 %collective-permute-start.48 = (bf16[432,1152]{1,0:T(8,128)(2,1)S(1)}, bf16[432,1152]{1,0:T(8,128)(2,1)S(1)}, u32[]{:S(2)}, u32[]{:S(2)}) collective-permute-start(bf16[432,1152]{1,0:T(8,128)(2,1)S(1)} %get-tuple-element.129.refs_0_), channel_id=1, source_target_pairs={{8,0},{12,4},{16,24},{20,28},{9,1},{13,5},{17,25},{21,29},{10,2},{... | collective-permute-start | bytes 2985992 | tf_op jit(solution)/shard_map/ppermute | solution.py:615
  389.5 25.0 %collective-permute-start.49 = (bf16[432,1152]{1,0:T(8,128)(2,1)S(1)}, bf16[432,1152]{1,0:T(8,128)(2,1)S(1)}, u32[]{:S(2)}, u32[]{:S(2)}) collective-permute-start(bf16[432,1152]{1,0:T(8,128)(2,1)S(1)} %get-tuple-element.130.refs_2_), channel_id=1, source_target_pairs={{8,16},{12,20},{16,8},{20,12},{9,17},{13,21},{17,9},{21,13},{10,18... | collective-permute-start | bytes 2985992 | tf_op jit(solution)/shard_map/ppermute | solution.py:615
  390.2 23.4 %collective-permute-start.50 = (bf16[304,1280]{1,0:T(8,128)(2,1)S(1)}, bf16[304,1280]{1,0:T(8,128)(2,1)S(1)}, u32[]{:S(2)}, u32[]{:S(2)}) collective-permute-start(bf16[304,1280]{1,0:T(8,128)(2,1)S(1)} %get-tuple-element.131.refs_4_), channel_id=1, source_target_pairs={{0,8},{4,12},{24,16},{28,20},{1,9},{5,13},{25,17},{29,21},{2,10},{... | collective-permute-start | bytes 2334728 | tf_op jit(solution)/shard_map/ppermute | solution.py:615
  415.2 26.6 %collective-permute-start.53 = (bf16[432,1152]{1,0:T(8,128)(2,1)S(1)}, bf16[432,1152]{1,0:T(8,128)(2,1)S(1)}, u32[]{:S(2)}, u32[]{:S(2)}) collective-permute-start(bf16[432,1152]{1,0:T(8,128)(2,1)S(1)} %get-tuple-element.134.refs_0_), channel_id=1, source_target_pairs={{8,0},{12,4},{16,24},{20,28},{9,1},{13,5},{17,25},{21,29},{10,2},{... | collective-permute-start | bytes 2985992 | tf_op jit(solution)/shard_map/ppermute | solution.py:615
  442.1 20.0 %collective-permute-start.57 = (bf16[304,1280]{1,0:T(8,128)(2,1)S(1)}, bf16[304,1280]{1,0:T(8,128)(2,1)S(1)}, u32[]{:S(2)}, u32[]{:S(2)}) collective-permute-start(bf16[304,1280]{1,0:T(8,128)(2,1)S(1)} %get-tuple-element.138.refs_0_), channel_id=1, source_target_pairs={{8,0},{12,4},{16,24},{20,28},{9,1},{13,5},{17,25},{21,29},{10,2},{... | collective-permute-start | bytes 2334728 | tf_op jit(solution)/shard_map/ppermute | solution.py:615
  443.4 18.8 %collective-permute-start.59 = (bf16[432,1152]{1,0:T(8,128)(2,1)S(1)}, bf16[432,1152]{1,0:T(8,128)(2,1)}, u32[]{:S(2)}, u32[]{:S(2)}) collective-permute-start(bf16[432,1152]{1,0:T(8,128)(2,1)S(1)} %get-tuple-element.140.refs_0_), channel_id=1, source_target_pairs={{0,4},{4,0},{8,12},{12,8},{16,20},{20,16},{24,28},{28,24},{1,5},{5... | collective-permute-start | bytes 2985992 | tf_op jit(solution)/shard_map/ppermute | solution.py:17
  443.5 18.8 %collective-permute-start.60 = (bf16[432,1152]{1,0:T(8,128)(2,1)S(1)}, bf16[432,1152]{1,0:T(8,128)(2,1)}, u32[]{:S(2)}, u32[]{:S(2)}) collective-permute-start(bf16[432,1152]{1,0:T(8,128)(2,1)S(1)} %get-tuple-element.141.refs_1_), channel_id=1, source_target_pairs={{0,4},{4,0},{8,12},{12,8},{16,20},{20,16},{24,28},{28,24},{1,5},{5... | collective-permute-start | bytes 2985992 | tf_op jit(solution)/shard_map/ppermute | solution.py:17
  (122 other events, 1038.8 us)

commit v10 on v9

--- a/solution.py
+++ b/solution.py
@@ -970,18 +970,16 @@
     waiting = fresh(
         ["down"], *weight_grad([[hiddens[i] for i in range(group)]], [pieces[i] for i in range(group)])
     )
+    pieces[final] = line.advance([waiting.pop(0)], pieces[final])
     gate_parts, upper_parts, parts = ffn_backward_blocks(
         [pieces[final]], gate_weight, up_weight, down_weight, [slopes[final]], [acts[final]]
     )
     grad_gates[final], grad_uppers[final] = gate_parts[0], upper_parts[0]
     returned[final] = swapped(parts[0], "fsdp", final)
-    grad_gates[final] = line.advance(
-        [waiting.pop(0)], after(grad_gates[final], *[returned[mask] for mask in rings[1:-1]])
-    )
     other, mine = weight_grad(
         [[grad_gates[i] for i in range(group)], [grad_uppers[i] for i in range(group)]], ffn_blocks
     )
-    other = line.advance([waiting.pop(0)] if waiting else [], after(other, returned[final]))
+    other = line.advance([waiting.pop(0)] if waiting else [], after(other, *[returned[mask] for mask in masks]))
     waiting = fresh(["gate", "up"], other, mine)
 
     def advance(gate=None):
@@ -994,12 +992,10 @@
     grad_query_low, grad_gain_query, grad_far, grad_pair = attention_backward(
         *attention_args, query_new, grad_mixed, heads
     )
-    backs = []
-    for step in range(1, hops + 1):
-        grad_far = passed_along(grad_far, "fsdp", -1)
-        backs.append(grad_far[-rows:])
-        grad_far = grad_far[:-rows]
-    grad_pair = advance(grad_pair)
+    backs = [
+        passed_along(grad_far[(hops - step) * rows : (hops - step + 1) * rows], "fsdp", -step)
+        for step in range(1, hops + 1)
+    ]
     other, mine, grad_in = input_backward(
         grad_pair,
         backs,
@@ -1020,14 +1016,17 @@
     )
     other = advance(other)
     weight_parts = owner_parts(other, mine)
+    weight_parts[0] = advance(weight_parts[0])
+    near = [weight_parts[mask] for mask in masks if bin(mask).count("1") == 1]
     while waiting:
-        weight_parts[0] = advance(weight_parts[0])
+        weight_parts[0] = advance(after(weight_parts[0], *near))
     line.advance([("weights", weight_parts)])
     grad_down = whole_grad(line, "down", units)
     grad_down = line.advance([], grad_down)
     grad_gate_w = whole_grad(line, "gate", units)
     grad_gate_w = line.advance([], grad_gate_w)
     grad_up_w = whole_grad(line, "up", units)
+    grad_up_w = line.advance([], grad_up_w)
     owned = core_join(line.finished("weights"), 1).astype(jnp.float32)
     inner = heads * head_size
     columns = [0, inner, inner + head_size, inner + 2 * head_size, wide + inner]

time: 479 us -> 475 us (level)
  waiting for transfers between devices: 196 us -> 184 us
  local copies, waits for them, and re-layouts: 43.8 us -> 50.1 us
    ppermute x17, waiting for transfers between devices: 91.8 us -> 66.8 us  [exchanged(): return lax.ppermute(block, 'replica', route)]
    ppermute x40, waiting for transfers between devices: 89.2 us -> 108 us  [swapped(): return lax.ppermute(block, axis, route)]
    ppermute x40, starting transfers between devices: 30.1 us -> 39.1 us  [swapped(): return lax.ppermute(block, axis, route)]
    ppermute x4, waiting for transfers between devices: 15.2 us -> 8.68 us  [passed_along(): return lax.ppermute(block, axis, route)]
    unnamed x188 -> x204, local copies, waits for them, and re-layouts: 29.5 us -> 34.5 us
  transfers between devices with their start and end apart: 61 -> 61, of which waited for: 28 -> 26; matrix products, arithmetic and copies ran while one was open for 12% -> 12% of each run, Pallas kernels for 15% -> 14%
where the time goes in v10:
time: 475 us; the launch traced here: 466 us
  waiting for transfers between devices  184 us (39%)
  Pallas kernels  94.3 us (20%)
  starting transfers between devices  83.4 us (18%)
  local copies, waits for them, and re-layouts  50.1 us (11%)
  matrix products  43.7 us (9%)
  other arithmetic  8.37 us (2%)
    ppermute x40, waiting for transfers between devices, swapped(): return lax.ppermute(block, axis, route)  108 us
    ppermute x17, waiting for transfers between devices, exchanged(): return lax.ppermute(block, 'replica', route)  66.8 us
    dot_general x22, matrix products, contract(): lax.dot_general(left, right, (((left_dim,), (right_dim,)), ((), ())), pre...  42.5 us
    ppermute x40, starting transfers between devices, swapped(): return lax.ppermute(block, axis, route)  39.1 us
    ppermute x17, starting transfers between devices, exchanged(): return lax.ppermute(block, 'replica', route)  35.3 us
    unnamed x204, local copies, waits for them, and re-layouts  34.5 us
    pallas_call x2, Pallas kernels, weight_grad(): pl.pallas_call(kernel, grid_spec=pltpu.PrefetchScalarGridSpec(num_scalar_...  23.7 us
    pallas_call x10, Pallas kernels, advance(): pl.pallas_call(kernel, grid_spec=pltpu.PrefetchScalarGridSpec(num_scalar_...  21.9 us
  transfers between devices with their start and end apart: 61, of which 26 were waited for; matrix products, arithmetic and copies ran while one was open for 12% of the time, Pallas kernels for 14%

profile of v10, /device:TPU:0, one launch (start us, length us, event | category | flops | bytes accessed | tf_op | source)
XLA Modules:
  0.0 466.1 jit_solution(15745350865438642953)
XLA Ops:
  12.6 5.1 %collective-permute-done.refs_1_.refs_3_ = bf16[144,1536]{1,0:T(8,128)(2,1)S(1)} collective-permute-done((bf16[144,1536]{1,0:T(8,128)(2,1)S(1)}, bf16[144,1536]{1,0:T(8,128)(2,1)S(1)}, u32[]{:S(2)}, u32[]{:S(2)}) %collective-permute-start) | collective-permute-done | bytes 442400 | tf_op jit(solution)/shard_map/ppermute | solution.py:17
  17.7 10.3 %collective-permute-done.1.refs_2_.refs_4_ = bf16[144,1536]{1,0:T(8,128)(2,1)} collective-permute-done((bf16[144,1536]{1,0:T(8,128)(2,1)S(1)}, bf16[144,1536]{1,0:T(8,128)(2,1)}, u32[]{:S(2)}, u32[]{:S(2)}) %collective-permute-start.1) | collective-permute-done | bytes 442400 | tf_op jit(solution)/shard_map/ppermute | solution.py:17
  45.1 4.1 collective-permute-start.10
  51.6 10.2 %collective-permute-done.12.refs_2_ = bf16[144,1024]{1,0:T(8,128)(2,1)} collective-permute-done((bf16[144,1024]{1,0:T(8,128)(2,1)S(1)}, bf16[144,1024]{1,0:T(8,128)(2,1)}, u32[]{:S(2)}, u32[]{:S(2)}) %collective-permute-start.12) | collective-permute-done | bytes 294944 | tf_op jit(solution)/shard_map/ppermute | solution.py:17
  67.7 4.1 attention_forward.1
  82.5 10.4 %collective-permute-done.17.refs_1_ = bf16[256,1152]{1,0:T(8,128)(2,1)} collective-permute-done((bf16[256,1152]{1,0:T(8,128)(2,1)}, bf16[256,1152]{1,0:T(8,128)(2,1)}, u32[]{:S(2)}, u32[]{:S(2)}) %collective-permute-start.17) | collective-permute-done | bytes 589856 | tf_op jit(solution)/shard_map/ppermute | solution.py:17
  96.5 3.7 convolution_bitcast_fusion.10
  124.2 13.1 %collective-permute-done.21 = bf16[256,1152]{1,0:T(8,128)(2,1)S(1)} collective-permute-done((bf16[256,1152]{1,0:T(8,128)(2,1)S(1)}, bf16[256,1152]{1,0:T(8,128)(2,1)S(1)}, u32[]{:S(2)}, u32[]{:S(2)}) %collective-permute-start.21) | collective-permute-done | bytes 589856 | tf_op jit(solution)/shard_map/ppermute | solution.py:17
  148.5 6.5 %collective-permute-done.23.refs_0_.refs_1_ = bf16[256,1152]{1,0:T(8,128)(2,1)S(1)} collective-permute-done((bf16[256,1152]{1,0:T(8,128)(2,1)S(1)}, bf16[256,1152]{1,0:T(8,128)(2,1)S(1)}, u32[]{:S(2)}, u32[]{:S(2)}) %collective-permute-start.23) | collective-permute-done | bytes 589856 | tf_op jit(solution)/shard_map/ppermute | solution.py:17
  155.1 4.6 collective-permute-done.24.refs_0_.refs_2_
  172.3 7.4 %weight_grad.2 = (bf16[2,432,1152]{2,1,0:T(8,128)(2,1)}, bf16[2,432,1152]{2,1,0:T(8,128)(2,1)}) custom-call(s32[1]{0:T(128)} %bitcast.core_ref, bf16[256,1152]{1,0:T(8,128)(2,1)S(1)} %get-tuple-element.181.refs_0_, bf16[256,1152]{1,0:T(8,128)(2,1)S(1)} %after.18.refs_1_, bf16[256,1152]{1,0:T(8,128)(2,1)S(1)} %after.19.refs_2_, ...), custom_call_target="tpu_custom_call" | custom-call | tf_op jit(solution)/shard_map/weight_grad/pallas_call | solution.py:445
  179.7 4.3 collective-permute-done.26.refs_1_.refs_3_
  196.5 10.1 %ffn_backward.1 = (bf16[1728,256]{1,0:T(8,128)(2,1)S(1)}, bf16[1728,256]{1,0:T(8,128)(2,1)S(1)}, bf16[256,1152]{1,0:T(8,128)(2,1)S(1)}) custom-call(bf16[256,1152]{1,0:T(8,128)(2,1)S(1)} %copy-done.10, bf16[1728,1152]{1,0:T(8,128)(2,1)} %refs_1_.5, bf16[1728,1152]{1,0:T(8,128)(2,1)} %refs_2_.5, bf16[1728,1152]{1,0:T(8,128)(2,1)} %refs_3_.1, ...), custom_call_target="tpu_custom_call" | custom-call | tf_op jit(solution)/shard_map/ffn_backward/pallas_call | solution.py:195
  209.1 16.3 %weight_grad.3 = (bf16[4,432,1152]{2,1,0:T(8,128)(2,1)}, bf16[4,432,1152]{2,1,0:T(8,128)(2,1)}) custom-call(s32[1]{0:T(128)} %bitcast.core_ref, bf16[256,1152]{1,0:T(8,128)(2,1)S(1)} %copy-done.21, bf16[256,1152]{1,0:T(8,128)(2,1)} %collective-permute-done.17.refs_1_, bf16[256,1152]{1,0:T(8,128)(2,1)} %after.15.refs_2_, bf16[256,1152]{1,0:T(8,128)(2,1)S(1)} %copy-done.40, ...), custom_call_target="tpu_custom_call" | custom-call | tf_op jit(solution)/shard_map/weight_grad/pallas_call | solution.py:445
  232.5 4.1 collective-permute-start.32
  252.2 5.4 %collective-permute-done.32.refs_3_ = bf16[432,1152]{1,0:T(8,128)(2,1)} collective-permute-done((bf16[432,1152]{1,0:T(8,128)(2,1)}, bf16[432,1152]{1,0:T(8,128)(2,1)}, u32[]{:S(2)}, u32[]{:S(2)}) %collective-permute-start.32) | collective-permute-done | bytes 995360 | tf_op jit(solution)/shard_map/ppermute | solution.py:615
  257.7 4.9 %line_step.12 = (bf16[432,1152]{1,0:T(8,128)(2,1)S(1)}, bf16[432,1152]{1,0:T(8,128)(2,1)}, bf16[432,1152]{1,0:T(8,128)(2,1)S(1)}, bf16[432,1152]{1,0:T(8,128)(2,1)}, bf16[256,1024]{1,0:T(8,128)(2,1)S(1)}) custom-call(s32[1]{0:T(128)} %bitcast.19.place_ref, bf16[432,1152]{1,0:T(8,128)(2,1)} %get-tuple-element.91.refs_0_, ...), custom_call_target="tpu_custom_call", output_to_operand_aliasing={{4}: (7, {})} | custom-call | tf_op jit(solution)/shard_map/line_step/pallas_call | solution.py:700
  266.8 6.6 %attention_backward.1 = (bf16[256,1024]{1,0:T(8,128)(2,1)S(1)}, f32[1,256]{1,0:T(1,128)S(1)}, bf16[512,512]{1,0:T(8,128)(2,1)S(1)}, f32[256,512]{1,0:T(8,128)S(1)}) custom-call(f32[256,1536]{1,0:T(8,128)S(1)} %copy-done.3, bf16[1,256]{1,0:T(2,128)(2,1)S(1)} %broadcast_in_dim_reshape_squeeze.2.gain_ref, f32[256,128]{1,0:T(8,128)S(1)} %copy-done.49, ...), custom_call_target="tpu_custom_call" | custom-call | tf_op jit(solution)/shard_map/attention_backward/pallas_call | solution.py:590
  279.9 4.4 collective-permute-done.34.refs_1_
  291.4 9.1 %input_backward.1 = (bf16[4,304,1280]{2,1,0:T(8,128)(2,1)}, bf16[4,304,1280]{2,1,0:T(8,128)(2,1)}, f32[256,1152]{1,0:T(8,128)}) custom-call(s32[1]{0:T(128)} %bitcast.core_ref, f32[256,512]{1,0:T(8,128)S(1)} %copy-done.75, bf16[256,512]{1,0:T(8,128)(2,1)S(1)} %collective-permute-done.34.refs_1_, bf16[256,512]{1,0:T(8,128)(2,1)S(1)} %collective-permute-done.35.refs_2_, ...), custom_call_target="tpu_custom_call" | custom-call | tf_op jit(solution)/shard_map/input_backward/pallas_call | solution.py:351
  307.5 4.1 collective-permute-done.40.far_ref
  313.3 17.1 %collective-permute-done.38.refs_1_ = bf16[432,1152]{1,0:T(8,128)(2,1)S(1)} collective-permute-done((bf16[432,1152]{1,0:T(8,128)(2,1)S(1)}, bf16[432,1152]{1,0:T(8,128)(2,1)S(1)}, u32[]{:S(2)}, u32[]{:S(2)}) %collective-permute-start.38) | collective-permute-done | bytes 995360 | tf_op jit(solution)/shard_map/ppermute | solution.py:615
  333.2 3.7 collective-permute-start.41
  337.6 5.8 %collective-permute-start.43 = (bf16[304,1280]{1,0:T(8,128)(2,1)S(1)}, bf16[304,1280]{1,0:T(8,128)(2,1)S(1)}, u32[]{:S(2)}, u32[]{:S(2)}) collective-permute-start(bf16[304,1280]{1,0:T(8,128)(2,1)S(1)} %get-tuple-element.123), channel_id=1, source_target_pairs={{0,1},{1,0},{2,3},{3,2},{4,5},{5,4},{6,7},{7,6},{8,9},{9,8},{10,11... | collective-permute-start | bytes 2334728 | tf_op jit(solution)/shard_map/ppermute | solution.py:17
  343.4 16.6 %collective-permute-done.43.refs_1_.refs_6_ = bf16[304,1280]{1,0:T(8,128)(2,1)S(1)} collective-permute-done((bf16[304,1280]{1,0:T(8,128)(2,1)S(1)}, bf16[304,1280]{1,0:T(8,128)(2,1)S(1)}, u32[]{:S(2)}, u32[]{:S(2)}) %collective-permute-start.43) | collective-permute-done | bytes 778272 | tf_op jit(solution)/shard_map/ppermute | solution.py:17
  370.9 15.2 %collective-permute-done.47.refs_8_ = bf16[304,1280]{1,0:T(8,128)(2,1)S(1)} collective-permute-done((bf16[304,1280]{1,0:T(8,128)(2,1)S(1)}, bf16[304,1280]{1,0:T(8,128)(2,1)S(1)}, u32[]{:S(2)}, u32[]{:S(2)}) %collective-permute-start.47) | collective-permute-done | bytes 778272 | tf_op jit(solution)/shard_map/ppermute | solution.py:17
  389.8 7.8 %collective-permute-start.50 = (bf16[304,1280]{1,0:T(8,128)(2,1)S(1)}, bf16[304,1280]{1,0:T(8,128)(2,1)S(1)}, u32[]{:S(2)}, u32[]{:S(2)}) collective-permute-start(bf16[304,1280]{1,0:T(8,128)(2,1)S(1)} %get-tuple-element.133.refs_4_), channel_id=1, source_target_pairs={{0,8},{4,12},{24,16},{28,20},{1,9},{5,13},{25,17},{29,21},{2,10},{... | collective-permute-start | bytes 2334728 | tf_op jit(solution)/shard_map/ppermute | solution.py:615
  397.7 3.6 whole_grad.3.refs_6_
  401.7 9.3 %collective-permute-done.50.refs_5_ = bf16[304,1280]{1,0:T(8,128)(2,1)S(1)} collective-permute-done((bf16[304,1280]{1,0:T(8,128)(2,1)S(1)}, bf16[304,1280]{1,0:T(8,128)(2,1)S(1)}, u32[]{:S(2)}, u32[]{:S(2)}) %collective-permute-start.50) | collective-permute-done | bytes 778272 | tf_op jit(solution)/shard_map/ppermute | solution.py:615
  414.9 3.6 whole_grad.4.refs_4_
  418.4 17.7 %collective-permute-done.53.refs_1_ = bf16[432,1152]{1,0:T(8,128)(2,1)S(1)} collective-permute-done((bf16[432,1152]{1,0:T(8,128)(2,1)S(1)}, bf16[432,1152]{1,0:T(8,128)(2,1)S(1)}, u32[]{:S(2)}, u32[]{:S(2)}) %collective-permute-start.53) | collective-permute-done | bytes 995360 | tf_op jit(solution)/shard_map/ppermute | solution.py:615
  442.7 15.6 %collective-permute-done.57.refs_1_ = bf16[304,1280]{1,0:T(8,128)(2,1)S(1)} collective-permute-done((bf16[304,1280]{1,0:T(8,128)(2,1)S(1)}, bf16[304,1280]{1,0:T(8,128)(2,1)S(1)}, u32[]{:S(2)}, u32[]{:S(2)}) %collective-permute-start.57) | collective-permute-done | bytes 778272 | tf_op jit(solution)/shard_map/ppermute | solution.py:615
  (413 shorter events, 198.7 us)
Async XLA Ops:
  6.7 21.3 %collective-permute-start.1 = (bf16[144,1536]{1,0:T(8,128)(2,1)S(1)}, bf16[144,1536]{1,0:T(8,128)(2,1)}, u32[]{:S(2)}, u32[]{:S(2)}) collective-permute-start(bf16[144,1536]{1,0:T(8,128)(2,1)S(1)} %pack.2), channel_id=1, source_target_pairs={{0,2},{1,3},{2,0},{3,1},{4,6},{5,7},{6,4},{7,5},{8,10},{9,11},{10,... | collective-permute-start | bytes 1327112 | tf_op jit(solution)/shard_map/ppermute | solution.py:17
  8.2 24.0 %collective-permute-start.5 = (bf16[144,1536]{1,0:T(8,128)(2,1)S(1)}, bf16[144,1536]{1,0:T(8,128)(2,1)}, u32[]{:S(2)}, u32[]{:S(2)}) collective-permute-start(bf16[144,1536]{1,0:T(8,128)(2,1)S(1)} %pack.2), channel_id=1, source_target_pairs={{0,3},{1,2},{2,1},{3,0},{4,7},{5,6},{6,5},{7,4},{8,11},{9,10},{10,... | collective-permute-start | bytes 1327112 | tf_op jit(solution)/shard_map/ppermute | solution.py:17
  43.1 18.7 %collective-permute-start.12 = (bf16[144,1024]{1,0:T(8,128)(2,1)S(1)}, bf16[144,1024]{1,0:T(8,128)(2,1)}, u32[]{:S(2)}, u32[]{:S(2)}) collective-permute-start(bf16[144,1024]{1,0:T(8,128)(2,1)S(1)} %after.13), channel_id=1, source_target_pairs={{0,2},{1,3},{2,0},{3,1},{4,6},{5,7},{6,4},{7,5},{8,10},{9,11},{10,... | collective-permute-start | bytes 884744 | tf_op jit(solution)/shard_map/ppermute | solution.py:17
  45.1 18.5 %collective-permute-start.10 = (bf16[256,512]{1,0:T(8,128)(2,1)S(1)}, bf16[256,512]{1,0:T(8,128)(2,1)}, u32[]{:S(2)}, u32[]{:S(2)}) collective-permute-start(bf16[256,512]{1,0:T(8,128)(2,1)S(1)} %pad_maximum_fusion.refs_1_), channel_id=1, source_target_pairs={{0,1},{1,2},{2,3},{4,5},{5,6},{6,7},{8,9},{9,10},{10,11},{12,13},{... | collective-permute-start | bytes 786440 | tf_op jit(solution)/shard_map/ppermute | solution.py:813
  51.6 20.3 %collective-permute-start.14 = (bf16[144,1024]{1,0:T(8,128)(2,1)S(1)}, bf16[144,1024]{1,0:T(8,128)(2,1)}, u32[]{:S(2)}, u32[]{:S(2)}) collective-permute-start(bf16[144,1024]{1,0:T(8,128)(2,1)S(1)} %collective-permute-done.11.refs_1_), channel_id=1, source_target_pairs={{0,4},{4,0},{8,12},{12,8},{16,20},{20,16},{24,28},{28,24},{1,5},{5... | collective-permute-start | bytes 884744 | tf_op jit(solution)/shard_map/ppermute | solution.py:17
  104.5 32.9 %collective-permute-start.20 = (bf16[256,1152]{1,0:T(8,128)(2,1)S(1)}, bf16[256,1152]{1,0:T(8,128)(2,1)S(1)}, u32[]{:S(2)}, u32[]{:S(2)}) collective-permute-start(bf16[256,1152]{1,0:T(8,128)(2,1)S(1)} %convolution_convert_fusion.3.refs_1_), channel_id=1, source_target_pairs={{0,1},{1,0},{2,3},{3,2},{4,5},{5,4},{6,7},{7,6},{8,9},{9,8},{10,11... | collective-permute-start | bytes 1769480 | tf_op jit(solution)/shard_map/ppermute | solution.py:17
  111.7 25.6 %collective-permute-start.21 = (bf16[256,1152]{1,0:T(8,128)(2,1)S(1)}, bf16[256,1152]{1,0:T(8,128)(2,1)S(1)}, u32[]{:S(2)}, u32[]{:S(2)}) collective-permute-start(bf16[256,1152]{1,0:T(8,128)(2,1)S(1)} %convolution_convert_fusion.2.refs_1_), channel_id=1, source_target_pairs={{0,2},{1,3},{2,0},{3,1},{4,6},{5,7},{6,4},{7,5},{8,10},{9,11},{10,... | collective-permute-start | bytes 1769480 | tf_op jit(solution)/shard_map/ppermute | solution.py:17
  118.6 18.7 %collective-permute-start.22 = (bf16[256,1152]{1,0:T(8,128)(2,1)S(1)}, bf16[256,1152]{1,0:T(8,128)(2,1)S(1)}, u32[]{:S(2)}, u32[]{:S(2)}) collective-permute-start(bf16[256,1152]{1,0:T(8,128)(2,1)S(1)} %convolution_convert_fusion.1.refs_1_), channel_id=1, source_target_pairs={{0,3},{1,2},{2,1},{3,0},{4,7},{5,6},{6,5},{7,4},{8,11},{9,10},{10,... | collective-permute-start | bytes 1769480 | tf_op jit(solution)/shard_map/ppermute | solution.py:17
  189.8 36.7 %collective-permute-start.27 = (bf16[432,1152]{1,0:T(8,128)(2,1)S(1)}, bf16[432,1152]{1,0:T(8,128)(2,1)S(1)}, u32[]{:S(2)}, u32[]{:S(2)}) collective-permute-start(bf16[432,1152]{1,0:T(8,128)(2,1)S(1)} %get-tuple-element.85.refs_0_), channel_id=1, source_target_pairs={{0,8},{4,12},{24,16},{28,20},{1,9},{5,13},{25,17},{29,21},{2,10},{... | collective-permute-start | bytes 2985992 | tf_op jit(solution)/shard_map/ppermute | solution.py:615
  193.3 32.0 %collective-permute-start.29 = (bf16[256,1152]{1,0:T(8,128)(2,1)}, bf16[256,1152]{1,0:T(8,128)(2,1)S(1)}, u32[]{:S(2)}, u32[]{:S(2)}) collective-permute-start(bf16[256,1152]{1,0:T(8,128)(2,1)} %fusion.3.refs_1_), channel_id=1, source_target_pairs={{0,2},{1,3},{2,0},{3,1},{4,6},{5,7},{6,4},{7,5},{8,10},{9,11},{10,... | collective-permute-start | bytes 1769480 | tf_op jit(solution)/shard_map/ppermute | solution.py:17
  195.2 30.2 %collective-permute-start.28 = (bf16[256,1152]{1,0:T(8,128)(2,1)S(1)}, bf16[256,1152]{1,0:T(8,128)(2,1)S(1)}, u32[]{:S(2)}, u32[]{:S(2)}) collective-permute-start(bf16[256,1152]{1,0:T(8,128)(2,1)S(1)} %copy-done.67), channel_id=1, source_target_pairs={{0,1},{1,0},{2,3},{3,2},{4,5},{5,4},{6,7},{7,6},{8,9},{9,8},{10,11... | collective-permute-start | bytes 1769480 | tf_op jit(solution)/shard_map/ppermute | solution.py:17
  230.9 26.7 %collective-permute-start.33 = (bf16[4,432,1152]{2,1,0:T(8,128)(2,1)}, bf16[4,432,1152]{2,1,0:T(8,128)(2,1)}, u32[]{:S(2)}, u32[]{:S(2)}) collective-permute-start(bf16[4,432,1152]{2,1,0:T(8,128)(2,1)} %get-tuple-element.94), channel_id=1, source_target_pairs={{0,4},{4,0},{8,12},{12,8},{16,20},{20,16},{24,28},{28,24},{1,5},{5... | collective-permute-start | bytes 11943944 | tf_op jit(solution)/shard_map/ppermute | solution.py:17
  230.9 21.3 %collective-permute-start.31 = (bf16[432,1152]{1,0:T(8,128)(2,1)}, bf16[432,1152]{1,0:T(8,128)(2,1)}, u32[]{:S(2)}, u32[]{:S(2)}) collective-permute-start(bf16[432,1152]{1,0:T(8,128)(2,1)} %get-tuple-element.91.refs_0_), channel_id=1, source_target_pairs={{8,16},{12,20},{16,8},{20,12},{9,17},{13,21},{17,9},{21,13},{10,18... | collective-permute-start | bytes 2985992 | tf_op jit(solution)/shard_map/ppermute | solution.py:615
  232.5 25.1 %collective-permute-start.32 = (bf16[432,1152]{1,0:T(8,128)(2,1)}, bf16[432,1152]{1,0:T(8,128)(2,1)}, u32[]{:S(2)}, u32[]{:S(2)}) collective-permute-start(bf16[432,1152]{1,0:T(8,128)(2,1)} %get-tuple-element.92.refs_2_), channel_id=1, source_target_pairs={{0,8},{4,12},{24,16},{28,20},{1,9},{5,13},{25,17},{29,21},{2,10},{... | collective-permute-start | bytes 2985992 | tf_op jit(solution)/shard_map/ppermute | solution.py:615
  262.6 37.9 %collective-permute-start.36 = (bf16[432,1152]{1,0:T(8,128)(2,1)}, bf16[432,1152]{1,0:T(8,128)(2,1)}, u32[]{:S(2)}, u32[]{:S(2)}) collective-permute-start(bf16[432,1152]{1,0:T(8,128)(2,1)} %get-tuple-element.107), channel_id=1, source_target_pairs={{0,8},{4,12},{24,16},{28,20},{8,0},{12,4},{16,24},{20,28},{1,9},{5... | collective-permute-start | bytes 2985992 | tf_op jit(solution)/shard_map/ppermute | solution.py:615
  265.1 35.4 %collective-permute-start.37 = (bf16[432,1152]{1,0:T(8,128)(2,1)}, bf16[432,1152]{1,0:T(8,128)(2,1)}, u32[]{:S(2)}, u32[]{:S(2)}) collective-permute-start(bf16[432,1152]{1,0:T(8,128)(2,1)} %get-tuple-element.108.refs_2_), channel_id=1, source_target_pairs={{8,16},{12,20},{16,8},{20,12},{9,17},{13,21},{17,9},{21,13},{10,18... | collective-permute-start | bytes 2985992 | tf_op jit(solution)/shard_map/ppermute | solution.py:615
  306.0 24.4 %collective-permute-start.38 = (bf16[432,1152]{1,0:T(8,128)(2,1)S(1)}, bf16[432,1152]{1,0:T(8,128)(2,1)S(1)}, u32[]{:S(2)}, u32[]{:S(2)}) collective-permute-start(bf16[432,1152]{1,0:T(8,128)(2,1)S(1)} %get-tuple-element.112), channel_id=1, source_target_pairs={{0,8},{4,12},{24,16},{28,20},{8,0},{12,4},{16,24},{20,28},{1,9},{5... | collective-permute-start | bytes 2985992 | tf_op jit(solution)/shard_map/ppermute | solution.py:615
  306.8 23.6 %collective-permute-start.39 = (bf16[432,1152]{1,0:T(8,128)(2,1)S(1)}, bf16[432,1152]{1,0:T(8,128)(2,1)S(1)}, u32[]{:S(2)}, u32[]{:S(2)}) collective-permute-start(bf16[432,1152]{1,0:T(8,128)(2,1)S(1)} %get-tuple-element.113.refs_2_), channel_id=1, source_target_pairs={{8,16},{12,20},{16,8},{20,12},{9,17},{13,21},{17,9},{21,13},{10,18... | collective-permute-start | bytes 2985992 | tf_op jit(solution)/shard_map/ppermute | solution.py:615
  333.2 28.3 %collective-permute-start.41 = (bf16[432,1152]{1,0:T(8,128)(2,1)S(1)}, bf16[432,1152]{1,0:T(8,128)(2,1)S(1)}, u32[]{:S(2)}, u32[]{:S(2)}) collective-permute-start(bf16[432,1152]{1,0:T(8,128)(2,1)S(1)} %get-tuple-element.119), channel_id=1, source_target_pairs={{0,8},{4,12},{24,16},{28,20},{8,0},{12,4},{16,24},{20,28},{1,9},{5... | collective-permute-start | bytes 2985992 | tf_op jit(solution)/shard_map/ppermute | solution.py:615
  336.9 24.6 %collective-permute-start.42 = (bf16[432,1152]{1,0:T(8,128)(2,1)S(1)}, bf16[432,1152]{1,0:T(8,128)(2,1)S(1)}, u32[]{:S(2)}, u32[]{:S(2)}) collective-permute-start(bf16[432,1152]{1,0:T(8,128)(2,1)S(1)} %get-tuple-element.120.refs_2_), channel_id=1, source_target_pairs={{8,16},{12,20},{16,8},{20,12},{9,17},{13,21},{17,9},{21,13},{10,18... | collective-permute-start | bytes 2985992 | tf_op jit(solution)/shard_map/ppermute | solution.py:615
  337.6 22.4 %collective-permute-start.43 = (bf16[304,1280]{1,0:T(8,128)(2,1)S(1)}, bf16[304,1280]{1,0:T(8,128)(2,1)S(1)}, u32[]{:S(2)}, u32[]{:S(2)}) collective-permute-start(bf16[304,1280]{1,0:T(8,128)(2,1)S(1)} %get-tuple-element.123), channel_id=1, source_target_pairs={{0,1},{1,0},{2,3},{3,2},{4,5},{5,4},{6,7},{7,6},{8,9},{9,8},{10,11... | collective-permute-start | bytes 2334728 | tf_op jit(solution)/shard_map/ppermute | solution.py:17
  364.3 22.4 %collective-permute-start.45 = (bf16[432,1152]{1,0:T(8,128)(2,1)S(1)}, bf16[432,1152]{1,0:T(8,128)(2,1)S(1)}, u32[]{:S(2)}, u32[]{:S(2)}) collective-permute-start(bf16[432,1152]{1,0:T(8,128)(2,1)S(1)} %get-tuple-element.126), channel_id=1, source_target_pairs={{0,8},{4,12},{24,16},{28,20},{8,0},{12,4},{16,24},{20,28},{1,9},{5... | collective-permute-start | bytes 2985992 | tf_op jit(solution)/shard_map/ppermute | solution.py:615
  366.4 20.3 %collective-permute-start.46 = (bf16[432,1152]{1,0:T(8,128)(2,1)S(1)}, bf16[432,1152]{1,0:T(8,128)(2,1)S(1)}, u32[]{:S(2)}, u32[]{:S(2)}) collective-permute-start(bf16[432,1152]{1,0:T(8,128)(2,1)S(1)} %get-tuple-element.127.refs_2_), channel_id=1, source_target_pairs={{8,16},{12,20},{16,8},{20,12},{9,17},{13,21},{17,9},{21,13},{10,18... | collective-permute-start | bytes 2985992 | tf_op jit(solution)/shard_map/ppermute | solution.py:615
  367.1 19.0 %collective-permute-start.47 = (bf16[304,1280]{1,0:T(8,128)(2,1)S(1)}, bf16[304,1280]{1,0:T(8,128)(2,1)S(1)}, u32[]{:S(2)}, u32[]{:S(2)}) collective-permute-start(bf16[304,1280]{1,0:T(8,128)(2,1)S(1)} %get-tuple-element.130), channel_id=1, source_target_pairs={{0,3},{1,2},{2,1},{3,0},{4,7},{5,6},{6,5},{7,4},{8,11},{9,10},{10,... | collective-permute-start | bytes 2334728 | tf_op jit(solution)/shard_map/ppermute | solution.py:17
  370.4 27.2 %collective-permute-start.51 = (bf16[432,1152]{1,0:T(8,128)(2,1)S(1)}, bf16[432,1152]{1,0:T(8,128)(2,1)S(1)}, u32[]{:S(2)}, u32[]{:S(2)}) collective-permute-start(bf16[432,1152]{1,0:T(8,128)(2,1)S(1)} %get-tuple-element.134.refs_0_), channel_id=1, source_target_pairs={{0,4},{4,0},{8,12},{12,8},{16,20},{20,16},{24,28},{28,24},{1,5},{5... | collective-permute-start | bytes 2985992 | tf_op jit(solution)/shard_map/ppermute | solution.py:17
  370.4 27.3 %collective-permute-start.52 = (bf16[432,1152]{1,0:T(8,128)(2,1)S(1)}, bf16[432,1152]{1,0:T(8,128)(2,1)S(1)}, u32[]{:S(2)}, u32[]{:S(2)}) collective-permute-start(bf16[432,1152]{1,0:T(8,128)(2,1)S(1)} %get-tuple-element.135.refs_1_), channel_id=1, source_target_pairs={{0,4},{4,0},{8,12},{12,8},{16,20},{20,16},{24,28},{28,24},{1,5},{5... | collective-permute-start | bytes 2985992 | tf_op jit(solution)/shard_map/ppermute | solution.py:17
  387.8 24.3 %collective-permute-start.48 = (bf16[432,1152]{1,0:T(8,128)(2,1)S(1)}, bf16[432,1152]{1,0:T(8,128)(2,1)S(1)}, u32[]{:S(2)}, u32[]{:S(2)}) collective-permute-start(bf16[432,1152]{1,0:T(8,128)(2,1)S(1)} %get-tuple-element.131.refs_0_), channel_id=1, source_target_pairs={{8,0},{12,4},{16,24},{20,28},{9,1},{13,5},{17,25},{21,29},{10,2},{... | collective-permute-start | bytes 2985992 | tf_op jit(solution)/shard_map/ppermute | solution.py:615
  389.1 23.0 %collective-permute-start.49 = (bf16[432,1152]{1,0:T(8,128)(2,1)S(1)}, bf16[432,1152]{1,0:T(8,128)(2,1)S(1)}, u32[]{:S(2)}, u32[]{:S(2)}) collective-permute-start(bf16[432,1152]{1,0:T(8,128)(2,1)S(1)} %get-tuple-element.132.refs_2_), channel_id=1, source_target_pairs={{8,16},{12,20},{16,8},{20,12},{9,17},{13,21},{17,9},{21,13},{10,18... | collective-permute-start | bytes 2985992 | tf_op jit(solution)/shard_map/ppermute | solution.py:615
  389.8 21.2 %collective-permute-start.50 = (bf16[304,1280]{1,0:T(8,128)(2,1)S(1)}, bf16[304,1280]{1,0:T(8,128)(2,1)S(1)}, u32[]{:S(2)}, u32[]{:S(2)}) collective-permute-start(bf16[304,1280]{1,0:T(8,128)(2,1)S(1)} %get-tuple-element.133.refs_4_), channel_id=1, source_target_pairs={{0,8},{4,12},{24,16},{28,20},{1,9},{5,13},{25,17},{29,21},{2,10},{... | collective-permute-start | bytes 2334728 | tf_op jit(solution)/shard_map/ppermute | solution.py:615
  412.8 23.4 %collective-permute-start.53 = (bf16[432,1152]{1,0:T(8,128)(2,1)S(1)}, bf16[432,1152]{1,0:T(8,128)(2,1)S(1)}, u32[]{:S(2)}, u32[]{:S(2)}) collective-permute-start(bf16[432,1152]{1,0:T(8,128)(2,1)S(1)} %get-tuple-element.136.refs_0_), channel_id=1, source_target_pairs={{8,0},{12,4},{16,24},{20,28},{9,1},{13,5},{17,25},{21,29},{10,2},{... | collective-permute-start | bytes 2985992 | tf_op jit(solution)/shard_map/ppermute | solution.py:615
  414.8 23.2 %collective-permute-start.58 = (bf16[432,1152]{1,0:T(8,128)(2,1)S(1)}, bf16[432,1152]{1,0:T(8,128)(2,1)S(1)}, u32[]{:S(2)}, u32[]{:S(2)}) collective-permute-start(bf16[432,1152]{1,0:T(8,128)(2,1)S(1)} %get-tuple-element.141.refs_0_), channel_id=1, source_target_pairs={{0,4},{4,0},{8,12},{12,8},{16,20},{20,16},{24,28},{28,24},{1,5},{5... | collective-permute-start | bytes 2985992 | tf_op jit(solution)/shard_map/ppermute | solution.py:17
  436.6 21.6 %collective-permute-start.57 = (bf16[304,1280]{1,0:T(8,128)(2,1)S(1)}, bf16[304,1280]{1,0:T(8,128)(2,1)S(1)}, u32[]{:S(2)}, u32[]{:S(2)}) collective-permute-start(bf16[304,1280]{1,0:T(8,128)(2,1)S(1)} %get-tuple-element.140.refs_0_), channel_id=1, source_target_pairs={{8,0},{12,4},{16,24},{20,28},{9,1},{13,5},{17,25},{21,29},{10,2},{... | collective-permute-start | bytes 2334728 | tf_op jit(solution)/shard_map/ppermute | solution.py:615
  (130 other events, 1025.8 us)

commit v11 on v10

--- a/solution.py
+++ b/solution.py
@@ -976,11 +976,14 @@
     )
     grad_gates[final], grad_uppers[final] = gate_parts[0], upper_parts[0]
     returned[final] = swapped(parts[0], "fsdp", final)
-    other, mine = weight_grad(
-        [[grad_gates[i] for i in range(group)], [grad_uppers[i] for i in range(group)]], ffn_blocks
-    )
-    other = line.advance([waiting.pop(0)] if waiting else [], after(other, *[returned[mask] for mask in masks]))
-    waiting = fresh(["gate", "up"], other, mine)
+    other, mine = weight_grad([[grad_gates[i] for i in range(group)]], ffn_blocks)
+    other = after(other, *[returned[mask] for mask in rings[1:-1]])
+    gate_chunks = fresh(["gate"], other, mine)
+    grad_uppers[0] = line.advance(
+        [waiting.pop(0)] if waiting else [], after(grad_uppers[0], other)
+    )
+    other, mine = weight_grad([[grad_uppers[i] for i in range(group)]], ffn_blocks)
+    waiting = gate_chunks + fresh(["up"], after(other, returned[final]), mine)
 
     def advance(gate=None):
         return line.advance([waiting.pop(0)] if waiting else [], gate)
@@ -996,6 +999,7 @@
         passed_along(grad_far[(hops - step) * rows : (hops - step + 1) * rows], "fsdp", -step)
         for step in range(1, hops + 1)
     ]
+    grad_pair = advance(grad_pair)
     other, mine, grad_in = input_backward(
         grad_pair,
         backs,
@@ -1016,7 +1020,6 @@
     )
     other = advance(other)
     weight_parts = owner_parts(other, mine)
-    weight_parts[0] = advance(weight_parts[0])
     near = [weight_parts[mask] for mask in masks if bin(mask).count("1") == 1]
     while waiting:
         weight_parts[0] = advance(after(weight_parts[0], *near))

time: 475 us -> 469 us (0.987)
  waiting for transfers between devices: 184 us -> 176 us
    ppermute x17, waiting for transfers between devices: 66.8 us -> 49.2 us  [exchanged(): return lax.ppermute(block, 'replica', route)]
    ppermute x40 -> x41, waiting for transfers between devices: 108 us -> 116 us  [swapped(): return lax.ppermute(block, axis, route)]
    unnamed x204 -> x216, local copies, waits for them, and re-layouts: 34.5 us -> 37.1 us
    pallas_call x2 -> x3, Pallas kernels: 23.7 us -> 24.8 us  [weight_grad(): pl.pallas_call(kernel, grid_spec=pltpu.PrefetchScalarGridSpec(num_scalar_...]
    ppermute x40 -> x41, starting transfers between devices: 39.1 us -> 39.9 us  [swapped(): return lax.ppermute(block, axis, route)]
  transfers between devices with their start and end apart: 61 -> 62, of which waited for: 26 -> 27; matrix products, arithmetic and copies ran while one was open for 12% -> 12% of each run, Pallas kernels for 14% -> 16%
where the time goes in v11:
time: 469 us; the launch traced here: 462 us
  waiting for transfers between devices  176 us (38%)
  Pallas kernels  97.5 us (21%)
  starting transfers between devices  82.3 us (18%)
  local copies, waits for them, and re-layouts  51.5 us (11%)
  matrix products  44.7 us (10%)
  other arithmetic  7.84 us (2%)
    ppermute x41, waiting for transfers between devices, swapped(): return lax.ppermute(block, axis, route)  116 us
    ppermute x17, waiting for transfers between devices, exchanged(): return lax.ppermute(block, 'replica', route)  49.2 us
    dot_general x22, matrix products, contract(): lax.dot_general(left, right, (((left_dim,), (right_dim,)), ((), ())), pre...  43.5 us
    ppermute x41, starting transfers between devices, swapped(): return lax.ppermute(block, axis, route)  39.9 us
    unnamed x216, local copies, waits for them, and re-layouts  37.1 us
    ppermute x17, starting transfers between devices, exchanged(): return lax.ppermute(block, 'replica', route)  32.1 us
    pallas_call x3, Pallas kernels, weight_grad(): pl.pallas_call(kernel, grid_spec=pltpu.PrefetchScalarGridSpec(num_scalar_...  24.8 us
    pallas_call x10, Pallas kernels, advance(): pl.pallas_call(kernel, grid_spec=pltpu.PrefetchScalarGridSpec(num_scalar_...  22 us
  transfers between devices with their start and end apart: 62, of which 27 were waited for; matrix products, arithmetic and copies ran while one was open for 12% of the time, Pallas kernels for 16%

profile of v11, /device:TPU:0, one launch (start us, length us, event | category | flops | bytes accessed | tf_op | source)
XLA Modules:
  0.0 462.4 jit_solution(17480047230849822599)
XLA Ops:
  12.6 5.1 %collective-permute-done.refs_1_.refs_3_ = bf16[144,1536]{1,0:T(8,128)(2,1)S(1)} collective-permute-done((bf16[144,1536]{1,0:T(8,128)(2,1)S(1)}, bf16[144,1536]{1,0:T(8,128)(2,1)S(1)}, u32[]{:S(2)}, u32[]{:S(2)}) %collective-permute-start) | collective-permute-done | bytes 442400 | tf_op jit(solution)/shard_map/ppermute | solution.py:17
  17.7 10.3 %collective-permute-done.1.refs_2_.refs_4_ = bf16[144,1536]{1,0:T(8,128)(2,1)} collective-permute-done((bf16[144,1536]{1,0:T(8,128)(2,1)S(1)}, bf16[144,1536]{1,0:T(8,128)(2,1)}, u32[]{:S(2)}, u32[]{:S(2)}) %collective-permute-start.1) | collective-permute-done | bytes 442400 | tf_op jit(solution)/shard_map/ppermute | solution.py:17
  44.3 3.9 collective-permute-start.10
  51.6 9.7 %collective-permute-done.12.refs_2_ = bf16[144,1024]{1,0:T(8,128)(2,1)} collective-permute-done((bf16[144,1024]{1,0:T(8,128)(2,1)S(1)}, bf16[144,1024]{1,0:T(8,128)(2,1)}, u32[]{:S(2)}, u32[]{:S(2)}) %collective-permute-start.12) | collective-permute-done | bytes 294944 | tf_op jit(solution)/shard_map/ppermute | solution.py:17
  63.0 3.6 collective-permute-done.9
  67.9 4.0 attention_forward.1
  82.6 10.8 %collective-permute-done.17.refs_1_ = bf16[256,1152]{1,0:T(8,128)(2,1)} collective-permute-done((bf16[256,1152]{1,0:T(8,128)(2,1)}, bf16[256,1152]{1,0:T(8,128)(2,1)}, u32[]{:S(2)}, u32[]{:S(2)}) %collective-permute-start.17) | collective-permute-done | bytes 589856 | tf_op jit(solution)/shard_map/ppermute | solution.py:17
  97.2 3.7 convolution_bitcast_fusion.10
  124.9 13.5 %collective-permute-done.21 = bf16[256,1152]{1,0:T(8,128)(2,1)S(1)} collective-permute-done((bf16[256,1152]{1,0:T(8,128)(2,1)S(1)}, bf16[256,1152]{1,0:T(8,128)(2,1)S(1)}, u32[]{:S(2)}, u32[]{:S(2)}) %collective-permute-start.21) | collective-permute-done | bytes 589856 | tf_op jit(solution)/shard_map/ppermute | solution.py:17
  149.4 5.8 %collective-permute-done.23.refs_0_.refs_1_ = bf16[256,1152]{1,0:T(8,128)(2,1)S(1)} collective-permute-done((bf16[256,1152]{1,0:T(8,128)(2,1)S(1)}, bf16[256,1152]{1,0:T(8,128)(2,1)S(1)}, u32[]{:S(2)}, u32[]{:S(2)}) %collective-permute-start.23) | collective-permute-done | bytes 589856 | tf_op jit(solution)/shard_map/ppermute | solution.py:17
  155.2 8.1 %collective-permute-start.25 = (bf16[256,1152]{1,0:T(8,128)(2,1)S(1)}, bf16[256,1152]{1,0:T(8,128)(2,1)S(1)}, u32[]{:S(2)}, u32[]{:S(2)}) collective-permute-start(bf16[256,1152]{1,0:T(8,128)(2,1)S(1)} %after.22), channel_id=1, source_target_pairs={{0,3},{1,2},{2,1},{3,0},{4,7},{5,6},{6,5},{7,4},{8,11},{9,10},{10,... | collective-permute-start | bytes 1769480 | tf_op jit(solution)/shard_map/ppermute | solution.py:17
  175.4 7.5 %weight_grad.3 = (bf16[2,432,1152]{2,1,0:T(8,128)(2,1)}, bf16[2,432,1152]{2,1,0:T(8,128)(2,1)}) custom-call(s32[1]{0:T(128)} %bitcast.core_ref, bf16[256,1152]{1,0:T(8,128)(2,1)S(1)} %get-tuple-element.185.refs_0_, bf16[256,1152]{1,0:T(8,128)(2,1)S(1)} %after.20.refs_1_, bf16[256,1152]{1,0:T(8,128)(2,1)S(1)} %after.21.refs_2_, ...), custom_call_target="tpu_custom_call" | custom-call | tf_op jit(solution)/shard_map/weight_grad/pallas_call | solution.py:445
  196.9 10.9 %ffn_backward.1 = (bf16[1728,256]{1,0:T(8,128)(2,1)S(1)}, bf16[1728,256]{1,0:T(8,128)(2,1)S(1)}, bf16[256,1152]{1,0:T(8,128)(2,1)}) custom-call(bf16[256,1152]{1,0:T(8,128)(2,1)S(1)} %copy-done.12, bf16[1728,1152]{1,0:T(8,128)(2,1)} %refs_1_.5, bf16[1728,1152]{1,0:T(8,128)(2,1)} %refs_2_.5, bf16[1728,1152]{1,0:T(8,128)(2,1)} %refs_3_.1, ...), custom_call_target="tpu_custom_call" | custom-call | tf_op jit(solution)/shard_map/ffn_backward/pallas_call | solution.py:195
  208.8 8.7 %weight_grad.4 = (bf16[2,432,1152]{2,1,0:T(8,128)(2,1)}, bf16[2,432,1152]{2,1,0:T(8,128)(2,1)}) custom-call(s32[1]{0:T(128)} %bitcast.core_ref, bf16[256,1152]{1,0:T(8,128)(2,1)S(1)} %copy-done.14, bf16[256,1152]{1,0:T(8,128)(2,1)} %collective-permute-done.17.refs_1_, bf16[256,1152]{1,0:T(8,128)(2,1)} %after.17.refs_2_, bf16[256,1152]{1,0:T(8,128)(2,1)S(1)} %copy-done.26, ...), custom_call_target="tpu_custom_call" | custom-call | tf_op jit(solution)/shard_map/weight_grad/pallas_call | solution.py:445
  225.3 5.2 %collective-permute-start.31 = (bf16[432,1152]{1,0:T(8,128)(2,1)}, bf16[432,1152]{1,0:T(8,128)(2,1)}, u32[]{:S(2)}, u32[]{:S(2)}) collective-permute-start(bf16[432,1152]{1,0:T(8,128)(2,1)} %get-tuple-element.91.refs_2_), channel_id=1, source_target_pairs={{0,8},{4,12},{24,16},{28,20},{1,9},{5,13},{25,17},{29,21},{2,10},{... | collective-permute-start | bytes 2985992 | tf_op jit(solution)/shard_map/ppermute | solution.py:615
  234.7 10.9 %collective-permute-done.33.refs_3_.refs_1_ = bf16[256,1152]{1,0:T(8,128)(2,1)} collective-permute-done((bf16[256,1152]{1,0:T(8,128)(2,1)}, bf16[256,1152]{1,0:T(8,128)(2,1)}, u32[]{:S(2)}, u32[]{:S(2)}) %collective-permute-start.33) | collective-permute-done | bytes 589856 | tf_op jit(solution)/shard_map/ppermute | solution.py:17
  249.7 3.8 resid_backward.1
  255.4 4.1 line_step.12
  261.3 8.7 %weight_grad.5 = (bf16[2,432,1152]{2,1,0:T(8,128)(2,1)}, bf16[2,432,1152]{2,1,0:T(8,128)(2,1)}) custom-call(s32[1]{0:T(128)} %bitcast.core_ref, bf16[256,1152]{1,0:T(8,128)(2,1)S(1)} %copy-done.15, bf16[256,1152]{1,0:T(8,128)(2,1)} %collective-permute-done.17.refs_1_, bf16[256,1152]{1,0:T(8,128)(2,1)} %after.17.refs_2_, bf16[256,1152]{1,0:T(8,128)(2,1)S(1)} %copy-done.27, ...), custom_call_target="tpu_custom_call" | custom-call | tf_op jit(solution)/shard_map/weight_grad/pallas_call | solution.py:445
  271.8 6.6 %attention_backward.1 = (bf16[256,1024]{1,0:T(8,128)(2,1)S(1)}, f32[1,256]{1,0:T(1,128)S(1)}, bf16[512,512]{1,0:T(8,128)(2,1)S(1)}, f32[256,512]{1,0:T(8,128)S(1)}) custom-call(f32[256,1536]{1,0:T(8,128)S(1)} %copy-done.1, bf16[1,256]{1,0:T(2,128)(2,1)S(1)} %broadcast_in_dim_reshape_squeeze.2.gain_ref, f32[256,128]{1,0:T(8,128)S(1)} %copy-done.54, ...), custom_call_target="tpu_custom_call" | custom-call | tf_op jit(solution)/shard_map/attention_backward/pallas_call | solution.py:590
  286.6 3.6 line_step.13
  300.6 5.4 %collective-permute-done.36.refs_1_ = bf16[256,512]{1,0:T(8,128)(2,1)} collective-permute-done((bf16[256,512]{1,0:T(8,128)(2,1)}, bf16[256,512]{1,0:T(8,128)(2,1)}, u32[]{:S(2)}, u32[]{:S(2)}) %collective-permute-start.36) | collective-permute-done | bytes 262176 | tf_op jit(solution)/shard_map/ppermute | solution.py:813
  311.0 8.9 %input_backward.1 = (bf16[4,304,1280]{2,1,0:T(8,128)(2,1)}, bf16[4,304,1280]{2,1,0:T(8,128)(2,1)}, f32[256,1152]{1,0:T(8,128)}) custom-call(s32[1]{0:T(128)} %bitcast.core_ref, f32[256,512]{1,0:T(8,128)S(1)} %get-tuple-element.102.refs_0_, bf16[256,512]{1,0:T(8,128)(2,1)} %collective-permute-done.36.refs_1_, ...), custom_call_target="tpu_custom_call" | custom-call | tf_op jit(solution)/shard_map/input_backward/pallas_call | solution.py:351
  326.9 4.1 collective-permute-done.43.far_ref
  332.7 4.3 collective-permute-start.44
  337.0 17.7 %collective-permute-done.44.refs_1_.refs_6_ = bf16[304,1280]{1,0:T(8,128)(2,1)S(1)} collective-permute-done((bf16[304,1280]{1,0:T(8,128)(2,1)S(1)}, bf16[304,1280]{1,0:T(8,128)(2,1)S(1)}, u32[]{:S(2)}, u32[]{:S(2)}) %collective-permute-start.44) | collective-permute-done | bytes 778272 | tf_op jit(solution)/shard_map/ppermute | solution.py:17
  362.0 18.3 %collective-permute-done.48.refs_8_ = bf16[304,1280]{1,0:T(8,128)(2,1)S(1)} collective-permute-done((bf16[304,1280]{1,0:T(8,128)(2,1)S(1)}, bf16[304,1280]{1,0:T(8,128)(2,1)S(1)}, u32[]{:S(2)}, u32[]{:S(2)}) %collective-permute-start.48) | collective-permute-done | bytes 778272 | tf_op jit(solution)/shard_map/ppermute | solution.py:17
  385.2 8.1 %collective-permute-start.51 = (bf16[304,1280]{1,0:T(8,128)(2,1)S(1)}, bf16[304,1280]{1,0:T(8,128)(2,1)S(1)}, u32[]{:S(2)}, u32[]{:S(2)}) collective-permute-start(bf16[304,1280]{1,0:T(8,128)(2,1)S(1)} %get-tuple-element.137.refs_4_), channel_id=1, source_target_pairs={{0,8},{4,12},{24,16},{28,20},{1,9},{5,13},{25,17},{29,21},{2,10},{... | collective-permute-start | bytes 2334728 | tf_op jit(solution)/shard_map/ppermute | solution.py:615
  393.3 3.6 whole_grad.3.refs_6_
  397.4 10.1 %collective-permute-done.51.refs_5_ = bf16[304,1280]{1,0:T(8,128)(2,1)S(1)} collective-permute-done((bf16[304,1280]{1,0:T(8,128)(2,1)S(1)}, bf16[304,1280]{1,0:T(8,128)(2,1)S(1)}, u32[]{:S(2)}, u32[]{:S(2)}) %collective-permute-start.51) | collective-permute-done | bytes 778272 | tf_op jit(solution)/shard_map/ppermute | solution.py:615
  414.6 18.2 %collective-permute-done.54.refs_1_ = bf16[432,1152]{1,0:T(8,128)(2,1)S(1)} collective-permute-done((bf16[432,1152]{1,0:T(8,128)(2,1)S(1)}, bf16[432,1152]{1,0:T(8,128)(2,1)S(1)}, u32[]{:S(2)}, u32[]{:S(2)}) %collective-permute-start.54) | collective-permute-done | bytes 995360 | tf_op jit(solution)/shard_map/ppermute | solution.py:615
  439.3 15.6 %collective-permute-done.58.refs_1_ = bf16[304,1280]{1,0:T(8,128)(2,1)S(1)} collective-permute-done((bf16[304,1280]{1,0:T(8,128)(2,1)S(1)}, bf16[304,1280]{1,0:T(8,128)(2,1)S(1)}, u32[]{:S(2)}, u32[]{:S(2)}) %collective-permute-start.58) | collective-permute-done | bytes 778272 | tf_op jit(solution)/shard_map/ppermute | solution.py:615
  (430 shorter events, 197.3 us)
Async XLA Ops:
  6.7 21.3 %collective-permute-start.1 = (bf16[144,1536]{1,0:T(8,128)(2,1)S(1)}, bf16[144,1536]{1,0:T(8,128)(2,1)}, u32[]{:S(2)}, u32[]{:S(2)}) collective-permute-start(bf16[144,1536]{1,0:T(8,128)(2,1)S(1)} %pack.2), channel_id=1, source_target_pairs={{0,2},{1,3},{2,0},{3,1},{4,6},{5,7},{6,4},{7,5},{8,10},{9,11},{10,... | collective-permute-start | bytes 1327112 | tf_op jit(solution)/shard_map/ppermute | solution.py:17
  8.2 24.1 %collective-permute-start.5 = (bf16[144,1536]{1,0:T(8,128)(2,1)S(1)}, bf16[144,1536]{1,0:T(8,128)(2,1)}, u32[]{:S(2)}, u32[]{:S(2)}) collective-permute-start(bf16[144,1536]{1,0:T(8,128)(2,1)S(1)} %pack.2), channel_id=1, source_target_pairs={{0,3},{1,2},{2,1},{3,0},{4,7},{5,6},{6,5},{7,4},{8,11},{9,10},{10,... | collective-permute-start | bytes 1327112 | tf_op jit(solution)/shard_map/ppermute | solution.py:17
  42.1 19.2 %collective-permute-start.12 = (bf16[144,1024]{1,0:T(8,128)(2,1)S(1)}, bf16[144,1024]{1,0:T(8,128)(2,1)}, u32[]{:S(2)}, u32[]{:S(2)}) collective-permute-start(bf16[144,1024]{1,0:T(8,128)(2,1)S(1)} %after.15), channel_id=1, source_target_pairs={{0,2},{1,3},{2,0},{3,1},{4,6},{5,7},{6,4},{7,5},{8,10},{9,11},{10,... | collective-permute-start | bytes 884744 | tf_op jit(solution)/shard_map/ppermute | solution.py:17
  51.6 20.3 %collective-permute-start.14 = (bf16[144,1024]{1,0:T(8,128)(2,1)S(1)}, bf16[144,1024]{1,0:T(8,128)(2,1)}, u32[]{:S(2)}, u32[]{:S(2)}) collective-permute-start(bf16[144,1024]{1,0:T(8,128)(2,1)S(1)} %collective-permute-done.11.refs_1_), channel_id=1, source_target_pairs={{0,4},{4,0},{8,12},{12,8},{16,20},{20,16},{24,28},{28,24},{1,5},{5... | collective-permute-start | bytes 884744 | tf_op jit(solution)/shard_map/ppermute | solution.py:17
  105.1 33.4 %collective-permute-start.20 = (bf16[256,1152]{1,0:T(8,128)(2,1)S(1)}, bf16[256,1152]{1,0:T(8,128)(2,1)S(1)}, u32[]{:S(2)}, u32[]{:S(2)}) collective-permute-start(bf16[256,1152]{1,0:T(8,128)(2,1)S(1)} %convolution_convert_fusion.3.refs_1_), channel_id=1, source_target_pairs={{0,1},{1,0},{2,3},{3,2},{4,5},{5,4},{6,7},{7,6},{8,9},{9,8},{10,11... | collective-permute-start | bytes 1769480 | tf_op jit(solution)/shard_map/ppermute | solution.py:17
  112.3 26.1 %collective-permute-start.21 = (bf16[256,1152]{1,0:T(8,128)(2,1)S(1)}, bf16[256,1152]{1,0:T(8,128)(2,1)S(1)}, u32[]{:S(2)}, u32[]{:S(2)}) collective-permute-start(bf16[256,1152]{1,0:T(8,128)(2,1)S(1)} %convolution_convert_fusion.2.refs_1_), channel_id=1, source_target_pairs={{0,2},{1,3},{2,0},{3,1},{4,6},{5,7},{6,4},{7,5},{8,10},{9,11},{10,... | collective-permute-start | bytes 1769480 | tf_op jit(solution)/shard_map/ppermute | solution.py:17
  155.2 20.1 %collective-permute-start.25 = (bf16[256,1152]{1,0:T(8,128)(2,1)S(1)}, bf16[256,1152]{1,0:T(8,128)(2,1)S(1)}, u32[]{:S(2)}, u32[]{:S(2)}) collective-permute-start(bf16[256,1152]{1,0:T(8,128)(2,1)S(1)} %after.22), channel_id=1, source_target_pairs={{0,3},{1,2},{2,1},{3,0},{4,7},{5,6},{6,5},{7,4},{8,11},{9,10},{10,... | collective-permute-start | bytes 1769480 | tf_op jit(solution)/shard_map/ppermute | solution.py:17
  182.8 34.7 %collective-permute-start.28 = (bf16[256,1152]{1,0:T(8,128)(2,1)}, bf16[256,1152]{1,0:T(8,128)(2,1)}, u32[]{:S(2)}, u32[]{:S(2)}) collective-permute-start(bf16[256,1152]{1,0:T(8,128)(2,1)} %fusion.2.refs_1_), channel_id=1, source_target_pairs={{0,1},{1,0},{2,3},{3,2},{4,5},{5,4},{6,7},{7,6},{8,9},{9,8},{10,11... | collective-permute-start | bytes 1769480 | tf_op jit(solution)/shard_map/ppermute | solution.py:17
  182.8 34.7 %collective-permute-start.29 = (bf16[256,1152]{1,0:T(8,128)(2,1)}, bf16[256,1152]{1,0:T(8,128)(2,1)}, u32[]{:S(2)}, u32[]{:S(2)}) collective-permute-start(bf16[256,1152]{1,0:T(8,128)(2,1)} %fusion.3.refs_1_), channel_id=1, source_target_pairs={{0,2},{1,3},{2,0},{3,1},{4,6},{5,7},{6,4},{7,5},{8,10},{9,11},{10,... | collective-permute-start | bytes 1769480 | tf_op jit(solution)/shard_map/ppermute | solution.py:17
  192.9 25.8 %collective-permute-start.27 = (bf16[432,1152]{1,0:T(8,128)(2,1)S(1)}, bf16[432,1152]{1,0:T(8,128)(2,1)S(1)}, u32[]{:S(2)}, u32[]{:S(2)}) collective-permute-start(bf16[432,1152]{1,0:T(8,128)(2,1)S(1)} %get-tuple-element.86.refs_0_), channel_id=1, source_target_pairs={{0,8},{4,12},{24,16},{28,20},{1,9},{5,13},{25,17},{29,21},{2,10},{... | collective-permute-start | bytes 2985992 | tf_op jit(solution)/shard_map/ppermute | solution.py:615
  217.5 37.8 %collective-permute-start.32 = (bf16[2,432,1152]{2,1,0:T(8,128)(2,1)}, bf16[2,432,1152]{2,1,0:T(8,128)(2,1)}, u32[]{:S(2)}, u32[]{:S(2)}) collective-permute-start(bf16[2,432,1152]{2,1,0:T(8,128)(2,1)} %after.24.refs_1_), channel_id=1, source_target_pairs={{0,4},{4,0},{8,12},{12,8},{16,20},{20,16},{24,28},{28,24},{1,5},{5... | collective-permute-start | bytes 5971976 | tf_op jit(solution)/shard_map/ppermute | solution.py:17
  223.6 31.7 %collective-permute-start.30 = (bf16[432,1152]{1,0:T(8,128)(2,1)}, bf16[432,1152]{1,0:T(8,128)(2,1)}, u32[]{:S(2)}, u32[]{:S(2)}) collective-permute-start(bf16[432,1152]{1,0:T(8,128)(2,1)} %get-tuple-element.90.refs_0_), channel_id=1, source_target_pairs={{8,16},{12,20},{16,8},{20,12},{9,17},{13,21},{17,9},{21,13},{10,18... | collective-permute-start | bytes 2985992 | tf_op jit(solution)/shard_map/ppermute | solution.py:615
  225.3 30.1 %collective-permute-start.31 = (bf16[432,1152]{1,0:T(8,128)(2,1)}, bf16[432,1152]{1,0:T(8,128)(2,1)}, u32[]{:S(2)}, u32[]{:S(2)}) collective-permute-start(bf16[432,1152]{1,0:T(8,128)(2,1)} %get-tuple-element.91.refs_2_), channel_id=1, source_target_pairs={{0,8},{4,12},{24,16},{28,20},{1,9},{5,13},{25,17},{29,21},{2,10},{... | collective-permute-start | bytes 2985992 | tf_op jit(solution)/shard_map/ppermute | solution.py:615
  260.5 21.8 %collective-permute-start.34 = (bf16[432,1152]{1,0:T(8,128)(2,1)S(1)}, bf16[432,1152]{1,0:T(8,128)(2,1)S(1)}, u32[]{:S(2)}, u32[]{:S(2)}) collective-permute-start(bf16[432,1152]{1,0:T(8,128)(2,1)S(1)} %get-tuple-element.96), channel_id=1, source_target_pairs={{0,8},{4,12},{24,16},{28,20},{8,0},{12,4},{16,24},{20,28},{1,9},{5... | collective-permute-start | bytes 2985992 | tf_op jit(solution)/shard_map/ppermute | solution.py:615
  260.5 22.7 %collective-permute-start.35 = (bf16[432,1152]{1,0:T(8,128)(2,1)S(1)}, bf16[432,1152]{1,0:T(8,128)(2,1)S(1)}, u32[]{:S(2)}, u32[]{:S(2)}) collective-permute-start(bf16[432,1152]{1,0:T(8,128)(2,1)S(1)} %get-tuple-element.97.refs_2_), channel_id=1, source_target_pairs={{8,16},{12,20},{16,8},{20,12},{9,17},{13,21},{17,9},{21,13},{10,18... | collective-permute-start | bytes 2985992 | tf_op jit(solution)/shard_map/ppermute | solution.py:615
  270.0 49.9 %collective-permute-start.40 = (bf16[2,432,1152]{2,1,0:T(8,128)(2,1)}, bf16[2,432,1152]{2,1,0:T(8,128)(2,1)}, u32[]{:S(2)}, u32[]{:S(2)}) collective-permute-start(bf16[2,432,1152]{2,1,0:T(8,128)(2,1)} %after.26), channel_id=1, source_target_pairs={{0,4},{4,0},{8,12},{12,8},{16,20},{20,16},{24,28},{28,24},{1,5},{5... | collective-permute-start | bytes 5971976 | tf_op jit(solution)/shard_map/ppermute | solution.py:17
  292.3 27.6 %collective-permute-start.38 = (bf16[432,1152]{1,0:T(8,128)(2,1)}, bf16[432,1152]{1,0:T(8,128)(2,1)}, u32[]{:S(2)}, u32[]{:S(2)}) collective-permute-start(bf16[432,1152]{1,0:T(8,128)(2,1)} %get-tuple-element.112), channel_id=1, source_target_pairs={{0,8},{4,12},{24,16},{28,20},{8,0},{12,4},{16,24},{20,28},{1,9},{5... | collective-permute-start | bytes 2985992 | tf_op jit(solution)/shard_map/ppermute | solution.py:615
  294.9 25.0 %collective-permute-start.39 = (bf16[432,1152]{1,0:T(8,128)(2,1)}, bf16[432,1152]{1,0:T(8,128)(2,1)}, u32[]{:S(2)}, u32[]{:S(2)}) collective-permute-start(bf16[432,1152]{1,0:T(8,128)(2,1)} %get-tuple-element.113.refs_2_), channel_id=1, source_target_pairs={{8,16},{12,20},{16,8},{20,12},{9,17},{13,21},{17,9},{21,13},{10,18... | collective-permute-start | bytes 2985992 | tf_op jit(solution)/shard_map/ppermute | solution.py:615
  325.4 30.7 %collective-permute-start.41 = (bf16[432,1152]{1,0:T(8,128)(2,1)S(1)}, bf16[432,1152]{1,0:T(8,128)(2,1)S(1)}, u32[]{:S(2)}, u32[]{:S(2)}) collective-permute-start(bf16[432,1152]{1,0:T(8,128)(2,1)S(1)} %get-tuple-element.121), channel_id=1, source_target_pairs={{0,8},{4,12},{24,16},{28,20},{8,0},{12,4},{16,24},{20,28},{1,9},{5... | collective-permute-start | bytes 2985992 | tf_op jit(solution)/shard_map/ppermute | solution.py:615
  326.2 29.9 %collective-permute-start.42 = (bf16[432,1152]{1,0:T(8,128)(2,1)S(1)}, bf16[432,1152]{1,0:T(8,128)(2,1)S(1)}, u32[]{:S(2)}, u32[]{:S(2)}) collective-permute-start(bf16[432,1152]{1,0:T(8,128)(2,1)S(1)} %get-tuple-element.122.refs_2_), channel_id=1, source_target_pairs={{8,16},{12,20},{16,8},{20,12},{9,17},{13,21},{17,9},{21,13},{10,18... | collective-permute-start | bytes 2985992 | tf_op jit(solution)/shard_map/ppermute | solution.py:615
  332.7 22.0 %collective-permute-start.44 = (bf16[304,1280]{1,0:T(8,128)(2,1)S(1)}, bf16[304,1280]{1,0:T(8,128)(2,1)S(1)}, u32[]{:S(2)}, u32[]{:S(2)}) collective-permute-start(bf16[304,1280]{1,0:T(8,128)(2,1)S(1)} %get-tuple-element.127), channel_id=1, source_target_pairs={{0,1},{1,0},{2,3},{3,2},{4,5},{5,4},{6,7},{7,6},{8,9},{9,8},{10,11... | collective-permute-start | bytes 2334728 | tf_op jit(solution)/shard_map/ppermute | solution.py:17
  337.0 19.1 %collective-permute-start.45 = (bf16[304,1280]{1,0:T(8,128)(2,1)S(1)}, bf16[304,1280]{1,0:T(8,128)(2,1)S(1)}, u32[]{:S(2)}, u32[]{:S(2)}) collective-permute-start(bf16[304,1280]{1,0:T(8,128)(2,1)S(1)} %get-tuple-element.128), channel_id=1, source_target_pairs={{0,2},{1,3},{2,0},{3,1},{4,6},{5,7},{6,4},{7,5},{8,10},{9,11},{10,... | collective-permute-start | bytes 2334728 | tf_op jit(solution)/shard_map/ppermute | solution.py:17
  359.0 23.0 %collective-permute-start.46 = (bf16[432,1152]{1,0:T(8,128)(2,1)S(1)}, bf16[432,1152]{1,0:T(8,128)(2,1)S(1)}, u32[]{:S(2)}, u32[]{:S(2)}) collective-permute-start(bf16[432,1152]{1,0:T(8,128)(2,1)S(1)} %get-tuple-element.130), channel_id=1, source_target_pairs={{0,8},{4,12},{24,16},{28,20},{8,0},{12,4},{16,24},{20,28},{1,9},{5... | collective-permute-start | bytes 2985992 | tf_op jit(solution)/shard_map/ppermute | solution.py:615
  360.6 21.4 %collective-permute-start.47 = (bf16[432,1152]{1,0:T(8,128)(2,1)S(1)}, bf16[432,1152]{1,0:T(8,128)(2,1)S(1)}, u32[]{:S(2)}, u32[]{:S(2)}) collective-permute-start(bf16[432,1152]{1,0:T(8,128)(2,1)S(1)} %get-tuple-element.131.refs_2_), channel_id=1, source_target_pairs={{8,16},{12,20},{16,8},{20,12},{9,17},{13,21},{17,9},{21,13},{10,18... | collective-permute-start | bytes 2985992 | tf_op jit(solution)/shard_map/ppermute | solution.py:615
  361.5 31.8 %collective-permute-start.52 = (bf16[432,1152]{1,0:T(8,128)(2,1)S(1)}, bf16[432,1152]{1,0:T(8,128)(2,1)S(1)}, u32[]{:S(2)}, u32[]{:S(2)}) collective-permute-start(bf16[432,1152]{1,0:T(8,128)(2,1)S(1)} %copy-done.74), channel_id=1, source_target_pairs={{0,4},{4,0},{8,12},{12,8},{16,20},{20,16},{24,28},{28,24},{1,5},{5... | collective-permute-start | bytes 2985992 | tf_op jit(solution)/shard_map/ppermute | solution.py:17
  361.5 31.8 %collective-permute-start.53 = (bf16[432,1152]{1,0:T(8,128)(2,1)S(1)}, bf16[432,1152]{1,0:T(8,128)(2,1)S(1)}, u32[]{:S(2)}, u32[]{:S(2)}) collective-permute-start(bf16[432,1152]{1,0:T(8,128)(2,1)S(1)} %get-tuple-element.139.refs_1_), channel_id=1, source_target_pairs={{0,4},{4,0},{8,12},{12,8},{16,20},{20,16},{24,28},{28,24},{1,5},{5... | collective-permute-start | bytes 2985992 | tf_op jit(solution)/shard_map/ppermute | solution.py:17
  383.2 24.9 %collective-permute-start.49 = (bf16[432,1152]{1,0:T(8,128)(2,1)S(1)}, bf16[432,1152]{1,0:T(8,128)(2,1)S(1)}, u32[]{:S(2)}, u32[]{:S(2)}) collective-permute-start(bf16[432,1152]{1,0:T(8,128)(2,1)S(1)} %get-tuple-element.135.refs_0_), channel_id=1, source_target_pairs={{8,0},{12,4},{16,24},{20,28},{9,1},{13,5},{17,25},{21,29},{10,2},{... | collective-permute-start | bytes 2985992 | tf_op jit(solution)/shard_map/ppermute | solution.py:615
  384.5 23.6 %collective-permute-start.50 = (bf16[432,1152]{1,0:T(8,128)(2,1)S(1)}, bf16[432,1152]{1,0:T(8,128)(2,1)S(1)}, u32[]{:S(2)}, u32[]{:S(2)}) collective-permute-start(bf16[432,1152]{1,0:T(8,128)(2,1)S(1)} %get-tuple-element.136.refs_2_), channel_id=1, source_target_pairs={{8,16},{12,20},{16,8},{20,12},{9,17},{13,21},{17,9},{21,13},{10,18... | collective-permute-start | bytes 2985992 | tf_op jit(solution)/shard_map/ppermute | solution.py:615
  385.2 22.3 %collective-permute-start.51 = (bf16[304,1280]{1,0:T(8,128)(2,1)S(1)}, bf16[304,1280]{1,0:T(8,128)(2,1)S(1)}, u32[]{:S(2)}, u32[]{:S(2)}) collective-permute-start(bf16[304,1280]{1,0:T(8,128)(2,1)S(1)} %get-tuple-element.137.refs_4_), channel_id=1, source_target_pairs={{0,8},{4,12},{24,16},{28,20},{1,9},{5,13},{25,17},{29,21},{2,10},{... | collective-permute-start | bytes 2334728 | tf_op jit(solution)/shard_map/ppermute | solution.py:615
  408.7 24.0 %collective-permute-start.54 = (bf16[432,1152]{1,0:T(8,128)(2,1)S(1)}, bf16[432,1152]{1,0:T(8,128)(2,1)S(1)}, u32[]{:S(2)}, u32[]{:S(2)}) collective-permute-start(bf16[432,1152]{1,0:T(8,128)(2,1)S(1)} %get-tuple-element.140.refs_0_), channel_id=1, source_target_pairs={{8,0},{12,4},{16,24},{20,28},{9,1},{13,5},{17,25},{21,29},{10,2},{... | collective-permute-start | bytes 2985992 | tf_op jit(solution)/shard_map/ppermute | solution.py:615
  410.9 23.6 %collective-permute-start.59 = (bf16[432,1152]{1,0:T(8,128)(2,1)S(1)}, bf16[432,1152]{1,0:T(8,128)(2,1)S(1)}, u32[]{:S(2)}, u32[]{:S(2)}) collective-permute-start(bf16[432,1152]{1,0:T(8,128)(2,1)S(1)} %get-tuple-element.145.refs_0_), channel_id=1, source_target_pairs={{0,4},{4,0},{8,12},{12,8},{16,20},{20,16},{24,28},{28,24},{1,5},{5... | collective-permute-start | bytes 2985992 | tf_op jit(solution)/shard_map/ppermute | solution.py:17
  433.2 21.6 %collective-permute-start.58 = (bf16[304,1280]{1,0:T(8,128)(2,1)S(1)}, bf16[304,1280]{1,0:T(8,128)(2,1)S(1)}, u32[]{:S(2)}, u32[]{:S(2)}) collective-permute-start(bf16[304,1280]{1,0:T(8,128)(2,1)S(1)} %get-tuple-element.144.refs_0_), channel_id=1, source_target_pairs={{8,0},{12,4},{16,24},{20,28},{9,1},{13,5},{17,25},{21,29},{10,2},{... | collective-permute-start | bytes 2334728 | tf_op jit(solution)/shard_map/ppermute | solution.py:615
  (137 other events, 1085.6 us)

commit v12 on v11

--- a/solution.py
+++ b/solution.py
@@ -982,8 +982,9 @@
     grad_uppers[0] = line.advance(
         [waiting.pop(0)] if waiting else [], after(grad_uppers[0], other)
     )
-    other, mine = weight_grad([[grad_uppers[i] for i in range(group)]], ffn_blocks)
-    waiting = gate_chunks + fresh(["up"], after(other, returned[final]), mine)
+    up_other, mine = weight_grad([[grad_uppers[i] for i in range(group)]], ffn_blocks)
+    waiting = gate_chunks + fresh(["up"], up_other, mine)
+    returned[0] = after(returned[0], up_other)
 
     def advance(gate=None):
         return line.advance([waiting.pop(0)] if waiting else [], gate)
@@ -999,7 +1000,7 @@
         passed_along(grad_far[(hops - step) * rows : (hops - step + 1) * rows], "fsdp", -step)
         for step in range(1, hops + 1)
     ]
-    grad_pair = advance(grad_pair)
+    grad_pair = advance(after(grad_pair, *backs))
     other, mine, grad_in = input_backward(
         grad_pair,
         backs,

time: 469 us -> 468 us (level)
    ppermute x41, waiting for transfers between devices: 116 us -> 108 us  [swapped(): return lax.ppermute(block, axis, route)]
    ppermute x17, starting transfers between devices: 32.1 us -> 40 us  [exchanged(): return lax.ppermute(block, 'replica', route)]
    unnamed x216 -> x202, local copies, waits for them, and re-layouts: 37.1 us -> 35.6 us
  transfers between devices with their start and end apart: 62 -> 62, of which waited for: 27 -> 28; matrix products, arithmetic and copies ran while one was open for 12% -> 12% of each run, Pallas kernels for 16% -> 16%
where the time goes in v12:
time: 468 us; the launch traced here: 462 us
  waiting for transfers between devices  173 us (37%)
  Pallas kernels  97.3 us (21%)
  starting transfers between devices  85.9 us (18%)
  local copies, waits for them, and re-layouts  51.1 us (11%)
  matrix products  44.6 us (10%)
  other arithmetic  7.84 us (2%)
    ppermute x41, waiting for transfers between devices, swapped(): return lax.ppermute(block, axis, route)  108 us
    ppermute x17, waiting for transfers between devices, exchanged(): return lax.ppermute(block, 'replica', route)  51.1 us
    dot_general x22, matrix products, contract(): lax.dot_general(left, right, (((left_dim,), (right_dim,)), ((), ())), pre...  43.4 us
    ppermute x17, starting transfers between devices, exchanged(): return lax.ppermute(block, 'replica', route)  40 us
    ppermute x41, starting transfers between devices, swapped(): return lax.ppermute(block, axis, route)  36 us
    unnamed x202, local copies, waits for them, and re-layouts  35.6 us
    pallas_call x3, Pallas kernels, weight_grad(): pl.pallas_call(kernel, grid_spec=pltpu.PrefetchScalarGridSpec(num_scalar_...  25.3 us
    pallas_call x10, Pallas kernels, advance(): pl.pallas_call(kernel, grid_spec=pltpu.PrefetchScalarGridSpec(num_scalar_...  21.6 us
  transfers between devices with their start and end apart: 62, of which 28 were waited for; matrix products, arithmetic and copies ran while one was open for 12% of the time, Pallas kernels for 16%

profile of v12, /device:TPU:0, one launch (start us, length us, event | category | flops | bytes accessed | tf_op | source)
XLA Modules:
  0.0 462.0 jit_solution(8582625101674557745)
XLA Ops:
  12.6 5.1 %collective-permute-done.refs_1_.refs_3_ = bf16[144,1536]{1,0:T(8,128)(2,1)S(1)} collective-permute-done((bf16[144,1536]{1,0:T(8,128)(2,1)S(1)}, bf16[144,1536]{1,0:T(8,128)(2,1)S(1)}, u32[]{:S(2)}, u32[]{:S(2)}) %collective-permute-start) | collective-permute-done | bytes 442400 | tf_op jit(solution)/shard_map/ppermute | solution.py:17
  17.7 10.3 %collective-permute-done.1.refs_2_.refs_4_ = bf16[144,1536]{1,0:T(8,128)(2,1)} collective-permute-done((bf16[144,1536]{1,0:T(8,128)(2,1)S(1)}, bf16[144,1536]{1,0:T(8,128)(2,1)}, u32[]{:S(2)}, u32[]{:S(2)}) %collective-permute-start.1) | collective-permute-done | bytes 442400 | tf_op jit(solution)/shard_map/ppermute | solution.py:17
  44.3 3.9 collective-permute-start.10
  51.6 9.7 %collective-permute-done.12.refs_2_ = bf16[144,1024]{1,0:T(8,128)(2,1)} collective-permute-done((bf16[144,1024]{1,0:T(8,128)(2,1)S(1)}, bf16[144,1024]{1,0:T(8,128)(2,1)}, u32[]{:S(2)}, u32[]{:S(2)}) %collective-permute-start.12) | collective-permute-done | bytes 294944 | tf_op jit(solution)/shard_map/ppermute | solution.py:17
  63.0 3.6 collective-permute-done.9
  67.9 4.0 attention_forward.1
  82.6 10.8 %collective-permute-done.17.refs_1_ = bf16[256,1152]{1,0:T(8,128)(2,1)} collective-permute-done((bf16[256,1152]{1,0:T(8,128)(2,1)}, bf16[256,1152]{1,0:T(8,128)(2,1)}, u32[]{:S(2)}, u32[]{:S(2)}) %collective-permute-start.17) | collective-permute-done | bytes 589856 | tf_op jit(solution)/shard_map/ppermute | solution.py:17
  97.2 3.7 convolution_bitcast_fusion.10
  124.9 13.5 %collective-permute-done.21 = bf16[256,1152]{1,0:T(8,128)(2,1)S(1)} collective-permute-done((bf16[256,1152]{1,0:T(8,128)(2,1)S(1)}, bf16[256,1152]{1,0:T(8,128)(2,1)S(1)}, u32[]{:S(2)}, u32[]{:S(2)}) %collective-permute-start.21) | collective-permute-done | bytes 589856 | tf_op jit(solution)/shard_map/ppermute | solution.py:17
  149.3 6.8 %collective-permute-done.23.refs_0_.refs_1_ = bf16[256,1152]{1,0:T(8,128)(2,1)S(1)} collective-permute-done((bf16[256,1152]{1,0:T(8,128)(2,1)S(1)}, bf16[256,1152]{1,0:T(8,128)(2,1)S(1)}, u32[]{:S(2)}, u32[]{:S(2)}) %collective-permute-start.23) | collective-permute-done | bytes 589856 | tf_op jit(solution)/shard_map/ppermute | solution.py:17
  156.1 5.1 %collective-permute-done.24.refs_0_.refs_2_ = bf16[256,1152]{1,0:T(8,128)(2,1)S(1)} collective-permute-done((bf16[256,1152]{1,0:T(8,128)(2,1)S(1)}, bf16[256,1152]{1,0:T(8,128)(2,1)S(1)}, u32[]{:S(2)}, u32[]{:S(2)}) %collective-permute-start.24) | collective-permute-done | bytes 589856 | tf_op jit(solution)/shard_map/ppermute | solution.py:17
  174.7 7.5 %weight_grad.3 = (bf16[2,432,1152]{2,1,0:T(8,128)(2,1)}, bf16[2,432,1152]{2,1,0:T(8,128)(2,1)}) custom-call(s32[1]{0:T(128)} %bitcast.core_ref, bf16[256,1152]{1,0:T(8,128)(2,1)S(1)} %get-tuple-element.185.refs_0_, bf16[256,1152]{1,0:T(8,128)(2,1)S(1)} %after.21.refs_1_, bf16[256,1152]{1,0:T(8,128)(2,1)S(1)} %after.22.refs_2_, ...), custom_call_target="tpu_custom_call" | custom-call | tf_op jit(solution)/shard_map/weight_grad/pallas_call | solution.py:445
  196.9 11.0 %ffn_backward.1 = (bf16[1728,256]{1,0:T(8,128)(2,1)S(1)}, bf16[1728,256]{1,0:T(8,128)(2,1)S(1)}, bf16[256,1152]{1,0:T(8,128)(2,1)}) custom-call(bf16[256,1152]{1,0:T(8,128)(2,1)S(1)} %copy-done.12, bf16[1728,1152]{1,0:T(8,128)(2,1)} %refs_1_.5, bf16[1728,1152]{1,0:T(8,128)(2,1)} %refs_2_.5, bf16[1728,1152]{1,0:T(8,128)(2,1)} %refs_3_.1, ...), custom_call_target="tpu_custom_call" | custom-call | tf_op jit(solution)/shard_map/ffn_backward/pallas_call | solution.py:195
  207.9 9.0 %weight_grad.4 = (bf16[2,432,1152]{2,1,0:T(8,128)(2,1)}, bf16[2,432,1152]{2,1,0:T(8,128)(2,1)}) custom-call(s32[1]{0:T(128)} %bitcast.core_ref, bf16[256,1152]{1,0:T(8,128)(2,1)S(1)} %copy-done.14, bf16[256,1152]{1,0:T(8,128)(2,1)} %collective-permute-done.17.refs_1_, bf16[256,1152]{1,0:T(8,128)(2,1)} %after.18.refs_2_, bf16[256,1152]{1,0:T(8,128)(2,1)S(1)} %copy-done.26, ...), custom_call_target="tpu_custom_call" | custom-call | tf_op jit(solution)/shard_map/weight_grad/pallas_call | solution.py:445
  224.6 5.7 %collective-permute-start.31 = (bf16[432,1152]{1,0:T(8,128)(2,1)}, bf16[432,1152]{1,0:T(8,128)(2,1)}, u32[]{:S(2)}, u32[]{:S(2)}) collective-permute-start(bf16[432,1152]{1,0:T(8,128)(2,1)} %get-tuple-element.91.refs_2_), channel_id=1, source_target_pairs={{0,8},{4,12},{24,16},{28,20},{1,9},{5,13},{25,17},{29,21},{2,10},{... | collective-permute-start | bytes 2985992 | tf_op jit(solution)/shard_map/ppermute | solution.py:615
  241.4 8.8 %weight_grad.5 = (bf16[2,432,1152]{2,1,0:T(8,128)(2,1)}, bf16[2,432,1152]{2,1,0:T(8,128)(2,1)}) custom-call(s32[1]{0:T(128)} %bitcast.core_ref, bf16[256,1152]{1,0:T(8,128)(2,1)S(1)} %copy-done.15, bf16[256,1152]{1,0:T(8,128)(2,1)} %collective-permute-done.17.refs_1_, bf16[256,1152]{1,0:T(8,128)(2,1)} %after.18.refs_2_, bf16[256,1152]{1,0:T(8,128)(2,1)S(1)} %copy-done.27, ...), custom_call_target="tpu_custom_call" | custom-call | tf_op jit(solution)/shard_map/weight_grad/pallas_call | solution.py:445
  251.6 3.6 resid_backward.1
  258.3 3.7 line_step.12
  263.0 6.6 %attention_backward.1 = (bf16[256,1024]{1,0:T(8,128)(2,1)S(1)}, f32[1,256]{1,0:T(1,128)S(1)}, bf16[512,512]{1,0:T(8,128)(2,1)S(1)}, f32[256,512]{1,0:T(8,128)S(1)}) custom-call(f32[256,1536]{1,0:T(8,128)S(1)} %copy-done.1, bf16[1,256]{1,0:T(2,128)(2,1)S(1)} %broadcast_in_dim_reshape_squeeze.2.gain_ref, f32[256,128]{1,0:T(8,128)S(1)} %copy-done.54, ...), custom_call_target="tpu_custom_call" | custom-call | tf_op jit(solution)/shard_map/attention_backward/pallas_call | solution.py:590
  272.3 8.0 %collective-permute-done.36.refs_1_ = bf16[256,512]{1,0:T(8,128)(2,1)S(1)} collective-permute-done((bf16[256,512]{1,0:T(8,128)(2,1)S(1)}, bf16[256,512]{1,0:T(8,128)(2,1)S(1)}, u32[]{:S(2)}, u32[]{:S(2)}) %collective-permute-start.36) | collective-permute-done | bytes 262176 | tf_op jit(solution)/shard_map/ppermute | solution.py:813
  284.5 3.6 line_step.13
  291.1 3.6 collective-permute-start.38
  303.3 8.8 %input_backward.1 = (bf16[4,304,1280]{2,1,0:T(8,128)(2,1)}, bf16[4,304,1280]{2,1,0:T(8,128)(2,1)}, f32[256,1152]{1,0:T(8,128)}) custom-call(s32[1]{0:T(128)} %bitcast.core_ref, f32[256,512]{1,0:T(8,128)S(1)} %get-tuple-element.106.refs_0_, bf16[256,512]{1,0:T(8,128)(2,1)S(1)} %collective-permute-done.36.refs_1_, ...), custom_call_target="tpu_custom_call" | custom-call | tf_op jit(solution)/shard_map/input_backward/pallas_call | solution.py:351
  320.7 3.7 collective-permute-start.41
  328.0 6.2 %collective-permute-start.44 = (bf16[304,1280]{1,0:T(8,128)(2,1)S(1)}, bf16[304,1280]{1,0:T(8,128)(2,1)S(1)}, u32[]{:S(2)}, u32[]{:S(2)}) collective-permute-start(bf16[304,1280]{1,0:T(8,128)(2,1)S(1)} %get-tuple-element.127), channel_id=1, source_target_pairs={{0,1},{1,0},{2,3},{3,2},{4,5},{5,4},{6,7},{7,6},{8,9},{9,8},{10,11... | collective-permute-start | bytes 2334728 | tf_op jit(solution)/shard_map/ppermute | solution.py:17
  334.2 17.7 %collective-permute-done.44.refs_1_.refs_6_ = bf16[304,1280]{1,0:T(8,128)(2,1)S(1)} collective-permute-done((bf16[304,1280]{1,0:T(8,128)(2,1)S(1)}, bf16[304,1280]{1,0:T(8,128)(2,1)S(1)}, u32[]{:S(2)}, u32[]{:S(2)}) %collective-permute-start.44) | collective-permute-done | bytes 778272 | tf_op jit(solution)/shard_map/ppermute | solution.py:17
  356.2 3.7 collective-permute-start.46
  361.3 18.3 %collective-permute-done.48.refs_8_ = bf16[304,1280]{1,0:T(8,128)(2,1)S(1)} collective-permute-done((bf16[304,1280]{1,0:T(8,128)(2,1)S(1)}, bf16[304,1280]{1,0:T(8,128)(2,1)S(1)}, u32[]{:S(2)}, u32[]{:S(2)}) %collective-permute-start.48) | collective-permute-done | bytes 778272 | tf_op jit(solution)/shard_map/ppermute | solution.py:17
  384.3 8.4 %collective-permute-start.51 = (bf16[304,1280]{1,0:T(8,128)(2,1)S(1)}, bf16[304,1280]{1,0:T(8,128)(2,1)S(1)}, u32[]{:S(2)}, u32[]{:S(2)}) collective-permute-start(bf16[304,1280]{1,0:T(8,128)(2,1)S(1)} %get-tuple-element.137.refs_4_), channel_id=1, source_target_pairs={{0,8},{4,12},{24,16},{28,20},{1,9},{5,13},{25,17},{29,21},{2,10},{... | collective-permute-start | bytes 2334728 | tf_op jit(solution)/shard_map/ppermute | solution.py:615
  396.7 10.4 %collective-permute-done.51.refs_5_ = bf16[304,1280]{1,0:T(8,128)(2,1)S(1)} collective-permute-done((bf16[304,1280]{1,0:T(8,128)(2,1)S(1)}, bf16[304,1280]{1,0:T(8,128)(2,1)S(1)}, u32[]{:S(2)}, u32[]{:S(2)}) %collective-permute-start.51) | collective-permute-done | bytes 778272 | tf_op jit(solution)/shard_map/ppermute | solution.py:615
  413.9 18.5 %collective-permute-done.54.refs_1_ = bf16[432,1152]{1,0:T(8,128)(2,1)S(1)} collective-permute-done((bf16[432,1152]{1,0:T(8,128)(2,1)S(1)}, bf16[432,1152]{1,0:T(8,128)(2,1)S(1)}, u32[]{:S(2)}, u32[]{:S(2)}) %collective-permute-start.54) | collective-permute-done | bytes 995360 | tf_op jit(solution)/shard_map/ppermute | solution.py:615
  438.9 15.6 %collective-permute-done.58.refs_1_ = bf16[304,1280]{1,0:T(8,128)(2,1)S(1)} collective-permute-done((bf16[304,1280]{1,0:T(8,128)(2,1)S(1)}, bf16[304,1280]{1,0:T(8,128)(2,1)S(1)}, u32[]{:S(2)}, u32[]{:S(2)}) %collective-permute-start.58) | collective-permute-done | bytes 778272 | tf_op jit(solution)/shard_map/ppermute | solution.py:615
  (417 shorter events, 200.9 us)
Async XLA Ops:
  6.7 21.3 %collective-permute-start.1 = (bf16[144,1536]{1,0:T(8,128)(2,1)S(1)}, bf16[144,1536]{1,0:T(8,128)(2,1)}, u32[]{:S(2)}, u32[]{:S(2)}) collective-permute-start(bf16[144,1536]{1,0:T(8,128)(2,1)S(1)} %pack.2), channel_id=1, source_target_pairs={{0,2},{1,3},{2,0},{3,1},{4,6},{5,7},{6,4},{7,5},{8,10},{9,11},{10,... | collective-permute-start | bytes 1327112 | tf_op jit(solution)/shard_map/ppermute | solution.py:17
  8.2 24.1 %collective-permute-start.5 = (bf16[144,1536]{1,0:T(8,128)(2,1)S(1)}, bf16[144,1536]{1,0:T(8,128)(2,1)}, u32[]{:S(2)}, u32[]{:S(2)}) collective-permute-start(bf16[144,1536]{1,0:T(8,128)(2,1)S(1)} %pack.2), channel_id=1, source_target_pairs={{0,3},{1,2},{2,1},{3,0},{4,7},{5,6},{6,5},{7,4},{8,11},{9,10},{10,... | collective-permute-start | bytes 1327112 | tf_op jit(solution)/shard_map/ppermute | solution.py:17
  42.1 19.2 %collective-permute-start.12 = (bf16[144,1024]{1,0:T(8,128)(2,1)S(1)}, bf16[144,1024]{1,0:T(8,128)(2,1)}, u32[]{:S(2)}, u32[]{:S(2)}) collective-permute-start(bf16[144,1024]{1,0:T(8,128)(2,1)S(1)} %after.16), channel_id=1, source_target_pairs={{0,2},{1,3},{2,0},{3,1},{4,6},{5,7},{6,4},{7,5},{8,10},{9,11},{10,... | collective-permute-start | bytes 884744 | tf_op jit(solution)/shard_map/ppermute | solution.py:17
  51.6 20.3 %collective-permute-start.14 = (bf16[144,1024]{1,0:T(8,128)(2,1)S(1)}, bf16[144,1024]{1,0:T(8,128)(2,1)}, u32[]{:S(2)}, u32[]{:S(2)}) collective-permute-start(bf16[144,1024]{1,0:T(8,128)(2,1)S(1)} %collective-permute-done.11.refs_1_), channel_id=1, source_target_pairs={{0,4},{4,0},{8,12},{12,8},{16,20},{20,16},{24,28},{28,24},{1,5},{5... | collective-permute-start | bytes 884744 | tf_op jit(solution)/shard_map/ppermute | solution.py:17
  105.1 33.4 %collective-permute-start.20 = (bf16[256,1152]{1,0:T(8,128)(2,1)S(1)}, bf16[256,1152]{1,0:T(8,128)(2,1)S(1)}, u32[]{:S(2)}, u32[]{:S(2)}) collective-permute-start(bf16[256,1152]{1,0:T(8,128)(2,1)S(1)} %convolution_convert_fusion.3.refs_1_), channel_id=1, source_target_pairs={{0,1},{1,0},{2,3},{3,2},{4,5},{5,4},{6,7},{7,6},{8,9},{9,8},{10,11... | collective-permute-start | bytes 1769480 | tf_op jit(solution)/shard_map/ppermute | solution.py:17
  112.3 26.2 %collective-permute-start.21 = (bf16[256,1152]{1,0:T(8,128)(2,1)S(1)}, bf16[256,1152]{1,0:T(8,128)(2,1)S(1)}, u32[]{:S(2)}, u32[]{:S(2)}) collective-permute-start(bf16[256,1152]{1,0:T(8,128)(2,1)S(1)} %convolution_convert_fusion.2.refs_1_), channel_id=1, source_target_pairs={{0,2},{1,3},{2,0},{3,1},{4,6},{5,7},{6,4},{7,5},{8,10},{9,11},{10,... | collective-permute-start | bytes 1769480 | tf_op jit(solution)/shard_map/ppermute | solution.py:17
  182.1 34.7 %collective-permute-start.28 = (bf16[256,1152]{1,0:T(8,128)(2,1)}, bf16[256,1152]{1,0:T(8,128)(2,1)}, u32[]{:S(2)}, u32[]{:S(2)}) collective-permute-start(bf16[256,1152]{1,0:T(8,128)(2,1)} %fusion.2.refs_1_), channel_id=1, source_target_pairs={{0,1},{1,0},{2,3},{3,2},{4,5},{5,4},{6,7},{7,6},{8,9},{9,8},{10,11... | collective-permute-start | bytes 1769480 | tf_op jit(solution)/shard_map/ppermute | solution.py:17
  182.4 34.5 %collective-permute-start.29 = (bf16[256,1152]{1,0:T(8,128)(2,1)}, bf16[256,1152]{1,0:T(8,128)(2,1)}, u32[]{:S(2)}, u32[]{:S(2)}) collective-permute-start(bf16[256,1152]{1,0:T(8,128)(2,1)} %fusion.3.refs_1_), channel_id=1, source_target_pairs={{0,2},{1,3},{2,0},{3,1},{4,6},{5,7},{6,4},{7,5},{8,10},{9,11},{10,... | collective-permute-start | bytes 1769480 | tf_op jit(solution)/shard_map/ppermute | solution.py:17
  192.2 25.9 %collective-permute-start.27 = (bf16[432,1152]{1,0:T(8,128)(2,1)S(1)}, bf16[432,1152]{1,0:T(8,128)(2,1)S(1)}, u32[]{:S(2)}, u32[]{:S(2)}) collective-permute-start(bf16[432,1152]{1,0:T(8,128)(2,1)S(1)} %get-tuple-element.86.refs_0_), channel_id=1, source_target_pairs={{0,8},{4,12},{24,16},{28,20},{1,9},{5,13},{25,17},{29,21},{2,10},{... | collective-permute-start | bytes 2985992 | tf_op jit(solution)/shard_map/ppermute | solution.py:615
  216.9 41.3 %collective-permute-start.32 = (bf16[2,432,1152]{2,1,0:T(8,128)(2,1)}, bf16[2,432,1152]{2,1,0:T(8,128)(2,1)}, u32[]{:S(2)}, u32[]{:S(2)}) collective-permute-start(bf16[2,432,1152]{2,1,0:T(8,128)(2,1)} %after.25.refs_1_), channel_id=1, source_target_pairs={{0,4},{4,0},{8,12},{12,8},{16,20},{20,16},{24,28},{28,24},{1,5},{5... | collective-permute-start | bytes 5971976 | tf_op jit(solution)/shard_map/ppermute | solution.py:17
  223.0 35.2 %collective-permute-start.30 = (bf16[432,1152]{1,0:T(8,128)(2,1)}, bf16[432,1152]{1,0:T(8,128)(2,1)}, u32[]{:S(2)}, u32[]{:S(2)}) collective-permute-start(bf16[432,1152]{1,0:T(8,128)(2,1)} %get-tuple-element.90.refs_0_), channel_id=1, source_target_pairs={{8,16},{12,20},{16,8},{20,12},{9,17},{13,21},{17,9},{21,13},{10,18... | collective-permute-start | bytes 2985992 | tf_op jit(solution)/shard_map/ppermute | solution.py:615
  224.6 33.6 %collective-permute-start.31 = (bf16[432,1152]{1,0:T(8,128)(2,1)}, bf16[432,1152]{1,0:T(8,128)(2,1)}, u32[]{:S(2)}, u32[]{:S(2)}) collective-permute-start(bf16[432,1152]{1,0:T(8,128)(2,1)} %get-tuple-element.91.refs_2_), channel_id=1, source_target_pairs={{0,8},{4,12},{24,16},{28,20},{1,9},{5,13},{25,17},{29,21},{2,10},{... | collective-permute-start | bytes 2985992 | tf_op jit(solution)/shard_map/ppermute | solution.py:615
  230.3 19.9 %collective-permute-start.33 = (bf16[256,1152]{1,0:T(8,128)(2,1)}, bf16[256,1152]{1,0:T(8,128)(2,1)}, u32[]{:S(2)}, u32[]{:S(2)}) collective-permute-start(bf16[256,1152]{1,0:T(8,128)(2,1)} %get-tuple-element.96), channel_id=1, source_target_pairs={{0,3},{1,2},{2,1},{3,0},{4,7},{5,6},{6,5},{7,4},{8,11},{9,10},{10,... | collective-permute-start | bytes 1769480 | tf_op jit(solution)/shard_map/ppermute | solution.py:17
  262.0 22.5 %collective-permute-start.34 = (bf16[432,1152]{1,0:T(8,128)(2,1)S(1)}, bf16[432,1152]{1,0:T(8,128)(2,1)S(1)}, u32[]{:S(2)}, u32[]{:S(2)}) collective-permute-start(bf16[432,1152]{1,0:T(8,128)(2,1)S(1)} %get-tuple-element.99), channel_id=1, source_target_pairs={{0,8},{4,12},{24,16},{28,20},{8,0},{12,4},{16,24},{20,28},{1,9},{5... | collective-permute-start | bytes 2985992 | tf_op jit(solution)/shard_map/ppermute | solution.py:615
  262.1 22.4 %collective-permute-start.35 = (bf16[432,1152]{1,0:T(8,128)(2,1)S(1)}, bf16[432,1152]{1,0:T(8,128)(2,1)S(1)}, u32[]{:S(2)}, u32[]{:S(2)}) collective-permute-start(bf16[432,1152]{1,0:T(8,128)(2,1)S(1)} %get-tuple-element.100.refs_2_), channel_id=1, source_target_pairs={{8,16},{12,20},{16,8},{20,12},{9,17},{13,21},{17,9},{21,13},{10,18... | collective-permute-start | bytes 2985992 | tf_op jit(solution)/shard_map/ppermute | solution.py:615
  262.8 49.2 %collective-permute-start.40 = (bf16[2,432,1152]{2,1,0:T(8,128)(2,1)}, bf16[2,432,1152]{2,1,0:T(8,128)(2,1)}, u32[]{:S(2)}, u32[]{:S(2)}) collective-permute-start(bf16[2,432,1152]{2,1,0:T(8,128)(2,1)} %get-tuple-element.95.refs_1_), channel_id=1, source_target_pairs={{0,4},{4,0},{8,12},{12,8},{16,20},{20,16},{24,28},{28,24},{1,5},{5... | collective-permute-start | bytes 5971976 | tf_op jit(solution)/shard_map/ppermute | solution.py:17
  291.1 24.1 %collective-permute-start.38 = (bf16[432,1152]{1,0:T(8,128)(2,1)}, bf16[432,1152]{1,0:T(8,128)(2,1)}, u32[]{:S(2)}, u32[]{:S(2)}) collective-permute-start(bf16[432,1152]{1,0:T(8,128)(2,1)} %get-tuple-element.115), channel_id=1, source_target_pairs={{0,8},{4,12},{24,16},{28,20},{8,0},{12,4},{16,24},{20,28},{1,9},{5... | collective-permute-start | bytes 2985992 | tf_op jit(solution)/shard_map/ppermute | solution.py:615
  294.7 20.5 %collective-permute-start.39 = (bf16[432,1152]{1,0:T(8,128)(2,1)}, bf16[432,1152]{1,0:T(8,128)(2,1)}, u32[]{:S(2)}, u32[]{:S(2)}) collective-permute-start(bf16[432,1152]{1,0:T(8,128)(2,1)} %get-tuple-element.116.refs_2_), channel_id=1, source_target_pairs={{8,16},{12,20},{16,8},{20,12},{9,17},{13,21},{17,9},{21,13},{10,18... | collective-permute-start | bytes 2985992 | tf_op jit(solution)/shard_map/ppermute | solution.py:615
  320.7 32.6 %collective-permute-start.41 = (bf16[432,1152]{1,0:T(8,128)(2,1)S(1)}, bf16[432,1152]{1,0:T(8,128)(2,1)S(1)}, u32[]{:S(2)}, u32[]{:S(2)}) collective-permute-start(bf16[432,1152]{1,0:T(8,128)(2,1)S(1)} %get-tuple-element.121), channel_id=1, source_target_pairs={{0,8},{4,12},{24,16},{28,20},{8,0},{12,4},{16,24},{20,28},{1,9},{5... | collective-permute-start | bytes 2985992 | tf_op jit(solution)/shard_map/ppermute | solution.py:615
  324.4 29.0 %collective-permute-start.42 = (bf16[432,1152]{1,0:T(8,128)(2,1)S(1)}, bf16[432,1152]{1,0:T(8,128)(2,1)S(1)}, u32[]{:S(2)}, u32[]{:S(2)}) collective-permute-start(bf16[432,1152]{1,0:T(8,128)(2,1)S(1)} %get-tuple-element.122.refs_2_), channel_id=1, source_target_pairs={{8,16},{12,20},{16,8},{20,12},{9,17},{13,21},{17,9},{21,13},{10,18... | collective-permute-start | bytes 2985992 | tf_op jit(solution)/shard_map/ppermute | solution.py:615
  328.0 23.9 %collective-permute-start.44 = (bf16[304,1280]{1,0:T(8,128)(2,1)S(1)}, bf16[304,1280]{1,0:T(8,128)(2,1)S(1)}, u32[]{:S(2)}, u32[]{:S(2)}) collective-permute-start(bf16[304,1280]{1,0:T(8,128)(2,1)S(1)} %get-tuple-element.127), channel_id=1, source_target_pairs={{0,1},{1,0},{2,3},{3,2},{4,5},{5,4},{6,7},{7,6},{8,9},{9,8},{10,11... | collective-permute-start | bytes 2334728 | tf_op jit(solution)/shard_map/ppermute | solution.py:17
  334.2 19.1 %collective-permute-start.45 = (bf16[304,1280]{1,0:T(8,128)(2,1)S(1)}, bf16[304,1280]{1,0:T(8,128)(2,1)S(1)}, u32[]{:S(2)}, u32[]{:S(2)}) collective-permute-start(bf16[304,1280]{1,0:T(8,128)(2,1)S(1)} %get-tuple-element.128), channel_id=1, source_target_pairs={{0,2},{1,3},{2,0},{3,1},{4,6},{5,7},{6,4},{7,5},{8,10},{9,11},{10,... | collective-permute-start | bytes 2334728 | tf_op jit(solution)/shard_map/ppermute | solution.py:17
  356.2 24.9 %collective-permute-start.46 = (bf16[432,1152]{1,0:T(8,128)(2,1)S(1)}, bf16[432,1152]{1,0:T(8,128)(2,1)S(1)}, u32[]{:S(2)}, u32[]{:S(2)}) collective-permute-start(bf16[432,1152]{1,0:T(8,128)(2,1)S(1)} %get-tuple-element.130), channel_id=1, source_target_pairs={{0,8},{4,12},{24,16},{28,20},{8,0},{12,4},{16,24},{20,28},{1,9},{5... | collective-permute-start | bytes 2985992 | tf_op jit(solution)/shard_map/ppermute | solution.py:615
  359.9 21.2 %collective-permute-start.47 = (bf16[432,1152]{1,0:T(8,128)(2,1)S(1)}, bf16[432,1152]{1,0:T(8,128)(2,1)S(1)}, u32[]{:S(2)}, u32[]{:S(2)}) collective-permute-start(bf16[432,1152]{1,0:T(8,128)(2,1)S(1)} %get-tuple-element.131.refs_2_), channel_id=1, source_target_pairs={{8,16},{12,20},{16,8},{20,12},{9,17},{13,21},{17,9},{21,13},{10,18... | collective-permute-start | bytes 2985992 | tf_op jit(solution)/shard_map/ppermute | solution.py:615
  360.7 31.9 %collective-permute-start.52 = (bf16[432,1152]{1,0:T(8,128)(2,1)S(1)}, bf16[432,1152]{1,0:T(8,128)(2,1)S(1)}, u32[]{:S(2)}, u32[]{:S(2)}) collective-permute-start(bf16[432,1152]{1,0:T(8,128)(2,1)S(1)} %copy-done.68), channel_id=1, source_target_pairs={{0,4},{4,0},{8,12},{12,8},{16,20},{20,16},{24,28},{28,24},{1,5},{5... | collective-permute-start | bytes 2985992 | tf_op jit(solution)/shard_map/ppermute | solution.py:17
  360.8 31.9 %collective-permute-start.53 = (bf16[432,1152]{1,0:T(8,128)(2,1)S(1)}, bf16[432,1152]{1,0:T(8,128)(2,1)S(1)}, u32[]{:S(2)}, u32[]{:S(2)}) collective-permute-start(bf16[432,1152]{1,0:T(8,128)(2,1)S(1)} %get-tuple-element.139.refs_1_), channel_id=1, source_target_pairs={{0,4},{4,0},{8,12},{12,8},{16,20},{20,16},{24,28},{28,24},{1,5},{5... | collective-permute-start | bytes 2985992 | tf_op jit(solution)/shard_map/ppermute | solution.py:17
  382.2 25.2 %collective-permute-start.49 = (bf16[432,1152]{1,0:T(8,128)(2,1)S(1)}, bf16[432,1152]{1,0:T(8,128)(2,1)S(1)}, u32[]{:S(2)}, u32[]{:S(2)}) collective-permute-start(bf16[432,1152]{1,0:T(8,128)(2,1)S(1)} %get-tuple-element.135.refs_0_), channel_id=1, source_target_pairs={{8,0},{12,4},{16,24},{20,28},{9,1},{13,5},{17,25},{21,29},{10,2},{... | collective-permute-start | bytes 2985992 | tf_op jit(solution)/shard_map/ppermute | solution.py:615
  383.5 23.9 %collective-permute-start.50 = (bf16[432,1152]{1,0:T(8,128)(2,1)S(1)}, bf16[432,1152]{1,0:T(8,128)(2,1)S(1)}, u32[]{:S(2)}, u32[]{:S(2)}) collective-permute-start(bf16[432,1152]{1,0:T(8,128)(2,1)S(1)} %get-tuple-element.136.refs_2_), channel_id=1, source_target_pairs={{8,16},{12,20},{16,8},{20,12},{9,17},{13,21},{17,9},{21,13},{10,18... | collective-permute-start | bytes 2985992 | tf_op jit(solution)/shard_map/ppermute | solution.py:615
  384.3 22.9 %collective-permute-start.51 = (bf16[304,1280]{1,0:T(8,128)(2,1)S(1)}, bf16[304,1280]{1,0:T(8,128)(2,1)S(1)}, u32[]{:S(2)}, u32[]{:S(2)}) collective-permute-start(bf16[304,1280]{1,0:T(8,128)(2,1)S(1)} %get-tuple-element.137.refs_4_), channel_id=1, source_target_pairs={{0,8},{4,12},{24,16},{28,20},{1,9},{5,13},{25,17},{29,21},{2,10},{... | collective-permute-start | bytes 2334728 | tf_op jit(solution)/shard_map/ppermute | solution.py:615
  408.1 24.3 %collective-permute-start.54 = (bf16[432,1152]{1,0:T(8,128)(2,1)S(1)}, bf16[432,1152]{1,0:T(8,128)(2,1)S(1)}, u32[]{:S(2)}, u32[]{:S(2)}) collective-permute-start(bf16[432,1152]{1,0:T(8,128)(2,1)S(1)} %get-tuple-element.140.refs_0_), channel_id=1, source_target_pairs={{8,0},{12,4},{16,24},{20,28},{9,1},{13,5},{17,25},{21,29},{10,2},{... | collective-permute-start | bytes 2985992 | tf_op jit(solution)/shard_map/ppermute | solution.py:615
  410.3 23.9 %collective-permute-start.59 = (bf16[432,1152]{1,0:T(8,128)(2,1)S(1)}, bf16[432,1152]{1,0:T(8,128)(2,1)S(1)}, u32[]{:S(2)}, u32[]{:S(2)}) collective-permute-start(bf16[432,1152]{1,0:T(8,128)(2,1)S(1)} %get-tuple-element.145.refs_0_), channel_id=1, source_target_pairs={{0,4},{4,0},{8,12},{12,8},{16,20},{20,16},{24,28},{28,24},{1,5},{5... | collective-permute-start | bytes 2985992 | tf_op jit(solution)/shard_map/ppermute | solution.py:17
  432.8 21.6 %collective-permute-start.58 = (bf16[304,1280]{1,0:T(8,128)(2,1)S(1)}, bf16[304,1280]{1,0:T(8,128)(2,1)S(1)}, u32[]{:S(2)}, u32[]{:S(2)}) collective-permute-start(bf16[304,1280]{1,0:T(8,128)(2,1)S(1)} %get-tuple-element.144.refs_0_), channel_id=1, source_target_pairs={{8,0},{12,4},{16,24},{20,28},{9,1},{13,5},{17,25},{21,29},{10,2},{... | collective-permute-start | bytes 2334728 | tf_op jit(solution)/shard_map/ppermute | solution.py:615
  (130 other events, 1017.6 us)
